TPU v7x, 512 devices: a whole 4x4x16 slice. The times are simulated.
512 devices in a mesh: lat: 32 (over z, core), dep: 16 (over y, x).
Axes of the slice: x: 4, y: 4, z: 16, core: 2. Of those that a mesh axis runs over, the one named last changes fastest.
Arguments:
- pressure_prev: float32 [128, 2048, 512], P('dep', 'lat'), may hold values from -6 to 6
- pressure_now: float32 [128, 2048, 512], P('dep', 'lat'), may hold values from -6 to 6
- materials: int32 [128, 2048, 512], P('dep', 'lat'), may hold values from 0 to 15
- courant_table: float32 [16], replicated, may hold values from 0.1 to 0.45
- tf_weights: float32 [4, 8], replicated, may hold values from 0.05 to 1.5
- source_cell: int32 [3], replicated, may hold values from 0 to 2047, as said below
- start_step: int32 [1], replicated, may hold values from 0 to 23
Outputs:
- pressure: float32 [128, 2048, 512], P('dep', 'lat')
- image: float32 [4, 2048, 512], P(None, 'lat', 'dep')
Inputs may be any that keep to these rules, and one draw needn't show every extreme that they name: source_cell holds a depth index below 128, an x index below 2048 and a y index below 512; along the dimension with the most cells (depth first on ties, then x) the index is that dimension's last cell.
All inputs are finite; a program needn't handle non-finite values.
Results may differ from a plain program's by a relative error of at most 0.000051.
Values sent between devices are 32-bit elements; how exact they have to be, the bound alone decides.
No kernel may reach another device: no remote copies, remote signals or barrier semaphores. Data moves between devices by JAX's collectives and lax.ppermute only.
A program may use at most 64 MiB of HBM per device.

v0:
```python
import jax
import jax.numpy as jnp
from jax import lax
from jax.sharding import PartitionSpec as P

STEPS = 3
MATS = 16
BUMPS = 8


def with_halo(value, sides, width):
    for axis, dim in sides:
        size, length = (lax.axis_size(axis), value.shape[dim])
        up = [(i, (i + 1) % size) for i in range(size - 1)]
        down = [(j, i) for i, j in up]
        last = lax.slice_in_dim(value, length - width, length, axis=dim)
        first = lax.slice_in_dim(value, 0, width, axis=dim)
        before = lax.ppermute(last, axis, up)
        after = lax.ppermute(first, axis, down)
        value = jnp.concatenate([before, value, after], axis=dim)
    return value


def laplace_inner(extended):
    core = extended[2:-2, 2:-2, :]
    ypadded = jnp.pad(core, ((0, 0), (0, 0), (2, 2)))
    total = 3.0 * -2.5 * core
    total = total + 4.0 / 3.0 * (extended[3:-1, 2:-2, :] + extended[1:-3, 2:-2, :])
    total = total - 1.0 / 12.0 * (extended[4:, 2:-2, :] + extended[:-4, 2:-2, :])
    total = total + 4.0 / 3.0 * (extended[2:-2, 3:-1, :] + extended[2:-2, 1:-3, :])
    total = total - 1.0 / 12.0 * (extended[2:-2, 4:, :] + extended[2:-2, :-4, :])
    total = total + 4.0 / 3.0 * (ypadded[:, :, 3:-1] + ypadded[:, :, 1:-3])
    total = total - 1.0 / 12.0 * (ypadded[:, :, 4:] + ypadded[:, :, :-4])
    return total


def wavelet(level):
    shifted = 0.3 * (level.astype(jnp.float32) - 10.0)
    return 4.0 * (1.0 - 2.0 * shifted * shifted) * jnp.exp(-shifted * shifted)


def render_terms(field, tf_weights):
    colours = [jnp.zeros_like(field) for channel in range(3)]
    extinct = jnp.zeros_like(field)
    for bump_index in range(BUMPS):
        centre = -3.0 + 6.0 * bump_index / (BUMPS - 1)
        scaled = (field - centre) / 0.8
        bump = jnp.exp(-scaled * scaled)
        colours = [
            colours[channel] + tf_weights[channel, bump_index] * bump for channel in range(3)
        ]
        extinct = extinct + tf_weights[3, bump_index] * bump
    return (colours, extinct)


def point_source(shape, source_cell, depth_start, lateral_start, amplitude):
    depth_ids = lax.broadcasted_iota(jnp.int32, shape, 0) + depth_start
    lateral_ids = lax.broadcasted_iota(jnp.int32, shape, 1) + lateral_start
    column_ids = lax.broadcasted_iota(jnp.int32, shape, 2)
    struck = (
        (depth_ids == source_cell[0])
        & (lateral_ids == source_cell[1])
        & (column_ids == source_cell[2])
    )
    return jnp.where(struck, amplitude, jnp.float32(0.0))


def on_device(
    pressure_prev, pressure_now, materials, courant_table, tf_weights, source_cell, start_step
):
    depth_cells, lateral_cells, columns = pressure_now.shape
    depth_count = lax.axis_size("dep")
    depth_base = lax.axis_index("dep") * depth_cells
    lateral_base = lax.axis_index("lat") * lateral_cells
    squared = courant_table * courant_table
    stiffness = jnp.zeros(pressure_now.shape, jnp.float32)
    for material in range(MATS):
        stiffness = jnp.where(materials == material, squared[material], stiffness)
    previous, current = (pressure_prev, pressure_now)
    for sweep_index in range(STEPS):
        extended = with_halo(current, (("lat", 1), ("dep", 0)), 2)
        advanced = 2.0 * current - previous + stiffness * laplace_inner(extended)
        amplitude = wavelet(start_step[0] + sweep_index)
        advanced = advanced + point_source(
            advanced.shape, source_cell, depth_base, lateral_base, amplitude
        )
        previous, current = (current, advanced)
    colours, extinct = render_terms(current, tf_weights)
    sigma = extinct * (1.5 / (depth_cells * depth_count))
    prefix = jnp.cumsum(sigma, axis=0) - sigma
    weight = jnp.exp(-prefix) * (1.0 - jnp.exp(-sigma))
    slab_depth = jnp.sum(sigma, axis=0)
    slab_colour = jnp.stack(
        [
            jnp.sum(weight * colours[0], axis=0),
            jnp.sum(weight * colours[1], axis=0),
            jnp.sum(weight * colours[2], axis=0),
        ]
    )
    partials = jnp.concatenate([slab_colour, slab_depth[None]], axis=0)[None]
    received = lax.all_to_all(partials, "dep", split_axis=3, concat_axis=0, tiled=True)
    depths = received[:, 3]
    before = jnp.cumsum(depths, axis=0) - depths
    attenuation = jnp.exp(-before)
    colour = jnp.sum(attenuation[:, None] * received[:, :3], axis=0)
    opacity = 1.0 - jnp.exp(-jnp.sum(depths, axis=0))
    image = jnp.concatenate([colour, opacity[None]], axis=0)
    return (current, image)


def solution(mesh):
    in_specs = (
        P("dep", "lat", None),
        P("dep", "lat", None),
        P("dep", "lat", None),
        P(),
        P(),
        P(),
        P(),
    )
    out_specs = (P("dep", "lat", None), P(None, "lat", "dep"))
    return jax.shard_map(
        on_device, mesh=mesh, in_specs=in_specs, out_specs=out_specs, check_vma=False
    )
```

profile of v0, /device:TPU:1, one launch (start us, length us, event | category | flops | bytes accessed | tf_op | source)
XLA Modules:
  0.0 166.8 jit_solution(18314503596916764977)
XLA Ops:
  0.6 1.1 fusion.82
  1.7 4.9 %collective-permute-start = (f32[8,2,512]{2,1,0:T(2,128)S(1)}, f32[8,2,512]{2,1,0:T(2,128)S(1)}, u32[]{:S(2)}, u32[]{:S(2)}) collective-permute-start(f32[8,2,512]{2,1,0:T(2,128)S(1)} %get-tuple-element.26), channel_id=1, source_target_pairs={{0,16},{16,32},{32,48},{48,64},{64,80},{80,96},{96,112},{112,128},... | collective-permute-start | bytes 98312 | tf_op jit(solution)/shard_map/ppermute | solution.py:18
  6.7 5.1 %collective-permute-start.1 = (f32[8,2,512]{2,1,0:T(2,128)S(1)}, f32[8,2,512]{2,1,0:T(2,128)S(1)}, u32[]{:S(2)}, u32[]{:S(2)}) collective-permute-start(f32[8,2,512]{2,1,0:T(2,128)S(1)} %get-tuple-element.25), channel_id=1, source_target_pairs={{16,0},{32,16},{48,32},{64,48},{80,64},{96,80},{112,96},{128,112},... | collective-permute-start | bytes 98312 | tf_op jit(solution)/shard_map/ppermute | solution.py:19
  13.3 1.4 fusion.86
  16.0 1.1 pad_maximum_fusion.16
  17.1 1.3 collective-permute-start.2
  18.4 4.0 %collective-permute-start.3 = (f32[2,68,512]{2,1,0:T(8,128)S(1)}, f32[2,68,512]{2,1,0:T(8,128)S(1)}, u32[]{:S(2)}, u32[]{:S(2)}) collective-permute-start(f32[2,68,512]{2,1,0:T(8,128)S(1)} %get-tuple-element.20), channel_id=1, source_target_pairs={{0,1},{1,2},{2,3},{3,4},{4,5},{5,6},{6,7},{7,8},{8,9},{9,10},{10,1... | collective-permute-start | bytes 835592 | tf_op jit(solution)/shard_map/ppermute | solution.py:18
  24.0 3.8 %collective-permute-done.2 = f32[2,68,512]{2,1,0:T(8,128)S(1)} collective-permute-done((f32[2,68,512]{2,1,0:T(8,128)S(1)}, f32[2,68,512]{2,1,0:T(8,128)S(1)}, u32[]{:S(2)}, u32[]{:S(2)}) %collective-permute-start.2) | collective-permute-done | bytes 278560 | tf_op jit(solution)/shard_map/ppermute | solution.py:19
  27.7 1.4 collective-permute-done.3
  29.6 12.9 %fusion.38 = f32[8,64,512]{2,1,0:T(8,128)S(1)} fusion(f32[8,2,512]{2,1,0:T(2,128)S(1)} %collective-permute-done, f32[8,64,512]{2,1,0:T(8,128)S(1)} %copy-done, f32[8,66,512]{2,1,0:T(8,128)S(1)} %constant_dynamic-update-slice_fusion, f32[10,68,512]{2,1,0:T(8,128)S(1)} %get-tuple-element.18, f32[10,68,512]{2,1,0:T(8,128)S(1)} %get-tuple-element.17, ...), kind=kLoop, calls=%fused_computation.77 | loop fusion | flops 15990784 | bytes 10519180 | tf_op jit(solution)/shard_map/add | solution.py:84
  42.5 1.9 %collective-permute-start.4 = (f32[8,2,512]{2,1,0:T(2,128)S(1)}, f32[8,2,512]{2,1,0:T(2,128)S(1)}, u32[]{:S(2)}, u32[]{:S(2)}) collective-permute-start(f32[8,2,512]{2,1,0:T(2,128)S(1)} %get-tuple-element.24), channel_id=1, source_target_pairs={{0,16},{16,32},{32,48},{48,64},{64,80},{80,96},{96,112},{112,128},... | collective-permute-start | bytes 98312 | tf_op jit(solution)/shard_map/ppermute | solution.py:18
  44.4 2.4 %collective-permute-start.5 = (f32[8,2,512]{2,1,0:T(2,128)S(1)}, f32[8,2,512]{2,1,0:T(2,128)S(1)}, u32[]{:S(2)}, u32[]{:S(2)}) collective-permute-start(f32[8,2,512]{2,1,0:T(2,128)S(1)} %get-tuple-element.23), channel_id=1, source_target_pairs={{16,0},{32,16},{48,32},{64,48},{80,64},{96,80},{112,96},{128,112},... | collective-permute-start | bytes 98312 | tf_op jit(solution)/shard_map/ppermute | solution.py:19
  46.8 2.8 %collective-permute-done.5 = f32[8,2,512]{2,1,0:T(2,128)S(1)} collective-permute-done((f32[8,2,512]{2,1,0:T(2,128)S(1)}, f32[8,2,512]{2,1,0:T(2,128)S(1)}, u32[]{:S(2)}, u32[]{:S(2)}) %collective-permute-start.5) | collective-permute-done | bytes 32800 | tf_op jit(solution)/shard_map/ppermute | solution.py:19
  49.7 1.3 collective-permute-start.6
  51.0 4.8 %collective-permute-start.7 = (f32[2,68,512]{2,1,0:T(8,128)S(1)}, f32[2,68,512]{2,1,0:T(8,128)S(1)}, u32[]{:S(2)}, u32[]{:S(2)}) collective-permute-start(f32[2,68,512]{2,1,0:T(8,128)S(1)} %get-tuple-element.16), channel_id=1, source_target_pairs={{0,1},{1,2},{2,3},{3,4},{4,5},{5,6},{6,7},{7,8},{8,9},{9,10},{10,1... | collective-permute-start | bytes 835592 | tf_op jit(solution)/shard_map/ppermute | solution.py:18
  55.9 3.8 %collective-permute-done.6 = f32[2,68,512]{2,1,0:T(8,128)S(1)} collective-permute-done((f32[2,68,512]{2,1,0:T(8,128)S(1)}, f32[2,68,512]{2,1,0:T(8,128)S(1)}, u32[]{:S(2)}, u32[]{:S(2)}) %collective-permute-start.6) | collective-permute-done | bytes 278560 | tf_op jit(solution)/shard_map/ppermute | solution.py:19
  59.7 1.8 %collective-permute-done.7 = f32[2,68,512]{2,1,0:T(8,128)S(1)} collective-permute-done((f32[2,68,512]{2,1,0:T(8,128)S(1)}, f32[2,68,512]{2,1,0:T(8,128)S(1)}, u32[]{:S(2)}, u32[]{:S(2)}) %collective-permute-start.7) | collective-permute-done | bytes 278560 | tf_op jit(solution)/shard_map/ppermute | solution.py:18
  61.9 13.0 %fusion.27 = f32[8,64,512]{2,1,0:T(8,128)S(1)} fusion(f32[8,2,512]{2,1,0:T(2,128)S(1)} %collective-permute-done.4, f32[8,64,512]{2,1,0:T(8,128)S(1)} %fusion.38, f32[8,2,512]{2,1,0:T(2,128)S(1)} %collective-permute-done.5, f32[10,68,512]{2,1,0:T(8,128)S(1)} %get-tuple-element.14, f32[10,68,512]{2,1,0:T(8,128)S(1)} %get-tuple-element.13, ...), kind=kLoop, calls=%fused_computation.66 | loop fusion | flops 16515072 | bytes 8454796 | tf_op jit(solution)/shard_map/add | solution.py:84
  74.9 3.8 %collective-permute-start.8 = (f32[8,2,512]{2,1,0:T(2,128)S(1)}, f32[8,2,512]{2,1,0:T(2,128)S(1)}, u32[]{:S(2)}, u32[]{:S(2)}) collective-permute-start(f32[8,2,512]{2,1,0:T(2,128)S(1)} %get-tuple-element.22), channel_id=1, source_target_pairs={{0,16},{16,32},{32,48},{48,64},{64,80},{80,96},{96,112},{112,128},... | collective-permute-start | bytes 98312 | tf_op jit(solution)/shard_map/ppermute | solution.py:18
  78.7 1.9 %collective-permute-start.9 = (f32[8,2,512]{2,1,0:T(2,128)S(1)}, f32[8,2,512]{2,1,0:T(2,128)S(1)}, u32[]{:S(2)}, u32[]{:S(2)}) collective-permute-start(f32[8,2,512]{2,1,0:T(2,128)S(1)} %get-tuple-element.21), channel_id=1, source_target_pairs={{16,0},{32,16},{48,32},{64,48},{80,64},{96,80},{112,96},{128,112},... | collective-permute-start | bytes 98312 | tf_op jit(solution)/shard_map/ppermute | solution.py:19
  80.7 3.3 %collective-permute-done.9 = f32[8,2,512]{2,1,0:T(2,128)S(1)} collective-permute-done((f32[8,2,512]{2,1,0:T(2,128)S(1)}, f32[8,2,512]{2,1,0:T(2,128)S(1)}, u32[]{:S(2)}, u32[]{:S(2)}) %collective-permute-start.9) | collective-permute-done | bytes 32800 | tf_op jit(solution)/shard_map/ppermute | solution.py:19
  84.1 1.3 collective-permute-start.10
  85.4 4.8 %collective-permute-start.11 = (f32[2,68,512]{2,1,0:T(8,128)S(1)}, f32[2,68,512]{2,1,0:T(8,128)S(1)}, u32[]{:S(2)}, u32[]{:S(2)}) collective-permute-start(f32[2,68,512]{2,1,0:T(8,128)S(1)} %get-tuple-element.12), channel_id=1, source_target_pairs={{0,1},{1,2},{2,3},{3,4},{4,5},{5,6},{6,7},{7,8},{8,9},{9,10},{10,1... | collective-permute-start | bytes 835592 | tf_op jit(solution)/shard_map/ppermute | solution.py:18
  91.6 1.9 %collective-permute-done.10 = f32[2,68,512]{2,1,0:T(8,128)S(1)} collective-permute-done((f32[2,68,512]{2,1,0:T(8,128)S(1)}, f32[2,68,512]{2,1,0:T(8,128)S(1)}, u32[]{:S(2)}, u32[]{:S(2)}) %collective-permute-start.10) | collective-permute-done | bytes 278560 | tf_op jit(solution)/shard_map/ppermute | solution.py:19
  93.5 1.8 %collective-permute-done.11 = f32[2,68,512]{2,1,0:T(8,128)S(1)} collective-permute-done((f32[2,68,512]{2,1,0:T(8,128)S(1)}, f32[2,68,512]{2,1,0:T(8,128)S(1)}, u32[]{:S(2)}, u32[]{:S(2)}) %collective-permute-start.11) | collective-permute-done | bytes 278560 | tf_op jit(solution)/shard_map/ppermute | solution.py:18
  95.6 20.4 %fusion.78 = (f32[64,512]{1,0:T(8,128)S(1)}, f32[8,64,512]{2,1,0:T(8,128)S(1)}, f32[8,64,512]{2,1,0:T(8,128)S(1)}) fusion(f32[]{:T(128)} %bitcast.32, f32[]{:T(128)} %bitcast.31, f32[]{:T(128)} %bitcast.30, f32[]{:T(128)} %bitcast.29, f32[]{:T(128)} %bitcast.28, f32[]{:T(128)} %bitcast.27, f32[]{:T(128)} %bitcast.26, f32[]{:T(128)} %bitcast.25, ...), kind=kLoop, calls=%fused_computation.152 | loop fusion | flops 29327360 | bytes 9634476 | tf_op jit(solution)/shard_map/reduce_sum | solution.py:92
  116.0 14.4 %multiply_reduce_fusion.2 = (f32[64,512]{1,0:T(8,128)S(1)}, f32[64,512]{1,0:T(8,128)S(1)}, f32[8,64,512]{2,1,0:T(8,128)S(1)}) fusion(f32[]{:T(128)} %bitcast.40, f32[]{:T(128)} %bitcast.39, f32[]{:T(128)} %bitcast.38, f32[]{:T(128)} %bitcast.37, f32[]{:T(128)} %bitcast.36, f32[]{:T(128)} %bitcast.35, f32[]{:T(128)} %bitcast.34, f32[]{:T(128)} %bitcast.33, ...), kind=kOutput, calls=%fused_computation.129 | output fusion | flops 20381696 | bytes 3407936 | tf_op jit(solution)/shard_map/jit(cumsum)/reduce_window_sum | solution.py:90
  130.5 7.1 %multiply_reduce_fusion.1 = f32[64,512]{1,0:T(8,128)S(1)} fusion(f32[8,64,512]{2,1,0:T(8,128)S(1)} %get-tuple-element.78, f32[]{:T(128)} %bitcast.49, f32[]{:T(128)} %bitcast.48, f32[]{:T(128)} %bitcast.47, f32[]{:T(128)} %bitcast.46, f32[]{:T(128)} %bitcast.45, f32[]{:T(128)} %bitcast.44, f32[]{:T(128)} %bitcast.43, f32[]{:T(128)} %bitcast.42, ...), kind=kLoop, calls=%fused_computation.128 | loop fusion | flops 12812288 | bytes 2228256 | tf_op jit(solution)/shard_map/reduce_sum | solution.py:96
  138.0 1.0 reshape.64
  139.0 22.7 %all_to_all.18 = f32[16,1,8192]{2,1,0:T(1,128)S(1)} all-to-all(f32[16,1,8192]{2,1,0:T(1,128)S(1)} %reshape.64), channel_id=1, replica_groups=mesh['lat'=32,'dep'=16] {'dep'}, dimensions={0} | all-to-all | bytes 1048576 | tf_op jit(solution)/shard_map/all_to_all | solution.py:101
  162.2 1.9 %reduce.1 = f32[16,8192]{1,0:T(8,128)S(1)} reduce(f32[16,1,8192]{2,1,0:T(1,128)S(1)} %all_to_all.18, f32[]{:T(128)} %broadcast.254), dimensions={1}, to_apply=%all_to_all.13.reduce_sub_computation | reduce | bytes 1048580 | tf_op jit(solution)/shard_map/all_to_all | solution.py:101
  164.8 0.8 copy.12
  (44 shorter events, 9.2 us)
Async XLA Ops:
  0.6 23.2 %copy-start = (f32[8,64,512]{2,1,0:T(8,128)S(1)}, f32[8,64,512]{2,1,0:T(8,128)}, u32[]{:S(2)}) copy-start(f32[8,64,512]{2,1,0:T(8,128)} %param.8) | copy-start | bytes 3145732
  1.7 14.3 %collective-permute-start = (f32[8,2,512]{2,1,0:T(2,128)S(1)}, f32[8,2,512]{2,1,0:T(2,128)S(1)}, u32[]{:S(2)}, u32[]{:S(2)}) collective-permute-start(f32[8,2,512]{2,1,0:T(2,128)S(1)} %get-tuple-element.26), channel_id=1, source_target_pairs={{0,16},{16,32},{32,48},{48,64},{64,80},{80,96},{96,112},{112,128},... | collective-permute-start | bytes 98312 | tf_op jit(solution)/shard_map/ppermute | solution.py:18
  6.7 9.3 %collective-permute-start.1 = (f32[8,2,512]{2,1,0:T(2,128)S(1)}, f32[8,2,512]{2,1,0:T(2,128)S(1)}, u32[]{:S(2)}, u32[]{:S(2)}) collective-permute-start(f32[8,2,512]{2,1,0:T(2,128)S(1)} %get-tuple-element.25), channel_id=1, source_target_pairs={{16,0},{32,16},{48,32},{64,48},{80,64},{96,80},{112,96},{128,112},... | collective-permute-start | bytes 98312 | tf_op jit(solution)/shard_map/ppermute | solution.py:19
  17.1 10.6 %collective-permute-start.2 = (f32[2,68,512]{2,1,0:T(8,128)S(1)}, f32[2,68,512]{2,1,0:T(8,128)S(1)}, u32[]{:S(2)}, u32[]{:S(2)}) collective-permute-start(f32[2,68,512]{2,1,0:T(8,128)S(1)} %get-tuple-element.19), channel_id=1, source_target_pairs={{1,0},{2,1},{3,2},{4,3},{5,4},{6,5},{7,6},{8,7},{9,8},{10,9},{11,1... | collective-permute-start | bytes 835592 | tf_op jit(solution)/shard_map/ppermute | solution.py:19
  18.4 10.7 %collective-permute-start.3 = (f32[2,68,512]{2,1,0:T(8,128)S(1)}, f32[2,68,512]{2,1,0:T(8,128)S(1)}, u32[]{:S(2)}, u32[]{:S(2)}) collective-permute-start(f32[2,68,512]{2,1,0:T(8,128)S(1)} %get-tuple-element.20), channel_id=1, source_target_pairs={{0,1},{1,2},{2,3},{3,4},{4,5},{5,6},{6,7},{7,8},{8,9},{9,10},{10,1... | collective-permute-start | bytes 835592 | tf_op jit(solution)/shard_map/ppermute | solution.py:18
  23.9 5.6 %copy-start.1 = (s32[8,64,512]{2,1,0:T(8,128)S(1)}, s32[8,64,512]{2,1,0:T(8,128)}, u32[]{:S(2)}) copy-start(s32[8,64,512]{2,1,0:T(8,128)} %param.9) | copy-start | bytes 3145732
  23.9 5.6 %copy-start.4 = (f32[8,64,512]{2,1,0:T(8,128)S(1)}, f32[8,64,512]{2,1,0:T(8,128)}, u32[]{:S(2)}) copy-start(f32[8,64,512]{2,1,0:T(8,128)} %param.7) | copy-start | bytes 3145732
  42.5 4.3 %collective-permute-start.4 = (f32[8,2,512]{2,1,0:T(2,128)S(1)}, f32[8,2,512]{2,1,0:T(2,128)S(1)}, u32[]{:S(2)}, u32[]{:S(2)}) collective-permute-start(f32[8,2,512]{2,1,0:T(2,128)S(1)} %get-tuple-element.24), channel_id=1, source_target_pairs={{0,16},{16,32},{32,48},{48,64},{64,80},{80,96},{96,112},{112,128},... | collective-permute-start | bytes 98312 | tf_op jit(solution)/shard_map/ppermute | solution.py:18
  44.4 5.2 %collective-permute-start.5 = (f32[8,2,512]{2,1,0:T(2,128)S(1)}, f32[8,2,512]{2,1,0:T(2,128)S(1)}, u32[]{:S(2)}, u32[]{:S(2)}) collective-permute-start(f32[8,2,512]{2,1,0:T(2,128)S(1)} %get-tuple-element.23), channel_id=1, source_target_pairs={{16,0},{32,16},{48,32},{64,48},{80,64},{96,80},{112,96},{128,112},... | collective-permute-start | bytes 98312 | tf_op jit(solution)/shard_map/ppermute | solution.py:19
  49.7 9.9 %collective-permute-start.6 = (f32[2,68,512]{2,1,0:T(8,128)S(1)}, f32[2,68,512]{2,1,0:T(8,128)S(1)}, u32[]{:S(2)}, u32[]{:S(2)}) collective-permute-start(f32[2,68,512]{2,1,0:T(8,128)S(1)} %get-tuple-element.15), channel_id=1, source_target_pairs={{1,0},{2,1},{3,2},{4,3},{5,4},{6,5},{7,6},{8,7},{9,8},{10,9},{11,1... | collective-permute-start | bytes 835592 | tf_op jit(solution)/shard_map/ppermute | solution.py:19
  51.0 10.4 %collective-permute-start.7 = (f32[2,68,512]{2,1,0:T(8,128)S(1)}, f32[2,68,512]{2,1,0:T(8,128)S(1)}, u32[]{:S(2)}, u32[]{:S(2)}) collective-permute-start(f32[2,68,512]{2,1,0:T(8,128)S(1)} %get-tuple-element.16), channel_id=1, source_target_pairs={{0,1},{1,2},{2,3},{3,4},{4,5},{5,6},{6,7},{7,8},{8,9},{9,10},{10,1... | collective-permute-start | bytes 835592 | tf_op jit(solution)/shard_map/ppermute | solution.py:18
  55.9 6.0 %copy-start.2 = (s32[8,64,512]{2,1,0:T(8,128)S(1)}, s32[8,64,512]{2,1,0:T(8,128)}, u32[]{:S(2)}) copy-start(s32[8,64,512]{2,1,0:T(8,128)} %param.9) | copy-start | bytes 3145732
  74.9 15.3 %copy-start.6 = (f32[4,8]{1,0:T(4,128)S(1)}, f32[4,8]{1,0:T(4,128)}, u32[]{:S(2)}) copy-start(f32[4,8]{1,0:T(4,128)} %param.11) | copy-start | bytes 388
  74.9 5.7 %collective-permute-start.8 = (f32[8,2,512]{2,1,0:T(2,128)S(1)}, f32[8,2,512]{2,1,0:T(2,128)S(1)}, u32[]{:S(2)}, u32[]{:S(2)}) collective-permute-start(f32[8,2,512]{2,1,0:T(2,128)S(1)} %get-tuple-element.22), channel_id=1, source_target_pairs={{0,16},{16,32},{32,48},{48,64},{64,80},{80,96},{96,112},{112,128},... | collective-permute-start | bytes 98312 | tf_op jit(solution)/shard_map/ppermute | solution.py:18
  78.7 5.2 %collective-permute-start.9 = (f32[8,2,512]{2,1,0:T(2,128)S(1)}, f32[8,2,512]{2,1,0:T(2,128)S(1)}, u32[]{:S(2)}, u32[]{:S(2)}) collective-permute-start(f32[8,2,512]{2,1,0:T(2,128)S(1)} %get-tuple-element.21), channel_id=1, source_target_pairs={{16,0},{32,16},{48,32},{64,48},{80,64},{96,80},{112,96},{128,112},... | collective-permute-start | bytes 98312 | tf_op jit(solution)/shard_map/ppermute | solution.py:19
  84.1 9.4 %collective-permute-start.10 = (f32[2,68,512]{2,1,0:T(8,128)S(1)}, f32[2,68,512]{2,1,0:T(8,128)S(1)}, u32[]{:S(2)}, u32[]{:S(2)}) collective-permute-start(f32[2,68,512]{2,1,0:T(8,128)S(1)} %get-tuple-element.11), channel_id=1, source_target_pairs={{1,0},{2,1},{3,2},{4,3},{5,4},{6,5},{7,6},{8,7},{9,8},{10,9},{11,1... | collective-permute-start | bytes 835592 | tf_op jit(solution)/shard_map/ppermute | solution.py:19
  85.4 9.9 %collective-permute-start.11 = (f32[2,68,512]{2,1,0:T(8,128)S(1)}, f32[2,68,512]{2,1,0:T(8,128)S(1)}, u32[]{:S(2)}, u32[]{:S(2)}) collective-permute-start(f32[2,68,512]{2,1,0:T(8,128)S(1)} %get-tuple-element.12), channel_id=1, source_target_pairs={{0,1},{1,2},{2,3},{3,4},{4,5},{5,6},{6,7},{7,8},{8,9},{9,10},{10,1... | collective-permute-start | bytes 835592 | tf_op jit(solution)/shard_map/ppermute | solution.py:18
  91.6 4.0 %copy-start.3 = (s32[8,64,512]{2,1,0:T(8,128)S(1)}, s32[8,64,512]{2,1,0:T(8,128)}, u32[]{:S(2)}) copy-start(s32[8,64,512]{2,1,0:T(8,128)} %param.9) | copy-start | bytes 3145732
  116.0 14.5 %copy-start.5 = (f32[8,64,512]{2,1,0:T(8,128)}, f32[8,64,512]{2,1,0:T(8,128)S(1)}, u32[]{:S(2)}) copy-start(f32[8,64,512]{2,1,0:T(8,128)S(1)} %get-tuple-element.8) | copy-start | bytes 3145732
where the time goes:
time: 169 us; the launch traced here: 167 us
  other arithmetic  75.3 us (45%)
  starting transfers between devices  37.5 us (22%)
  blocking collectives  22.7 us (13%)
  waiting for transfers between devices  20.5 us (12%)
  local copies, waits for them, and re-layouts  8.93 us (5%)
  between operations  1.89 us (1%)
    add x2, other arithmetic, on_device(): advanced + point_source(advanced.shape, source_cell, depth_base, lateral_...  25.9 us
    ppermute x6, starting transfers between devices, with_halo(): before = lax.ppermute(last, axis, up)  24.2 us
    all_to_all x1, blocking collectives, on_device(): lax.all_to_all(partials, 'dep', split_axis=3, concat_axis=0, tiled=True)  22.7 us
    reduce_sum x1, other arithmetic, on_device(): slab_depth = jnp.sum(sigma, axis=0)  20.4 us
    ppermute x6, waiting for transfers between devices, with_halo(): after = lax.ppermute(first, axis, down)  15.6 us
    another operation x1, other arithmetic, on_device(): prefix = jnp.cumsum(sigma, axis=0) - sigma  14.4 us
    ppermute x6, starting transfers between devices, with_halo(): after = lax.ppermute(first, axis, down)  13.3 us
    reduce_sum x1, other arithmetic, on_device(): jnp.sum(weight * colours[1], axis=0)  7.11 us
  transfers between devices with their start and end apart: 12, of which 8 were waited for; matrix products, arithmetic and copies ran while one was open for 4% of the time, Pallas kernels for 0%

commit v1 on v0

v1 whole, which is shorter than its diff:
```python
import functools
import math

import jax
import jax.numpy as jnp
from jax import lax
from jax.experimental import pallas as pl
from jax.experimental.pallas import tpu as pltpu
from jax.sharding import PartitionSpec as P

BUMPS = 8
Z, X, T = 8, 64, 4
ROWS = X + 32
CORE = 16
VMEM = pl.BlockSpec(memory_space=pltpu.VMEM)
SMEM = pl.BlockSpec(memory_space=pltpu.SMEM)
UP1, RIGHT1, SRC_Z, SRC_X, SRC_Y = range(5)


def lane_masks():
    lane = lax.broadcasted_iota(jnp.int32, (8, 128), 1)
    return lane < 1, lane < 2, lane >= 127, lane >= 126


def columns_sum(c, masks):
    zero = jnp.zeros((8, 128), jnp.float32)
    low1, low2, high1, high2 = masks
    a1 = [pltpu.roll(v, 1, 1) for v in c]
    a2 = [pltpu.roll(v, 2, 1) for v in c]
    b1 = [pltpu.roll(v, 127, 1) for v in c]
    b2 = [pltpu.roll(v, 126, 1) for v in c]
    out = []
    for i in range(T):
        first, last = i == 0, i == T - 1
        near = jnp.where(low1, zero if first else a1[i - 1], a1[i]) + jnp.where(
            high1, zero if last else b1[i + 1], b1[i]
        )
        far = jnp.where(low2, zero if first else a2[i - 1], a2[i]) + jnp.where(
            high2, zero if last else b2[i + 1], b2[i]
        )
        out.append((near, far))
    return out


def plane_terms(ref, k, row, masks):
    c = [ref[k, i, pl.ds(row, 8), :] for i in range(T)]
    sums = columns_sum(c, masks)
    out = []
    for i in range(T):
        near = sums[i][0] + (ref[k, i, pl.ds(row - 1, 8), :] + ref[k, i, pl.ds(row + 1, 8), :])
        far = sums[i][1] + (ref[k, i, pl.ds(row - 2, 8), :] + ref[k, i, pl.ds(row + 2, 8), :])
        out.append((c[i], near, far))
    return out


def full_terms(ref, k, row, masks):
    out = []
    for i, (c, near, far) in enumerate(plane_terms(ref, k, row, masks)):
        rows = pl.ds(row, 8)
        near = near + (ref[k - 1, i, rows, :] + ref[k + 1, i, rows, :])
        far = far + (ref[k - 2, i, rows, :] + ref[k + 2, i, rows, :])
        out.append((c, 16.0 * near - far - 90.0 * c))
    return out


def strike(ref, ints, amplitude, layers, rows_low, rows_high):
    z, x, y = ints[SRC_Z], ints[SRC_X], ints[SRC_Y]
    row = x + CORE
    here = (z >= 0) & (z < layers) & (row >= rows_low) & (row < rows_high)

    @pl.when(here)
    def _():
        tile, lane = y // 128, y % 128
        old = ref[z + 2, tile, pl.ds(row, 1), :]
        ids = lax.broadcasted_iota(jnp.int32, (1, 128), 1)
        ref[z + 2, tile, pl.ds(row, 1), :] = old + jnp.where(ids == lane, amplitude, 0.0)


def stiffness(table, materials):
    return jnp.take_along_axis(table, materials, axis=1, mode="promise_in_bounds")


def pack_depth(flags, now_a, now_b, mat_a, mat_b, table_ref, out_a, out_b):
    table = table_ref[...]
    for now, mat, out in ((now_a, mat_a, out_a), (now_b, mat_b, out_b)):
        for k in range(2):
            for i in range(T):
                lanes = slice(128 * i, 128 * i + 128)
                out[k, i] = now[k, :, lanes]
                for t in range(X // 8):
                    rows = slice(8 * t, 8 * t + 8)
                    out[2 + k, i, rows, :] = stiffness(table, mat[k, rows, lanes])


def pack_lateral(flags, now_a, now_b, prev_a, prev_b, mat_a, mat_b, table_ref, out_a, out_b):
    table = table_ref[...]
    upper_half = lax.broadcasted_iota(jnp.int32, (8, 128), 0) >= 4
    right1 = flags[RIGHT1] == 1
    for slot, (now, prev, mat, out) in enumerate(((now_a, prev_a, mat_a, out_a), (now_b, prev_b, mat_b, out_b))):
        keep = upper_half == (right1 if slot == 0 else jnp.logical_not(right1))

        def layer(k, carry, now=now, prev=prev, mat=mat, out=out, keep=keep):
            for i in range(T):
                lanes = slice(128 * i, 128 * i + 128)
                out[k, i, 0:8, :] = now[k, :, lanes]
                moved = pltpu.roll(stiffness(table, mat[k, :, lanes]), 4, 0)
                out[k, i, 8:16, :] = jnp.where(keep, prev[k, :, lanes], moved)
            return carry

        lax.fori_loop(0, Z, layer, 0)


def advance_alone(
    ints, amplitudes, now_ref, prev_ref, mat_ref, table_ref, lat_a, lat_b, now_out, stiff_out, one_out, out_a, out_b,
    now, prev, one, two,
):
    table = table_ref[...]
    masks = lane_masks()
    right1 = ints[RIGHT1] == 1
    zeros = jnp.zeros((T, ROWS, 128), jnp.float32)
    for k in (0, 1, Z + 2, Z + 3):
        now[k] = zeros
        one[k] = zeros

    def fill(k, carry):
        for i in range(T):
            lanes = slice(128 * i, 128 * i + 128)
            now[k + 2, i, CORE : CORE + X, :] = now_ref[k, :, lanes]
            prev[k, i, CORE : CORE + X, :] = prev_ref[k, :, lanes]
            now_out[k, i, CORE : CORE + X, :] = now_ref[k, :, lanes]
            for t in range(X // 8):
                stiff_out[k, i, CORE + 8 * t : CORE + 8 * t + 8, :] = stiffness(
                    table, mat_ref[k, 8 * t : 8 * t + 8, lanes]
                )
            for half, row in ((0, CORE + X), (1, CORE - 8)):
                wanted = right1 if half == 0 else jnp.logical_not(right1)
                got = jnp.where(wanted, lat_a[k, i], lat_b[k, i])
                now[k + 2, i, row : row + 8, :] = got[0:8]
                now_out[k, i, row : row + 8, :] = got[0:8]
                prev[k, i, row : row + 8, :] = got[8:16]
                stiff_out[k, i, row : row + 8, :] = pltpu.roll(got[8:16], 4, 0)
        return carry

    lax.fori_loop(0, Z, fill, 0)

    def first(k, carry):
        for row in range(CORE - 8, CORE + X + 8, 8):
            rows = pl.ds(row, 8)
            for i, (c, lap) in enumerate(full_terms(now, k + 2, row, masks)):
                one[k + 2, i, rows, :] = 2.0 * c - prev[k, i, rows, :] + stiff_out[k, i, rows, :] * lap
        return carry

    lax.fori_loop(0, Z, first, 0)
    strike(one, ints, amplitudes[0], Z, CORE - 8, CORE + X + 8)

    def second(n, carry):
        k = jnp.where(n < 2, n, n + 4)
        for row in range(CORE, CORE + X, 8):
            rows = pl.ds(row, 8)
            for i, (c, lap) in enumerate(full_terms(one, k + 2, row, masks)):
                two[k + 2, i, rows, :] = 2.0 * c - now[k + 2, i, rows, :] + stiff_out[k, i, rows, :] * lap
        return carry

    lax.fori_loop(0, 4, second, 0)
    strike(two, ints, amplitudes[1], Z, CORE, CORE + X)

    def keep(k, carry):
        one_out[k] = one[k + 2]
        return carry

    lax.fori_loop(0, Z, keep, 0)

    sub = lax.broadcasted_iota(jnp.int32, (8, 128), 0)
    left, right = slice(CORE - 8, CORE), slice(CORE + X, CORE + X + 8)

    def message(z, out):
        for k in range(2):
            for i in range(T):
                out[k, i, 0:X, :] = one[z + k + 2, i, CORE : CORE + X, :]
                out[2 + k, i, 0:X, :] = two[z + k + 2, i, CORE : CORE + X, :]
                out[k, i, X : X + 8, :] = jnp.where(sub >= 4, now[z + k + 2, i, left, :], now[z + k + 2, i, right, :])
                ones = jnp.where(sub >= 4, one[z + k + 2, i, left, :], one[z + k + 2, i, right, :])
                stiff = jnp.where(sub >= 4, stiff_out[z + k, i, left, :], stiff_out[z + k, i, right, :])
                outer = (sub < 2) | (sub >= 6)
                out[2 + k, i, X : X + 8, :] = jnp.where(outer, ones, pltpu.roll(stiff, 4, 0))

    up1 = ints[UP1] == 1

    @pl.when(up1)
    def _():
        message(Z - 2, out_a)
        message(0, out_b)

    @pl.when(jnp.logical_not(up1))
    def _():
        message(0, out_a)
        message(Z - 2, out_b)


def clamp_for_bumps(p):
    return jnp.minimum(jnp.maximum(p, -7.4), 7.4)


def finish(
    ints, amplitudes, weights, now, stiff, one_in, early_a, early_b, late_a, late_b, pressure, partial,
    one, two, delta, halo_stiff, halo_two,
):
    masks = lane_masks()
    up1 = ints[UP1] == 1
    core = slice(CORE, CORE + X)
    left, right = slice(CORE - 8, CORE), slice(CORE + X, CORE + X + 8)

    def copy(k, carry):
        one[k + 2] = one_in[k]
        return carry

    lax.fori_loop(0, Z, copy, 0)

    for high in (False, True):
        use_a = up1 if high else jnp.logical_not(up1)
        base = 2 if high else 0
        edge = Z - 2 if high else 0

        def rows_of(k, i, t, early_a=early_a, early_b=early_b, use_a=use_a):
            rows = slice(8 * t, 8 * t + 8)
            return jnp.where(use_a, early_a[k, i, rows, :], early_b[k, i, rows, :])

        def late_of(k, i, t, use_a=use_a):
            rows = slice(8 * t, 8 * t + 8)
            return jnp.where(use_a, late_a[k, i, rows, :], late_b[k, i, rows, :])

        near, far = (0, 1) if high else (1, 0)
        n_in, n_next = (Z - 1, Z - 2) if high else (0, 1)
        for i in range(T):
            for t in range(-1, X // 8 + 1):
                row = CORE + 8 * t
                rows = slice(row, row + 8)
                inside = 0 <= t < X // 8
                if inside:
                    zero_h = [rows_of(k, i, t) for k in range(2)]
                    st_h = [rows_of(2 + k, i, t) for k in range(2)]
                    one_h = [late_of(k, i, t) for k in range(2)]
                    for k in range(2):
                        halo_two[base + k, i, 8 * t : 8 * t + 8, :] = late_of(2 + k, i, t)
                else:
                    zero_h = [late_of(k, i, X // 8) for k in range(2)]
                    one_h = [late_of(2 + k, i, X // 8) for k in range(2)]
                    st_h = [pltpu.roll(v, 4, 0) for v in one_h]
                one[n_in + 2, i, rows, :] += stiff[n_in, i, rows, :] * (16.0 * zero_h[near] - zero_h[far])
                one[n_next + 2, i, rows, :] -= stiff[n_next, i, rows, :] * zero_h[near]
                d_near = st_h[near] * (16.0 * now[n_in, i, rows, :] - now[n_next, i, rows, :])
                d_far = -st_h[far] * now[n_in, i, rows, :]
                zi = Z + 2 if high else 0
                one[zi + near, i, rows, :] = one_h[near] + d_near
                one[zi + far, i, rows, :] = one_h[far] + d_far
                delta[base + near, i, rows, :] = d_near
                delta[base + far, i, rows, :] = d_far
                if inside:
                    halo_stiff[base + near, i, 8 * t : 8 * t + 8, :] = st_h[near]
                    halo_stiff[base + far, i, 8 * t : 8 * t + 8, :] = st_h[far]

    def second(k, carry):
        for row in range(CORE - 8, CORE + X + 8, 8):
            rows = pl.ds(row, 8)
            for i, (c, lap) in enumerate(full_terms(one, k + 2, row, masks)):
                two[k + 2, i, rows, :] = 2.0 * c - now[k, i, rows, :] + stiff[k, i, rows, :] * lap
        return carry

    lax.fori_loop(0, Z, second, 0)
    strike(two, ints, amplitudes[1], Z, CORE - 8, CORE + X + 8)

    for high in (False, True):
        base = 2 if high else 0
        zi = Z + 2 if high else 0
        near, far = (0, 1) if high else (1, 0)
        n_in, n_next = (Z + 1, Z) if high else (2, 3)

        def tile(t, carry, base=base, zi=zi, near=near, far=far, n_in=n_in, n_next=n_next):
            row = pl.multiple_of(CORE + 8 * t, 8)
            rows, own = pl.ds(row, 8), pl.ds(pl.multiple_of(8 * t, 8), 8)
            terms = {k: plane_terms(delta, base + k, row, masks) for k in range(2)}
            for i in range(T):
                for k in range(2):
                    c, near_sum, far_sum = terms[k][i]
                    near_sum = near_sum + terms[1 - k][i][0]
                    if k == near:
                        near_sum = near_sum + one[n_in, i, rows, :]
                        far_sum = far_sum + one[n_next, i, rows, :]
                    else:
                        far_sum = far_sum + one[n_in, i, rows, :]
                    lap = 16.0 * near_sum - far_sum - 90.0 * c
                    two[zi + k, i, rows, :] = (
                        halo_two[base + k, i, own, :] + 2.0 * c + halo_stiff[base + k, i, own, :] * lap
                    )
            return carry

        lax.fori_loop(0, X // 8, tile, 0)

    def third(k, carry):
        for row in range(CORE, CORE + X, 8):
            rows = pl.ds(row, 8)
            for i, (c, lap) in enumerate(full_terms(two, k + 2, row, masks)):
                one[k + 2, i, rows, :] = 2.0 * c - one[k + 2, i, rows, :] + stiff[k, i, rows, :] * lap
        return carry

    lax.fori_loop(0, Z, third, 0)
    strike(one, ints, amplitudes[2], Z, CORE, CORE + X)

    group = lax.broadcasted_iota(jnp.int32, (8, 128), 1) // 32
    step = 6.0 / (BUMPS - 1)
    half_rate = step / (0.8 * 0.8)
    half = BUMPS // 2

    def render(t, carry):
        rows = pl.ds(pl.multiple_of(CORE + 8 * t, 8), 8)
        own = pl.ds(pl.multiple_of(8 * t, 8), 8)
        for i in range(T):
            colour = [jnp.zeros((8, 128), jnp.float32) for _ in range(3)]
            through = jnp.ones((8, 128), jnp.float32)
            depth = jnp.zeros((8, 128), jnp.float32)
            for k in range(Z):
                p = one[k + 2, i, rows, :]
                pressure[k, own, 128 * i : 128 * i + 128] = p
                p = clamp_for_bumps(p)
                gauss = jnp.exp(p * p * (-1.0 / 0.64))
                rise = jnp.exp(p * half_rate)
                fall = jnp.exp(p * -half_rate)
                up, down = rise * rise, fall * fall
                above, below = gauss * rise, gauss * fall
                value = []
                for n in range(4):
                    a = weights[n, BUMPS - 1] * up + weights[n, BUMPS - 2]
                    b = weights[n, 0] * down + weights[n, 1]
                    for j in range(2, half):
                        a = a * up + weights[n, BUMPS - 1 - j]
                        b = b * down + weights[n, j]
                    value.append(a * above + b * below)
                sigma = value[3]
                stay = jnp.exp(-sigma)
                weight = through * (1.0 - stay)
                through = through * stay
                depth = depth + sigma
                colour = [colour[n] + weight * value[n] for n in range(3)]
            parts = colour + [depth]
            for q in range(4):
                packed = None
                for n in range(4):
                    shift = (32 * (n - q)) % 128
                    moved = parts[n] if shift == 0 else pltpu.roll(parts[n], shift, 1)
                    packed = moved if packed is None else jnp.where(group == n, moved, packed)
                partial[4 * i + q, own, :] = packed
        return carry

    lax.fori_loop(0, X // 8, render, 0)


def composite(parts, image):
    group = lax.broadcasted_iota(jnp.int32, (8, 128), 1) // 32

    def tile(t, carry):
        rows = pl.ds(pl.multiple_of(8 * t, 8), 8)
        before = jnp.zeros((8, 128), jnp.float32)
        total = jnp.zeros((8, 128), jnp.float32)
        for d in range(parts.shape[0]):
            v = parts[d, rows, :]
            total = total + jnp.exp(-before) * v
            depth = v
            for n in range(3):
                depth = jnp.where(group == n, pltpu.roll(v, 32 * (n + 1), 1), depth)
            before = before + depth
        total = jnp.where(group == 3, 1.0 - jnp.exp(-before), total)
        for n in range(4):
            moved = total if n == 0 else pltpu.roll(total, 128 - 32 * n, 1)
            image[n, rows, :] = moved[:, 0:32]
        return carry

    lax.fori_loop(0, X // 8, tile, 0)


def wavelet(level):
    shifted = 0.3 * (level.astype(jnp.float32) - 10.0)
    return 4.0 * (1.0 - 2.0 * shifted * shifted) * jnp.exp(-shifted * shifted)


def swaps(n_lat, n_dep, kind):
    out = []
    for lat in range(n_lat):
        for dep in range(n_dep):
            other_lat, other_dep = lat, dep
            if kind in ("d1", "d2"):
                up = ((lat % 2 == 0) == (dep % 2 == 0)) == (kind == "d1")
                other_dep = dep + 1 if up else dep - 1
            else:
                right = (lat % 2 == 0) == (kind == "l1")
                other_lat = lat + 1 if right else lat - 1
            if 0 <= other_lat < n_lat and 0 <= other_dep < n_dep:
                out.append((lat * n_dep + dep, other_lat * n_dep + other_dep))
    return out


def on_device(n_lat, n_dep, pressure_prev, pressure_now, materials, courant_table, tf_weights, source_cell, start_step):
    f32 = jnp.float32
    lat, dep = lax.axis_index("lat"), lax.axis_index("dep")
    up1 = ((lat % 2 == 0) == (dep % 2 == 0)).astype(jnp.int32)
    right1 = (lat % 2 == 0).astype(jnp.int32)
    ints = jnp.stack([up1, right1, source_cell[0] - dep * Z, source_cell[1] - lat * X, source_cell[2]])
    amplitudes = wavelet(start_step[0] + jnp.arange(3))
    table = jnp.broadcast_to(jnp.pad(courant_table * courant_table * (1.0 / 12.0), (0, 112))[None], (8, 128))
    centres = [(-3.0 + 6.0 * j / (BUMPS - 1)) / 0.8 for j in range(BUMPS)]
    scale = jnp.asarray([math.exp(-c * c) for c in centres], f32)
    rows = jnp.asarray([1.0, 1.0, 1.0, 1.5 / (Z * n_dep)], f32)
    weights = tf_weights * scale[None] * rows[:, None]

    def swap(v, kind):
        return lax.ppermute(v, ("lat", "dep"), swaps(n_lat, n_dep, kind))

    def shape(*dims):
        return jax.ShapeDtypeStruct(dims, f32)

    params = pltpu.CompilerParams(vmem_limit_bytes=48 * 1024 * 1024)

    def layers(slot):
        place = (lambda g, f: (3 * f[UP1], 0, 0)) if slot == 0 else (lambda g, f: (3 - 3 * f[UP1], 0, 0))
        return pl.BlockSpec((2, X, 512), place)

    def edge(slot):
        last = X // 8 - 1
        place = (lambda g, f: (0, last * f[RIGHT1], 0)) if slot == 0 else (lambda g, f: (0, last - last * f[RIGHT1], 0))
        return pl.BlockSpec((Z, 8, 512), place)

    def whole(*dims):
        return pl.BlockSpec(dims, lambda g, f: (0,) * len(dims))

    early = pl.pallas_call(
        pack_depth,
        grid_spec=pltpu.PrefetchScalarGridSpec(
            num_scalar_prefetch=1,
            grid=(1,),
            in_specs=[layers(0), layers(1), layers(0), layers(1), whole(8, 128)],
            out_specs=[whole(4, T, X, 128)] * 2,
        ),
        out_shape=[shape(4, T, X, 128)] * 2,
        compiler_params=params,
        name="pack_depth",
    )(ints, pressure_now, pressure_now, materials, materials, table)
    side = pl.pallas_call(
        pack_lateral,
        grid_spec=pltpu.PrefetchScalarGridSpec(
            num_scalar_prefetch=1,
            grid=(1,),
            in_specs=[edge(0), edge(1)] * 3 + [whole(8, 128)],
            out_specs=[whole(Z, T, 16, 128)] * 2,
        ),
        out_shape=[shape(Z, T, 16, 128)] * 2,
        compiler_params=params,
        name="pack_lateral",
    )(ints, pressure_now, pressure_now, pressure_prev, pressure_prev, materials, materials, table)
    early_a = swap(early[0], "d1")
    side_a = swap(side[0], "l1")
    side_b = swap(side[1], "l2")
    early_b = swap(early[1], "d2")

    padded = pltpu.VMEM((Z + 4, T, ROWS, 128), f32)
    now, stiff, one, late_1, late_2 = pl.pallas_call(
        advance_alone,
        in_specs=[SMEM, SMEM] + [VMEM] * 6,
        out_specs=[VMEM] * 5,
        out_shape=[shape(Z, T, ROWS, 128)] * 3 + [shape(4, T, X + 8, 128)] * 2,
        scratch_shapes=[padded, pltpu.VMEM((Z, T, ROWS, 128), f32), padded, padded],
        compiler_params=params,
        name="advance_alone",
    )(ints, amplitudes, pressure_now, pressure_prev, materials, table, side_a, side_b)
    late_a = swap(late_1, "d1")
    late_b = swap(late_2, "d2")

    pressure, partial = pl.pallas_call(
        finish,
        in_specs=[SMEM, SMEM, SMEM] + [VMEM] * 7,
        out_specs=[VMEM] * 2,
        out_shape=[shape(Z, X, 512), shape(n_dep, X, 128)],
        scratch_shapes=[
            padded,
            padded,
            pltpu.VMEM((4, T, ROWS, 128), f32),
            pltpu.VMEM((4, T, X, 128), f32),
            pltpu.VMEM((4, T, X, 128), f32),
        ],
        compiler_params=params,
        name="finish",
    )(ints, amplitudes, weights, now, stiff, one, early_a, early_b, late_a, late_b)
    parts = lax.all_to_all(partial, "dep", 0, 0, tiled=True)
    image = pl.pallas_call(
        composite,
        in_specs=[VMEM],
        out_specs=VMEM,
        out_shape=shape(4, X, 512 // n_dep),
        compiler_params=params,
        name="composite",
    )(parts)
    return pressure, image


def solution(mesh):
    block = P("dep", "lat", None)
    return jax.shard_map(
        functools.partial(on_device, mesh.shape["lat"], mesh.shape["dep"]),
        mesh=mesh,
        in_specs=(block, block, block, P(), P(), P(), P()),
        out_specs=(block, P(None, "lat", "dep")),
        check_vma=False,
    )
```

time: 169 us -> 90.7 us (0.54)
  the two profiles are of different devices: /device:TPU:1 before, /device:TPU:256 now
where the time goes in v1:
time: 90.7 us; the launch traced here: 90.2 us
  Pallas kernels  23.5 us (26%)
  waiting for transfers between devices  21.5 us (24%)
  blocking collectives  20.2 us (22%)
  starting transfers between devices  14.9 us (16%)
  local copies, waits for them, and re-layouts  6.64 us (7%)
  between operations  2.67 us (3%)
    ppermute x6, waiting for transfers between devices, swap(): return lax.ppermute(v, ('lat', 'dep'), swaps(n_lat, n_dep, kind))  21.5 us
    all_to_all x1, blocking collectives, on_device(): parts = lax.all_to_all(partial, 'dep', 0, 0, tiled=True)  20.2 us
    ppermute x6, starting transfers between devices, swap(): return lax.ppermute(v, ('lat', 'dep'), swaps(n_lat, n_dep, kind))  14.9 us
    pallas_call x1, Pallas kernels, on_device(): pl.pallas_call(finish, in_specs=[SMEM, SMEM, SMEM] + [VMEM] * 7, out_spec...  12.1 us
    pallas_call x1, Pallas kernels, on_device(): pl.pallas_call(advance_alone, in_specs=[SMEM, SMEM] + [VMEM] * 6, out_spe...  7.05 us
    unnamed x19, local copies, waits for them, and re-layouts  4.44 us
    pallas_call x1, Pallas kernels, on_device(): pl.pallas_call(pack_lateral, grid_spec=pltpu.PrefetchScalarGridSpec(num_s...  1.84 us
  transfers between devices with their start and end apart: 6, of which 2 were waited for; matrix products, arithmetic and copies ran while one was open for 0% of the time, Pallas kernels for 1%

profile of v1, /device:TPU:256, one launch (start us, length us, event | category | flops | bytes accessed | tf_op | source)
XLA Modules:
  0.0 90.2 jit_solution(2681448213804802510)
XLA Ops:
  0.7 0.7 multiply_multiply_fusion.1
  1.3 1.4 %fusion.2 = (s32[1]{0:T(128)}, s32[1]{0:T(128)}, s32[1]{0:T(128)}) fusion(s32[3]{0:T(128)} %param.14), kind=kLoop, calls=%fused_computation.5 | loop fusion | bytes 24 | tf_op jit(solution)/shard_map/slice | solution.py:406
  3.9 0.8 stack.27.flags.ints
  4.7 1.2 %copy-done = f32[8,64,512]{2,1,0:T(8,128)S(1)} copy-done((f32[8,64,512]{2,1,0:T(8,128)S(1)}, f32[8,64,512]{2,1,0:T(8,128)}, u32[]{:S(2)}) %copy-start) | copy-done | bytes 1048600
  5.9 1.2 %copy-done.1 = s32[8,64,512]{2,1,0:T(8,128)S(1)} copy-done((s32[8,64,512]{2,1,0:T(8,128)S(1)}, s32[8,64,512]{2,1,0:T(8,128)}, u32[]{:S(2)}) %copy-start.1) | copy-done | bytes 1048600
  7.2 1.2 %copy-done.3 = f32[8,64,512]{2,1,0:T(8,128)S(1)} copy-done((f32[8,64,512]{2,1,0:T(8,128)S(1)}, f32[8,64,512]{2,1,0:T(8,128)}, u32[]{:S(2)}) %copy-start.3) | copy-done | bytes 1048600
  8.4 1.8 %pack_lateral.1 = (f32[8,4,16,128]{3,2,1,0:T(8,128)S(1)}, f32[8,4,16,128]{3,2,1,0:T(8,128)S(1)}) custom-call(s32[5]{0:T(128)S(1)} %stack.27.flags.ints, f32[8,64,512]{2,1,0:T(8,128)S(1)} %copy-done, f32[8,64,512]{2,1,0:T(8,128)S(1)} %copy-done, f32[8,64,512]{2,1,0:T(8,128)S(1)} %copy-done.3, f32[8,64,512]{2,1,0:T(8,128)S(1)} %copy-done.3, ...), custom_call_target="tpu_custom_call" | custom-call | tf_op jit(solution)/shard_map/pack_lateral/pallas_call | solution.py:446
  10.2 1.9 %collective-permute-start = (f32[8,4,16,128]{3,2,1,0:T(8,128)S(1)}, f32[8,4,16,128]{3,2,1,0:T(8,128)S(1)}, u32[]{:S(2)}, u32[]{:S(2)}) collective-permute-start(f32[8,4,16,128]{3,2,1,0:T(8,128)S(1)} %get-tuple-element.13), channel_id=1, source_target_pairs={{0,16},{1,17},{2,18},{3,19},{4,20},{5,21},{6,22},{7,23},{8,24},{9,... | collective-permute-start | bytes 786440 | tf_op jit(solution)/shard_map/ppermute | solution.py:415
  12.2 2.1 %collective-permute-start.1 = (f32[8,4,16,128]{3,2,1,0:T(8,128)S(1)}, f32[8,4,16,128]{3,2,1,0:T(8,128)S(1)}, u32[]{:S(2)}, u32[]{:S(2)}) collective-permute-start(f32[8,4,16,128]{3,2,1,0:T(8,128)S(1)} %get-tuple-element.14), channel_id=1, source_target_pairs={{16,32},{17,33},{18,34},{19,35},{20,36},{21,37},{22,38},{23,39},{2... | collective-permute-start | bytes 786440 | tf_op jit(solution)/shard_map/ppermute | solution.py:415
  15.0 0.0 copy-start.2
  15.0 0.0 collective-permute-done.lat_a
  15.0 6.1 %collective-permute-done.1.lat_b = f32[8,4,16,128]{3,2,1,0:T(8,128)S(1)} collective-permute-done((f32[8,4,16,128]{3,2,1,0:T(8,128)S(1)}, f32[8,4,16,128]{3,2,1,0:T(8,128)S(1)}, u32[]{:S(2)}, u32[]{:S(2)}) %collective-permute-start.1) | collective-permute-done | bytes 262176 | tf_op jit(solution)/shard_map/ppermute | solution.py:415
  21.1 7.0 %advance_alone.1 = (f32[8,4,96,128]{3,2,1,0:T(8,128)}, f32[8,4,96,128]{3,2,1,0:T(8,128)}, f32[8,4,96,128]{3,2,1,0:T(8,128)}, f32[4,4,72,128]{3,2,1,0:T(8,128)S(1)}, f32[4,4,72,128]{3,2,1,0:T(8,128)S(1)}) custom-call(s32[5]{0:T(128)S(1)} %stack.27.flags.ints, f32[3]{0:T(128)S(1)} %fusion.1.amplitudes, f32[8,64,512]{2,1,0:T(8,128)S(1)} %copy-done, ...), custom_call_target="tpu_custom_call" | custom-call | tf_op jit(solution)/shard_map/advance_alone/pallas_call | solution.py:464
  28.1 3.4 %collective-permute-start.4 = (f32[4,4,72,128]{3,2,1,0:T(8,128)S(1)}, f32[4,4,72,128]{3,2,1,0:T(8,128)S(1)}, u32[]{:S(2)}, u32[]{:S(2)}) collective-permute-start(f32[4,4,72,128]{3,2,1,0:T(8,128)S(1)} %get-tuple-element.20), channel_id=1, source_target_pairs={{0,1},{1,0},{2,3},{3,2},{4,5},{5,4},{6,7},{7,6},{8,9},{9,8},{10,11... | collective-permute-start | bytes 1769480 | tf_op jit(solution)/shard_map/ppermute | solution.py:415
  31.5 0.0 copy-start.6
  31.5 0.0 copy-start.7
  31.5 0.0 copy-start.8
  31.5 0.0 copy-start.4
  31.6 0.0 copy-start.5
  31.6 0.8 collective-permute-start.5
  32.4 1.0 %pack_depth.1 = (f32[4,4,64,128]{3,2,1,0:T(8,128)S(1)}, f32[4,4,64,128]{3,2,1,0:T(8,128)S(1)}) custom-call(s32[5]{0:T(128)S(1)} %stack.27.flags.ints, f32[8,64,512]{2,1,0:T(8,128)S(1)} %copy-done, f32[8,64,512]{2,1,0:T(8,128)S(1)} %copy-done, s32[8,64,512]{2,1,0:T(8,128)S(1)} %copy-done.2, s32[8,64,512]{2,1,0:T(8,128)S(1)} %copy-done.2, ...), custom_call_target="tpu_custom_call" | custom-call | tf_op jit(solution)/shard_map/pack_depth/pallas_call | solution.py:434
  33.4 5.9 %collective-permute-start.2 = (f32[4,4,64,128]{3,2,1,0:T(8,128)S(1)}, f32[4,4,64,128]{3,2,1,0:T(8,128)S(1)}, u32[]{:S(2)}, u32[]{:S(2)}) collective-permute-start(f32[4,4,64,128]{3,2,1,0:T(8,128)S(1)} %get-tuple-element.18), channel_id=1, source_target_pairs={{0,1},{1,0},{2,3},{3,2},{4,5},{5,4},{6,7},{7,6},{8,9},{9,8},{10,11... | collective-permute-start | bytes 1572872 | tf_op jit(solution)/shard_map/ppermute | solution.py:415
  39.3 0.7 collective-permute-start.3
  40.1 0.1 multiply_multiply_fusion.weights
  40.1 15.4 %collective-permute-done.2.early_a = f32[4,4,64,128]{3,2,1,0:T(8,128)S(1)} collective-permute-done((f32[4,4,64,128]{3,2,1,0:T(8,128)S(1)}, f32[4,4,64,128]{3,2,1,0:T(8,128)S(1)}, u32[]{:S(2)}, u32[]{:S(2)}) %collective-permute-start.2) | collective-permute-done | bytes 524320 | tf_op jit(solution)/shard_map/ppermute | solution.py:415
  55.5 0.0 collective-permute-done.3.early_b
  55.5 0.0 collective-permute-done.4.late_a
  55.6 0.0 collective-permute-done.5.late_b
  55.6 12.1 %finish.1 = (f32[8,64,512]{2,1,0:T(8,128)}, f32[16,64,128]{2,1,0:T(8,128)S(1)}) custom-call(s32[5]{0:T(128)S(1)} %stack.27.flags.ints, f32[3]{0:T(128)S(1)} %fusion.1.amplitudes, f32[4,8]{1,0:T(4,128)S(1)} %multiply_multiply_fusion.weights, f32[8,4,96,128]{3,2,1,0:T(8,128)S(1)} %copy-done.4, f32[8,4,96,128]{3,2,1,0:T(8,128)S(1)} %copy-done.5, ...), custom_call_target="tpu_custom_call" | custom-call | tf_op jit(solution)/shard_map/finish/pallas_call | solution.py:476
  67.7 20.2 %all_to_all.5.parts = f32[16,64,128]{2,1,0:T(8,128)S(1)} all-to-all(f32[16,64,128]{2,1,0:T(8,128)S(1)} %get-tuple-element.23), channel_id=1, replica_groups=mesh['lat'=32,'dep'=16] {'dep'}, dimensions={0} | all-to-all | bytes 1048576 | tf_op jit(solution)/shard_map/all_to_all | solution.py:491
  87.9 1.6 %composite.1 = f32[4,64,32]{2,1,0:T(8,128)S(1)} custom-call(f32[16,64,128]{2,1,0:T(8,128)S(1)} %all_to_all.5.parts), custom_call_target="tpu_custom_call" | custom-call | tf_op jit(solution)/shard_map/composite/pallas_call | solution.py:492
  89.5 0.7 copy.11
  (12 shorter events, 0.0 us)
Async XLA Ops:
  4.7 1.2 %copy-start = (f32[8,64,512]{2,1,0:T(8,128)S(1)}, f32[8,64,512]{2,1,0:T(8,128)}, u32[]{:S(2)}) copy-start(f32[8,64,512]{2,1,0:T(8,128)} %now_b.3) | copy-start | bytes 3145732
  5.9 1.2 %copy-start.1 = (s32[8,64,512]{2,1,0:T(8,128)S(1)}, s32[8,64,512]{2,1,0:T(8,128)}, u32[]{:S(2)}) copy-start(s32[8,64,512]{2,1,0:T(8,128)} %mat_b.3) | copy-start | bytes 3145732
  7.2 1.2 %copy-start.3 = (f32[8,64,512]{2,1,0:T(8,128)S(1)}, f32[8,64,512]{2,1,0:T(8,128)}, u32[]{:S(2)}) copy-start(f32[8,64,512]{2,1,0:T(8,128)} %prev_ref.1) | copy-start | bytes 3145732
  10.2 4.7 %collective-permute-start = (f32[8,4,16,128]{3,2,1,0:T(8,128)S(1)}, f32[8,4,16,128]{3,2,1,0:T(8,128)S(1)}, u32[]{:S(2)}, u32[]{:S(2)}) collective-permute-start(f32[8,4,16,128]{3,2,1,0:T(8,128)S(1)} %get-tuple-element.13), channel_id=1, source_target_pairs={{0,16},{1,17},{2,18},{3,19},{4,20},{5,21},{6,22},{7,23},{8,24},{9,... | collective-permute-start | bytes 786440 | tf_op jit(solution)/shard_map/ppermute | solution.py:415
  12.2 8.9 %collective-permute-start.1 = (f32[8,4,16,128]{3,2,1,0:T(8,128)S(1)}, f32[8,4,16,128]{3,2,1,0:T(8,128)S(1)}, u32[]{:S(2)}, u32[]{:S(2)}) collective-permute-start(f32[8,4,16,128]{3,2,1,0:T(8,128)S(1)} %get-tuple-element.14), channel_id=1, source_target_pairs={{16,32},{17,33},{18,34},{19,35},{20,36},{21,37},{22,38},{23,39},{2... | collective-permute-start | bytes 786440 | tf_op jit(solution)/shard_map/ppermute | solution.py:415
  15.0 17.5 %copy-start.2 = (s32[8,64,512]{2,1,0:T(8,128)S(1)}, s32[8,64,512]{2,1,0:T(8,128)}, u32[]{:S(2)}) copy-start(s32[8,64,512]{2,1,0:T(8,128)} %mat_b.3) | copy-start | bytes 3145732
  28.1 27.4 %collective-permute-start.4 = (f32[4,4,72,128]{3,2,1,0:T(8,128)S(1)}, f32[4,4,72,128]{3,2,1,0:T(8,128)S(1)}, u32[]{:S(2)}, u32[]{:S(2)}) collective-permute-start(f32[4,4,72,128]{3,2,1,0:T(8,128)S(1)} %get-tuple-element.20), channel_id=1, source_target_pairs={{0,1},{1,0},{2,3},{3,2},{4,5},{5,4},{6,7},{7,6},{8,9},{9,8},{10,11... | collective-permute-start | bytes 1769480 | tf_op jit(solution)/shard_map/ppermute | solution.py:415
  31.5 8.5 %copy-start.6 = (f32[4,8]{1,0:T(4,128)S(1)}, f32[4,8]{1,0:T(4,128)}, u32[]{:S(2)}) copy-start(f32[4,8]{1,0:T(4,128)} %param.13) | copy-start | bytes 388
  31.5 8.5 %copy-start.7 = (f32[4]{0:T(128)S(1)}, f32[4]{0:T(128)}, u32[]{:S(2)}) copy-start(f32[4]{0:T(128)} %constant.54.clone) | copy-start | bytes 52
  31.5 8.5 %copy-start.8 = (f32[8]{0:T(128)S(1)}, f32[8]{0:T(128)}, u32[]{:S(2)}) copy-start(f32[8]{0:T(128)} %constant.53.clone) | copy-start | bytes 100
  31.5 24.0 %copy-start.4 = (f32[8,4,96,128]{3,2,1,0:T(8,128)S(1)}, f32[8,4,96,128]{3,2,1,0:T(8,128)}, u32[]{:S(2)}) copy-start(f32[8,4,96,128]{3,2,1,0:T(8,128)} %get-tuple-element.15.now) | copy-start | bytes 4718596
  31.6 24.0 %copy-start.5 = (f32[8,4,96,128]{3,2,1,0:T(8,128)S(1)}, f32[8,4,96,128]{3,2,1,0:T(8,128)}, u32[]{:S(2)}) copy-start(f32[8,4,96,128]{3,2,1,0:T(8,128)} %get-tuple-element.16.stiff) | copy-start | bytes 4718596
  31.6 24.0 %collective-permute-start.5 = (f32[4,4,72,128]{3,2,1,0:T(8,128)S(1)}, f32[4,4,72,128]{3,2,1,0:T(8,128)S(1)}, u32[]{:S(2)}, u32[]{:S(2)}) collective-permute-start(f32[4,4,72,128]{3,2,1,0:T(8,128)S(1)} %get-tuple-element.21), channel_id=1, source_target_pairs={{1,2},{2,1},{3,4},{4,3},{5,6},{6,5},{7,8},{8,7},{9,10},{10,9},{11,... | collective-permute-start | bytes 1769480 | tf_op jit(solution)/shard_map/ppermute | solution.py:415
  33.4 22.2 %collective-permute-start.2 = (f32[4,4,64,128]{3,2,1,0:T(8,128)S(1)}, f32[4,4,64,128]{3,2,1,0:T(8,128)S(1)}, u32[]{:S(2)}, u32[]{:S(2)}) collective-permute-start(f32[4,4,64,128]{3,2,1,0:T(8,128)S(1)} %get-tuple-element.18), channel_id=1, source_target_pairs={{0,1},{1,0},{2,3},{3,2},{4,5},{5,4},{6,7},{7,6},{8,9},{9,8},{10,11... | collective-permute-start | bytes 1572872 | tf_op jit(solution)/shard_map/ppermute | solution.py:415
  39.3 16.2 %collective-permute-start.3 = (f32[4,4,64,128]{3,2,1,0:T(8,128)S(1)}, f32[4,4,64,128]{3,2,1,0:T(8,128)S(1)}, u32[]{:S(2)}, u32[]{:S(2)}) collective-permute-start(f32[4,4,64,128]{3,2,1,0:T(8,128)S(1)} %get-tuple-element.19), channel_id=1, source_target_pairs={{1,2},{2,1},{3,4},{4,3},{5,6},{6,5},{7,8},{8,7},{9,10},{10,9},{11,... | collective-permute-start | bytes 1572872 | tf_op jit(solution)/shard_map/ppermute | solution.py:415

commit v2 on v1

--- a/solution.py
+++ b/solution.py
@@ -14,7 +14,7 @@
 CORE = 16
 VMEM = pl.BlockSpec(memory_space=pltpu.VMEM)
 SMEM = pl.BlockSpec(memory_space=pltpu.SMEM)
-UP1, RIGHT1, SRC_Z, SRC_X, SRC_Y = range(5)
+HBM = pl.BlockSpec(memory_space=pltpu.HBM)
 
 
 def lane_masks():
@@ -63,60 +63,102 @@
     return out
 
 
-def strike(ref, ints, amplitude, layers, rows_low, rows_high):
-    z, x, y = ints[SRC_Z], ints[SRC_X], ints[SRC_Y]
+def strike(ref, outer, place, amplitude, layers, rows_low, rows_high):
+    z, x, y = place
     row = x + CORE
     here = (z >= 0) & (z < layers) & (row >= rows_low) & (row < rows_high)
 
     @pl.when(here)
     def _():
         tile, lane = y // 128, y % 128
-        old = ref[z + 2, tile, pl.ds(row, 1), :]
+        old = ref[z + outer, tile, pl.ds(row, 1), :]
         ids = lax.broadcasted_iota(jnp.int32, (1, 128), 1)
-        ref[z + 2, tile, pl.ds(row, 1), :] = old + jnp.where(ids == lane, amplitude, 0.0)
+        ref[z + outer, tile, pl.ds(row, 1), :] = old + jnp.where(ids == lane, amplitude, 0.0)
 
 
 def stiffness(table, materials):
     return jnp.take_along_axis(table, materials, axis=1, mode="promise_in_bounds")
 
 
-def pack_depth(flags, now_a, now_b, mat_a, mat_b, table_ref, out_a, out_b):
-    table = table_ref[...]
-    for now, mat, out in ((now_a, mat_a, out_a), (now_b, mat_b, out_b)):
+def ways():
+    lat, dep = lax.axis_index("lat"), lax.axis_index("dep")
+    return (lat + dep + 1) % 2, (lat + 1) % 2
+
+
+def source_place(cell):
+    return cell[0] - lax.axis_index("dep") * Z, cell[1] - lax.axis_index("lat") * X, cell[2]
+
+
+def wavelet(start, step):
+    level = jnp.full((1, 128), start[0] + step, jnp.int32).astype(jnp.float32)
+    shifted = 0.3 * (level - 10.0)
+    return 4.0 * (1.0 - 2.0 * shifted * shifted) * jnp.exp(-shifted * shifted)
+
+
+def stiffness_table(courant):
+    lane = lax.broadcasted_iota(jnp.int32, (8, 128), 1)
+    table = jnp.zeros((8, 128), jnp.float32)
+    for m in range(16):
+        table = jnp.where(lane == m, courant[m], table)
+    return table * table * (1.0 / 12.0)
+
+
+def pack(
+    courant, now, prev, mat, early_1, early_2, side_1, side_2,
+    now_z, mat_z, now_x, prev_x, mat_x, depth_sems, side_sems,
+):
+    up1, right1 = ways()
+    waits = []
+    for slot in range(2):
+        first = 6 * up1 if slot == 0 else 6 - 6 * up1
+        for n, (src, dst) in enumerate(((now, now_z), (mat, mat_z))):
+            waits.append(
+                pltpu.make_async_copy(src.at[pl.ds(first, 2)], dst.at[slot], depth_sems.at[2 * slot + n])
+            )
+    for slot in range(2):
+        row = pl.multiple_of((X - 8) * right1 if slot == 0 else (X - 8) - (X - 8) * right1, 8)
+        for n, (src, dst) in enumerate(((now, now_x), (prev, prev_x), (mat, mat_x))):
+            waits.append(
+                pltpu.make_async_copy(src.at[:, pl.ds(row, 8), :], dst.at[slot], side_sems.at[3 * slot + n])
+            )
+    for copy in waits:
+        copy.start()
+    table = stiffness_table(courant)
+    upper_half = (lax.broadcasted_iota(jnp.int32, (8, 128), 0) >= 4).astype(jnp.int32)
+    for slot, out in enumerate((early_1, early_2)):
+        waits[2 * slot].wait()
+        waits[2 * slot + 1].wait()
         for k in range(2):
             for i in range(T):
                 lanes = slice(128 * i, 128 * i + 128)
-                out[k, i] = now[k, :, lanes]
+                out[k, i] = now_z[slot, k, :, lanes]
                 for t in range(X // 8):
                     rows = slice(8 * t, 8 * t + 8)
-                    out[2 + k, i, rows, :] = stiffness(table, mat[k, rows, lanes])
-
-
-def pack_lateral(flags, now_a, now_b, prev_a, prev_b, mat_a, mat_b, table_ref, out_a, out_b):
-    table = table_ref[...]
-    upper_half = lax.broadcasted_iota(jnp.int32, (8, 128), 0) >= 4
-    right1 = flags[RIGHT1] == 1
-    for slot, (now, prev, mat, out) in enumerate(((now_a, prev_a, mat_a, out_a), (now_b, prev_b, mat_b, out_b))):
-        keep = upper_half == (right1 if slot == 0 else jnp.logical_not(right1))
-
-        def layer(k, carry, now=now, prev=prev, mat=mat, out=out, keep=keep):
+                    out[2 + k, i, rows, :] = stiffness(table, mat_z[slot, k, rows, lanes])
+    for slot, out in enumerate((side_1, side_2)):
+        for n in range(3):
+            waits[4 + 3 * slot + n].wait()
+        keep = upper_half == (right1 if slot == 0 else 1 - right1)
+
+        def layer(k, carry, slot=slot, out=out, keep=keep):
             for i in range(T):
                 lanes = slice(128 * i, 128 * i + 128)
-                out[k, i, 0:8, :] = now[k, :, lanes]
-                moved = pltpu.roll(stiffness(table, mat[k, :, lanes]), 4, 0)
-                out[k, i, 8:16, :] = jnp.where(keep, prev[k, :, lanes], moved)
+                out[k, i, 0:8, :] = now_x[slot, k, :, lanes]
+                moved = pltpu.roll(stiffness(table, mat_x[slot, k, :, lanes]), 4, 0)
+                out[k, i, 8:16, :] = jnp.where(keep, prev_x[slot, k, :, lanes], moved)
             return carry
 
         lax.fori_loop(0, Z, layer, 0)
 
 
 def advance_alone(
-    ints, amplitudes, now_ref, prev_ref, mat_ref, table_ref, lat_a, lat_b, now_out, stiff_out, one_out, out_a, out_b,
-    now, prev, one, two,
+    cell, start, courant, now_ref, prev_ref, mat_ref, lat_a, lat_b, now_out, stiff_out, one_out, two_out,
+    now, prev, one,
 ):
-    table = table_ref[...]
+    table = stiffness_table(courant)
     masks = lane_masks()
-    right1 = ints[RIGHT1] == 1
+    place = source_place(cell)
+    right1 = ways()[1] == 1
     zeros = jnp.zeros((T, ROWS, 128), jnp.float32)
     for k in (0, 1, Z + 2, Z + 3):
         now[k] = zeros
@@ -151,18 +193,20 @@
         return carry
 
     lax.fori_loop(0, Z, first, 0)
-    strike(one, ints, amplitudes[0], Z, CORE - 8, CORE + X + 8)
+    strike(one, 2, place, wavelet(start, 0), Z, CORE - 8, CORE + X + 8)
 
     def second(n, carry):
         k = jnp.where(n < 2, n, n + 4)
         for row in range(CORE, CORE + X, 8):
             rows = pl.ds(row, 8)
             for i, (c, lap) in enumerate(full_terms(one, k + 2, row, masks)):
-                two[k + 2, i, rows, :] = 2.0 * c - now[k + 2, i, rows, :] + stiff_out[k, i, rows, :] * lap
+                two_out[n, i, rows, :] = 2.0 * c - now[k + 2, i, rows, :] + stiff_out[k, i, rows, :] * lap
         return carry
 
     lax.fori_loop(0, 4, second, 0)
-    strike(two, ints, amplitudes[1], Z, CORE, CORE + X)
+    z = place[0]
+    inner = (z >= 2) & (z < Z - 2)
+    strike(two_out, 0, (jnp.where(inner, -1, jnp.where(z < 2, z, z - 4)),) + place[1:], wavelet(start, 1), 4, CORE, CORE + X)
 
     def keep(k, carry):
         one_out[k] = one[k + 2]
@@ -170,31 +214,23 @@
 
     lax.fori_loop(0, Z, keep, 0)
 
+
+def pack_late(now, stiff, one, two, early_a, early_b, out_a, out_b):
     sub = lax.broadcasted_iota(jnp.int32, (8, 128), 0)
     left, right = slice(CORE - 8, CORE), slice(CORE + X, CORE + X + 8)
-
-    def message(z, out):
+    up1 = ways()[0]
+    for slot, out in ((0, out_a), (1, out_b)):
+        high = up1 if slot == 0 else 1 - up1
         for k in range(2):
+            z = (Z - 2) * high + k
             for i in range(T):
-                out[k, i, 0:X, :] = one[z + k + 2, i, CORE : CORE + X, :]
-                out[2 + k, i, 0:X, :] = two[z + k + 2, i, CORE : CORE + X, :]
-                out[k, i, X : X + 8, :] = jnp.where(sub >= 4, now[z + k + 2, i, left, :], now[z + k + 2, i, right, :])
-                ones = jnp.where(sub >= 4, one[z + k + 2, i, left, :], one[z + k + 2, i, right, :])
-                stiff = jnp.where(sub >= 4, stiff_out[z + k, i, left, :], stiff_out[z + k, i, right, :])
+                out[k, i, 0:X, :] = one[z, i, CORE : CORE + X, :]
+                out[2 + k, i, 0:X, :] = two[2 * high + k, i, CORE : CORE + X, :]
+                out[k, i, X : X + 8, :] = jnp.where(sub >= 4, now[z, i, left, :], now[z, i, right, :])
+                ones = jnp.where(sub >= 4, one[z, i, left, :], one[z, i, right, :])
+                side = jnp.where(sub >= 4, stiff[z, i, left, :], stiff[z, i, right, :])
                 outer = (sub < 2) | (sub >= 6)
-                out[2 + k, i, X : X + 8, :] = jnp.where(outer, ones, pltpu.roll(stiff, 4, 0))
-
-    up1 = ints[UP1] == 1
-
-    @pl.when(up1)
-    def _():
-        message(Z - 2, out_a)
-        message(0, out_b)
-
-    @pl.when(jnp.logical_not(up1))
-    def _():
-        message(0, out_a)
-        message(Z - 2, out_b)
+                out[2 + k, i, X : X + 8, :] = jnp.where(outer, ones, pltpu.roll(side, 4, 0))
 
 
 def clamp_for_bumps(p):
@@ -202,11 +238,16 @@
 
 
 def finish(
-    ints, amplitudes, weights, now, stiff, one_in, early_a, early_b, late_a, late_b, pressure, partial,
-    one, two, delta, halo_stiff, halo_two,
+    n_dep, cell, start, transfer, now, stiff, one_in, early_a, early_b, late_a, late_b, pressure, partial,
+    one, two, delta, halo_stiff, halo_two, weights,
 ):
     masks = lane_masks()
-    up1 = ints[UP1] == 1
+    place = source_place(cell)
+    up1 = ways()[0] == 1
+    for n in range(4):
+        for j in range(BUMPS):
+            centre = (-3.0 + 6.0 * j / (BUMPS - 1)) / 0.8
+            weights[n, j] = transfer[n, j] * (math.exp(-centre * centre) * (1.5 / (Z * n_dep) if n == 3 else 1.0))
     core = slice(CORE, CORE + X)
     left, right = slice(CORE - 8, CORE), slice(CORE + X, CORE + X + 8)
 
@@ -267,7 +308,7 @@
         return carry
 
     lax.fori_loop(0, Z, second, 0)
-    strike(two, ints, amplitudes[1], Z, CORE - 8, CORE + X + 8)
+    strike(two, 2, place, wavelet(start, 1), Z, CORE - 8, CORE + X + 8)
 
     for high in (False, True):
         base = 2 if high else 0
@@ -304,7 +345,7 @@
         return carry
 
     lax.fori_loop(0, Z, third, 0)
-    strike(one, ints, amplitudes[2], Z, CORE, CORE + X)
+    strike(one, 2, place, wavelet(start, 2), Z, CORE, CORE + X)
 
     group = lax.broadcasted_iota(jnp.int32, (8, 128), 1) // 32
     step = 6.0 / (BUMPS - 1)
@@ -355,31 +396,17 @@
 
 
 def composite(parts, image):
-    group = lax.broadcasted_iota(jnp.int32, (8, 128), 1) // 32
-
-    def tile(t, carry):
-        rows = pl.ds(pl.multiple_of(8 * t, 8), 8)
-        before = jnp.zeros((8, 128), jnp.float32)
-        total = jnp.zeros((8, 128), jnp.float32)
-        for d in range(parts.shape[0]):
-            v = parts[d, rows, :]
-            total = total + jnp.exp(-before) * v
-            depth = v
-            for n in range(3):
-                depth = jnp.where(group == n, pltpu.roll(v, 32 * (n + 1), 1), depth)
-            before = before + depth
-        total = jnp.where(group == 3, 1.0 - jnp.exp(-before), total)
-        for n in range(4):
-            moved = total if n == 0 else pltpu.roll(total, 128 - 32 * n, 1)
-            image[n, rows, :] = moved[:, 0:32]
-        return carry
-
-    lax.fori_loop(0, X // 8, tile, 0)
-
-
-def wavelet(level):
-    shifted = 0.3 * (level.astype(jnp.float32) - 10.0)
-    return 4.0 * (1.0 - 2.0 * shifted * shifted) * jnp.exp(-shifted * shifted)
+    group = lax.broadcasted_iota(jnp.int32, (X, 128), 1) // 32
+    before = jnp.zeros((X, 128), jnp.float32)
+    total = jnp.zeros((X, 128), jnp.float32)
+    for d in range(parts.shape[0]):
+        v = parts[d]
+        total = total + jnp.exp(-before) * v
+        depth = v
+        for n in range(3):
+            depth = jnp.where(group == n, pltpu.roll(v, 32 * (n + 1), 1), depth)
+        before = before + depth
+    image[...] = jnp.where(group == 3, 1.0 - jnp.exp(-before), total).T
 
 
 def swaps(n_lat, n_dep, kind):
@@ -400,16 +427,6 @@
 
 def on_device(n_lat, n_dep, pressure_prev, pressure_now, materials, courant_table, tf_weights, source_cell, start_step):
     f32 = jnp.float32
-    lat, dep = lax.axis_index("lat"), lax.axis_index("dep")
-    up1 = ((lat % 2 == 0) == (dep % 2 == 0)).astype(jnp.int32)
-    right1 = (lat % 2 == 0).astype(jnp.int32)
-    ints = jnp.stack([up1, right1, source_cell[0] - dep * Z, source_cell[1] - lat * X, source_cell[2]])
-    amplitudes = wavelet(start_step[0] + jnp.arange(3))
-    table = jnp.broadcast_to(jnp.pad(courant_table * courant_table * (1.0 / 12.0), (0, 112))[None], (8, 128))
-    centres = [(-3.0 + 6.0 * j / (BUMPS - 1)) / 0.8 for j in range(BUMPS)]
-    scale = jnp.asarray([math.exp(-c * c) for c in centres], f32)
-    rows = jnp.asarray([1.0, 1.0, 1.0, 1.5 / (Z * n_dep)], f32)
-    weights = tf_weights * scale[None] * rows[:, None]
 
     def swap(v, kind):
         return lax.ppermute(v, ("lat", "dep"), swaps(n_lat, n_dep, kind))
@@ -417,65 +434,54 @@
     def shape(*dims):
         return jax.ShapeDtypeStruct(dims, f32)
 
-    params = pltpu.CompilerParams(vmem_limit_bytes=48 * 1024 * 1024)
-
-    def layers(slot):
-        place = (lambda g, f: (3 * f[UP1], 0, 0)) if slot == 0 else (lambda g, f: (3 - 3 * f[UP1], 0, 0))
-        return pl.BlockSpec((2, X, 512), place)
-
-    def edge(slot):
-        last = X // 8 - 1
-        place = (lambda g, f: (0, last * f[RIGHT1], 0)) if slot == 0 else (lambda g, f: (0, last - last * f[RIGHT1], 0))
-        return pl.BlockSpec((Z, 8, 512), place)
-
-    def whole(*dims):
-        return pl.BlockSpec(dims, lambda g, f: (0,) * len(dims))
-
-    early = pl.pallas_call(
-        pack_depth,
-        grid_spec=pltpu.PrefetchScalarGridSpec(
-            num_scalar_prefetch=1,
-            grid=(1,),
-            in_specs=[layers(0), layers(1), layers(0), layers(1), whole(8, 128)],
-            out_specs=[whole(4, T, X, 128)] * 2,
-        ),
-        out_shape=[shape(4, T, X, 128)] * 2,
+    params = pltpu.CompilerParams(vmem_limit_bytes=24 * 1024 * 1024)
+    i32 = jnp.int32
+    early_1, early_2, side_1, side_2 = pl.pallas_call(
+        pack,
+        in_specs=[SMEM] + [HBM] * 3,
+        out_specs=[VMEM] * 4,
+        out_shape=[shape(4, T, X, 128)] * 2 + [shape(Z, T, 16, 128)] * 2,
+        scratch_shapes=[
+            pltpu.VMEM((2, 2, X, 512), f32),
+            pltpu.VMEM((2, 2, X, 512), i32),
+            pltpu.VMEM((2, Z, 8, 512), f32),
+            pltpu.VMEM((2, Z, 8, 512), f32),
+            pltpu.VMEM((2, Z, 8, 512), i32),
+            pltpu.SemaphoreType.DMA((4,)),
+            pltpu.SemaphoreType.DMA((6,)),
+        ],
         compiler_params=params,
-        name="pack_depth",
-    )(ints, pressure_now, pressure_now, materials, materials, table)
-    side = pl.pallas_call(
-        pack_lateral,
-        grid_spec=pltpu.PrefetchScalarGridSpec(
-            num_scalar_prefetch=1,
-            grid=(1,),
-            in_specs=[edge(0), edge(1)] * 3 + [whole(8, 128)],
-            out_specs=[whole(Z, T, 16, 128)] * 2,
-        ),
-        out_shape=[shape(Z, T, 16, 128)] * 2,
-        compiler_params=params,
-        name="pack_lateral",
-    )(ints, pressure_now, pressure_now, pressure_prev, pressure_prev, materials, materials, table)
-    early_a = swap(early[0], "d1")
-    side_a = swap(side[0], "l1")
-    side_b = swap(side[1], "l2")
-    early_b = swap(early[1], "d2")
+        name="pack",
+    )(courant_table, pressure_now, pressure_prev, materials)
+    early_a = swap(early_1, "d1")
+    side_a = swap(side_1, "l1")
+    side_b = swap(side_2, "l2")
+    early_b = swap(early_2, "d2")
 
     padded = pltpu.VMEM((Z + 4, T, ROWS, 128), f32)
-    now, stiff, one, late_1, late_2 = pl.pallas_call(
+    now, stiff, one, two = pl.pallas_call(
         advance_alone,
-        in_specs=[SMEM, SMEM] + [VMEM] * 6,
-        out_specs=[VMEM] * 5,
-        out_shape=[shape(Z, T, ROWS, 128)] * 3 + [shape(4, T, X + 8, 128)] * 2,
-        scratch_shapes=[padded, pltpu.VMEM((Z, T, ROWS, 128), f32), padded, padded],
+        in_specs=[SMEM] * 3 + [VMEM] * 5,
+        out_specs=[VMEM] * 4,
+        out_shape=[shape(Z, T, ROWS, 128)] * 3 + [shape(4, T, ROWS, 128)],
+        scratch_shapes=[padded, pltpu.VMEM((Z, T, ROWS, 128), f32), padded],
         compiler_params=params,
         name="advance_alone",
-    )(ints, amplitudes, pressure_now, pressure_prev, materials, table, side_a, side_b)
+    )(source_cell, start_step, courant_table, pressure_now, pressure_prev, materials, side_a, side_b)
+    late_1, late_2 = pl.pallas_call(
+        pack_late,
+        in_specs=[VMEM] * 4 + [pl.BlockSpec(memory_space=pl.ANY)] * 2,
+        out_specs=[VMEM] * 2,
+        out_shape=[shape(4, T, X + 8, 128)] * 2,
+        compiler_params=params,
+        name="pack_late",
+    )(now, stiff, one, two, early_a, early_b)
     late_a = swap(late_1, "d1")
     late_b = swap(late_2, "d2")
 
     pressure, partial = pl.pallas_call(
-        finish,
-        in_specs=[SMEM, SMEM, SMEM] + [VMEM] * 7,
+        functools.partial(finish, n_dep),
+        in_specs=[SMEM] * 3 + [VMEM] * 7,
         out_specs=[VMEM] * 2,
         out_shape=[shape(Z, X, 512), shape(n_dep, X, 128)],
         scratch_shapes=[
@@ -484,20 +490,21 @@
             pltpu.VMEM((4, T, ROWS, 128), f32),
             pltpu.VMEM((4, T, X, 128), f32),
             pltpu.VMEM((4, T, X, 128), f32),
+            pltpu.SMEM((4, BUMPS), f32),
         ],
         compiler_params=params,
         name="finish",
-    )(ints, amplitudes, weights, now, stiff, one, early_a, early_b, late_a, late_b)
+    )(source_cell, start_step, tf_weights, now, stiff, one, early_a, early_b, late_a, late_b)
     parts = lax.all_to_all(partial, "dep", 0, 0, tiled=True)
     image = pl.pallas_call(
         composite,
         in_specs=[VMEM],
         out_specs=VMEM,
-        out_shape=shape(4, X, 512 // n_dep),
+        out_shape=shape(128, X),
         compiler_params=params,
         name="composite",
     )(parts)
-    return pressure, image
+    return pressure, jnp.swapaxes(image.reshape(4, 512 // n_dep, X), 1, 2)
 
 
 def solution(mesh):

time: 90.7 us -> 80 us (0.88)
  the two profiles are of different devices: /device:TPU:256 before, /device:TPU:1 now
where the time goes in v2:
time: 80 us; the launch traced here: 79 us
  starting transfers between devices  21.5 us (27%)
  Pallas kernels  20.3 us (25%)
  blocking collectives  18.8 us (24%)
  waiting for transfers between devices  12.7 us (16%)
  local copies, waits for them, and re-layouts  4.33 us (5%)
  between operations  1.4 us (2%)
    ppermute x6, starting transfers between devices, swap(): return lax.ppermute(v, ('lat', 'dep'), swaps(n_lat, n_dep, kind))  21.5 us
    all_to_all x1, blocking collectives, on_device(): parts = lax.all_to_all(partial, 'dep', 0, 0, tiled=True)  18.8 us
    ppermute x6, waiting for transfers between devices, swap(): return lax.ppermute(v, ('lat', 'dep'), swaps(n_lat, n_dep, kind))  12.7 us
    pallas_call x1, Pallas kernels, on_device(): pl.pallas_call(functools.partial(finish, n_dep), in_specs=[SMEM] * 3 + [V...  11.4 us
    pallas_call x1, Pallas kernels, on_device(): pl.pallas_call(advance_alone, in_specs=[SMEM] * 3 + [VMEM] * 5, out_specs...  4.91 us
    unnamed x12, local copies, waits for them, and re-layouts  4.33 us
    pallas_call x1, Pallas kernels, on_device(): pl.pallas_call(pack, in_specs=[SMEM] + [HBM] * 3, out_specs=[VMEM] * 4, o...  2.66 us
  transfers between devices with their start and end apart: 6, of which 2 were waited for; matrix products, arithmetic and copies ran while one was open for 0% of the time, Pallas kernels for 6%

profile of v2, /device:TPU:1, one launch (start us, length us, event | category | flops | bytes accessed | tf_op | source)
XLA Modules:
  0.0 79.0 jit_solution(78192812953333402)
XLA Ops:
  0.6 0.0 copy-start
  0.6 1.2 %copy-done = f32[8,64,512]{2,1,0:T(8,128)S(1)} copy-done((f32[8,64,512]{2,1,0:T(8,128)S(1)}, f32[8,64,512]{2,1,0:T(8,128)}, u32[]{:S(2)}) %copy-start) | copy-done | bytes 1048600
  1.9 0.0 copy-start.1
  1.9 1.2 %copy-done.1 = f32[8,64,512]{2,1,0:T(8,128)S(1)} copy-done((f32[8,64,512]{2,1,0:T(8,128)S(1)}, f32[8,64,512]{2,1,0:T(8,128)}, u32[]{:S(2)}) %copy-start.1) | copy-done | bytes 1048600
  3.1 0.0 copy-start.2
  3.1 1.2 %copy-done.2 = s32[8,64,512]{2,1,0:T(8,128)S(1)} copy-done((s32[8,64,512]{2,1,0:T(8,128)S(1)}, s32[8,64,512]{2,1,0:T(8,128)}, u32[]{:S(2)}) %copy-start.2) | copy-done | bytes 1048600
  4.3 0.0 copy-start.5
  4.3 0.7 copy-done.5
  5.0 0.0 copy-start.4
  5.0 2.7 %pack.1 = (f32[4,4,64,128]{3,2,1,0:T(8,128)S(1)}, f32[4,4,64,128]{3,2,1,0:T(8,128)S(1)}, f32[8,4,16,128]{3,2,1,0:T(8,128)S(1)}, f32[8,4,16,128]{3,2,1,0:T(8,128)S(1)}) custom-call(f32[16]{0:T(128)S(1)} %copy-done.5, f32[8,64,512]{2,1,0:T(8,128)S(1)} %copy-done, f32[8,64,512]{2,1,0:T(8,128)S(1)} %copy-done.1, s32[8,64,512]{2,1,0:T(8,128)S(1)} %copy-done.2), custom_call_target="tpu_custom_call" | custom-call | tf_op jit(solution)/shard_map/pack/pallas_call | solution.py:439
  7.6 0.7 collective-permute-start.2
  8.3 6.4 %collective-permute-start.3 = (f32[4,4,64,128]{3,2,1,0:T(8,128)S(1)}, f32[4,4,64,128]{3,2,1,0:T(8,128)S(1)}, u32[]{:S(2)}, u32[]{:S(2)}) collective-permute-start(f32[4,4,64,128]{3,2,1,0:T(8,128)S(1)} %get-tuple-element.20), channel_id=1, source_target_pairs={{1,2},{2,1},{3,4},{4,3},{5,6},{6,5},{7,8},{8,7},{9,10},{10,9},{11,... | collective-permute-start | bytes 1572872 | tf_op jit(solution)/shard_map/ppermute | solution.py:432
  14.7 4.3 %collective-permute-start = (f32[8,4,16,128]{3,2,1,0:T(8,128)S(1)}, f32[8,4,16,128]{3,2,1,0:T(8,128)S(1)}, u32[]{:S(2)}, u32[]{:S(2)}) collective-permute-start(f32[8,4,16,128]{3,2,1,0:T(8,128)S(1)} %get-tuple-element.14), channel_id=1, source_target_pairs={{0,16},{1,17},{2,18},{3,19},{4,20},{5,21},{6,22},{7,23},{8,24},{9,... | collective-permute-start | bytes 786440 | tf_op jit(solution)/shard_map/ppermute | solution.py:432
  19.1 1.9 %collective-permute-start.1 = (f32[8,4,16,128]{3,2,1,0:T(8,128)S(1)}, f32[8,4,16,128]{3,2,1,0:T(8,128)S(1)}, u32[]{:S(2)}, u32[]{:S(2)}) collective-permute-start(f32[8,4,16,128]{3,2,1,0:T(8,128)S(1)} %get-tuple-element.15), channel_id=1, source_target_pairs={{16,32},{17,33},{18,34},{19,35},{20,36},{21,37},{22,38},{23,39},{2... | collective-permute-start | bytes 786440 | tf_op jit(solution)/shard_map/ppermute | solution.py:432
  21.6 0.0 collective-permute-done.lat_a
  21.6 5.4 %collective-permute-done.1.lat_b = f32[8,4,16,128]{3,2,1,0:T(8,128)S(1)} collective-permute-done((f32[8,4,16,128]{3,2,1,0:T(8,128)S(1)}, f32[8,4,16,128]{3,2,1,0:T(8,128)S(1)}, u32[]{:S(2)}, u32[]{:S(2)}) %collective-permute-start.1) | collective-permute-done | bytes 262176 | tf_op jit(solution)/shard_map/ppermute | solution.py:432
  27.0 0.0 copy-done.4
  27.1 4.9 %advance_alone.1 = (f32[8,4,96,128]{3,2,1,0:T(8,128)S(1)}, f32[8,4,96,128]{3,2,1,0:T(8,128)S(1)}, f32[8,4,96,128]{3,2,1,0:T(8,128)S(1)}, f32[4,4,96,128]{3,2,1,0:T(8,128)S(1)}) custom-call(s32[3]{0:T(128)S(1)} %copy-done.4, s32[1]{0:T(128)S(6)} %copy.9.start, f32[16]{0:T(128)S(1)} %copy-done.5, f32[8,64,512]{2,1,0:T(8,128)S(1)} %copy-done, ...), custom_call_target="tpu_custom_call" | custom-call | tf_op jit(solution)/shard_map/advance_alone/pallas_call | solution.py:462
  32.0 0.0 collective-permute-done.2.early_a
  32.0 0.0 collective-permute-done.3.early_b
  32.0 0.0 copy-start.3
  32.0 0.1 pack_late.1
  32.1 0.7 collective-permute-start.4
  32.8 7.5 %collective-permute-start.5 = (f32[4,4,72,128]{3,2,1,0:T(8,128)S(1)}, f32[4,4,72,128]{3,2,1,0:T(8,128)S(1)}, u32[]{:S(2)}, u32[]{:S(2)}) collective-permute-start(f32[4,4,72,128]{3,2,1,0:T(8,128)S(1)} %get-tuple-element.23), channel_id=1, source_target_pairs={{1,2},{2,1},{3,4},{4,3},{5,6},{6,5},{7,8},{8,7},{9,10},{10,9},{11,... | collective-permute-start | bytes 1769480 | tf_op jit(solution)/shard_map/ppermute | solution.py:432
  40.3 0.0 collective-permute-done.4.late_a
  40.4 7.2 %collective-permute-done.5.late_b = f32[4,4,72,128]{3,2,1,0:T(8,128)S(1)} collective-permute-done((f32[4,4,72,128]{3,2,1,0:T(8,128)S(1)}, f32[4,4,72,128]{3,2,1,0:T(8,128)S(1)}, u32[]{:S(2)}, u32[]{:S(2)}) %collective-permute-start.5) | collective-permute-done | bytes 589856 | tf_op jit(solution)/shard_map/ppermute | solution.py:432
  47.6 0.0 copy-done.3
  47.6 11.4 %finish.1 = (f32[8,64,512]{2,1,0:T(8,128)}, f32[16,64,128]{2,1,0:T(8,128)S(1)}) custom-call(s32[3]{0:T(128)S(1)} %copy-done.4, s32[1]{0:T(128)S(6)} %copy.9.start, f32[4,8]{1,0:T(4,128)S(1)} %copy-done.3, f32[8,4,96,128]{3,2,1,0:T(8,128)S(1)} %get-tuple-element.16.now, f32[8,4,96,128]{3,2,1,0:T(8,128)S(1)} %get-tuple-element.17.stiff, ...), custom_call_target="tpu_custom_call" | custom-call | tf_op jit(solution)/shard_map/finish/pallas_call | solution.py:482
  59.0 18.8 %all_to_all.5.parts = f32[16,64,128]{2,1,0:T(8,128)S(1)} all-to-all(f32[16,64,128]{2,1,0:T(8,128)S(1)} %get-tuple-element.25), channel_id=1, replica_groups=mesh['lat'=32,'dep'=16] {'dep'}, dimensions={0} | all-to-all | bytes 1048576 | tf_op jit(solution)/shard_map/all_to_all | solution.py:498
  77.8 1.2 %composite.1 = f32[128,64]{1,0:T(8,128)} custom-call(f32[16,64,128]{2,1,0:T(8,128)S(1)} %all_to_all.5.parts), custom_call_target="tpu_custom_call" | custom-call | tf_op jit(solution)/shard_map/composite/pallas_call | solution.py:499
Async XLA Ops:
  0.6 1.2 %copy-start = (f32[8,64,512]{2,1,0:T(8,128)S(1)}, f32[8,64,512]{2,1,0:T(8,128)}, u32[]{:S(2)}) copy-start(f32[8,64,512]{2,1,0:T(8,128)} %now_ref.1) | copy-start | bytes 3145732
  1.9 1.2 %copy-start.1 = (f32[8,64,512]{2,1,0:T(8,128)S(1)}, f32[8,64,512]{2,1,0:T(8,128)}, u32[]{:S(2)}) copy-start(f32[8,64,512]{2,1,0:T(8,128)} %prev_ref.1) | copy-start | bytes 3145732
  3.1 1.2 %copy-start.2 = (s32[8,64,512]{2,1,0:T(8,128)S(1)}, s32[8,64,512]{2,1,0:T(8,128)}, u32[]{:S(2)}) copy-start(s32[8,64,512]{2,1,0:T(8,128)} %mat_ref.1) | copy-start | bytes 3145732
  4.3 0.7 copy-start.5
  5.0 22.1 %copy-start.4 = (s32[3]{0:T(128)S(1)}, s32[3]{0:T(128)}, u32[]{:S(2)}) copy-start(s32[3]{0:T(128)} %cell.3) | copy-start | bytes 40
  7.6 24.3 %collective-permute-start.2 = (f32[4,4,64,128]{3,2,1,0:T(8,128)S(1)}, f32[4,4,64,128]{3,2,1,0:T(8,128)S(1)}, u32[]{:S(2)}, u32[]{:S(2)}) collective-permute-start(f32[4,4,64,128]{3,2,1,0:T(8,128)S(1)} %get-tuple-element.19), channel_id=1, source_target_pairs={{0,1},{1,0},{2,3},{3,2},{4,5},{5,4},{6,7},{7,6},{8,9},{9,8},{10,11... | collective-permute-start | bytes 1572872 | tf_op jit(solution)/shard_map/ppermute | solution.py:432
  8.3 23.6 %collective-permute-start.3 = (f32[4,4,64,128]{3,2,1,0:T(8,128)S(1)}, f32[4,4,64,128]{3,2,1,0:T(8,128)S(1)}, u32[]{:S(2)}, u32[]{:S(2)}) collective-permute-start(f32[4,4,64,128]{3,2,1,0:T(8,128)S(1)} %get-tuple-element.20), channel_id=1, source_target_pairs={{1,2},{2,1},{3,4},{4,3},{5,6},{6,5},{7,8},{8,7},{9,10},{10,9},{11,... | collective-permute-start | bytes 1572872 | tf_op jit(solution)/shard_map/ppermute | solution.py:432
  14.7 6.9 %collective-permute-start = (f32[8,4,16,128]{3,2,1,0:T(8,128)S(1)}, f32[8,4,16,128]{3,2,1,0:T(8,128)S(1)}, u32[]{:S(2)}, u32[]{:S(2)}) collective-permute-start(f32[8,4,16,128]{3,2,1,0:T(8,128)S(1)} %get-tuple-element.14), channel_id=1, source_target_pairs={{0,16},{1,17},{2,18},{3,19},{4,20},{5,21},{6,22},{7,23},{8,24},{9,... | collective-permute-start | bytes 786440 | tf_op jit(solution)/shard_map/ppermute | solution.py:432
  19.1 8.0 %collective-permute-start.1 = (f32[8,4,16,128]{3,2,1,0:T(8,128)S(1)}, f32[8,4,16,128]{3,2,1,0:T(8,128)S(1)}, u32[]{:S(2)}, u32[]{:S(2)}) collective-permute-start(f32[8,4,16,128]{3,2,1,0:T(8,128)S(1)} %get-tuple-element.15), channel_id=1, source_target_pairs={{16,32},{17,33},{18,34},{19,35},{20,36},{21,37},{22,38},{23,39},{2... | collective-permute-start | bytes 786440 | tf_op jit(solution)/shard_map/ppermute | solution.py:432
  32.0 15.6 %copy-start.3 = (f32[4,8]{1,0:T(4,128)S(1)}, f32[4,8]{1,0:T(4,128)}, u32[]{:S(2)}) copy-start(f32[4,8]{1,0:T(4,128)} %transfer.1) | copy-start | bytes 388
  32.1 8.2 %collective-permute-start.4 = (f32[4,4,72,128]{3,2,1,0:T(8,128)S(1)}, f32[4,4,72,128]{3,2,1,0:T(8,128)S(1)}, u32[]{:S(2)}, u32[]{:S(2)}) collective-permute-start(f32[4,4,72,128]{3,2,1,0:T(8,128)S(1)} %get-tuple-element.22), channel_id=1, source_target_pairs={{0,1},{1,0},{2,3},{3,2},{4,5},{5,4},{6,7},{7,6},{8,9},{9,8},{10,11... | collective-permute-start | bytes 1769480 | tf_op jit(solution)/shard_map/ppermute | solution.py:432
  32.8 14.8 %collective-permute-start.5 = (f32[4,4,72,128]{3,2,1,0:T(8,128)S(1)}, f32[4,4,72,128]{3,2,1,0:T(8,128)S(1)}, u32[]{:S(2)}, u32[]{:S(2)}) collective-permute-start(f32[4,4,72,128]{3,2,1,0:T(8,128)S(1)} %get-tuple-element.23), channel_id=1, source_target_pairs={{1,2},{2,1},{3,4},{4,3},{5,6},{6,5},{7,8},{8,7},{9,10},{10,9},{11,... | collective-permute-start | bytes 1769480 | tf_op jit(solution)/shard_map/ppermute | solution.py:432

commit v3 on v2

--- a/solution.py
+++ b/solution.py
@@ -12,6 +12,7 @@
 Z, X, T = 8, 64, 4
 ROWS = X + 32
 CORE = 16
+INNER_LIMIT = 44 * 1024 * 1024
 VMEM = pl.BlockSpec(memory_space=pltpu.VMEM)
 SMEM = pl.BlockSpec(memory_space=pltpu.SMEM)
 HBM = pl.BlockSpec(memory_space=pltpu.HBM)
@@ -151,14 +152,58 @@
         lax.fori_loop(0, Z, layer, 0)
 
 
-def advance_alone(
-    cell, start, courant, now_ref, prev_ref, mat_ref, lat_a, lat_b, now_out, stiff_out, one_out, two_out,
-    now, prev, one,
+INNER = range(CORE + 8, CORE + X - 8, 8)
+OUTER = (CORE - 8, CORE, CORE + X - 8, CORE + X)
+
+
+def advance_inner(courant, now_in, prev_in, mat_in, now_out, stiff_out, one_out, prev_out, now, prev, mat, sems):
+    copies = [
+        pltpu.make_async_copy(src, dst, sems.at[n]) for n, (src, dst) in enumerate(((now_in, now), (mat_in, mat), (prev_in, prev)))
+    ]
+    for copy in copies:
+        copy.start()
+    table = stiffness_table(courant)
+    masks = lane_masks()
+    zeros = jnp.zeros((T, X, 128), jnp.float32)
+    for k in (0, 1, Z + 2, Z + 3):
+        now_out[k] = zeros
+    copies[0].wait()
+
+    def fill(k, carry):
+        for i in range(T):
+            now_out[k + 2, i] = now[k, :, 128 * i : 128 * i + 128]
+        return carry
+
+    lax.fori_loop(0, Z, fill, 0)
+    copies[1].wait()
+    copies[2].wait()
+
+    def first(k, carry):
+        for i in range(T):
+            lanes = slice(128 * i, 128 * i + 128)
+            prev_out[k, i, 0:8, :] = prev[k, 0:8, lanes]
+            prev_out[k, i, 8:16, :] = prev[k, X - 8 : X, lanes]
+            for t in range(X // 8):
+                rows = slice(8 * t, 8 * t + 8)
+                stiff_out[k, i, rows, :] = stiffness(table, mat[k, rows, lanes])
+        for row in range(8, X - 8, 8):
+            rows = slice(row, row + 8)
+            for i, (c, lap) in enumerate(full_terms(now_out, k + 2, row, masks)):
+                before = prev[k, rows, 128 * i : 128 * i + 128]
+                one_out[k, i, rows, :] = 2.0 * c - before + stiff_out[k, i, rows, :] * lap
+        return carry
+
+    lax.fori_loop(0, Z, first, 0)
+
+
+def advance_outer(
+    cell, start, now_in, stiff_in, one_in, prev_in, lat_a, lat_b, now_side, stiff_side, one_out, two_out,
+    now, prev_side, one,
 ):
-    table = stiffness_table(courant)
     masks = lane_masks()
     place = source_place(cell)
     right1 = ways()[1] == 1
+    core = slice(CORE, CORE + X)
     zeros = jnp.zeros((T, ROWS, 128), jnp.float32)
     for k in (0, 1, Z + 2, Z + 3):
         now[k] = zeros
@@ -166,30 +211,32 @@
 
     def fill(k, carry):
         for i in range(T):
-            lanes = slice(128 * i, 128 * i + 128)
-            now[k + 2, i, CORE : CORE + X, :] = now_ref[k, :, lanes]
-            prev[k, i, CORE : CORE + X, :] = prev_ref[k, :, lanes]
-            now_out[k, i, CORE : CORE + X, :] = now_ref[k, :, lanes]
-            for t in range(X // 8):
-                stiff_out[k, i, CORE + 8 * t : CORE + 8 * t + 8, :] = stiffness(
-                    table, mat_ref[k, 8 * t : 8 * t + 8, lanes]
-                )
-            for half, row in ((0, CORE + X), (1, CORE - 8)):
-                wanted = right1 if half == 0 else jnp.logical_not(right1)
+            now[k + 2, i, core, :] = now_in[k + 2, i]
+            one[k + 2, i, CORE + 8 : CORE + X - 8, :] = one_in[k, i, 8 : X - 8, :]
+            for left in (False, True):
+                wanted = jnp.logical_not(right1) if left else right1
                 got = jnp.where(wanted, lat_a[k, i], lat_b[k, i])
+                row = CORE - 8 if left else CORE + X
+                half = slice(0, 8) if left else slice(8, 16)
                 now[k + 2, i, row : row + 8, :] = got[0:8]
-                now_out[k, i, row : row + 8, :] = got[0:8]
-                prev[k, i, row : row + 8, :] = got[8:16]
-                stiff_out[k, i, row : row + 8, :] = pltpu.roll(got[8:16], 4, 0)
+                now_side[k, i, half, :] = got[0:8]
+                prev_side[k, i, half, :] = got[8:16]
+                stiff_side[k, i, half, :] = pltpu.roll(got[8:16], 4, 0)
         return carry
 
     lax.fori_loop(0, Z, fill, 0)
 
     def first(k, carry):
-        for row in range(CORE - 8, CORE + X + 8, 8):
-            rows = pl.ds(row, 8)
+        for row in OUTER:
+            rows = slice(row, row + 8)
             for i, (c, lap) in enumerate(full_terms(now, k + 2, row, masks)):
-                one[k + 2, i, rows, :] = 2.0 * c - prev[k, i, rows, :] + stiff_out[k, i, rows, :] * lap
+                if row < CORE or row == CORE + X:
+                    half = slice(0, 8) if row < CORE else slice(8, 16)
+                    before, stiff = prev_side[k, i, half, :], stiff_side[k, i, half, :]
+                else:
+                    half = slice(0, 8) if row == CORE else slice(8, 16)
+                    before, stiff = prev_in[k, i, half, :], stiff_in[k, i, row - CORE : row - CORE + 8, :]
+                one[k + 2, i, rows, :] = 2.0 * c - before + stiff * lap
         return carry
 
     lax.fori_loop(0, Z, first, 0)
@@ -198,9 +245,10 @@
     def second(n, carry):
         k = jnp.where(n < 2, n, n + 4)
         for row in range(CORE, CORE + X, 8):
-            rows = pl.ds(row, 8)
+            rows = slice(row, row + 8)
             for i, (c, lap) in enumerate(full_terms(one, k + 2, row, masks)):
-                two_out[n, i, rows, :] = 2.0 * c - now[k + 2, i, rows, :] + stiff_out[k, i, rows, :] * lap
+                stiff = stiff_in[k, i, row - CORE : row - CORE + 8, :]
+                two_out[n, i, rows, :] = 2.0 * c - now[k + 2, i, rows, :] + stiff * lap
         return carry
 
     lax.fori_loop(0, 4, second, 0)
@@ -215,7 +263,7 @@
     lax.fori_loop(0, Z, keep, 0)
 
 
-def pack_late(now, stiff, one, two, early_a, early_b, out_a, out_b):
+def pack_late(now_side, stiff_side, one, two, early_a, early_b, out_a, out_b):
     sub = lax.broadcasted_iota(jnp.int32, (8, 128), 0)
     left, right = slice(CORE - 8, CORE), slice(CORE + X, CORE + X + 8)
     up1 = ways()[0]
@@ -226,9 +274,9 @@
             for i in range(T):
                 out[k, i, 0:X, :] = one[z, i, CORE : CORE + X, :]
                 out[2 + k, i, 0:X, :] = two[2 * high + k, i, CORE : CORE + X, :]
-                out[k, i, X : X + 8, :] = jnp.where(sub >= 4, now[z, i, left, :], now[z, i, right, :])
+                out[k, i, X : X + 8, :] = jnp.where(sub >= 4, now_side[z, i, 0:8, :], now_side[z, i, 8:16, :])
                 ones = jnp.where(sub >= 4, one[z, i, left, :], one[z, i, right, :])
-                side = jnp.where(sub >= 4, stiff[z, i, left, :], stiff[z, i, right, :])
+                side = jnp.where(sub >= 4, stiff_side[z, i, 0:8, :], stiff_side[z, i, 8:16, :])
                 outer = (sub < 2) | (sub >= 6)
                 out[2 + k, i, X : X + 8, :] = jnp.where(outer, ones, pltpu.roll(side, 4, 0))
 
@@ -237,9 +285,79 @@
     return jnp.minimum(jnp.maximum(p, -7.4), 7.4)
 
 
+SIDES = ((False, 0, 1, 0, 0, 1, 0), (True, 2, 0, 1, Z - 1, Z - 2, Z + 2))
+
+
+def halo_step(delta, one, halo_stiff, base, near, n_in, n_next, row, masks):
+    rows, own = pl.ds(row, 8), pl.ds(row - CORE, 8)
+    terms = {k: plane_terms(delta, base + k, row, masks) for k in range(2)}
+    out = {}
+    for i in range(T):
+        for k in range(2):
+            c, near_sum, far_sum = terms[k][i]
+            near_sum = near_sum + terms[1 - k][i][0]
+            if k == near:
+                near_sum = near_sum + one[n_in + 2, i, rows, :]
+                far_sum = far_sum + one[n_next + 2, i, rows, :]
+            else:
+                far_sum = far_sum + one[n_in + 2, i, rows, :]
+            lap = 16.0 * near_sum - far_sum - 90.0 * c
+            out[k, i] = 2.0 * c + halo_stiff[base + k, i, own, :] * lap
+    return out
+
+
+def couple(now, stiff, one_in, early_a, early_b, one, two, delta, halo_stiff, halo_two):
+    masks = lane_masks()
+    up1 = ways()[0] == 1
+
+    def copy(k, carry):
+        one[k + 2] = one_in[k]
+        return carry
+
+    lax.fori_loop(0, Z, copy, 0)
+    for high, base, near, far, n_in, n_next, zi in SIDES:
+        use_a = up1 if high else jnp.logical_not(up1)
+
+        def tile(t, carry, use_a=use_a, base=base, near=near, far=far, n_in=n_in, n_next=n_next, zi=zi):
+            own, rows = pl.ds(pl.multiple_of(8 * t, 8), 8), pl.ds(pl.multiple_of(CORE + 8 * t, 8), 8)
+            for i in range(T):
+                zero_h = [jnp.where(use_a, early_a[k, i, own, :], early_b[k, i, own, :]) for k in range(2)]
+                st_h = [jnp.where(use_a, early_a[2 + k, i, own, :], early_b[2 + k, i, own, :]) for k in range(2)]
+                one[n_in + 2, i, rows, :] += stiff[n_in, i, own, :] * (16.0 * zero_h[near] - zero_h[far])
+                one[n_next + 2, i, rows, :] -= stiff[n_next, i, own, :] * zero_h[near]
+                d_near = st_h[near] * (16.0 * now[n_in + 2, i, own, :] - now[n_next + 2, i, own, :])
+                d_far = -st_h[far] * now[n_in + 2, i, own, :]
+                for place, d, st in ((near, d_near, st_h[near]), (far, d_far, st_h[far])):
+                    one[zi + place, i, rows, :] = d
+                    delta[base + place, i, rows, :] = d
+                    halo_stiff[base + place, i, own, :] = st
+            return carry
+
+        lax.fori_loop(0, X // 8, tile, 0)
+
+    def second(k, carry):
+        for row in INNER:
+            rows = slice(row, row + 8)
+            for i, (c, lap) in enumerate(full_terms(one, k + 2, row, masks)):
+                own = slice(row - CORE, row - CORE + 8)
+                two[k + 2, i, rows, :] = 2.0 * c - now[k + 2, i, own, :] + stiff[k, i, own, :] * lap
+        return carry
+
+    lax.fori_loop(0, Z, second, 0)
+    for high, base, near, far, n_in, n_next, zi in SIDES:
+
+        def beyond(t, carry, base=base, near=near, n_in=n_in, n_next=n_next):
+            row = pl.multiple_of(CORE + 8 * t, 8)
+            for (k, i), v in halo_step(delta, one, halo_stiff, base, near, n_in, n_next, row, masks).items():
+                halo_two[base + k, i, pl.ds(pl.multiple_of(8 * t, 8), 8), :] = v
+            return carry
+
+        lax.fori_loop(1, X // 8 - 1, beyond, 0)
+
+
 def finish(
-    n_dep, cell, start, transfer, now, stiff, one_in, early_a, early_b, late_a, late_b, pressure, partial,
-    one, two, delta, halo_stiff, halo_two, weights,
+    n_dep, cell, start, transfer, now, stiff, now_side, stiff_side, one_in, two_in, delta_in, halo_stiff, halo_two,
+    late_a, late_b, pressure, partial, one, two, delta, weights,
 ):
     masks = lane_masks()
     place = source_place(cell)
@@ -248,100 +366,76 @@
         for j in range(BUMPS):
             centre = (-3.0 + 6.0 * j / (BUMPS - 1)) / 0.8
             weights[n, j] = transfer[n, j] * (math.exp(-centre * centre) * (1.5 / (Z * n_dep) if n == 3 else 1.0))
-    core = slice(CORE, CORE + X)
-    left, right = slice(CORE - 8, CORE), slice(CORE + X, CORE + X + 8)
 
     def copy(k, carry):
-        one[k + 2] = one_in[k]
-        return carry
-
-    lax.fori_loop(0, Z, copy, 0)
-
-    for high in (False, True):
+        one[k] = one_in[k]
+        two[k, :, CORE + 8 : CORE + X - 8, :] = two_in[k, :, CORE + 8 : CORE + X - 8, :]
+        return carry
+
+    lax.fori_loop(0, Z + 4, copy, 0)
+    for k in range(4):
+        delta[k] = delta_in[k]
+
+    for high, base, near, far, n_in, n_next, zi in SIDES:
         use_a = up1 if high else jnp.logical_not(up1)
-        base = 2 if high else 0
-        edge = Z - 2 if high else 0
-
-        def rows_of(k, i, t, early_a=early_a, early_b=early_b, use_a=use_a):
-            rows = slice(8 * t, 8 * t + 8)
-            return jnp.where(use_a, early_a[k, i, rows, :], early_b[k, i, rows, :])
-
-        def late_of(k, i, t, use_a=use_a):
-            rows = slice(8 * t, 8 * t + 8)
+
+        def late_of(k, i, row, use_a=use_a):
+            rows = pl.ds(row - CORE, 8)
             return jnp.where(use_a, late_a[k, i, rows, :], late_b[k, i, rows, :])
 
-        near, far = (0, 1) if high else (1, 0)
-        n_in, n_next = (Z - 1, Z - 2) if high else (0, 1)
-        for i in range(T):
-            for t in range(-1, X // 8 + 1):
-                row = CORE + 8 * t
-                rows = slice(row, row + 8)
-                inside = 0 <= t < X // 8
-                if inside:
-                    zero_h = [rows_of(k, i, t) for k in range(2)]
-                    st_h = [rows_of(2 + k, i, t) for k in range(2)]
-                    one_h = [late_of(k, i, t) for k in range(2)]
-                    for k in range(2):
-                        halo_two[base + k, i, 8 * t : 8 * t + 8, :] = late_of(2 + k, i, t)
+        for row in (CORE - 8, CORE + X):
+            rows, half = slice(row, row + 8), slice(0, 8) if row < CORE else slice(8, 16)
+            for i in range(T):
+                zero_h = [late_of(k, i, CORE + X) for k in range(2)]
+                one_h = [late_of(2 + k, i, CORE + X) for k in range(2)]
+                st_h = [pltpu.roll(v, 4, 0) for v in one_h]
+                one[n_in + 2, i, rows, :] += stiff_side[n_in, i, half, :] * (16.0 * zero_h[near] - zero_h[far])
+                one[n_next + 2, i, rows, :] -= stiff_side[n_next, i, half, :] * zero_h[near]
+                d_near = st_h[near] * (16.0 * now_side[n_in, i, half, :] - now_side[n_next, i, half, :])
+                d_far = -st_h[far] * now_side[n_in, i, half, :]
+                for at, d in ((near, d_near), (far, d_far)):
+                    one[zi + at, i, rows, :] = one_h[at] + d
+                    delta[base + at, i, rows, :] = d
+
+        def inner(t, carry, base=base, near=near, far=far, n_in=n_in, n_next=n_next, zi=zi, late_of=late_of):
+            row = pl.multiple_of(CORE + 8 * t, 8)
+            rows, own = pl.ds(row, 8), pl.ds(pl.multiple_of(8 * t, 8), 8)
+            for i in range(T):
+                one_h = [late_of(k, i, row) for k in range(2)]
+                for k in range(2):
+                    one[zi + k, i, rows, :] += one_h[k]
+                    two[zi + k, i, rows, :] = late_of(2 + k, i, row) + halo_two[base + k, i, own, :]
+                two[n_in + 2, i, rows, :] += stiff[n_in, i, own, :] * (16.0 * one_h[near] - one_h[far])
+                two[n_next + 2, i, rows, :] -= stiff[n_next, i, own, :] * one_h[near]
+            return carry
+
+        lax.fori_loop(0, X // 8, inner, 0)
+        for row in (CORE, CORE + X - 8):
+            for (k, i), v in halo_step(delta, one, halo_stiff, base, near, n_in, n_next, row, masks).items():
+                two[zi + k, i, row : row + 8, :] = late_of(2 + k, i, row) + v
+
+    def second(k, carry):
+        for row in OUTER:
+            rows = slice(row, row + 8)
+            for i, (c, lap) in enumerate(full_terms(one, k + 2, row, masks)):
+                if CORE <= row < CORE + X:
+                    own = slice(row - CORE, row - CORE + 8)
+                    before, st = now[k + 2, i, own, :], stiff[k, i, own, :]
                 else:
-                    zero_h = [late_of(k, i, X // 8) for k in range(2)]
-                    one_h = [late_of(2 + k, i, X // 8) for k in range(2)]
-                    st_h = [pltpu.roll(v, 4, 0) for v in one_h]
-                one[n_in + 2, i, rows, :] += stiff[n_in, i, rows, :] * (16.0 * zero_h[near] - zero_h[far])
-                one[n_next + 2, i, rows, :] -= stiff[n_next, i, rows, :] * zero_h[near]
-                d_near = st_h[near] * (16.0 * now[n_in, i, rows, :] - now[n_next, i, rows, :])
-                d_far = -st_h[far] * now[n_in, i, rows, :]
-                zi = Z + 2 if high else 0
-                one[zi + near, i, rows, :] = one_h[near] + d_near
-                one[zi + far, i, rows, :] = one_h[far] + d_far
-                delta[base + near, i, rows, :] = d_near
-                delta[base + far, i, rows, :] = d_far
-                if inside:
-                    halo_stiff[base + near, i, 8 * t : 8 * t + 8, :] = st_h[near]
-                    halo_stiff[base + far, i, 8 * t : 8 * t + 8, :] = st_h[far]
-
-    def second(k, carry):
-        for row in range(CORE - 8, CORE + X + 8, 8):
-            rows = pl.ds(row, 8)
-            for i, (c, lap) in enumerate(full_terms(one, k + 2, row, masks)):
-                two[k + 2, i, rows, :] = 2.0 * c - now[k, i, rows, :] + stiff[k, i, rows, :] * lap
+                    half = slice(0, 8) if row < CORE else slice(8, 16)
+                    before, st = now_side[k, i, half, :], stiff_side[k, i, half, :]
+                two[k + 2, i, rows, :] = 2.0 * c - before + st * lap
         return carry
 
     lax.fori_loop(0, Z, second, 0)
     strike(two, 2, place, wavelet(start, 1), Z, CORE - 8, CORE + X + 8)
-
-    for high in (False, True):
-        base = 2 if high else 0
-        zi = Z + 2 if high else 0
-        near, far = (0, 1) if high else (1, 0)
-        n_in, n_next = (Z + 1, Z) if high else (2, 3)
-
-        def tile(t, carry, base=base, zi=zi, near=near, far=far, n_in=n_in, n_next=n_next):
-            row = pl.multiple_of(CORE + 8 * t, 8)
-            rows, own = pl.ds(row, 8), pl.ds(pl.multiple_of(8 * t, 8), 8)
-            terms = {k: plane_terms(delta, base + k, row, masks) for k in range(2)}
-            for i in range(T):
-                for k in range(2):
-                    c, near_sum, far_sum = terms[k][i]
-                    near_sum = near_sum + terms[1 - k][i][0]
-                    if k == near:
-                        near_sum = near_sum + one[n_in, i, rows, :]
-                        far_sum = far_sum + one[n_next, i, rows, :]
-                    else:
-                        far_sum = far_sum + one[n_in, i, rows, :]
-                    lap = 16.0 * near_sum - far_sum - 90.0 * c
-                    two[zi + k, i, rows, :] = (
-                        halo_two[base + k, i, own, :] + 2.0 * c + halo_stiff[base + k, i, own, :] * lap
-                    )
-            return carry
-
-        lax.fori_loop(0, X // 8, tile, 0)
 
     def third(k, carry):
         for row in range(CORE, CORE + X, 8):
             rows = pl.ds(row, 8)
             for i, (c, lap) in enumerate(full_terms(two, k + 2, row, masks)):
-                one[k + 2, i, rows, :] = 2.0 * c - one[k + 2, i, rows, :] + stiff[k, i, rows, :] * lap
+                own = pl.ds(row - CORE, 8)
+                one[k + 2, i, rows, :] = 2.0 * c - one[k + 2, i, rows, :] + stiff[k, i, own, :] * lap
         return carry
 
     lax.fori_loop(0, Z, third, 0)
@@ -431,6 +525,11 @@
     def swap(v, kind):
         return lax.ppermute(v, ("lat", "dep"), swaps(n_lat, n_dep, kind))
 
+    def busy(microseconds):
+        return pl.CostEstimate(
+            flops=int(microseconds * 1.0e9), bytes_accessed=int(microseconds * 3.0e6), transcendentals=0
+        )
+
     def shape(*dims):
         return jax.ShapeDtypeStruct(dims, f32)
 
@@ -450,7 +549,7 @@
             pltpu.SemaphoreType.DMA((4,)),
             pltpu.SemaphoreType.DMA((6,)),
         ],
-        compiler_params=params,
+        compiler_params=pltpu.CompilerParams(vmem_limit_bytes=62 * 1024 * 1024),
         name="pack",
     )(courant_table, pressure_now, pressure_prev, materials)
     early_a = swap(early_1, "d1")
@@ -458,16 +557,28 @@
     side_b = swap(side_2, "l2")
     early_b = swap(early_2, "d2")
 
-    padded = pltpu.VMEM((Z + 4, T, ROWS, 128), f32)
-    now, stiff, one, two = pl.pallas_call(
-        advance_alone,
-        in_specs=[SMEM] * 3 + [VMEM] * 5,
+    padded = (Z + 4, T, ROWS, 128)
+    block, side = (Z, T, X, 128), (Z, T, 16, 128)
+    now, stiff, one, prev = pl.pallas_call(
+        advance_inner,
+        in_specs=[SMEM] + [HBM] * 3,
         out_specs=[VMEM] * 4,
-        out_shape=[shape(Z, T, ROWS, 128)] * 3 + [shape(4, T, ROWS, 128)],
-        scratch_shapes=[padded, pltpu.VMEM((Z, T, ROWS, 128), f32), padded],
+        out_shape=[shape(Z + 4, T, X, 128), shape(*block), shape(*block), shape(*side)],
+        scratch_shapes=[pltpu.VMEM((Z, X, 512), d) for d in (f32, f32, i32)] + [pltpu.SemaphoreType.DMA((3,))],
+        compiler_params=pltpu.CompilerParams(vmem_limit_bytes=INNER_LIMIT),
+        cost_estimate=busy(3.0),
+        name="advance_inner",
+    )(courant_table, pressure_now, pressure_prev, materials)
+    now_side, stiff_side, one, two = pl.pallas_call(
+        advance_outer,
+        in_specs=[SMEM] * 2 + [VMEM] * 6,
+        out_specs=[VMEM] * 4,
+        out_shape=[shape(*side)] * 2 + [shape(Z, T, ROWS, 128), shape(4, T, ROWS, 128)],
+        scratch_shapes=[pltpu.VMEM(padded, f32), pltpu.VMEM(side, f32), pltpu.VMEM(padded, f32)],
         compiler_params=params,
-        name="advance_alone",
-    )(source_cell, start_step, courant_table, pressure_now, pressure_prev, materials, side_a, side_b)
+        cost_estimate=busy(5.0),
+        name="advance_outer",
+    )(source_cell, start_step, now, stiff, one, prev, side_a, side_b)
     late_1, late_2 = pl.pallas_call(
         pack_late,
         in_specs=[VMEM] * 4 + [pl.BlockSpec(memory_space=pl.ANY)] * 2,
@@ -475,26 +586,35 @@
         out_shape=[shape(4, T, X + 8, 128)] * 2,
         compiler_params=params,
         name="pack_late",
-    )(now, stiff, one, two, early_a, early_b)
+    )(now_side, stiff_side, one, two, early_a, early_b)
     late_a = swap(late_1, "d1")
     late_b = swap(late_2, "d2")
-
+    one, two, delta, halo_stiff, halo_two = pl.pallas_call(
+        couple,
+        in_specs=[VMEM] * 5,
+        out_specs=[VMEM] * 5,
+        out_shape=[shape(*padded)] * 2 + [shape(4, T, ROWS, 128)] + [shape(4, T, X, 128)] * 2,
+        compiler_params=params,
+        cost_estimate=busy(4.0),
+        name="couple",
+    )(now, stiff, one, early_a, early_b)
     pressure, partial = pl.pallas_call(
         functools.partial(finish, n_dep),
-        in_specs=[SMEM] * 3 + [VMEM] * 7,
+        in_specs=[SMEM] * 3 + [VMEM] * 11,
         out_specs=[VMEM] * 2,
         out_shape=[shape(Z, X, 512), shape(n_dep, X, 128)],
         scratch_shapes=[
-            padded,
-            padded,
+            pltpu.VMEM(padded, f32),
+            pltpu.VMEM(padded, f32),
             pltpu.VMEM((4, T, ROWS, 128), f32),
-            pltpu.VMEM((4, T, X, 128), f32),
-            pltpu.VMEM((4, T, X, 128), f32),
             pltpu.SMEM((4, BUMPS), f32),
         ],
         compiler_params=params,
         name="finish",
-    )(source_cell, start_step, tf_weights, now, stiff, one, early_a, early_b, late_a, late_b)
+    )(
+        source_cell, start_step, tf_weights, now, stiff, now_side, stiff_side, one, two, delta, halo_stiff, halo_two,
+        late_a, late_b,
+    )
     parts = lax.all_to_all(partial, "dep", 0, 0, tiled=True)
     image = pl.pallas_call(
         composite,

time: 80 us -> 78.2 us (0.978)
  the two profiles are of different devices: /device:TPU:1 before, /device:TPU:96 now
where the time goes in v3:
time: 78.2 us; the launch traced here: 77.8 us
  Pallas kernels  25.2 us (32%)
  blocking collectives  22.9 us (29%)
  starting transfers between devices  17.7 us (23%)
  waiting for transfers between devices  8.1 us (10%)
  local copies, waits for them, and re-layouts  2.46 us (3%)
  between operations  1.46 us (2%)
    all_to_all x1, blocking collectives, on_device(): parts = lax.all_to_all(partial, 'dep', 0, 0, tiled=True)  22.9 us
    ppermute x6, starting transfers between devices, swap(): return lax.ppermute(v, ('lat', 'dep'), swaps(n_lat, n_dep, kind))  17.7 us
    pallas_call x1, Pallas kernels, on_device(): pl.pallas_call(functools.partial(finish, n_dep), in_specs=[SMEM] * 3 + [V...  9.22 us
    ppermute x6, waiting for transfers between devices, swap(): return lax.ppermute(v, ('lat', 'dep'), swaps(n_lat, n_dep, kind))  8.1 us
    pallas_call x1, Pallas kernels, on_device(): pl.pallas_call(pack, in_specs=[SMEM] + [HBM] * 3, out_specs=[VMEM] * 4, o...  5.06 us
    pallas_call x1, Pallas kernels, on_device(): pl.pallas_call(couple, in_specs=[VMEM] * 5, out_specs=[VMEM] * 5, out_sha...  3.46 us
    pallas_call x1, Pallas kernels, on_device(): pl.pallas_call(advance_inner, in_specs=[SMEM] + [HBM] * 3, out_specs=[VME...  3.15 us
    pallas_call x1, Pallas kernels, on_device(): pl.pallas_call(advance_outer, in_specs=[SMEM] * 2 + [VMEM] * 6, out_specs...  2.99 us
  transfers between devices with their start and end apart: 6, of which 1 were waited for; matrix products, arithmetic and copies ran while one was open for 0% of the time, Pallas kernels for 12%

profile of v3, /device:TPU:96, one launch (start us, length us, event | category | flops | bytes accessed | tf_op | source)
XLA Modules:
  0.0 77.8 jit_solution(16465939634557153645)
XLA Ops:
  0.6 0.0 copy-start.5
  0.6 0.0 copy-start
  0.6 5.1 %pack.1 = (f32[4,4,64,128]{3,2,1,0:T(8,128)}, f32[4,4,64,128]{3,2,1,0:T(8,128)}, f32[8,4,16,128]{3,2,1,0:T(8,128)}, f32[8,4,16,128]{3,2,1,0:T(8,128)}) custom-call(f32[16]{0:T(128)} %courant.3, f32[8,64,512]{2,1,0:T(8,128)} %now.1, f32[8,64,512]{2,1,0:T(8,128)} %prev.1, s32[8,64,512]{2,1,0:T(8,128)} %mat.1), custom_call_target="tpu_custom_call" | custom-call | tf_op jit(solution)/shard_map/pack/pallas_call | solution.py:538
  5.7 1.9 %collective-permute-start = (f32[8,4,16,128]{3,2,1,0:T(8,128)}, f32[8,4,16,128]{3,2,1,0:T(8,128)S(1)}, u32[]{:S(2)}, u32[]{:S(2)}) collective-permute-start(f32[8,4,16,128]{3,2,1,0:T(8,128)} %get-tuple-element.27), channel_id=1, source_target_pairs={{0,16},{1,17},{2,18},{3,19},{4,20},{5,21},{6,22},{7,23},{8,24},{9,... | collective-permute-start | bytes 786440 | tf_op jit(solution)/shard_map/ppermute | solution.py:526
  7.6 2.1 %collective-permute-start.1 = (f32[8,4,16,128]{3,2,1,0:T(8,128)}, f32[8,4,16,128]{3,2,1,0:T(8,128)S(1)}, u32[]{:S(2)}, u32[]{:S(2)}) collective-permute-start(f32[8,4,16,128]{3,2,1,0:T(8,128)} %get-tuple-element.28), channel_id=1, source_target_pairs={{16,32},{17,33},{18,34},{19,35},{20,36},{21,37},{22,38},{23,39},{2... | collective-permute-start | bytes 786440 | tf_op jit(solution)/shard_map/ppermute | solution.py:526
  9.8 3.4 %collective-permute-start.2 = (f32[4,4,64,128]{3,2,1,0:T(8,128)}, f32[4,4,64,128]{3,2,1,0:T(8,128)S(1)}, u32[]{:S(2)}, u32[]{:S(2)}) collective-permute-start(f32[4,4,64,128]{3,2,1,0:T(8,128)} %get-tuple-element.32), channel_id=1, source_target_pairs={{0,1},{1,0},{2,3},{3,2},{4,5},{5,4},{6,7},{7,6},{8,9},{9,8},{10,11... | collective-permute-start | bytes 1572872 | tf_op jit(solution)/shard_map/ppermute | solution.py:526
  13.2 0.7 collective-permute-start.3
  13.9 0.0 copy-done.5
  13.9 0.0 copy-done
  13.9 0.0 copy-start.1
  13.9 1.2 %copy-done.1 = f32[8,64,512]{2,1,0:T(8,128)S(1)} copy-done((f32[8,64,512]{2,1,0:T(8,128)S(1)}, f32[8,64,512]{2,1,0:T(8,128)}, u32[]{:S(2)}) %copy-start.1) | copy-done | bytes 1048600
  15.1 0.0 copy-start.2
  15.1 1.2 %copy-done.2 = s32[8,64,512]{2,1,0:T(8,128)S(1)} copy-done((s32[8,64,512]{2,1,0:T(8,128)S(1)}, s32[8,64,512]{2,1,0:T(8,128)}, u32[]{:S(2)}) %copy-start.2) | copy-done | bytes 1048600
  16.4 0.0 copy-start.4
  16.4 3.1 %advance_inner.1 = (f32[12,4,64,128]{3,2,1,0:T(8,128)S(1)}, f32[8,4,64,128]{3,2,1,0:T(8,128)S(1)}, f32[8,4,64,128]{3,2,1,0:T(8,128)S(1)}, f32[8,4,16,128]{3,2,1,0:T(8,128)S(1)}) custom-call(f32[16]{0:T(128)S(1)} %copy-done.5, f32[8,64,512]{2,1,0:T(8,128)S(1)} %copy-done, f32[8,64,512]{2,1,0:T(8,128)S(1)} %copy-done.1, s32[8,64,512]{2,1,0:T(8,128)S(1)} %copy-done.2), custom_call_target="tpu_custom_call" | custom-call | flops 3000000000 | bytes 9000000 | tf_op jit(solution)/shard_map/advance_inner/pallas_call | solution.py:562
  20.2 0.0 collective-permute-done.lat_a
  20.2 0.0 collective-permute-done.1.lat_b
  20.2 0.0 copy-done.4
  20.2 3.0 %advance_outer.1 = (f32[8,4,16,128]{3,2,1,0:T(8,128)S(1)}, f32[8,4,16,128]{3,2,1,0:T(8,128)S(1)}, f32[8,4,96,128]{3,2,1,0:T(8,128)S(1)}, f32[4,4,96,128]{3,2,1,0:T(8,128)S(1)}) custom-call(s32[3]{0:T(128)S(1)} %copy-done.4, s32[1]{0:T(128)S(6)} %copy.9.start, f32[12,4,64,128]{3,2,1,0:T(8,128)S(1)} %get-tuple-element.23.now_in.now, ...), custom_call_target="tpu_custom_call" | custom-call | flops 5000000000 | bytes 15000000 | tf_op jit(solution)/shard_map/advance_outer/pallas_call | solution.py:572
  23.2 0.0 collective-permute-done.2.early_a
  23.2 0.0 collective-permute-done.3.early_b
  23.2 0.1 pack_late.1
  23.3 8.9 %collective-permute-start.4 = (f32[4,4,72,128]{3,2,1,0:T(8,128)S(1)}, f32[4,4,72,128]{3,2,1,0:T(8,128)S(1)}, u32[]{:S(2)}, u32[]{:S(2)}) collective-permute-start(f32[4,4,72,128]{3,2,1,0:T(8,128)S(1)} %get-tuple-element.40), channel_id=1, source_target_pairs={{0,1},{1,0},{2,3},{3,2},{4,5},{5,4},{6,7},{7,6},{8,9},{9,8},{10,11... | collective-permute-start | bytes 1769480 | tf_op jit(solution)/shard_map/ppermute | solution.py:526
  32.2 0.0 copy-start.3
  32.2 0.7 collective-permute-start.5
  33.0 3.5 %couple.1 = (f32[12,4,96,128]{3,2,1,0:T(8,128)S(1)}, f32[12,4,96,128]{3,2,1,0:T(8,128)S(1)}, f32[4,4,96,128]{3,2,1,0:T(8,128)S(1)}, f32[4,4,64,128]{3,2,1,0:T(8,128)S(1)}, f32[4,4,64,128]{3,2,1,0:T(8,128)S(1)}) custom-call(f32[12,4,64,128]{3,2,1,0:T(8,128)S(1)} %get-tuple-element.23.now_in.now, f32[8,4,64,128]{3,2,1,0:T(8,128)S(1)} %get-tuple-element.24.stiff_in.stiff, ...), custom_call_target="tpu_custom_call" | custom-call | flops 4000000000 | bytes 12000000 | tf_op jit(solution)/shard_map/couple/pallas_call | solution.py:592
  36.4 8.1 %collective-permute-done.4.late_a = f32[4,4,72,128]{3,2,1,0:T(8,128)S(1)} collective-permute-done((f32[4,4,72,128]{3,2,1,0:T(8,128)S(1)}, f32[4,4,72,128]{3,2,1,0:T(8,128)S(1)}, u32[]{:S(2)}, u32[]{:S(2)}) %collective-permute-start.4) | collective-permute-done | bytes 589856 | tf_op jit(solution)/shard_map/ppermute | solution.py:526
  44.5 0.0 collective-permute-done.5.late_b
  44.5 0.0 copy-done.3
  44.5 9.2 %finish.1 = (f32[8,64,512]{2,1,0:T(8,128)}, f32[16,64,128]{2,1,0:T(8,128)S(1)}) custom-call(s32[3]{0:T(128)S(1)} %copy-done.4, s32[1]{0:T(128)S(6)} %copy.9.start, f32[4,8]{1,0:T(4,128)S(1)} %copy-done.3, f32[12,4,64,128]{3,2,1,0:T(8,128)S(1)} %get-tuple-element.23.now_in.now, f32[8,4,64,128]{3,2,1,0:T(8,128)S(1)} %get-tuple-element.24.stiff_in.stiff, ...), custom_call_target="tpu_custom_call" | custom-call | tf_op jit(solution)/shard_map/finish/pallas_call | solution.py:601
  53.7 22.9 %all_to_all.5.parts = f32[16,64,128]{2,1,0:T(8,128)S(1)} all-to-all(f32[16,64,128]{2,1,0:T(8,128)S(1)} %get-tuple-element.43), channel_id=1, replica_groups=mesh['lat'=32,'dep'=16] {'dep'}, dimensions={0} | all-to-all | bytes 1048576 | tf_op jit(solution)/shard_map/all_to_all | solution.py:618
  76.6 1.2 %composite.1 = f32[128,64]{1,0:T(8,128)} custom-call(f32[16,64,128]{2,1,0:T(8,128)S(1)} %all_to_all.5.parts), custom_call_target="tpu_custom_call" | custom-call | tf_op jit(solution)/shard_map/composite/pallas_call | solution.py:619
Async XLA Ops:
  0.6 13.2 %copy-start.5 = (f32[16]{0:T(128)S(1)}, f32[16]{0:T(128)}, u32[]{:S(2)}) copy-start(f32[16]{0:T(128)} %courant.3) | copy-start | bytes 196
  0.6 13.2 %copy-start = (f32[8,64,512]{2,1,0:T(8,128)S(1)}, f32[8,64,512]{2,1,0:T(8,128)}, u32[]{:S(2)}) copy-start(f32[8,64,512]{2,1,0:T(8,128)} %now.1) | copy-start | bytes 3145732
  5.7 14.4 %collective-permute-start = (f32[8,4,16,128]{3,2,1,0:T(8,128)}, f32[8,4,16,128]{3,2,1,0:T(8,128)S(1)}, u32[]{:S(2)}, u32[]{:S(2)}) collective-permute-start(f32[8,4,16,128]{3,2,1,0:T(8,128)} %get-tuple-element.27), channel_id=1, source_target_pairs={{0,16},{1,17},{2,18},{3,19},{4,20},{5,21},{6,22},{7,23},{8,24},{9,... | collective-permute-start | bytes 786440 | tf_op jit(solution)/shard_map/ppermute | solution.py:526
  7.6 12.5 %collective-permute-start.1 = (f32[8,4,16,128]{3,2,1,0:T(8,128)}, f32[8,4,16,128]{3,2,1,0:T(8,128)S(1)}, u32[]{:S(2)}, u32[]{:S(2)}) collective-permute-start(f32[8,4,16,128]{3,2,1,0:T(8,128)} %get-tuple-element.28), channel_id=1, source_target_pairs={{16,32},{17,33},{18,34},{19,35},{20,36},{21,37},{22,38},{23,39},{2... | collective-permute-start | bytes 786440 | tf_op jit(solution)/shard_map/ppermute | solution.py:526
  9.8 13.4 %collective-permute-start.2 = (f32[4,4,64,128]{3,2,1,0:T(8,128)}, f32[4,4,64,128]{3,2,1,0:T(8,128)S(1)}, u32[]{:S(2)}, u32[]{:S(2)}) collective-permute-start(f32[4,4,64,128]{3,2,1,0:T(8,128)} %get-tuple-element.32), channel_id=1, source_target_pairs={{0,1},{1,0},{2,3},{3,2},{4,5},{5,4},{6,7},{7,6},{8,9},{9,8},{10,11... | collective-permute-start | bytes 1572872 | tf_op jit(solution)/shard_map/ppermute | solution.py:526
  13.2 10.0 %collective-permute-start.3 = (f32[4,4,64,128]{3,2,1,0:T(8,128)}, f32[4,4,64,128]{3,2,1,0:T(8,128)S(1)}, u32[]{:S(2)}, u32[]{:S(2)}) collective-permute-start(f32[4,4,64,128]{3,2,1,0:T(8,128)} %get-tuple-element.33), channel_id=1, source_target_pairs={{1,2},{2,1},{3,4},{4,3},{5,6},{6,5},{7,8},{8,7},{9,10},{10,9},{11,... | collective-permute-start | bytes 1572872 | tf_op jit(solution)/shard_map/ppermute | solution.py:526
  13.9 1.2 %copy-start.1 = (f32[8,64,512]{2,1,0:T(8,128)S(1)}, f32[8,64,512]{2,1,0:T(8,128)}, u32[]{:S(2)}) copy-start(f32[8,64,512]{2,1,0:T(8,128)} %prev.1) | copy-start | bytes 3145732
  15.1 1.2 %copy-start.2 = (s32[8,64,512]{2,1,0:T(8,128)S(1)}, s32[8,64,512]{2,1,0:T(8,128)}, u32[]{:S(2)}) copy-start(s32[8,64,512]{2,1,0:T(8,128)} %mat.1) | copy-start | bytes 3145732
  16.4 3.8 %copy-start.4 = (s32[3]{0:T(128)S(1)}, s32[3]{0:T(128)}, u32[]{:S(2)}) copy-start(s32[3]{0:T(128)} %cell.3) | copy-start | bytes 40
  23.3 21.2 %collective-permute-start.4 = (f32[4,4,72,128]{3,2,1,0:T(8,128)S(1)}, f32[4,4,72,128]{3,2,1,0:T(8,128)S(1)}, u32[]{:S(2)}, u32[]{:S(2)}) collective-permute-start(f32[4,4,72,128]{3,2,1,0:T(8,128)S(1)} %get-tuple-element.40), channel_id=1, source_target_pairs={{0,1},{1,0},{2,3},{3,2},{4,5},{5,4},{6,7},{7,6},{8,9},{9,8},{10,11... | collective-permute-start | bytes 1769480 | tf_op jit(solution)/shard_map/ppermute | solution.py:526
  32.2 12.3 %copy-start.3 = (f32[4,8]{1,0:T(4,128)S(1)}, f32[4,8]{1,0:T(4,128)}, u32[]{:S(2)}) copy-start(f32[4,8]{1,0:T(4,128)} %transfer.1) | copy-start | bytes 388
  32.2 12.3 %collective-permute-start.5 = (f32[4,4,72,128]{3,2,1,0:T(8,128)S(1)}, f32[4,4,72,128]{3,2,1,0:T(8,128)S(1)}, u32[]{:S(2)}, u32[]{:S(2)}) collective-permute-start(f32[4,4,72,128]{3,2,1,0:T(8,128)S(1)} %get-tuple-element.41), channel_id=1, source_target_pairs={{1,2},{2,1},{3,4},{4,3},{5,6},{6,5},{7,8},{8,7},{9,10},{10,9},{11,... | collective-permute-start | bytes 1769480 | tf_op jit(solution)/shard_map/ppermute | solution.py:526

commit v4 on v3

--- a/solution.py
+++ b/solution.py
@@ -12,7 +12,6 @@
 Z, X, T = 8, 64, 4
 ROWS = X + 32
 CORE = 16
-INNER_LIMIT = 44 * 1024 * 1024
 VMEM = pl.BlockSpec(memory_space=pltpu.VMEM)
 SMEM = pl.BlockSpec(memory_space=pltpu.SMEM)
 HBM = pl.BlockSpec(memory_space=pltpu.HBM)
@@ -110,25 +109,36 @@
 ):
     up1, right1 = ways()
     waits = []
+    depth_waits, side_waits = [], []
+    for slot in range(2):
+        row = pl.multiple_of((X - 8) * right1 if slot == 0 else (X - 8) - (X - 8) * right1, 8)
+        for n, (src, dst) in enumerate(((now, now_x), (prev, prev_x), (mat, mat_x))):
+            side_waits.append(
+                pltpu.make_async_copy(src.at[:, pl.ds(row, 8), :], dst.at[slot], side_sems.at[3 * slot + n])
+            )
     for slot in range(2):
         first = 6 * up1 if slot == 0 else 6 - 6 * up1
         for n, (src, dst) in enumerate(((now, now_z), (mat, mat_z))):
-            waits.append(
+            depth_waits.append(
                 pltpu.make_async_copy(src.at[pl.ds(first, 2)], dst.at[slot], depth_sems.at[2 * slot + n])
             )
-    for slot in range(2):
-        row = pl.multiple_of((X - 8) * right1 if slot == 0 else (X - 8) - (X - 8) * right1, 8)
-        for n, (src, dst) in enumerate(((now, now_x), (prev, prev_x), (mat, mat_x))):
-            waits.append(
-                pltpu.make_async_copy(src.at[:, pl.ds(row, 8), :], dst.at[slot], side_sems.at[3 * slot + n])
-            )
-    for copy in waits:
+    for copy in side_waits + depth_waits:
         copy.start()
     table = stiffness_table(courant)
     upper_half = (lax.broadcasted_iota(jnp.int32, (8, 128), 0) >= 4).astype(jnp.int32)
+    for slot, out in enumerate((side_1, side_2)):
+        for n in range(3):
+            side_waits[3 * slot + n].wait()
+        keep = upper_half == (right1 if slot == 0 else 1 - right1)
+        for k in range(Z):
+            for i in range(T):
+                lanes = slice(128 * i, 128 * i + 128)
+                out[k, i, 0:8, :] = now_x[slot, k, :, lanes]
+                moved = pltpu.roll(stiffness(table, mat_x[slot, k, :, lanes]), 4, 0)
+                out[k, i, 8:16, :] = jnp.where(keep, prev_x[slot, k, :, lanes], moved)
     for slot, out in enumerate((early_1, early_2)):
-        waits[2 * slot].wait()
-        waits[2 * slot + 1].wait()
+        depth_waits[2 * slot].wait()
+        depth_waits[2 * slot + 1].wait()
         for k in range(2):
             for i in range(T):
                 lanes = slice(128 * i, 128 * i + 128)
@@ -136,20 +146,6 @@
                 for t in range(X // 8):
                     rows = slice(8 * t, 8 * t + 8)
                     out[2 + k, i, rows, :] = stiffness(table, mat_z[slot, k, rows, lanes])
-    for slot, out in enumerate((side_1, side_2)):
-        for n in range(3):
-            waits[4 + 3 * slot + n].wait()
-        keep = upper_half == (right1 if slot == 0 else 1 - right1)
-
-        def layer(k, carry, slot=slot, out=out, keep=keep):
-            for i in range(T):
-                lanes = slice(128 * i, 128 * i + 128)
-                out[k, i, 0:8, :] = now_x[slot, k, :, lanes]
-                moved = pltpu.roll(stiffness(table, mat_x[slot, k, :, lanes]), 4, 0)
-                out[k, i, 8:16, :] = jnp.where(keep, prev_x[slot, k, :, lanes], moved)
-            return carry
-
-        lax.fori_loop(0, Z, layer, 0)
 
 
 INNER = range(CORE + 8, CORE + X - 8, 8)
@@ -164,14 +160,15 @@
         copy.start()
     table = stiffness_table(courant)
     masks = lane_masks()
-    zeros = jnp.zeros((T, X, 128), jnp.float32)
+    zeros = jnp.zeros((T, ROWS, 128), jnp.float32)
     for k in (0, 1, Z + 2, Z + 3):
         now_out[k] = zeros
+        one_out[k] = zeros
     copies[0].wait()
 
     def fill(k, carry):
         for i in range(T):
-            now_out[k + 2, i] = now[k, :, 128 * i : 128 * i + 128]
+            now_out[k + 2, i, CORE : CORE + X, :] = now[k, :, 128 * i : 128 * i + 128]
         return carry
 
     lax.fori_loop(0, Z, fill, 0)
@@ -186,33 +183,26 @@
             for t in range(X // 8):
                 rows = slice(8 * t, 8 * t + 8)
                 stiff_out[k, i, rows, :] = stiffness(table, mat[k, rows, lanes])
-        for row in range(8, X - 8, 8):
-            rows = slice(row, row + 8)
+        for row in INNER:
+            own = slice(row - CORE, row - CORE + 8)
             for i, (c, lap) in enumerate(full_terms(now_out, k + 2, row, masks)):
-                before = prev[k, rows, 128 * i : 128 * i + 128]
-                one_out[k, i, rows, :] = 2.0 * c - before + stiff_out[k, i, rows, :] * lap
+                before = prev[k, own, 128 * i : 128 * i + 128]
+                one_out[k + 2, i, row : row + 8, :] = 2.0 * c - before + stiff_out[k, i, own, :] * lap
         return carry
 
     lax.fori_loop(0, Z, first, 0)
 
 
 def advance_outer(
-    cell, start, now_in, stiff_in, one_in, prev_in, lat_a, lat_b, now_side, stiff_side, one_out, two_out,
-    now, prev_side, one,
+    cell, start, now_in, stiff_in, one_in, prev_in, lat_a, lat_b, now, one, now_side, stiff_side, two_out,
+    prev_side,
 ):
+    del now_in, one_in
     masks = lane_masks()
-    place = source_place(cell)
     right1 = ways()[1] == 1
-    core = slice(CORE, CORE + X)
-    zeros = jnp.zeros((T, ROWS, 128), jnp.float32)
-    for k in (0, 1, Z + 2, Z + 3):
-        now[k] = zeros
-        one[k] = zeros
 
     def fill(k, carry):
         for i in range(T):
-            now[k + 2, i, core, :] = now_in[k + 2, i]
-            one[k + 2, i, CORE + 8 : CORE + X - 8, :] = one_in[k, i, 8 : X - 8, :]
             for left in (False, True):
                 wanted = jnp.logical_not(right1) if left else right1
                 got = jnp.where(wanted, lat_a[k, i], lat_b[k, i])
@@ -240,6 +230,7 @@
         return carry
 
     lax.fori_loop(0, Z, first, 0)
+    place = source_place(cell)
     strike(one, 2, place, wavelet(start, 0), Z, CORE - 8, CORE + X + 8)
 
     def second(n, carry):
@@ -255,12 +246,6 @@
     z = place[0]
     inner = (z >= 2) & (z < Z - 2)
     strike(two_out, 0, (jnp.where(inner, -1, jnp.where(z < 2, z, z - 4)),) + place[1:], wavelet(start, 1), 4, CORE, CORE + X)
-
-    def keep(k, carry):
-        one_out[k] = one[k + 2]
-        return carry
-
-    lax.fori_loop(0, Z, keep, 0)
 
 
 def pack_late(now_side, stiff_side, one, two, early_a, early_b, out_a, out_b):
@@ -272,10 +257,10 @@
         for k in range(2):
             z = (Z - 2) * high + k
             for i in range(T):
-                out[k, i, 0:X, :] = one[z, i, CORE : CORE + X, :]
+                out[k, i, 0:X, :] = one[z + 2, i, CORE : CORE + X, :]
                 out[2 + k, i, 0:X, :] = two[2 * high + k, i, CORE : CORE + X, :]
                 out[k, i, X : X + 8, :] = jnp.where(sub >= 4, now_side[z, i, 0:8, :], now_side[z, i, 8:16, :])
-                ones = jnp.where(sub >= 4, one[z, i, left, :], one[z, i, right, :])
+                ones = jnp.where(sub >= 4, one[z + 2, i, left, :], one[z + 2, i, right, :])
                 side = jnp.where(sub >= 4, stiff_side[z, i, 0:8, :], stiff_side[z, i, 8:16, :])
                 outer = (sub < 2) | (sub >= 6)
                 out[2 + k, i, X : X + 8, :] = jnp.where(outer, ones, pltpu.roll(side, 4, 0))
@@ -306,15 +291,10 @@
     return out
 
 
-def couple(now, stiff, one_in, early_a, early_b, one, two, delta, halo_stiff, halo_two):
+def couple(now, stiff, one_in, early_a, early_b, sent, one, two, delta, halo_stiff, halo_two):
+    del one_in, sent
     masks = lane_masks()
     up1 = ways()[0] == 1
-
-    def copy(k, carry):
-        one[k + 2] = one_in[k]
-        return carry
-
-    lax.fori_loop(0, Z, copy, 0)
     for high, base, near, far, n_in, n_next, zi in SIDES:
         use_a = up1 if high else jnp.logical_not(up1)
 
@@ -325,8 +305,8 @@
                 st_h = [jnp.where(use_a, early_a[2 + k, i, own, :], early_b[2 + k, i, own, :]) for k in range(2)]
                 one[n_in + 2, i, rows, :] += stiff[n_in, i, own, :] * (16.0 * zero_h[near] - zero_h[far])
                 one[n_next + 2, i, rows, :] -= stiff[n_next, i, own, :] * zero_h[near]
-                d_near = st_h[near] * (16.0 * now[n_in + 2, i, own, :] - now[n_next + 2, i, own, :])
-                d_far = -st_h[far] * now[n_in + 2, i, own, :]
+                d_near = st_h[near] * (16.0 * now[n_in + 2, i, rows, :] - now[n_next + 2, i, rows, :])
+                d_far = -st_h[far] * now[n_in + 2, i, rows, :]
                 for place, d, st in ((near, d_near, st_h[near]), (far, d_far, st_h[far])):
                     one[zi + place, i, rows, :] = d
                     delta[base + place, i, rows, :] = d
@@ -340,7 +320,7 @@
             rows = slice(row, row + 8)
             for i, (c, lap) in enumerate(full_terms(one, k + 2, row, masks)):
                 own = slice(row - CORE, row - CORE + 8)
-                two[k + 2, i, rows, :] = 2.0 * c - now[k + 2, i, own, :] + stiff[k, i, own, :] * lap
+                two[k + 2, i, rows, :] = 2.0 * c - now[k + 2, i, rows, :] + stiff[k, i, own, :] * lap
         return carry
 
     lax.fori_loop(0, Z, second, 0)
@@ -359,22 +339,13 @@
     n_dep, cell, start, transfer, now, stiff, now_side, stiff_side, one_in, two_in, delta_in, halo_stiff, halo_two,
     late_a, late_b, pressure, partial, one, two, delta, weights,
 ):
+    del one_in, two_in, delta_in
     masks = lane_masks()
-    place = source_place(cell)
     up1 = ways()[0] == 1
     for n in range(4):
         for j in range(BUMPS):
             centre = (-3.0 + 6.0 * j / (BUMPS - 1)) / 0.8
             weights[n, j] = transfer[n, j] * (math.exp(-centre * centre) * (1.5 / (Z * n_dep) if n == 3 else 1.0))
-
-    def copy(k, carry):
-        one[k] = one_in[k]
-        two[k, :, CORE + 8 : CORE + X - 8, :] = two_in[k, :, CORE + 8 : CORE + X - 8, :]
-        return carry
-
-    lax.fori_loop(0, Z + 4, copy, 0)
-    for k in range(4):
-        delta[k] = delta_in[k]
 
     for high, base, near, far, n_in, n_next, zi in SIDES:
         use_a = up1 if high else jnp.logical_not(up1)
@@ -419,15 +390,14 @@
             rows = slice(row, row + 8)
             for i, (c, lap) in enumerate(full_terms(one, k + 2, row, masks)):
                 if CORE <= row < CORE + X:
-                    own = slice(row - CORE, row - CORE + 8)
-                    before, st = now[k + 2, i, own, :], stiff[k, i, own, :]
+                    st = stiff[k, i, row - CORE : row - CORE + 8, :]
                 else:
-                    half = slice(0, 8) if row < CORE else slice(8, 16)
-                    before, st = now_side[k, i, half, :], stiff_side[k, i, half, :]
-                two[k + 2, i, rows, :] = 2.0 * c - before + st * lap
+                    st = stiff_side[k, i, 0:8, :] if row < CORE else stiff_side[k, i, 8:16, :]
+                two[k + 2, i, rows, :] = 2.0 * c - now[k + 2, i, rows, :] + st * lap
         return carry
 
     lax.fori_loop(0, Z, second, 0)
+    place = source_place(cell)
     strike(two, 2, place, wavelet(start, 1), Z, CORE - 8, CORE + X + 8)
 
     def third(k, carry):
@@ -533,13 +503,20 @@
     def shape(*dims):
         return jax.ShapeDtypeStruct(dims, f32)
 
+    def kept(*dims):
+        return pltpu.VMEM(dims, f32)
+
+    def in_hbm(v):
+        return pltpu.with_memory_space_constraint(v, pltpu.HBM)
+
     params = pltpu.CompilerParams(vmem_limit_bytes=24 * 1024 * 1024)
     i32 = jnp.int32
+    inputs = [in_hbm(v) for v in (pressure_now, pressure_prev, materials)]
     early_1, early_2, side_1, side_2 = pl.pallas_call(
         pack,
         in_specs=[SMEM] + [HBM] * 3,
         out_specs=[VMEM] * 4,
-        out_shape=[shape(4, T, X, 128)] * 2 + [shape(Z, T, 16, 128)] * 2,
+        out_shape=[kept(4, T, X, 128)] * 2 + [kept(Z, T, 16, 128)] * 2,
         scratch_shapes=[
             pltpu.VMEM((2, 2, X, 512), f32),
             pltpu.VMEM((2, 2, X, 512), i32),
@@ -549,12 +526,12 @@
             pltpu.SemaphoreType.DMA((4,)),
             pltpu.SemaphoreType.DMA((6,)),
         ],
-        compiler_params=pltpu.CompilerParams(vmem_limit_bytes=62 * 1024 * 1024),
+        compiler_params=params,
         name="pack",
-    )(courant_table, pressure_now, pressure_prev, materials)
-    early_a = swap(early_1, "d1")
+    )(courant_table, *inputs)
     side_a = swap(side_1, "l1")
     side_b = swap(side_2, "l2")
+    early_a = swap(early_1, "d1")
     early_b = swap(early_2, "d2")
 
     padded = (Z + 4, T, ROWS, 128)
@@ -563,18 +540,19 @@
         advance_inner,
         in_specs=[SMEM] + [HBM] * 3,
         out_specs=[VMEM] * 4,
-        out_shape=[shape(Z + 4, T, X, 128), shape(*block), shape(*block), shape(*side)],
+        out_shape=[kept(*padded), kept(*block), kept(*padded), kept(*side)],
         scratch_shapes=[pltpu.VMEM((Z, X, 512), d) for d in (f32, f32, i32)] + [pltpu.SemaphoreType.DMA((3,))],
-        compiler_params=pltpu.CompilerParams(vmem_limit_bytes=INNER_LIMIT),
+        compiler_params=params,
         cost_estimate=busy(3.0),
         name="advance_inner",
-    )(courant_table, pressure_now, pressure_prev, materials)
-    now_side, stiff_side, one, two = pl.pallas_call(
+    )(courant_table, *inputs)
+    now, one, now_side, stiff_side, two = pl.pallas_call(
         advance_outer,
         in_specs=[SMEM] * 2 + [VMEM] * 6,
-        out_specs=[VMEM] * 4,
-        out_shape=[shape(*side)] * 2 + [shape(Z, T, ROWS, 128), shape(4, T, ROWS, 128)],
-        scratch_shapes=[pltpu.VMEM(padded, f32), pltpu.VMEM(side, f32), pltpu.VMEM(padded, f32)],
+        out_specs=[VMEM] * 5,
+        out_shape=[kept(*padded)] * 2 + [kept(*side)] * 2 + [kept(4, T, ROWS, 128)],
+        scratch_shapes=[pltpu.VMEM(side, f32)],
+        input_output_aliases={2: 0, 4: 1},
         compiler_params=params,
         cost_estimate=busy(5.0),
         name="advance_outer",
@@ -583,7 +561,7 @@
         pack_late,
         in_specs=[VMEM] * 4 + [pl.BlockSpec(memory_space=pl.ANY)] * 2,
         out_specs=[VMEM] * 2,
-        out_shape=[shape(4, T, X + 8, 128)] * 2,
+        out_shape=[kept(4, T, X + 8, 128)] * 2,
         compiler_params=params,
         name="pack_late",
     )(now_side, stiff_side, one, two, early_a, early_b)
@@ -591,29 +569,26 @@
     late_b = swap(late_2, "d2")
     one, two, delta, halo_stiff, halo_two = pl.pallas_call(
         couple,
-        in_specs=[VMEM] * 5,
+        in_specs=[VMEM] * 5 + [pl.BlockSpec(memory_space=pl.ANY)],
         out_specs=[VMEM] * 5,
-        out_shape=[shape(*padded)] * 2 + [shape(4, T, ROWS, 128)] + [shape(4, T, X, 128)] * 2,
+        out_shape=[kept(*padded)] * 2 + [kept(4, T, ROWS, 128)] + [kept(4, T, X, 128)] * 2,
+        input_output_aliases={2: 0},
         compiler_params=params,
         cost_estimate=busy(4.0),
         name="couple",
-    )(now, stiff, one, early_a, early_b)
-    pressure, partial = pl.pallas_call(
+    )(now, stiff, one, early_a, early_b, late_1)
+    pressure, partial, _, _, _ = pl.pallas_call(
         functools.partial(finish, n_dep),
         in_specs=[SMEM] * 3 + [VMEM] * 11,
-        out_specs=[VMEM] * 2,
-        out_shape=[shape(Z, X, 512), shape(n_dep, X, 128)],
-        scratch_shapes=[
-            pltpu.VMEM(padded, f32),
-            pltpu.VMEM(padded, f32),
-            pltpu.VMEM((4, T, ROWS, 128), f32),
-            pltpu.SMEM((4, BUMPS), f32),
-        ],
+        out_specs=[VMEM] * 5,
+        out_shape=[shape(Z, X, 512), shape(n_dep, X, 128)] + [kept(*padded)] * 2 + [kept(4, T, ROWS, 128)],
+        scratch_shapes=[pltpu.SMEM((4, BUMPS), f32)],
+        input_output_aliases={7: 2, 8: 3, 9: 4},
         compiler_params=params,
         name="finish",
     )(
-        source_cell, start_step, tf_weights, now, stiff, now_side, stiff_side, one, two, delta, halo_stiff, halo_two,
-        late_a, late_b,
+        source_cell, start_step, tf_weights, now, stiff, now_side, stiff_side, one, two, delta, halo_stiff,
+        halo_two, late_a, late_b,
     )
     parts = lax.all_to_all(partial, "dep", 0, 0, tiled=True)
     image = pl.pallas_call(

time: 78.2 us -> 77.8 us (level)
  the two profiles are of different devices: /device:TPU:96 before, /device:TPU:1 now
where the time goes in v4:
time: 77.8 us; the launch traced here: 76.3 us
  Pallas kernels  23.8 us (31%)
  blocking collectives  20.3 us (26%)
  starting transfers between devices  15.9 us (20%)
  waiting for transfers between devices  14.3 us (18%)
  between operations  1.42 us (2%)
    all_to_all x1, blocking collectives, on_device(): parts = lax.all_to_all(partial, 'dep', 0, 0, tiled=True)  20.3 us
    ppermute x6, starting transfers between devices, swap(): return lax.ppermute(v, ('lat', 'dep'), swaps(n_lat, n_dep, kind))  15.9 us
    ppermute x6, waiting for transfers between devices, swap(): return lax.ppermute(v, ('lat', 'dep'), swaps(n_lat, n_dep, kind))  14.3 us
    pallas_call x1, Pallas kernels, on_device(): pl.pallas_call(functools.partial(finish, n_dep), in_specs=[SMEM] * 3 + [V...  8.91 us
    pallas_call x1, Pallas kernels, on_device(): pl.pallas_call(advance_inner, in_specs=[SMEM] + [HBM] * 3, out_specs=[VME...  4.69 us
    pallas_call x1, Pallas kernels, on_device(): pl.pallas_call(couple, in_specs=[VMEM] * 5 + [pl.BlockSpec(memory_space=p...  3.36 us
    pallas_call x1, Pallas kernels, on_device(): pl.pallas_call(pack, in_specs=[SMEM] + [HBM] * 3, out_specs=[VMEM] * 4, o...  2.78 us
    pallas_call x1, Pallas kernels, on_device(): pl.pallas_call(advance_outer, in_specs=[SMEM] * 2 + [VMEM] * 6, out_specs...  2.77 us
  transfers between devices with their start and end apart: 6, of which 2 were waited for; matrix products, arithmetic and copies ran while one was open for 0% of the time, Pallas kernels for 14%

profile of v4, /device:TPU:1, one launch (start us, length us, event | category | flops | bytes accessed | tf_op | source)
XLA Modules:
  0.0 76.3 jit_solution(17830731926744844156)
XLA Ops:
  0.6 0.0 copy-start.2
  0.6 0.6 copy-done.2
  1.3 2.8 %pack.1 = (f32[4,4,64,128]{3,2,1,0:T(8,128)S(1)}, f32[4,4,64,128]{3,2,1,0:T(8,128)S(1)}, f32[8,4,16,128]{3,2,1,0:T(8,128)S(1)}, f32[8,4,16,128]{3,2,1,0:T(8,128)S(1)}) custom-call(f32[16]{0:T(128)S(1)} %copy-done.2, f32[8,64,512]{2,1,0:T(8,128)} %now.1, f32[8,64,512]{2,1,0:T(8,128)} %prev.1, s32[8,64,512]{2,1,0:T(8,128)} %mat.1), custom_call_target="tpu_custom_call" | custom-call | tf_op jit(solution)/shard_map/pack/pallas_call | solution.py:515
  4.1 8.8 %collective-permute-start = (f32[8,4,16,128]{3,2,1,0:T(8,128)S(1)}, f32[8,4,16,128]{3,2,1,0:T(8,128)S(1)}, u32[]{:S(2)}, u32[]{:S(2)}) collective-permute-start(f32[8,4,16,128]{3,2,1,0:T(8,128)S(1)} %get-tuple-element.28), channel_id=1, source_target_pairs={{0,16},{1,17},{2,18},{3,19},{4,20},{5,21},{6,22},{7,23},{8,24},{9,... | collective-permute-start | bytes 786440 | tf_op jit(solution)/shard_map/ppermute | solution.py:496
  12.9 1.9 %collective-permute-start.1 = (f32[8,4,16,128]{3,2,1,0:T(8,128)S(1)}, f32[8,4,16,128]{3,2,1,0:T(8,128)S(1)}, u32[]{:S(2)}, u32[]{:S(2)}) collective-permute-start(f32[8,4,16,128]{3,2,1,0:T(8,128)S(1)} %get-tuple-element.29), channel_id=1, source_target_pairs={{16,32},{17,33},{18,34},{19,35},{20,36},{21,37},{22,38},{23,39},{2... | collective-permute-start | bytes 786440 | tf_op jit(solution)/shard_map/ppermute | solution.py:496
  14.8 0.7 collective-permute-start.2
  15.5 0.0 copy-start.1
  15.5 1.9 %collective-permute-start.3 = (f32[4,4,64,128]{3,2,1,0:T(8,128)S(1)}, f32[4,4,64,128]{3,2,1,0:T(8,128)S(1)}, u32[]{:S(2)}, u32[]{:S(2)}) collective-permute-start(f32[4,4,64,128]{3,2,1,0:T(8,128)S(1)} %get-tuple-element.35), channel_id=1, source_target_pairs={{1,2},{2,1},{3,4},{4,3},{5,6},{6,5},{7,8},{8,7},{9,10},{10,9},{11,... | collective-permute-start | bytes 1572872 | tf_op jit(solution)/shard_map/ppermute | solution.py:496
  17.4 4.7 %advance_inner.1 = (f32[12,4,96,128]{3,2,1,0:T(8,128)S(1)}, f32[8,4,64,128]{3,2,1,0:T(8,128)S(1)}, f32[12,4,96,128]{3,2,1,0:T(8,128)S(1)}, f32[8,4,16,128]{3,2,1,0:T(8,128)S(1)}) custom-call(f32[16]{0:T(128)S(1)} %copy-done.2, f32[8,64,512]{2,1,0:T(8,128)} %now.1, f32[8,64,512]{2,1,0:T(8,128)} %prev.1, s32[8,64,512]{2,1,0:T(8,128)} %mat.1), custom_call_target="tpu_custom_call" | custom-call | flops 3000000000 | bytes 9000000 | tf_op jit(solution)/shard_map/advance_inner/pallas_call | solution.py:539
  22.8 0.0 collective-permute-done.lat_a
  22.8 0.0 collective-permute-done.1.lat_b
  22.8 0.0 copy-done.1
  22.8 2.8 %advance_outer.1 = (f32[12,4,96,128]{3,2,1,0:T(8,128)S(1)}, f32[12,4,96,128]{3,2,1,0:T(8,128)S(1)}, f32[8,4,16,128]{3,2,1,0:T(8,128)S(1)}, f32[8,4,16,128]{3,2,1,0:T(8,128)S(1)}, f32[4,4,96,128]{3,2,1,0:T(8,128)S(1)}) custom-call(s32[3]{0:T(128)S(1)} %copy-done.1, s32[1]{0:T(128)S(6)} %copy.21.start, ...), custom_call_target="tpu_custom_call", output_to_operand_aliasing={{0}: (2, {}), {1}: (4, {})} | custom-call | flops 5000000000 | bytes 15000000 | tf_op jit(solution)/shard_map/advance_outer/pallas_call | solution.py:549
  25.6 0.0 collective-permute-done.2.early_a
  25.6 4.0 %collective-permute-done.3.early_b = f32[4,4,64,128]{3,2,1,0:T(8,128)S(1)} collective-permute-done((f32[4,4,64,128]{3,2,1,0:T(8,128)S(1)}, f32[4,4,64,128]{3,2,1,0:T(8,128)S(1)}, u32[]{:S(2)}, u32[]{:S(2)}) %collective-permute-start.3) | collective-permute-done | bytes 524320 | tf_op jit(solution)/shard_map/ppermute | solution.py:496
  29.6 0.1 pack_late.1
  29.7 1.9 %collective-permute-start.5 = (f32[4,4,72,128]{3,2,1,0:T(8,128)S(1)}, f32[4,4,72,128]{3,2,1,0:T(8,128)S(1)}, u32[]{:S(2)}, u32[]{:S(2)}) collective-permute-start(f32[4,4,72,128]{3,2,1,0:T(8,128)S(1)} %get-tuple-element.43), channel_id=1, source_target_pairs={{1,2},{2,1},{3,4},{4,3},{5,6},{6,5},{7,8},{8,7},{9,10},{10,9},{11,... | collective-permute-start | bytes 1769480 | tf_op jit(solution)/shard_map/ppermute | solution.py:496
  31.6 0.7 collective-permute-start.4
  32.3 0.0 copy-start
  32.3 3.4 %couple.1 = (f32[12,4,96,128]{3,2,1,0:T(8,128)S(1)}, f32[12,4,96,128]{3,2,1,0:T(8,128)S(1)}, f32[4,4,96,128]{3,2,1,0:T(8,128)S(1)}, f32[4,4,64,128]{3,2,1,0:T(8,128)S(1)}, f32[4,4,64,128]{3,2,1,0:T(8,128)S(1)}) custom-call(f32[12,4,96,128]{3,2,1,0:T(8,128)S(1)} %get-tuple-element.30.now, ...), custom_call_target="tpu_custom_call", output_to_operand_aliasing={{0}: (2, {})} | custom-call | flops 4000000000 | bytes 12000000 | tf_op jit(solution)/shard_map/couple/pallas_call | solution.py:570
  35.7 10.3 %collective-permute-done.5.late_b = f32[4,4,72,128]{3,2,1,0:T(8,128)S(1)} collective-permute-done((f32[4,4,72,128]{3,2,1,0:T(8,128)S(1)}, f32[4,4,72,128]{3,2,1,0:T(8,128)S(1)}, u32[]{:S(2)}, u32[]{:S(2)}) %collective-permute-start.5) | collective-permute-done | bytes 589856 | tf_op jit(solution)/shard_map/ppermute | solution.py:496
  46.0 0.0 collective-permute-done.4.late_a
  46.0 0.0 copy-done
  46.0 8.9 %finish.1 = (f32[8,64,512]{2,1,0:T(8,128)}, f32[16,64,128]{2,1,0:T(8,128)S(1)}, f32[12,4,96,128]{3,2,1,0:T(8,128)S(1)}, f32[12,4,96,128]{3,2,1,0:T(8,128)S(1)}, f32[4,4,96,128]{3,2,1,0:T(8,128)S(1)}) custom-call(s32[3]{0:T(128)S(1)} %copy-done.1, s32[1]{0:T(128)S(6)} %copy.21.start, ...), custom_call_target="tpu_custom_call", output_to_operand_aliasing={{2}: (7, {}), {3}: (8, {}), {4}: (9, {})} | custom-call | tf_op jit(solution)/shard_map/finish/pallas_call | solution.py:580
  54.9 20.3 %all_to_all.5.parts = f32[16,64,128]{2,1,0:T(8,128)S(1)} all-to-all(f32[16,64,128]{2,1,0:T(8,128)S(1)} %get-tuple-element.45), channel_id=1, replica_groups=mesh['lat'=32,'dep'=16] {'dep'}, dimensions={0} | all-to-all | bytes 1048576 | tf_op jit(solution)/shard_map/all_to_all | solution.py:593
  75.1 1.2 %composite.1 = f32[128,64]{1,0:T(8,128)} custom-call(f32[16,64,128]{2,1,0:T(8,128)S(1)} %all_to_all.5.parts), custom_call_target="tpu_custom_call" | custom-call | tf_op jit(solution)/shard_map/composite/pallas_call | solution.py:594
Async XLA Ops:
  0.6 0.7 copy-start.2
  4.1 18.7 %collective-permute-start = (f32[8,4,16,128]{3,2,1,0:T(8,128)S(1)}, f32[8,4,16,128]{3,2,1,0:T(8,128)S(1)}, u32[]{:S(2)}, u32[]{:S(2)}) collective-permute-start(f32[8,4,16,128]{3,2,1,0:T(8,128)S(1)} %get-tuple-element.28), channel_id=1, source_target_pairs={{0,16},{1,17},{2,18},{3,19},{4,20},{5,21},{6,22},{7,23},{8,24},{9,... | collective-permute-start | bytes 786440 | tf_op jit(solution)/shard_map/ppermute | solution.py:496
  12.9 9.9 %collective-permute-start.1 = (f32[8,4,16,128]{3,2,1,0:T(8,128)S(1)}, f32[8,4,16,128]{3,2,1,0:T(8,128)S(1)}, u32[]{:S(2)}, u32[]{:S(2)}) collective-permute-start(f32[8,4,16,128]{3,2,1,0:T(8,128)S(1)} %get-tuple-element.29), channel_id=1, source_target_pairs={{16,32},{17,33},{18,34},{19,35},{20,36},{21,37},{22,38},{23,39},{2... | collective-permute-start | bytes 786440 | tf_op jit(solution)/shard_map/ppermute | solution.py:496
  14.8 10.8 %collective-permute-start.2 = (f32[4,4,64,128]{3,2,1,0:T(8,128)S(1)}, f32[4,4,64,128]{3,2,1,0:T(8,128)S(1)}, u32[]{:S(2)}, u32[]{:S(2)}) collective-permute-start(f32[4,4,64,128]{3,2,1,0:T(8,128)S(1)} %get-tuple-element.34), channel_id=1, source_target_pairs={{0,1},{1,0},{2,3},{3,2},{4,5},{5,4},{6,7},{7,6},{8,9},{9,8},{10,11... | collective-permute-start | bytes 1572872 | tf_op jit(solution)/shard_map/ppermute | solution.py:496
  15.5 7.3 %copy-start.1 = (s32[3]{0:T(128)S(1)}, s32[3]{0:T(128)}, u32[]{:S(2)}) copy-start(s32[3]{0:T(128)} %cell.3) | copy-start | bytes 40
  15.5 14.1 %collective-permute-start.3 = (f32[4,4,64,128]{3,2,1,0:T(8,128)S(1)}, f32[4,4,64,128]{3,2,1,0:T(8,128)S(1)}, u32[]{:S(2)}, u32[]{:S(2)}) collective-permute-start(f32[4,4,64,128]{3,2,1,0:T(8,128)S(1)} %get-tuple-element.35), channel_id=1, source_target_pairs={{1,2},{2,1},{3,4},{4,3},{5,6},{6,5},{7,8},{8,7},{9,10},{10,9},{11,... | collective-permute-start | bytes 1572872 | tf_op jit(solution)/shard_map/ppermute | solution.py:496
  29.7 16.3 %collective-permute-start.5 = (f32[4,4,72,128]{3,2,1,0:T(8,128)S(1)}, f32[4,4,72,128]{3,2,1,0:T(8,128)S(1)}, u32[]{:S(2)}, u32[]{:S(2)}) collective-permute-start(f32[4,4,72,128]{3,2,1,0:T(8,128)S(1)} %get-tuple-element.43), channel_id=1, source_target_pairs={{1,2},{2,1},{3,4},{4,3},{5,6},{6,5},{7,8},{8,7},{9,10},{10,9},{11,... | collective-permute-start | bytes 1769480 | tf_op jit(solution)/shard_map/ppermute | solution.py:496
  31.6 14.4 %collective-permute-start.4 = (f32[4,4,72,128]{3,2,1,0:T(8,128)S(1)}, f32[4,4,72,128]{3,2,1,0:T(8,128)S(1)}, u32[]{:S(2)}, u32[]{:S(2)}) collective-permute-start(f32[4,4,72,128]{3,2,1,0:T(8,128)S(1)} %get-tuple-element.37.sent), channel_id=1, source_target_pairs={{0,1},{1,0},{2,3},{3,2},{4,5},{5,4},{6,7},{7,6},{8,9},{9,8},{10,11... | collective-permute-start | bytes 1769480 | tf_op jit(solution)/shard_map/ppermute | solution.py:496
  32.3 13.7 %copy-start = (f32[4,8]{1,0:T(4,128)S(1)}, f32[4,8]{1,0:T(4,128)}, u32[]{:S(2)}) copy-start(f32[4,8]{1,0:T(4,128)} %transfer.1) | copy-start | bytes 388

commit v5 on v4

--- a/solution.py
+++ b/solution.py
@@ -9,6 +9,7 @@
 from jax.sharding import PartitionSpec as P
 
 BUMPS = 8
+LOG2E = math.log2(math.e)
 Z, X, T = 8, 64, 4
 ROWS = X + 32
 CORE = 16
@@ -104,67 +105,53 @@
 
 
 def pack(
-    courant, now, prev, mat, early_1, early_2, side_1, side_2,
-    now_z, mat_z, now_x, prev_x, mat_x, depth_sems, side_sems,
+    courant_in, now_in, prev_in, mat_in, early_1, early_2, side_1, side_2, now, prev, mat, courant, sems,
 ):
     up1, right1 = ways()
-    waits = []
-    depth_waits, side_waits = [], []
-    for slot in range(2):
-        row = pl.multiple_of((X - 8) * right1 if slot == 0 else (X - 8) - (X - 8) * right1, 8)
-        for n, (src, dst) in enumerate(((now, now_x), (prev, prev_x), (mat, mat_x))):
-            side_waits.append(
-                pltpu.make_async_copy(src.at[:, pl.ds(row, 8), :], dst.at[slot], side_sems.at[3 * slot + n])
-            )
-    for slot in range(2):
+    copies = [
+        pltpu.make_async_copy(src, dst, sems.at[n])
+        for n, (src, dst) in enumerate(((courant_in, courant), (mat_in, mat), (now_in, now), (prev_in, prev)))
+    ]
+    for copy in copies:
+        copy.start()
+    upper_half = (lax.broadcasted_iota(jnp.int32, (8, 128), 0) >= 4).astype(jnp.int32)
+    copies[0].wait()
+    table = stiffness_table(courant)
+    copies[1].wait()
+    copies[2].wait()
+    for slot, out in enumerate((early_1, early_2)):
         first = 6 * up1 if slot == 0 else 6 - 6 * up1
-        for n, (src, dst) in enumerate(((now, now_z), (mat, mat_z))):
-            depth_waits.append(
-                pltpu.make_async_copy(src.at[pl.ds(first, 2)], dst.at[slot], depth_sems.at[2 * slot + n])
-            )
-    for copy in side_waits + depth_waits:
-        copy.start()
-    table = stiffness_table(courant)
-    upper_half = (lax.broadcasted_iota(jnp.int32, (8, 128), 0) >= 4).astype(jnp.int32)
+        for k in range(2):
+            for i in range(T):
+                lanes = slice(128 * i, 128 * i + 128)
+                out[k, i] = now[first + k, :, lanes]
+                for t in range(X // 8):
+                    rows = slice(8 * t, 8 * t + 8)
+                    out[2 + k, i, rows, :] = stiffness(table, mat[first + k, rows, lanes])
+    copies[3].wait()
     for slot, out in enumerate((side_1, side_2)):
-        for n in range(3):
-            side_waits[3 * slot + n].wait()
-        keep = upper_half == (right1 if slot == 0 else 1 - right1)
+        right = right1 if slot == 0 else 1 - right1
+        rows = pl.ds(pl.multiple_of((X - 8) * right, 8), 8)
+        keep = upper_half == right
         for k in range(Z):
             for i in range(T):
                 lanes = slice(128 * i, 128 * i + 128)
-                out[k, i, 0:8, :] = now_x[slot, k, :, lanes]
-                moved = pltpu.roll(stiffness(table, mat_x[slot, k, :, lanes]), 4, 0)
-                out[k, i, 8:16, :] = jnp.where(keep, prev_x[slot, k, :, lanes], moved)
-    for slot, out in enumerate((early_1, early_2)):
-        depth_waits[2 * slot].wait()
-        depth_waits[2 * slot + 1].wait()
-        for k in range(2):
-            for i in range(T):
-                lanes = slice(128 * i, 128 * i + 128)
-                out[k, i] = now_z[slot, k, :, lanes]
-                for t in range(X // 8):
-                    rows = slice(8 * t, 8 * t + 8)
-                    out[2 + k, i, rows, :] = stiffness(table, mat_z[slot, k, rows, lanes])
+                out[k, i, 0:8, :] = now[k, rows, lanes]
+                moved = pltpu.roll(stiffness(table, mat[k, rows, lanes]), 4, 0)
+                out[k, i, 8:16, :] = jnp.where(keep, prev[k, rows, lanes], moved)
 
 
 INNER = range(CORE + 8, CORE + X - 8, 8)
 OUTER = (CORE - 8, CORE, CORE + X - 8, CORE + X)
 
 
-def advance_inner(courant, now_in, prev_in, mat_in, now_out, stiff_out, one_out, prev_out, now, prev, mat, sems):
-    copies = [
-        pltpu.make_async_copy(src, dst, sems.at[n]) for n, (src, dst) in enumerate(((now_in, now), (mat_in, mat), (prev_in, prev)))
-    ]
-    for copy in copies:
-        copy.start()
+def advance_inner(courant, now, prev, mat, now_out, stiff_out, one_out, prev_out):
     table = stiffness_table(courant)
     masks = lane_masks()
     zeros = jnp.zeros((T, ROWS, 128), jnp.float32)
     for k in (0, 1, Z + 2, Z + 3):
         now_out[k] = zeros
         one_out[k] = zeros
-    copies[0].wait()
 
     def fill(k, carry):
         for i in range(T):
@@ -172,8 +159,6 @@
         return carry
 
     lax.fori_loop(0, Z, fill, 0)
-    copies[1].wait()
-    copies[2].wait()
 
     def first(k, carry):
         for i in range(T):
@@ -248,7 +233,7 @@
     strike(two_out, 0, (jnp.where(inner, -1, jnp.where(z < 2, z, z - 4)),) + place[1:], wavelet(start, 1), 4, CORE, CORE + X)
 
 
-def pack_late(now_side, stiff_side, one, two, early_a, early_b, out_a, out_b):
+def pack_late(now_side, stiff_side, one, two, out_a, out_b):
     sub = lax.broadcasted_iota(jnp.int32, (8, 128), 0)
     left, right = slice(CORE - 8, CORE), slice(CORE + X, CORE + X + 8)
     up1 = ways()[0]
@@ -345,7 +330,7 @@
     for n in range(4):
         for j in range(BUMPS):
             centre = (-3.0 + 6.0 * j / (BUMPS - 1)) / 0.8
-            weights[n, j] = transfer[n, j] * (math.exp(-centre * centre) * (1.5 / (Z * n_dep) if n == 3 else 1.0))
+            weights[n, j] = transfer[n, j] * (math.exp(-centre * centre) * (-LOG2E * 1.5 / (Z * n_dep) if n == 3 else 1.0))
 
     for high, base, near, far, n_in, n_next, zi in SIDES:
         use_a = up1 if high else jnp.logical_not(up1)
@@ -412,41 +397,49 @@
     strike(one, 2, place, wavelet(start, 2), Z, CORE, CORE + X)
 
     group = lax.broadcasted_iota(jnp.int32, (8, 128), 1) // 32
-    step = 6.0 / (BUMPS - 1)
-    half_rate = step / (0.8 * 0.8)
     half = BUMPS // 2
+    rate = 6.0 / (BUMPS - 1) / (0.8 * 0.8) * LOG2E
 
     def render(t, carry):
         rows = pl.ds(pl.multiple_of(CORE + 8 * t, 8), 8)
         own = pl.ds(pl.multiple_of(8 * t, 8), 8)
         for i in range(T):
-            colour = [jnp.zeros((8, 128), jnp.float32) for _ in range(3)]
+            zero = jnp.zeros((8, 128), jnp.float32)
+            seen = [zero] * BUMPS
             through = jnp.ones((8, 128), jnp.float32)
-            depth = jnp.zeros((8, 128), jnp.float32)
+            depth = zero
             for k in range(Z):
                 p = one[k + 2, i, rows, :]
                 pressure[k, own, 128 * i : 128 * i + 128] = p
                 p = clamp_for_bumps(p)
-                gauss = jnp.exp(p * p * (-1.0 / 0.64))
-                rise = jnp.exp(p * half_rate)
-                fall = jnp.exp(p * -half_rate)
+                gauss = jnp.exp2(p * p * (-LOG2E / 0.64))
+                rise = jnp.exp2(p * rate)
+                fall = jnp.exp2(p * -rate)
                 up, down = rise * rise, fall * fall
                 above, below = gauss * rise, gauss * fall
-                value = []
-                for n in range(4):
-                    a = weights[n, BUMPS - 1] * up + weights[n, BUMPS - 2]
-                    b = weights[n, 0] * down + weights[n, 1]
-                    for j in range(2, half):
-                        a = a * up + weights[n, BUMPS - 1 - j]
-                        b = b * down + weights[n, j]
-                    value.append(a * above + b * below)
-                sigma = value[3]
-                stay = jnp.exp(-sigma)
+                a = weights[3, BUMPS - 1] * up + weights[3, BUMPS - 2]
+                b = weights[3, 0] * down + weights[3, 1]
+                for j in range(2, half):
+                    a = a * up + weights[3, BUMPS - 1 - j]
+                    b = b * down + weights[3, j]
+                power = a * above + b * below
+                stay = jnp.exp2(power)
                 weight = through * (1.0 - stay)
                 through = through * stay
-                depth = depth + sigma
-                colour = [colour[n] + weight * value[n] for n in range(3)]
-            parts = colour + [depth]
+                depth = depth + power
+                above, below = weight * above, weight * below
+                for j in range(half):
+                    seen[half + j] = seen[half + j] + above
+                    seen[half - 1 - j] = seen[half - 1 - j] + below
+                    if j < half - 1:
+                        above, below = above * up, below * down
+            parts = []
+            for n in range(3):
+                colour = weights[n, 0] * seen[0]
+                for j in range(1, BUMPS):
+                    colour = colour + weights[n, j] * seen[j]
+                parts.append(colour)
+            parts.append(depth * (-1.0 / LOG2E))
             for q in range(4):
                 packed = None
                 for n in range(4):
@@ -511,24 +504,16 @@
 
     params = pltpu.CompilerParams(vmem_limit_bytes=24 * 1024 * 1024)
     i32 = jnp.int32
-    inputs = [in_hbm(v) for v in (pressure_now, pressure_prev, materials)]
-    early_1, early_2, side_1, side_2 = pl.pallas_call(
+    blocks = [pltpu.VMEM((Z, X, 512), d) for d in (f32, f32, i32)]
+    early_1, early_2, side_1, side_2, *inputs = pl.pallas_call(
         pack,
-        in_specs=[SMEM] + [HBM] * 3,
-        out_specs=[VMEM] * 4,
-        out_shape=[kept(4, T, X, 128)] * 2 + [kept(Z, T, 16, 128)] * 2,
-        scratch_shapes=[
-            pltpu.VMEM((2, 2, X, 512), f32),
-            pltpu.VMEM((2, 2, X, 512), i32),
-            pltpu.VMEM((2, Z, 8, 512), f32),
-            pltpu.VMEM((2, Z, 8, 512), f32),
-            pltpu.VMEM((2, Z, 8, 512), i32),
-            pltpu.SemaphoreType.DMA((4,)),
-            pltpu.SemaphoreType.DMA((6,)),
-        ],
+        in_specs=[HBM] * 4,
+        out_specs=[VMEM] * 7,
+        out_shape=[kept(4, T, X, 128)] * 2 + [kept(Z, T, 16, 128)] * 2 + blocks,
+        scratch_shapes=[pltpu.SMEM((16,), f32), pltpu.SemaphoreType.DMA((4,))],
         compiler_params=params,
         name="pack",
-    )(courant_table, *inputs)
+    )(*(in_hbm(v) for v in (courant_table, pressure_now, pressure_prev, materials)))
     side_a = swap(side_1, "l1")
     side_b = swap(side_2, "l2")
     early_a = swap(early_1, "d1")
@@ -538,10 +523,9 @@
     block, side = (Z, T, X, 128), (Z, T, 16, 128)
     now, stiff, one, prev = pl.pallas_call(
         advance_inner,
-        in_specs=[SMEM] + [HBM] * 3,
+        in_specs=[SMEM] + [VMEM] * 3,
         out_specs=[VMEM] * 4,
         out_shape=[kept(*padded), kept(*block), kept(*padded), kept(*side)],
-        scratch_shapes=[pltpu.VMEM((Z, X, 512), d) for d in (f32, f32, i32)] + [pltpu.SemaphoreType.DMA((3,))],
         compiler_params=params,
         cost_estimate=busy(3.0),
         name="advance_inner",
@@ -559,12 +543,12 @@
     )(source_cell, start_step, now, stiff, one, prev, side_a, side_b)
     late_1, late_2 = pl.pallas_call(
         pack_late,
-        in_specs=[VMEM] * 4 + [pl.BlockSpec(memory_space=pl.ANY)] * 2,
+        in_specs=[VMEM] * 4,
         out_specs=[VMEM] * 2,
         out_shape=[kept(4, T, X + 8, 128)] * 2,
         compiler_params=params,
         name="pack_late",
-    )(now_side, stiff_side, one, two, early_a, early_b)
+    )(now_side, stiff_side, one, two)
     late_a = swap(late_1, "d1")
     late_b = swap(late_2, "d2")
     one, two, delta, halo_stiff, halo_two = pl.pallas_call(

time: 77.8 us -> 69 us (0.89)
  the two profiles are of different devices: /device:TPU:1 before, /device:TPU:384 now
where the time goes in v5:
time: 69 us; the launch traced here: 68.7 us
  blocking collectives  21.3 us (31%)
  Pallas kernels  20.4 us (30%)
  starting transfers between devices  18 us (26%)
  waiting for transfers between devices  7.55 us (11%)
  between operations  1.44 us (2%)
    all_to_all x1, blocking collectives, on_device(): parts = lax.all_to_all(partial, 'dep', 0, 0, tiled=True)  21.3 us
    ppermute x6, starting transfers between devices, swap(): return lax.ppermute(v, ('lat', 'dep'), swaps(n_lat, n_dep, kind))  18 us
    pallas_call x1, Pallas kernels, on_device(): pl.pallas_call(functools.partial(finish, n_dep), in_specs=[SMEM] * 3 + [V...  7.76 us
    ppermute x6, waiting for transfers between devices, swap(): return lax.ppermute(v, ('lat', 'dep'), swaps(n_lat, n_dep, kind))  7.55 us
    pallas_call x1, Pallas kernels, on_device(): pl.pallas_call(couple, in_specs=[VMEM] * 5 + [pl.BlockSpec(memory_space=p...  3.33 us
    pallas_call x1, Pallas kernels, on_device(): pl.pallas_call(advance_inner, in_specs=[SMEM] + [VMEM] * 3, out_specs=[VM...  2.98 us
    pallas_call x1, Pallas kernels, on_device(): pl.pallas_call(advance_outer, in_specs=[SMEM] * 2 + [VMEM] * 6, out_specs...  2.74 us
    pallas_call x1, Pallas kernels, on_device(): pl.pallas_call(pack, in_specs=[HBM] * 4, out_specs=[VMEM] * 7, out_shape=...  2.28 us
  transfers between devices with their start and end apart: 6, of which 1 were waited for; matrix products, arithmetic and copies ran while one was open for 0% of the time, Pallas kernels for 13%

profile of v5, /device:TPU:384, one launch (start us, length us, event | category | flops | bytes accessed | tf_op | source)
XLA Modules:
  0.0 68.7 jit_solution(11278254864463804197)
XLA Ops:
  0.6 0.0 copy-start.2
  0.6 2.3 %pack.1 = (f32[4,4,64,128]{3,2,1,0:T(8,128)S(1)}, f32[4,4,64,128]{3,2,1,0:T(8,128)S(1)}, f32[8,4,16,128]{3,2,1,0:T(8,128)S(1)}, f32[8,4,16,128]{3,2,1,0:T(8,128)...) custom-call(f32[16]{0:T(128)} %courant.1, f32[8,64,512]{2,1,0:T(8,128)} %now_in.1, ...), custom_call_target="tpu_custom_call" | custom-call | tf_op jit(solution)/shard_map/pack/pallas_call | solution.py:508
  2.9 1.9 %collective-permute-start = (f32[8,4,16,128]{3,2,1,0:T(8,128)S(1)}, f32[8,4,16,128]{3,2,1,0:T(8,128)S(1)}, u32[]{:S(2)}, u32[]{:S(2)}) collective-permute-start(f32[8,4,16,128]{3,2,1,0:T(8,128)S(1)} %get-tuple-element.34), channel_id=1, source_target_pairs={{0,16},{1,17},{2,18},{3,19},{4,20},{5,21},{6,22},{7,23},{8,24},{9,... | collective-permute-start | bytes 786440 | tf_op jit(solution)/shard_map/ppermute | solution.py:489
  4.9 4.2 %collective-permute-start.1 = (f32[8,4,16,128]{3,2,1,0:T(8,128)S(1)}, f32[8,4,16,128]{3,2,1,0:T(8,128)S(1)}, u32[]{:S(2)}, u32[]{:S(2)}) collective-permute-start(f32[8,4,16,128]{3,2,1,0:T(8,128)S(1)} %get-tuple-element.35), channel_id=1, source_target_pairs={{16,32},{17,33},{18,34},{19,35},{20,36},{21,37},{22,38},{23,39},{2... | collective-permute-start | bytes 786440 | tf_op jit(solution)/shard_map/ppermute | solution.py:489
  9.1 3.4 %collective-permute-start.2 = (f32[4,4,64,128]{3,2,1,0:T(8,128)S(1)}, f32[4,4,64,128]{3,2,1,0:T(8,128)S(1)}, u32[]{:S(2)}, u32[]{:S(2)}) collective-permute-start(f32[4,4,64,128]{3,2,1,0:T(8,128)S(1)} %get-tuple-element.40), channel_id=1, source_target_pairs={{0,1},{1,0},{2,3},{3,2},{4,5},{5,4},{6,7},{7,6},{8,9},{9,8},{10,11... | collective-permute-start | bytes 1572872 | tf_op jit(solution)/shard_map/ppermute | solution.py:489
  12.5 0.7 %collective-permute-start.3 = (f32[4,4,64,128]{3,2,1,0:T(8,128)S(1)}, f32[4,4,64,128]{3,2,1,0:T(8,128)S(1)}, u32[]{:S(2)}, u32[]{:S(2)}) collective-permute-start(f32[4,4,64,128]{3,2,1,0:T(8,128)S(1)} %get-tuple-element.41), channel_id=1, source_target_pairs={{1,2},{2,1},{3,4},{4,3},{5,6},{6,5},{7,8},{8,7},{9,10},{10,9},{11,... | collective-permute-start | bytes 1572872 | tf_op jit(solution)/shard_map/ppermute | solution.py:489
  13.8 0.0 copy-done.2
  13.9 0.0 copy-start.1
  13.9 3.0 %advance_inner.1 = (f32[12,4,96,128]{3,2,1,0:T(8,128)S(1)}, f32[8,4,64,128]{3,2,1,0:T(8,128)S(1)}, f32[12,4,96,128]{3,2,1,0:T(8,128)S(1)}, f32[8,4,16,128]{3,2,1,0:T(8,128)S(1)}) custom-call(f32[16]{0:T(128)S(1)} %copy-done.2, f32[8,64,512]{2,1,0:T(8,128)S(1)} %get-tuple-element.27.now, f32[8,64,512]{2,1,0:T(8,128)S(1)} %get-tuple-element.28.prev, ...), custom_call_target="tpu_custom_call" | custom-call | flops 3000000000 | bytes 9000000 | tf_op jit(solution)/shard_map/advance_inner/pallas_call | solution.py:524
  16.9 0.0 collective-permute-done.lat_a
  16.9 0.0 collective-permute-done.1.lat_b
  16.9 0.0 copy-done.1
  16.9 2.7 %advance_outer.1 = (f32[12,4,96,128]{3,2,1,0:T(8,128)S(1)}, f32[12,4,96,128]{3,2,1,0:T(8,128)S(1)}, f32[8,4,16,128]{3,2,1,0:T(8,128)S(1)}, f32[8,4,16,128]{3,2,1,0:T(8,128)S(1)}, f32[4,4,96,128]{3,2,1,0:T(8,128)S(1)}) custom-call(s32[3]{0:T(128)S(1)} %copy-done.1, s32[1]{0:T(128)S(6)} %copy.21.start, ...), custom_call_target="tpu_custom_call", output_to_operand_aliasing={{0}: (2, {}), {1}: (4, {})} | custom-call | flops 5000000000 | bytes 15000000 | tf_op jit(solution)/shard_map/advance_outer/pallas_call | solution.py:533
  19.6 0.1 pack_late.1
  19.8 0.7 %collective-permute-start.5 = (f32[4,4,72,128]{3,2,1,0:T(8,128)S(1)}, f32[4,4,72,128]{3,2,1,0:T(8,128)S(1)}, u32[]{:S(2)}, u32[]{:S(2)}) collective-permute-start(f32[4,4,72,128]{3,2,1,0:T(8,128)S(1)} %get-tuple-element.49), channel_id=1, source_target_pairs={{1,2},{2,1},{3,4},{4,3},{5,6},{6,5},{7,8},{8,7},{9,10},{10,9},{11,... | collective-permute-start | bytes 1769480 | tf_op jit(solution)/shard_map/ppermute | solution.py:489
  20.5 7.0 %collective-permute-start.4 = (f32[4,4,72,128]{3,2,1,0:T(8,128)S(1)}, f32[4,4,72,128]{3,2,1,0:T(8,128)S(1)}, u32[]{:S(2)}, u32[]{:S(2)}) collective-permute-start(f32[4,4,72,128]{3,2,1,0:T(8,128)S(1)} %get-tuple-element.43.sent), channel_id=1, source_target_pairs={{0,1},{1,0},{2,3},{3,2},{4,5},{5,4},{6,7},{7,6},{8,9},{9,8},{10,11... | collective-permute-start | bytes 1769480 | tf_op jit(solution)/shard_map/ppermute | solution.py:489
  27.5 0.0 collective-permute-done.2.early_a
  27.5 0.0 collective-permute-done.3.early_b
  27.5 0.0 copy-start
  27.5 3.3 %couple.1 = (f32[12,4,96,128]{3,2,1,0:T(8,128)S(1)}, f32[12,4,96,128]{3,2,1,0:T(8,128)S(1)}, f32[4,4,96,128]{3,2,1,0:T(8,128)S(1)}, f32[4,4,64,128]{3,2,1,0:T(8,128)S(1)}, f32[4,4,64,128]{3,2,1,0:T(8,128)S(1)}) custom-call(f32[12,4,96,128]{3,2,1,0:T(8,128)S(1)} %get-tuple-element.36.now, ...), custom_call_target="tpu_custom_call", output_to_operand_aliasing={{0}: (2, {})} | custom-call | flops 4000000000 | bytes 12000000 | tf_op jit(solution)/shard_map/couple/pallas_call | solution.py:554
  30.9 0.0 collective-permute-done.5.late_b
  30.9 7.5 %collective-permute-done.4.late_a = f32[4,4,72,128]{3,2,1,0:T(8,128)S(1)} collective-permute-done((f32[4,4,72,128]{3,2,1,0:T(8,128)S(1)}, f32[4,4,72,128]{3,2,1,0:T(8,128)S(1)}, u32[]{:S(2)}, u32[]{:S(2)}) %collective-permute-start.4) | collective-permute-done | bytes 589856 | tf_op jit(solution)/shard_map/ppermute | solution.py:489
  38.4 0.0 copy-done
  38.4 7.8 %finish.1 = (f32[8,64,512]{2,1,0:T(8,128)}, f32[16,64,128]{2,1,0:T(8,128)S(1)}, f32[12,4,96,128]{3,2,1,0:T(8,128)S(1)}, f32[12,4,96,128]{3,2,1,0:T(8,128)S(1)}, f32[4,4,96,128]{3,2,1,0:T(8,128)S(1)}) custom-call(s32[3]{0:T(128)S(1)} %copy-done.1, s32[1]{0:T(128)S(6)} %copy.21.start, ...), custom_call_target="tpu_custom_call", output_to_operand_aliasing={{2}: (7, {}), {3}: (8, {}), {4}: (9, {})} | custom-call | tf_op jit(solution)/shard_map/finish/pallas_call | solution.py:564
  46.2 21.3 %all_to_all.5.parts = f32[16,64,128]{2,1,0:T(8,128)S(1)} all-to-all(f32[16,64,128]{2,1,0:T(8,128)S(1)} %get-tuple-element.51), channel_id=1, replica_groups=mesh['lat'=32,'dep'=16] {'dep'}, dimensions={0} | all-to-all | bytes 1048576 | tf_op jit(solution)/shard_map/all_to_all | solution.py:577
  67.5 1.2 %composite.1 = f32[128,64]{1,0:T(8,128)} custom-call(f32[16,64,128]{2,1,0:T(8,128)S(1)} %all_to_all.5.parts), custom_call_target="tpu_custom_call" | custom-call | tf_op jit(solution)/shard_map/composite/pallas_call | solution.py:578
Async XLA Ops:
  0.6 13.2 %copy-start.2 = (f32[16]{0:T(128)S(1)}, f32[16]{0:T(128)}, u32[]{:S(2)}) copy-start(f32[16]{0:T(128)} %courant.1) | copy-start | bytes 196
  2.9 13.9 %collective-permute-start = (f32[8,4,16,128]{3,2,1,0:T(8,128)S(1)}, f32[8,4,16,128]{3,2,1,0:T(8,128)S(1)}, u32[]{:S(2)}, u32[]{:S(2)}) collective-permute-start(f32[8,4,16,128]{3,2,1,0:T(8,128)S(1)} %get-tuple-element.34), channel_id=1, source_target_pairs={{0,16},{1,17},{2,18},{3,19},{4,20},{5,21},{6,22},{7,23},{8,24},{9,... | collective-permute-start | bytes 786440 | tf_op jit(solution)/shard_map/ppermute | solution.py:489
  4.9 12.0 %collective-permute-start.1 = (f32[8,4,16,128]{3,2,1,0:T(8,128)S(1)}, f32[8,4,16,128]{3,2,1,0:T(8,128)S(1)}, u32[]{:S(2)}, u32[]{:S(2)}) collective-permute-start(f32[8,4,16,128]{3,2,1,0:T(8,128)S(1)} %get-tuple-element.35), channel_id=1, source_target_pairs={{16,32},{17,33},{18,34},{19,35},{20,36},{21,37},{22,38},{23,39},{2... | collective-permute-start | bytes 786440 | tf_op jit(solution)/shard_map/ppermute | solution.py:489
  9.1 18.4 %collective-permute-start.2 = (f32[4,4,64,128]{3,2,1,0:T(8,128)S(1)}, f32[4,4,64,128]{3,2,1,0:T(8,128)S(1)}, u32[]{:S(2)}, u32[]{:S(2)}) collective-permute-start(f32[4,4,64,128]{3,2,1,0:T(8,128)S(1)} %get-tuple-element.40), channel_id=1, source_target_pairs={{0,1},{1,0},{2,3},{3,2},{4,5},{5,4},{6,7},{7,6},{8,9},{9,8},{10,11... | collective-permute-start | bytes 1572872 | tf_op jit(solution)/shard_map/ppermute | solution.py:489
  12.5 15.0 %collective-permute-start.3 = (f32[4,4,64,128]{3,2,1,0:T(8,128)S(1)}, f32[4,4,64,128]{3,2,1,0:T(8,128)S(1)}, u32[]{:S(2)}, u32[]{:S(2)}) collective-permute-start(f32[4,4,64,128]{3,2,1,0:T(8,128)S(1)} %get-tuple-element.41), channel_id=1, source_target_pairs={{1,2},{2,1},{3,4},{4,3},{5,6},{6,5},{7,8},{8,7},{9,10},{10,9},{11,... | collective-permute-start | bytes 1572872 | tf_op jit(solution)/shard_map/ppermute | solution.py:489
  13.9 3.0 %copy-start.1 = (s32[3]{0:T(128)S(1)}, s32[3]{0:T(128)}, u32[]{:S(2)}) copy-start(s32[3]{0:T(128)} %cell.3) | copy-start | bytes 40
  19.8 11.1 %collective-permute-start.5 = (f32[4,4,72,128]{3,2,1,0:T(8,128)S(1)}, f32[4,4,72,128]{3,2,1,0:T(8,128)S(1)}, u32[]{:S(2)}, u32[]{:S(2)}) collective-permute-start(f32[4,4,72,128]{3,2,1,0:T(8,128)S(1)} %get-tuple-element.49), channel_id=1, source_target_pairs={{1,2},{2,1},{3,4},{4,3},{5,6},{6,5},{7,8},{8,7},{9,10},{10,9},{11,... | collective-permute-start | bytes 1769480 | tf_op jit(solution)/shard_map/ppermute | solution.py:489
  20.5 18.0 %collective-permute-start.4 = (f32[4,4,72,128]{3,2,1,0:T(8,128)S(1)}, f32[4,4,72,128]{3,2,1,0:T(8,128)S(1)}, u32[]{:S(2)}, u32[]{:S(2)}) collective-permute-start(f32[4,4,72,128]{3,2,1,0:T(8,128)S(1)} %get-tuple-element.43.sent), channel_id=1, source_target_pairs={{0,1},{1,0},{2,3},{3,2},{4,5},{5,4},{6,7},{7,6},{8,9},{9,8},{10,11... | collective-permute-start | bytes 1769480 | tf_op jit(solution)/shard_map/ppermute | solution.py:489
  27.5 10.9 %copy-start = (f32[4,8]{1,0:T(4,128)S(1)}, f32[4,8]{1,0:T(4,128)}, u32[]{:S(2)}) copy-start(f32[4,8]{1,0:T(4,128)} %transfer.1) | copy-start | bytes 388

commit v6 on v5

--- a/solution.py
+++ b/solution.py
@@ -54,14 +54,41 @@
     return out
 
 
-def full_terms(ref, k, row, masks):
-    out = []
-    for i, (c, near, far) in enumerate(plane_terms(ref, k, row, masks)):
-        rows = pl.ds(row, 8)
-        near = near + (ref[k - 1, i, rows, :] + ref[k + 1, i, rows, :])
-        far = far + (ref[k - 2, i, rows, :] + ref[k + 2, i, rows, :])
-        out.append((c, 16.0 * near - far - 90.0 * c))
-    return out
+def band():
+    shape = (512, 256)
+    d = jnp.abs(lax.broadcasted_iota(jnp.int32, shape, 0) % 256 - lax.broadcasted_iota(jnp.int32, shape, 1))
+    return jnp.where(d == 0, -90.0, jnp.where(d == 1, 16.0, jnp.where(d == 2, -1.0, 0.0))).astype(jnp.bfloat16)
+
+
+def full_rows(ref, k, first, count, bands):
+    rows = slice(first, first + count)
+    factors = []
+    for h in range(2):
+        v = jnp.concatenate([ref[k, 2 * h, rows, :], ref[k, 2 * h + 1, rows, :]], axis=1)
+        high = v.astype(jnp.bfloat16)
+        low = (v - high.astype(jnp.float32)).astype(jnp.bfloat16)
+        factors.append(jnp.concatenate([high, low], axis=1))
+    product = jnp.dot(jnp.concatenate(factors, axis=0), bands, preferred_element_type=jnp.float32)
+    low1, low2, high1, high2 = lane_masks()
+    for r in range(0, count, 8):
+        row = first + r
+        here = slice(row, row + 8)
+        for i in range(T):
+            c = ref[k, i, here, :]
+            inside = product[count * (i // 2) + r : count * (i // 2) + r + 8, 128 * (i % 2) : 128 * (i % 2) + 128]
+            near = ref[k, i, row - 1 : row + 7, :] + ref[k, i, row + 1 : row + 9, :]
+            far = ref[k, i, row - 2 : row + 6, :] + ref[k, i, row + 2 : row + 10, :]
+            near = near + (ref[k - 1, i, here, :] + ref[k + 1, i, here, :])
+            far = far + (ref[k - 2, i, here, :] + ref[k + 2, i, here, :])
+            if i == 1:
+                v = ref[k, 2, here, :]
+                near = near + jnp.where(high1, pltpu.roll(v, 127, 1), 0.0)
+                far = far + jnp.where(high2, pltpu.roll(v, 126, 1), 0.0)
+            if i == 2:
+                v = ref[k, 1, here, :]
+                near = near + jnp.where(low1, pltpu.roll(v, 1, 1), 0.0)
+                far = far + jnp.where(low2, pltpu.roll(v, 2, 1), 0.0)
+            yield row, i, c, inside + (16.0 * near - far)
 
 
 def strike(ref, outer, place, amplitude, layers, rows_low, rows_high):
@@ -141,13 +168,13 @@
                 out[k, i, 8:16, :] = jnp.where(keep, prev[k, rows, lanes], moved)
 
 
-INNER = range(CORE + 8, CORE + X - 8, 8)
-OUTER = (CORE - 8, CORE, CORE + X - 8, CORE + X)
-
-
-def advance_inner(courant, now, prev, mat, now_out, stiff_out, one_out, prev_out):
+INNER = CORE + 8, X - 16
+OUTER = ((CORE - 8, 16), (CORE + X - 8, 16))
+
+
+def advance_inner(courant, now, prev, mat, now_out, stiff_out, one_out, prev_out, bands):
     table = stiffness_table(courant)
-    masks = lane_masks()
+    bands[...] = band()
     zeros = jnp.zeros((T, ROWS, 128), jnp.float32)
     for k in (0, 1, Z + 2, Z + 3):
         now_out[k] = zeros
@@ -168,22 +195,20 @@
             for t in range(X // 8):
                 rows = slice(8 * t, 8 * t + 8)
                 stiff_out[k, i, rows, :] = stiffness(table, mat[k, rows, lanes])
-        for row in INNER:
+        for row, i, c, lap in full_rows(now_out, k + 2, *INNER, bands[...]):
             own = slice(row - CORE, row - CORE + 8)
-            for i, (c, lap) in enumerate(full_terms(now_out, k + 2, row, masks)):
-                before = prev[k, own, 128 * i : 128 * i + 128]
-                one_out[k + 2, i, row : row + 8, :] = 2.0 * c - before + stiff_out[k, i, own, :] * lap
-        return carry
-
-    lax.fori_loop(0, Z, first, 0)
+            before = prev[k, own, 128 * i : 128 * i + 128]
+            one_out[k + 2, i, row : row + 8, :] = 2.0 * c - before + stiff_out[k, i, own, :] * lap
+        return carry
+
+    lax.fori_loop(0, Z, first, 0, unroll=2)
 
 
 def advance_outer(
-    cell, start, now_in, stiff_in, one_in, prev_in, lat_a, lat_b, now, one, now_side, stiff_side, two_out,
+    cell, start, bands, now_in, stiff_in, one_in, prev_in, lat_a, lat_b, now, one, now_side, stiff_side, two_out,
     prev_side,
 ):
     del now_in, one_in
-    masks = lane_masks()
     right1 = ways()[1] == 1
 
     def fill(k, carry):
@@ -202,32 +227,30 @@
     lax.fori_loop(0, Z, fill, 0)
 
     def first(k, carry):
-        for row in OUTER:
-            rows = slice(row, row + 8)
-            for i, (c, lap) in enumerate(full_terms(now, k + 2, row, masks)):
+        for part in OUTER:
+            for row, i, c, lap in full_rows(now, k + 2, *part, bands[...]):
                 if row < CORE or row == CORE + X:
                     half = slice(0, 8) if row < CORE else slice(8, 16)
                     before, stiff = prev_side[k, i, half, :], stiff_side[k, i, half, :]
                 else:
                     half = slice(0, 8) if row == CORE else slice(8, 16)
                     before, stiff = prev_in[k, i, half, :], stiff_in[k, i, row - CORE : row - CORE + 8, :]
-                one[k + 2, i, rows, :] = 2.0 * c - before + stiff * lap
-        return carry
-
-    lax.fori_loop(0, Z, first, 0)
+                one[k + 2, i, row : row + 8, :] = 2.0 * c - before + stiff * lap
+        return carry
+
+    lax.fori_loop(0, Z, first, 0, unroll=2)
     place = source_place(cell)
     strike(one, 2, place, wavelet(start, 0), Z, CORE - 8, CORE + X + 8)
 
     def second(n, carry):
         k = jnp.where(n < 2, n, n + 4)
-        for row in range(CORE, CORE + X, 8):
+        for row, i, c, lap in full_rows(one, k + 2, CORE, X, bands[...]):
             rows = slice(row, row + 8)
-            for i, (c, lap) in enumerate(full_terms(one, k + 2, row, masks)):
-                stiff = stiff_in[k, i, row - CORE : row - CORE + 8, :]
-                two_out[n, i, rows, :] = 2.0 * c - now[k + 2, i, rows, :] + stiff * lap
-        return carry
-
-    lax.fori_loop(0, 4, second, 0)
+            stiff = stiff_in[k, i, row - CORE : row - CORE + 8, :]
+            two_out[n, i, rows, :] = 2.0 * c - now[k + 2, i, rows, :] + stiff * lap
+        return carry
+
+    lax.fori_loop(0, 4, second, 0, unroll=2)
     z = place[0]
     inner = (z >= 2) & (z < Z - 2)
     strike(two_out, 0, (jnp.where(inner, -1, jnp.where(z < 2, z, z - 4)),) + place[1:], wavelet(start, 1), 4, CORE, CORE + X)
@@ -276,7 +299,7 @@
     return out
 
 
-def couple(now, stiff, one_in, early_a, early_b, sent, one, two, delta, halo_stiff, halo_two):
+def couple(bands, now, stiff, one_in, early_a, early_b, sent, one, two, delta, halo_stiff, halo_two):
     del one_in, sent
     masks = lane_masks()
     up1 = ways()[0] == 1
@@ -301,14 +324,12 @@
         lax.fori_loop(0, X // 8, tile, 0)
 
     def second(k, carry):
-        for row in INNER:
-            rows = slice(row, row + 8)
-            for i, (c, lap) in enumerate(full_terms(one, k + 2, row, masks)):
-                own = slice(row - CORE, row - CORE + 8)
-                two[k + 2, i, rows, :] = 2.0 * c - now[k + 2, i, rows, :] + stiff[k, i, own, :] * lap
-        return carry
-
-    lax.fori_loop(0, Z, second, 0)
+        for row, i, c, lap in full_rows(one, k + 2, *INNER, bands[...]):
+            rows, own = slice(row, row + 8), slice(row - CORE, row - CORE + 8)
+            two[k + 2, i, rows, :] = 2.0 * c - now[k + 2, i, rows, :] + stiff[k, i, own, :] * lap
+        return carry
+
+    lax.fori_loop(0, Z, second, 0, unroll=2)
     for high, base, near, far, n_in, n_next, zi in SIDES:
 
         def beyond(t, carry, base=base, near=near, n_in=n_in, n_next=n_next):
@@ -321,7 +342,7 @@
 
 
 def finish(
-    n_dep, cell, start, transfer, now, stiff, now_side, stiff_side, one_in, two_in, delta_in, halo_stiff, halo_two,
+    n_dep, cell, start, transfer, bands, now, stiff, now_side, stiff_side, one_in, two_in, delta_in, halo_stiff, halo_two,
     late_a, late_b, pressure, partial, one, two, delta, weights,
 ):
     del one_in, two_in, delta_in
@@ -371,9 +392,9 @@
                 two[zi + k, i, row : row + 8, :] = late_of(2 + k, i, row) + v
 
     def second(k, carry):
-        for row in OUTER:
-            rows = slice(row, row + 8)
-            for i, (c, lap) in enumerate(full_terms(one, k + 2, row, masks)):
+        for part in OUTER:
+            for row, i, c, lap in full_rows(one, k + 2, *part, bands[...]):
+                rows = slice(row, row + 8)
                 if CORE <= row < CORE + X:
                     st = stiff[k, i, row - CORE : row - CORE + 8, :]
                 else:
@@ -381,19 +402,18 @@
                 two[k + 2, i, rows, :] = 2.0 * c - now[k + 2, i, rows, :] + st * lap
         return carry
 
-    lax.fori_loop(0, Z, second, 0)
+    lax.fori_loop(0, Z, second, 0, unroll=2)
     place = source_place(cell)
     strike(two, 2, place, wavelet(start, 1), Z, CORE - 8, CORE + X + 8)
 
     def third(k, carry):
-        for row in range(CORE, CORE + X, 8):
-            rows = pl.ds(row, 8)
-            for i, (c, lap) in enumerate(full_terms(two, k + 2, row, masks)):
-                own = pl.ds(row - CORE, 8)
-                one[k + 2, i, rows, :] = 2.0 * c - one[k + 2, i, rows, :] + stiff[k, i, own, :] * lap
-        return carry
-
-    lax.fori_loop(0, Z, third, 0)
+        for row, i, c, lap in full_rows(two, k + 2, CORE, X, bands[...]):
+            rows, own = slice(row, row + 8), slice(row - CORE, row - CORE + 8)
+            three = 2.0 * c - one[k + 2, i, rows, :] + stiff[k, i, own, :] * lap
+            one[k + 2, i, rows, :] = three
+        return carry
+
+    lax.fori_loop(0, Z, third, 0, unroll=2)
     strike(one, 2, place, wavelet(start, 2), Z, CORE, CORE + X)
 
     group = lax.broadcasted_iota(jnp.int32, (8, 128), 1) // 32
@@ -520,27 +540,28 @@
     early_b = swap(early_2, "d2")
 
     padded = (Z + 4, T, ROWS, 128)
+    bands = pltpu.VMEM((512, 256), jnp.bfloat16)
     block, side = (Z, T, X, 128), (Z, T, 16, 128)
-    now, stiff, one, prev = pl.pallas_call(
+    now, stiff, one, prev, bands_made = pl.pallas_call(
         advance_inner,
         in_specs=[SMEM] + [VMEM] * 3,
-        out_specs=[VMEM] * 4,
-        out_shape=[kept(*padded), kept(*block), kept(*padded), kept(*side)],
+        out_specs=[VMEM] * 5,
+        out_shape=[kept(*padded), kept(*block), kept(*padded), kept(*side), bands],
         compiler_params=params,
         cost_estimate=busy(3.0),
         name="advance_inner",
     )(courant_table, *inputs)
     now, one, now_side, stiff_side, two = pl.pallas_call(
         advance_outer,
-        in_specs=[SMEM] * 2 + [VMEM] * 6,
+        in_specs=[SMEM] * 2 + [VMEM] * 7,
         out_specs=[VMEM] * 5,
         out_shape=[kept(*padded)] * 2 + [kept(*side)] * 2 + [kept(4, T, ROWS, 128)],
         scratch_shapes=[pltpu.VMEM(side, f32)],
-        input_output_aliases={2: 0, 4: 1},
+        input_output_aliases={3: 0, 5: 1},
         compiler_params=params,
         cost_estimate=busy(5.0),
         name="advance_outer",
-    )(source_cell, start_step, now, stiff, one, prev, side_a, side_b)
+    )(source_cell, start_step, bands_made, now, stiff, one, prev, side_a, side_b)
     late_1, late_2 = pl.pallas_call(
         pack_late,
         in_specs=[VMEM] * 4,
@@ -553,25 +574,25 @@
     late_b = swap(late_2, "d2")
     one, two, delta, halo_stiff, halo_two = pl.pallas_call(
         couple,
-        in_specs=[VMEM] * 5 + [pl.BlockSpec(memory_space=pl.ANY)],
+        in_specs=[VMEM] * 6 + [pl.BlockSpec(memory_space=pl.ANY)],
         out_specs=[VMEM] * 5,
         out_shape=[kept(*padded)] * 2 + [kept(4, T, ROWS, 128)] + [kept(4, T, X, 128)] * 2,
-        input_output_aliases={2: 0},
+        input_output_aliases={3: 0},
         compiler_params=params,
         cost_estimate=busy(4.0),
         name="couple",
-    )(now, stiff, one, early_a, early_b, late_1)
+    )(bands_made, now, stiff, one, early_a, early_b, late_1)
     pressure, partial, _, _, _ = pl.pallas_call(
         functools.partial(finish, n_dep),
-        in_specs=[SMEM] * 3 + [VMEM] * 11,
+        in_specs=[SMEM] * 3 + [VMEM] * 12,
         out_specs=[VMEM] * 5,
         out_shape=[shape(Z, X, 512), shape(n_dep, X, 128)] + [kept(*padded)] * 2 + [kept(4, T, ROWS, 128)],
         scratch_shapes=[pltpu.SMEM((4, BUMPS), f32)],
-        input_output_aliases={7: 2, 8: 3, 9: 4},
+        input_output_aliases={8: 2, 9: 3, 10: 4},
         compiler_params=params,
         name="finish",
     )(
-        source_cell, start_step, tf_weights, now, stiff, now_side, stiff_side, one, two, delta, halo_stiff,
+        source_cell, start_step, tf_weights, bands_made, now, stiff, now_side, stiff_side, one, two, delta, halo_stiff,
         halo_two, late_a, late_b,
     )
     parts = lax.all_to_all(partial, "dep", 0, 0, tiled=True)

time: 69 us -> 67.6 us (0.980)
  the two profiles are of different devices: /device:TPU:384 before, /device:TPU:1 now
where the time goes in v6:
time: 67.6 us; the launch traced here: 66.5 us
  blocking collectives  19.1 us (28%)
  Pallas kernels  18.6 us (28%)
  starting transfers between devices  17.1 us (25%)
  waiting for transfers between devices  10.3 us (15%)
  between operations  1.4 us (2%)
    all_to_all x1, blocking collectives, on_device(): parts = lax.all_to_all(partial, 'dep', 0, 0, tiled=True)  19.1 us
    ppermute x6, starting transfers between devices, swap(): return lax.ppermute(v, ('lat', 'dep'), swaps(n_lat, n_dep, kind))  17.1 us
    ppermute x6, waiting for transfers between devices, swap(): return lax.ppermute(v, ('lat', 'dep'), swaps(n_lat, n_dep, kind))  10.3 us
    pallas_call x1, Pallas kernels, on_device(): pl.pallas_call(functools.partial(finish, n_dep), in_specs=[SMEM] * 3 + [V...  7.19 us
    pallas_call x1, Pallas kernels, on_device(): pl.pallas_call(couple, in_specs=[VMEM] * 6 + [pl.BlockSpec(memory_space=p...  2.91 us
    pallas_call x1, Pallas kernels, on_device(): pl.pallas_call(advance_outer, in_specs=[SMEM] * 2 + [VMEM] * 7, out_specs...  2.51 us
    pallas_call x1, Pallas kernels, on_device(): pl.pallas_call(advance_inner, in_specs=[SMEM] + [VMEM] * 3, out_specs=[VM...  2.4 us
    pallas_call x1, Pallas kernels, on_device(): pl.pallas_call(pack, in_specs=[HBM] * 4, out_specs=[VMEM] * 7, out_shape=...  2.28 us
  transfers between devices with their start and end apart: 6, of which 3 were waited for; matrix products, arithmetic and copies ran while one was open for 0% of the time, Pallas kernels for 12%

profile of v6, /device:TPU:1, one launch (start us, length us, event | category | flops | bytes accessed | tf_op | source)
XLA Modules:
  0.0 66.5 jit_solution(6321566000488482378)
XLA Ops:
  0.6 0.0 copy-start.1
  0.6 2.3 %pack.1 = (f32[4,4,64,128]{3,2,1,0:T(8,128)S(1)}, f32[4,4,64,128]{3,2,1,0:T(8,128)S(1)}, f32[8,4,16,128]{3,2,1,0:T(8,128)S(1)}, f32[8,4,16,128]{3,2,1,0:T(8,128)...) custom-call(f32[16]{0:T(128)} %courant.1, f32[8,64,512]{2,1,0:T(8,128)} %now_in.1, ...), custom_call_target="tpu_custom_call" | custom-call | tf_op jit(solution)/shard_map/pack/pallas_call | solution.py:528
  2.9 8.8 %collective-permute-start = (f32[8,4,16,128]{3,2,1,0:T(8,128)S(1)}, f32[8,4,16,128]{3,2,1,0:T(8,128)S(1)}, u32[]{:S(2)}, u32[]{:S(2)}) collective-permute-start(f32[8,4,16,128]{3,2,1,0:T(8,128)S(1)} %get-tuple-element.36), channel_id=1, source_target_pairs={{0,16},{1,17},{2,18},{3,19},{4,20},{5,21},{6,22},{7,23},{8,24},{9,... | collective-permute-start | bytes 786440 | tf_op jit(solution)/shard_map/ppermute | solution.py:509
  11.7 1.9 %collective-permute-start.1 = (f32[8,4,16,128]{3,2,1,0:T(8,128)S(1)}, f32[8,4,16,128]{3,2,1,0:T(8,128)S(1)}, u32[]{:S(2)}, u32[]{:S(2)}) collective-permute-start(f32[8,4,16,128]{3,2,1,0:T(8,128)S(1)} %get-tuple-element.37), channel_id=1, source_target_pairs={{16,32},{17,33},{18,34},{19,35},{20,36},{21,37},{22,38},{23,39},{2... | collective-permute-start | bytes 786440 | tf_op jit(solution)/shard_map/ppermute | solution.py:509
  13.6 0.7 %collective-permute-start.2 = (f32[4,4,64,128]{3,2,1,0:T(8,128)S(1)}, f32[4,4,64,128]{3,2,1,0:T(8,128)S(1)}, u32[]{:S(2)}, u32[]{:S(2)}) collective-permute-start(f32[4,4,64,128]{3,2,1,0:T(8,128)S(1)} %get-tuple-element.42), channel_id=1, source_target_pairs={{0,1},{1,0},{2,3},{3,2},{4,5},{5,4},{6,7},{7,6},{8,9},{9,8},{10,11... | collective-permute-start | bytes 1572872 | tf_op jit(solution)/shard_map/ppermute | solution.py:509
  14.3 1.9 %collective-permute-start.3 = (f32[4,4,64,128]{3,2,1,0:T(8,128)S(1)}, f32[4,4,64,128]{3,2,1,0:T(8,128)S(1)}, u32[]{:S(2)}, u32[]{:S(2)}) collective-permute-start(f32[4,4,64,128]{3,2,1,0:T(8,128)S(1)} %get-tuple-element.43), channel_id=1, source_target_pairs={{1,2},{2,1},{3,4},{4,3},{5,6},{6,5},{7,8},{8,7},{9,10},{10,9},{11,... | collective-permute-start | bytes 1572872 | tf_op jit(solution)/shard_map/ppermute | solution.py:509
  16.9 0.0 copy-done.1
  16.9 0.0 copy-start.2
  16.9 2.4 %advance_inner.1 = (f32[12,4,96,128]{3,2,1,0:T(8,128)S(1)}, f32[8,4,64,128]{3,2,1,0:T(8,128)S(1)}, f32[12,4,96,128]{3,2,1,0:T(8,128)S(1)}, f32[8,4,16,128]{3,2,1,0:T(8,128)S(1)}, bf16[512,256]{1,0:T(8,128)(2,1)S(1)}) custom-call(f32[16]{0:T(128)S(1)} %copy-done.1, f32[8,64,512]{2,1,0:T(8,128)S(1)} %get-tuple-element.28.now, ...), custom_call_target="tpu_custom_call" | custom-call | flops 3000000000 | bytes 9000000 | tf_op jit(solution)/shard_map/advance_inner/pallas_call | solution.py:545
  19.3 0.0 collective-permute-done.lat_a
  19.4 0.3 collective-permute-done.1.lat_b
  19.7 0.0 copy-done.2
  19.7 2.5 %advance_outer.1 = (f32[12,4,96,128]{3,2,1,0:T(8,128)S(1)}, f32[12,4,96,128]{3,2,1,0:T(8,128)S(1)}, f32[8,4,16,128]{3,2,1,0:T(8,128)S(1)}, f32[8,4,16,128]{3,2,1,0:T(8,128)S(1)}, f32[4,4,96,128]{3,2,1,0:T(8,128)S(1)}) custom-call(s32[3]{0:T(128)S(1)} %copy-done.2, s32[1]{0:T(128)S(6)} %copy.21.start, ...), custom_call_target="tpu_custom_call", output_to_operand_aliasing={{0}: (3, {}), {1}: (5, {})} | custom-call | flops 5000000000 | bytes 15000000 | tf_op jit(solution)/shard_map/advance_outer/pallas_call | solution.py:554
  22.2 0.1 pack_late.1
  22.3 3.0 %collective-permute-start.5 = (f32[4,4,72,128]{3,2,1,0:T(8,128)S(1)}, f32[4,4,72,128]{3,2,1,0:T(8,128)S(1)}, u32[]{:S(2)}, u32[]{:S(2)}) collective-permute-start(f32[4,4,72,128]{3,2,1,0:T(8,128)S(1)} %get-tuple-element.51), channel_id=1, source_target_pairs={{1,2},{2,1},{3,4},{4,3},{5,6},{6,5},{7,8},{8,7},{9,10},{10,9},{11,... | collective-permute-start | bytes 1769480 | tf_op jit(solution)/shard_map/ppermute | solution.py:509
  25.4 0.7 %collective-permute-start.4 = (f32[4,4,72,128]{3,2,1,0:T(8,128)S(1)}, f32[4,4,72,128]{3,2,1,0:T(8,128)S(1)}, u32[]{:S(2)}, u32[]{:S(2)}) collective-permute-start(f32[4,4,72,128]{3,2,1,0:T(8,128)S(1)} %get-tuple-element.45.sent), channel_id=1, source_target_pairs={{0,1},{1,0},{2,3},{3,2},{4,5},{5,4},{6,7},{7,6},{8,9},{9,8},{10,11... | collective-permute-start | bytes 1769480 | tf_op jit(solution)/shard_map/ppermute | solution.py:509
  26.1 0.0 collective-permute-done.2.early_a
  26.1 2.3 %collective-permute-done.3.early_b = f32[4,4,64,128]{3,2,1,0:T(8,128)S(1)} collective-permute-done((f32[4,4,64,128]{3,2,1,0:T(8,128)S(1)}, f32[4,4,64,128]{3,2,1,0:T(8,128)S(1)}, u32[]{:S(2)}, u32[]{:S(2)}) %collective-permute-start.3) | collective-permute-done | bytes 524320 | tf_op jit(solution)/shard_map/ppermute | solution.py:509
  28.4 0.0 copy-start
  28.4 2.9 %couple.1 = (f32[12,4,96,128]{3,2,1,0:T(8,128)S(1)}, f32[12,4,96,128]{3,2,1,0:T(8,128)S(1)}, f32[4,4,96,128]{3,2,1,0:T(8,128)S(1)}, f32[4,4,64,128]{3,2,1,0:T(8,128)S(1)}, f32[4,4,64,128]{3,2,1,0:T(8,128)S(1)}) custom-call(bf16[512,256]{1,0:T(8,128)(2,1)S(1)} %get-tuple-element.31.bands, ...), custom_call_target="tpu_custom_call", output_to_operand_aliasing={{0}: (3, {})} | custom-call | flops 4000000000 | bytes 12000000 | tf_op jit(solution)/shard_map/couple/pallas_call | solution.py:575
  31.3 7.7 %collective-permute-done.5.late_b = f32[4,4,72,128]{3,2,1,0:T(8,128)S(1)} collective-permute-done((f32[4,4,72,128]{3,2,1,0:T(8,128)S(1)}, f32[4,4,72,128]{3,2,1,0:T(8,128)S(1)}, u32[]{:S(2)}, u32[]{:S(2)}) %collective-permute-start.5) | collective-permute-done | bytes 589856 | tf_op jit(solution)/shard_map/ppermute | solution.py:509
  39.0 0.0 collective-permute-done.4.late_a
  39.0 0.0 copy-done
  39.0 7.2 %finish.1 = (f32[8,64,512]{2,1,0:T(8,128)}, f32[16,64,128]{2,1,0:T(8,128)S(1)}, f32[12,4,96,128]{3,2,1,0:T(8,128)S(1)}, f32[12,4,96,128]{3,2,1,0:T(8,128)S(1)}, f32[4,4,96,128]{3,2,1,0:T(8,128)S(1)}) custom-call(s32[3]{0:T(128)S(1)} %copy-done.2, s32[1]{0:T(128)S(6)} %copy.21.start, ...), custom_call_target="tpu_custom_call", output_to_operand_aliasing={{2}: (8, {}), {3}: (9, {}), {4}: (10, {})} | custom-call | tf_op jit(solution)/shard_map/finish/pallas_call | solution.py:585
  46.2 19.1 %all_to_all.5.parts = f32[16,64,128]{2,1,0:T(8,128)S(1)} all-to-all(f32[16,64,128]{2,1,0:T(8,128)S(1)} %get-tuple-element.53), channel_id=1, replica_groups=mesh['lat'=32,'dep'=16] {'dep'}, dimensions={0} | all-to-all | bytes 1048576 | tf_op jit(solution)/shard_map/all_to_all | solution.py:598
  65.3 1.2 %composite.1 = f32[128,64]{1,0:T(8,128)} custom-call(f32[16,64,128]{2,1,0:T(8,128)S(1)} %all_to_all.5.parts), custom_call_target="tpu_custom_call" | custom-call | tf_op jit(solution)/shard_map/composite/pallas_call | solution.py:599
Async XLA Ops:
  0.6 16.3 %copy-start.1 = (f32[16]{0:T(128)S(1)}, f32[16]{0:T(128)}, u32[]{:S(2)}) copy-start(f32[16]{0:T(128)} %courant.1) | copy-start | bytes 196
  2.9 16.4 %collective-permute-start = (f32[8,4,16,128]{3,2,1,0:T(8,128)S(1)}, f32[8,4,16,128]{3,2,1,0:T(8,128)S(1)}, u32[]{:S(2)}, u32[]{:S(2)}) collective-permute-start(f32[8,4,16,128]{3,2,1,0:T(8,128)S(1)} %get-tuple-element.36), channel_id=1, source_target_pairs={{0,16},{1,17},{2,18},{3,19},{4,20},{5,21},{6,22},{7,23},{8,24},{9,... | collective-permute-start | bytes 786440 | tf_op jit(solution)/shard_map/ppermute | solution.py:509
  11.7 8.0 %collective-permute-start.1 = (f32[8,4,16,128]{3,2,1,0:T(8,128)S(1)}, f32[8,4,16,128]{3,2,1,0:T(8,128)S(1)}, u32[]{:S(2)}, u32[]{:S(2)}) collective-permute-start(f32[8,4,16,128]{3,2,1,0:T(8,128)S(1)} %get-tuple-element.37), channel_id=1, source_target_pairs={{16,32},{17,33},{18,34},{19,35},{20,36},{21,37},{22,38},{23,39},{2... | collective-permute-start | bytes 786440 | tf_op jit(solution)/shard_map/ppermute | solution.py:509
  13.6 12.5 %collective-permute-start.2 = (f32[4,4,64,128]{3,2,1,0:T(8,128)S(1)}, f32[4,4,64,128]{3,2,1,0:T(8,128)S(1)}, u32[]{:S(2)}, u32[]{:S(2)}) collective-permute-start(f32[4,4,64,128]{3,2,1,0:T(8,128)S(1)} %get-tuple-element.42), channel_id=1, source_target_pairs={{0,1},{1,0},{2,3},{3,2},{4,5},{5,4},{6,7},{7,6},{8,9},{9,8},{10,11... | collective-permute-start | bytes 1572872 | tf_op jit(solution)/shard_map/ppermute | solution.py:509
  14.3 14.1 %collective-permute-start.3 = (f32[4,4,64,128]{3,2,1,0:T(8,128)S(1)}, f32[4,4,64,128]{3,2,1,0:T(8,128)S(1)}, u32[]{:S(2)}, u32[]{:S(2)}) collective-permute-start(f32[4,4,64,128]{3,2,1,0:T(8,128)S(1)} %get-tuple-element.43), channel_id=1, source_target_pairs={{1,2},{2,1},{3,4},{4,3},{5,6},{6,5},{7,8},{8,7},{9,10},{10,9},{11,... | collective-permute-start | bytes 1572872 | tf_op jit(solution)/shard_map/ppermute | solution.py:509
  16.9 2.8 %copy-start.2 = (s32[3]{0:T(128)S(1)}, s32[3]{0:T(128)}, u32[]{:S(2)}) copy-start(s32[3]{0:T(128)} %cell.3) | copy-start | bytes 40
  22.3 16.6 %collective-permute-start.5 = (f32[4,4,72,128]{3,2,1,0:T(8,128)S(1)}, f32[4,4,72,128]{3,2,1,0:T(8,128)S(1)}, u32[]{:S(2)}, u32[]{:S(2)}) collective-permute-start(f32[4,4,72,128]{3,2,1,0:T(8,128)S(1)} %get-tuple-element.51), channel_id=1, source_target_pairs={{1,2},{2,1},{3,4},{4,3},{5,6},{6,5},{7,8},{8,7},{9,10},{10,9},{11,... | collective-permute-start | bytes 1769480 | tf_op jit(solution)/shard_map/ppermute | solution.py:509
  25.4 13.6 %collective-permute-start.4 = (f32[4,4,72,128]{3,2,1,0:T(8,128)S(1)}, f32[4,4,72,128]{3,2,1,0:T(8,128)S(1)}, u32[]{:S(2)}, u32[]{:S(2)}) collective-permute-start(f32[4,4,72,128]{3,2,1,0:T(8,128)S(1)} %get-tuple-element.45.sent), channel_id=1, source_target_pairs={{0,1},{1,0},{2,3},{3,2},{4,5},{5,4},{6,7},{7,6},{8,9},{9,8},{10,11... | collective-permute-start | bytes 1769480 | tf_op jit(solution)/shard_map/ppermute | solution.py:509
  28.4 10.6 %copy-start = (f32[4,8]{1,0:T(4,128)S(1)}, f32[4,8]{1,0:T(4,128)}, u32[]{:S(2)}) copy-start(f32[4,8]{1,0:T(4,128)} %transfer.1) | copy-start | bytes 388

commit v7 on v6

--- a/solution.py
+++ b/solution.py
@@ -91,12 +91,12 @@
             yield row, i, c, inside + (16.0 * near - far)
 
 
-def strike(ref, outer, place, amplitude, layers, rows_low, rows_high):
+def strike(ref, outer, place, amplitude, layers, rows):
     z, x, y = place
     row = x + CORE
-    here = (z >= 0) & (z < layers) & (row >= rows_low) & (row < rows_high)
-
-    @pl.when(here)
+    inside = functools.reduce(jnp.logical_or, [(row >= first) & (row < end) for first, end in rows])
+
+    @pl.when((z >= layers[0]) & (z < layers[1]) & inside)
     def _():
         tile, lane = y // 128, y % 128
         old = ref[z + outer, tile, pl.ds(row, 1), :]
@@ -109,8 +109,7 @@
 
 
 def ways():
-    lat, dep = lax.axis_index("lat"), lax.axis_index("dep")
-    return (lat + dep + 1) % 2, (lat + 1) % 2
+    return (lax.axis_index("dep") + 1) % 2, (lax.axis_index("lat") + 1) % 2
 
 
 def source_place(cell):
@@ -240,7 +239,7 @@
 
     lax.fori_loop(0, Z, first, 0, unroll=2)
     place = source_place(cell)
-    strike(one, 2, place, wavelet(start, 0), Z, CORE - 8, CORE + X + 8)
+    strike(one, 2, place, wavelet(start, 0), (0, Z), [(CORE - 8, CORE + X + 8)])
 
     def second(n, carry):
         k = jnp.where(n < 2, n, n + 4)
@@ -253,7 +252,8 @@
     lax.fori_loop(0, 4, second, 0, unroll=2)
     z = place[0]
     inner = (z >= 2) & (z < Z - 2)
-    strike(two_out, 0, (jnp.where(inner, -1, jnp.where(z < 2, z, z - 4)),) + place[1:], wavelet(start, 1), 4, CORE, CORE + X)
+    place = (jnp.where(inner, -1, jnp.where(z < 2, z, z - 4)),) + place[1:]
+    strike(two_out, 0, place, wavelet(start, 1), (0, 4), [(CORE, CORE + X)])
 
 
 def pack_late(now_side, stiff_side, one, two, out_a, out_b):
@@ -281,25 +281,23 @@
 SIDES = ((False, 0, 1, 0, 0, 1, 0), (True, 2, 0, 1, Z - 1, Z - 2, Z + 2))
 
 
-def halo_step(delta, one, halo_stiff, base, near, n_in, n_next, row, masks):
+def halo_step(delta, one, halo_stiff, base, near, far, n_in, n_next, row, masks):
     rows, own = pl.ds(row, 8), pl.ds(row - CORE, 8)
-    terms = {k: plane_terms(delta, base + k, row, masks) for k in range(2)}
-    out = {}
+    close, distant = plane_terms(delta, base + near, row, masks), plane_terms(delta, base + far, row, masks)
     for i in range(T):
-        for k in range(2):
-            c, near_sum, far_sum = terms[k][i]
-            near_sum = near_sum + terms[1 - k][i][0]
-            if k == near:
-                near_sum = near_sum + one[n_in + 2, i, rows, :]
-                far_sum = far_sum + one[n_next + 2, i, rows, :]
-            else:
-                far_sum = far_sum + one[n_in + 2, i, rows, :]
-            lap = 16.0 * near_sum - far_sum - 90.0 * c
-            out[k, i] = 2.0 * c + halo_stiff[base + k, i, own, :] * lap
-    return out
-
-
-def couple(bands, now, stiff, one_in, early_a, early_b, sent, one, two, delta, halo_stiff, halo_two):
+        inner, following = one[n_in + 2, i, rows, :], one[n_next + 2, i, rows, :]
+        for place, (c, near_sum, far_sum), (other, _, _), first, second in (
+            (near, close[i], distant[i], inner, following),
+            (far, distant[i], close[i], None, inner),
+        ):
+            near_sum = near_sum + other
+            if first is not None:
+                near_sum = near_sum + first
+            lap = 16.0 * near_sum - (far_sum + second) - 90.0 * c
+            yield place, i, 2.0 * c + halo_stiff[base + place, i, own, :] * lap
+
+
+def couple(cell, start, bands, now, stiff, one_in, early_a, early_b, sent, one, two, delta, halo_stiff, halo_two):
     del one_in, sent
     masks = lane_masks()
     up1 = ways()[0] == 1
@@ -330,68 +328,61 @@
         return carry
 
     lax.fori_loop(0, Z, second, 0, unroll=2)
+    strike(two, 2, source_place(cell), wavelet(start, 1), (0, Z), [(CORE + 8, CORE + X - 8)])
     for high, base, near, far, n_in, n_next, zi in SIDES:
 
-        def beyond(t, carry, base=base, near=near, n_in=n_in, n_next=n_next):
+        def beyond(t, carry, base=base, near=near, far=far, n_in=n_in, n_next=n_next):
             row = pl.multiple_of(CORE + 8 * t, 8)
-            for (k, i), v in halo_step(delta, one, halo_stiff, base, near, n_in, n_next, row, masks).items():
+            for k, i, v in halo_step(delta, one, halo_stiff, base, near, far, n_in, n_next, row, masks):
                 halo_two[base + k, i, pl.ds(pl.multiple_of(8 * t, 8), 8), :] = v
             return carry
 
         lax.fori_loop(1, X // 8 - 1, beyond, 0)
 
 
-def finish(
-    n_dep, cell, start, transfer, bands, now, stiff, now_side, stiff_side, one_in, two_in, delta_in, halo_stiff, halo_two,
-    late_a, late_b, pressure, partial, one, two, delta, weights,
-):
-    del one_in, two_in, delta_in
+def complete(second_half, cell, start, bands, stiff, now, now_side, stiff_side, one, two, delta, halo_stiff, halo_two, late, three):
     masks = lane_masks()
-    up1 = ways()[0] == 1
-    for n in range(4):
-        for j in range(BUMPS):
-            centre = (-3.0 + 6.0 * j / (BUMPS - 1)) / 0.8
-            weights[n, j] = transfer[n, j] * (math.exp(-centre * centre) * (-LOG2E * 1.5 / (Z * n_dep) if n == 3 else 1.0))
-
-    for high, base, near, far, n_in, n_next, zi in SIDES:
-        use_a = up1 if high else jnp.logical_not(up1)
-
-        def late_of(k, i, row, use_a=use_a):
-            rows = pl.ds(row - CORE, 8)
-            return jnp.where(use_a, late_a[k, i, rows, :], late_b[k, i, rows, :])
-
-        for row in (CORE - 8, CORE + X):
-            rows, half = slice(row, row + 8), slice(0, 8) if row < CORE else slice(8, 16)
-            for i in range(T):
-                zero_h = [late_of(k, i, CORE + X) for k in range(2)]
-                one_h = [late_of(2 + k, i, CORE + X) for k in range(2)]
-                st_h = [pltpu.roll(v, 4, 0) for v in one_h]
-                one[n_in + 2, i, rows, :] += stiff_side[n_in, i, half, :] * (16.0 * zero_h[near] - zero_h[far])
-                one[n_next + 2, i, rows, :] -= stiff_side[n_next, i, half, :] * zero_h[near]
-                d_near = st_h[near] * (16.0 * now_side[n_in, i, half, :] - now_side[n_next, i, half, :])
-                d_far = -st_h[far] * now_side[n_in, i, half, :]
-                for at, d in ((near, d_near), (far, d_far)):
-                    one[zi + at, i, rows, :] = one_h[at] + d
-                    delta[base + at, i, rows, :] = d
-
-        def inner(t, carry, base=base, near=near, far=far, n_in=n_in, n_next=n_next, zi=zi, late_of=late_of):
-            row = pl.multiple_of(CORE + 8 * t, 8)
-            rows, own = pl.ds(row, 8), pl.ds(pl.multiple_of(8 * t, 8), 8)
-            for i in range(T):
-                one_h = [late_of(k, i, row) for k in range(2)]
-                for k in range(2):
-                    one[zi + k, i, rows, :] += one_h[k]
-                    two[zi + k, i, rows, :] = late_of(2 + k, i, row) + halo_two[base + k, i, own, :]
-                two[n_in + 2, i, rows, :] += stiff[n_in, i, own, :] * (16.0 * one_h[near] - one_h[far])
-                two[n_next + 2, i, rows, :] -= stiff[n_next, i, own, :] * one_h[near]
-            return carry
-
-        lax.fori_loop(0, X // 8, inner, 0)
-        for row in (CORE, CORE + X - 8):
-            for (k, i), v in halo_step(delta, one, halo_stiff, base, near, n_in, n_next, row, masks).items():
-                two[zi + k, i, row : row + 8, :] = late_of(2 + k, i, row) + v
-
-    def second(k, carry):
+    place = source_place(cell)
+    high = 1 - ways()[0] if second_half else ways()[0]
+    base, near, far, n_in, n_next, zi = 2 * high, 1 - high, high, (Z - 1) * high, 1 + (Z - 3) * high, (Z + 2) * high
+
+    extra = slice(X, X + 8)
+    for row in (CORE - 8, CORE + X):
+        rows, half = slice(row, row + 8), slice(0, 8) if row < CORE else slice(8, 16)
+        for i in range(T):
+            zero_near, zero_far = late[near, i, extra, :], late[far, i, extra, :]
+            one[n_in + 2, i, rows, :] += stiff_side[n_in, i, half, :] * (16.0 * zero_near - zero_far)
+            one[n_next + 2, i, rows, :] -= stiff_side[n_next, i, half, :] * zero_near
+            first, second = now_side[n_in, i, half, :], now_side[n_next, i, half, :]
+            for at, term in ((near, 16.0 * first - second), (far, -first)):
+                v = late[2 + at, i, extra, :]
+                d = pltpu.roll(v, 4, 0) * term
+                one[zi + at, i, rows, :] = v + d
+                delta[base + at, i, rows, :] = d
+
+    def inner(t, carry):
+        row = pl.multiple_of(CORE + 8 * t, 8)
+        rows, own = pl.ds(row, 8), pl.ds(pl.multiple_of(8 * t, 8), 8)
+        for i in range(T):
+            one_near, one_far = late[near, i, own, :], late[far, i, own, :]
+            one[zi + near, i, rows, :] += one_near
+            one[zi + far, i, rows, :] += one_far
+            for k in range(2):
+                two[zi + k, i, rows, :] = late[2 + k, i, own, :] + halo_two[base + k, i, own, :]
+            two[n_in + 2, i, rows, :] += stiff[n_in, i, own, :] * (16.0 * one_near - one_far)
+            two[n_next + 2, i, rows, :] -= stiff[n_next, i, own, :] * one_near
+        return carry
+
+    lax.fori_loop(0, X // 8, inner, 0)
+    for row in (CORE, CORE + X - 8):
+        for k, i, v in halo_step(delta, one, halo_stiff, base, near, far, n_in, n_next, row, masks):
+            two[zi + k, i, row : row + 8, :] = late[2 + k, i, row - CORE : row - CORE + 8, :] + v
+
+    count = 4 if second_half else 6
+    lowest = (Z - count) * high
+
+    def second(n, carry):
+        k = lowest + n
         for part in OUTER:
             for row, i, c, lap in full_rows(one, k + 2, *part, bands[...]):
                 rows = slice(row, row + 8)
@@ -402,57 +393,113 @@
                 two[k + 2, i, rows, :] = 2.0 * c - now[k + 2, i, rows, :] + st * lap
         return carry
 
-    lax.fori_loop(0, Z, second, 0, unroll=2)
-    place = source_place(cell)
-    strike(two, 2, place, wavelet(start, 1), Z, CORE - 8, CORE + X + 8)
-
-    def third(k, carry):
+    lax.fori_loop(0, count, second, 0, unroll=2)
+    outer = [(CORE - 8, CORE + 8), (CORE + X - 8, CORE + X + 8)]
+    strike(two, 2, place, wavelet(start, 1), (lowest, lowest + count), outer)
+
+    def third(n, carry):
+        k = 4 * high + n
         for row, i, c, lap in full_rows(two, k + 2, CORE, X, bands[...]):
-            rows, own = slice(row, row + 8), slice(row - CORE, row - CORE + 8)
-            three = 2.0 * c - one[k + 2, i, rows, :] + stiff[k, i, own, :] * lap
-            one[k + 2, i, rows, :] = three
-        return carry
-
-    lax.fori_loop(0, Z, third, 0, unroll=2)
-    strike(one, 2, place, wavelet(start, 2), Z, CORE, CORE + X)
-
-    group = lax.broadcasted_iota(jnp.int32, (8, 128), 1) // 32
+            own = slice(row - CORE, row - CORE + 8)
+            before = one[k + 2, i, row : row + 8, :]
+            three[n, own, 128 * i : 128 * i + 128] = 2.0 * c - before + stiff[k, i, own, :] * lap
+        return carry
+
+    lax.fori_loop(0, 4, third, 0, unroll=2)
+    z, x, y = place
+    n = z - 4 * high
+
+    @pl.when((n >= 0) & (n < 4) & (x >= 0) & (x < X))
+    def _():
+        ids = lax.broadcasted_iota(jnp.int32, (1, 512), 1)
+        amplitude = jnp.concatenate([wavelet(start, 2)] * T, axis=1)
+        three[n, pl.ds(x, 1), :] = three[n, pl.ds(x, 1), :] + jnp.where(ids == y, amplitude, 0.0)
+
+
+def weigh(n_dep, transfer, weights):
+    for n in range(4):
+        for j in range(BUMPS):
+            centre = (-3.0 + 6.0 * j / (BUMPS - 1)) / 0.8
+            weights[n, j] = transfer[n, j] * (math.exp(-centre * centre) * (-LOG2E * 1.5 / (Z * n_dep) if n == 3 else 1.0))
+
+
+def look(weights, three, i, own):
     half = BUMPS // 2
     rate = 6.0 / (BUMPS - 1) / (0.8 * 0.8) * LOG2E
+    zero = jnp.zeros((8, 128), jnp.float32)
+    seen = [zero] * BUMPS
+    through = jnp.ones((8, 128), jnp.float32)
+    depth = zero
+    for n in range(4):
+        p = clamp_for_bumps(three[n, own, 128 * i : 128 * i + 128])
+        gauss = jnp.exp2(p * p * (-LOG2E / 0.64))
+        rise = jnp.exp2(p * rate)
+        fall = jnp.exp2(p * -rate)
+        up, down = rise * rise, fall * fall
+        above, below = gauss * rise, gauss * fall
+        a = weights[3, BUMPS - 1] * up + weights[3, BUMPS - 2]
+        b = weights[3, 0] * down + weights[3, 1]
+        for j in range(2, half):
+            a = a * up + weights[3, BUMPS - 1 - j]
+            b = b * down + weights[3, j]
+        power = a * above + b * below
+        stay = jnp.exp2(power)
+        weight = through * (1.0 - stay)
+        through = through * stay
+        depth = depth + power
+        above, below = weight * above, weight * below
+        for j in range(half):
+            seen[half + j] = seen[half + j] + above
+            seen[half - 1 - j] = seen[half - 1 - j] + below
+            if j < half - 1:
+                above, below = above * up, below * down
+    return seen, through, depth
+
+
+def finish_first(
+    n_dep, cell, start, transfer, bands, now, stiff, now_side, stiff_side, one_in, two_in, delta_in, halo_stiff, halo_two,
+    late, three, looked, one, two, delta, weights,
+):
+    del one_in, two_in, delta_in
+    weigh(n_dep, transfer, weights)
+    complete(False, cell, start, bands, stiff, now, now_side, stiff_side, one, two, delta, halo_stiff, halo_two, late, three)
 
     def render(t, carry):
-        rows = pl.ds(pl.multiple_of(CORE + 8 * t, 8), 8)
         own = pl.ds(pl.multiple_of(8 * t, 8), 8)
         for i in range(T):
-            zero = jnp.zeros((8, 128), jnp.float32)
-            seen = [zero] * BUMPS
-            through = jnp.ones((8, 128), jnp.float32)
-            depth = zero
-            for k in range(Z):
-                p = one[k + 2, i, rows, :]
-                pressure[k, own, 128 * i : 128 * i + 128] = p
-                p = clamp_for_bumps(p)
-                gauss = jnp.exp2(p * p * (-LOG2E / 0.64))
-                rise = jnp.exp2(p * rate)
-                fall = jnp.exp2(p * -rate)
-                up, down = rise * rise, fall * fall
-                above, below = gauss * rise, gauss * fall
-                a = weights[3, BUMPS - 1] * up + weights[3, BUMPS - 2]
-                b = weights[3, 0] * down + weights[3, 1]
-                for j in range(2, half):
-                    a = a * up + weights[3, BUMPS - 1 - j]
-                    b = b * down + weights[3, j]
-                power = a * above + b * below
-                stay = jnp.exp2(power)
-                weight = through * (1.0 - stay)
-                through = through * stay
-                depth = depth + power
-                above, below = weight * above, weight * below
-                for j in range(half):
-                    seen[half + j] = seen[half + j] + above
-                    seen[half - 1 - j] = seen[half - 1 - j] + below
-                    if j < half - 1:
-                        above, below = above * up, below * down
+            seen, through, depth = look(weights, three, i, own)
+            for j, v in enumerate(seen + [through, depth]):
+                looked[j, i, own, :] = v
+        return carry
+
+    lax.fori_loop(0, X // 8, render, 0)
+
+
+def finish_second(
+    n_dep, cell, start, transfer, bands, now, stiff, now_side, stiff_side, one_in, two_in, delta_in, halo_stiff, halo_two,
+    late, other, looked, pressure, partial, one, two, delta, weights, three, sems,
+):
+    del one_in, two_in, delta_in
+    high = 1 - ways()[0]
+    copies = [
+        pltpu.make_async_copy(other, pressure.at[pl.ds(4 - 4 * high, 4)], sems.at[0]),
+        pltpu.make_async_copy(three, pressure.at[pl.ds(4 * high, 4)], sems.at[1]),
+    ]
+    copies[0].start()
+    weigh(n_dep, transfer, weights)
+    complete(True, cell, start, bands, stiff, now, now_side, stiff_side, one, two, delta, halo_stiff, halo_two, late, three)
+    copies[1].start()
+    group = lax.broadcasted_iota(jnp.int32, (8, 128), 1) // 32
+    behind = high == 1
+
+    def render(t, carry):
+        own = pl.ds(pl.multiple_of(8 * t, 8), 8)
+        for i in range(T):
+            seen, through, depth = look(weights, three, i, own)
+            mine = jnp.where(behind, looked[BUMPS, i, own, :], 1.0)
+            others = jnp.where(behind, 1.0, through)
+            seen = [mine * seen[j] + others * looked[j, i, own, :] for j in range(BUMPS)]
+            depth = depth + looked[BUMPS + 1, i, own, :]
             parts = []
             for n in range(3):
                 colour = weights[n, 0] * seen[0]
@@ -470,6 +517,8 @@
         return carry
 
     lax.fori_loop(0, X // 8, render, 0)
+    for copy in copies:
+        copy.wait()
 
 
 def composite(parts, image):
@@ -492,7 +541,7 @@
         for dep in range(n_dep):
             other_lat, other_dep = lat, dep
             if kind in ("d1", "d2"):
-                up = ((lat % 2 == 0) == (dep % 2 == 0)) == (kind == "d1")
+                up = (dep % 2 == 0) == (kind == "d1")
                 other_dep = dep + 1 if up else dep - 1
             else:
                 right = (lat % 2 == 0) == (kind == "l1")
@@ -574,27 +623,38 @@
     late_b = swap(late_2, "d2")
     one, two, delta, halo_stiff, halo_two = pl.pallas_call(
         couple,
-        in_specs=[VMEM] * 6 + [pl.BlockSpec(memory_space=pl.ANY)],
+        in_specs=[SMEM] * 2 + [VMEM] * 6 + [pl.BlockSpec(memory_space=pl.ANY)],
         out_specs=[VMEM] * 5,
         out_shape=[kept(*padded)] * 2 + [kept(4, T, ROWS, 128)] + [kept(4, T, X, 128)] * 2,
-        input_output_aliases={3: 0},
+        input_output_aliases={5: 0},
         compiler_params=params,
         cost_estimate=busy(4.0),
         name="couple",
-    )(bands_made, now, stiff, one, early_a, early_b, late_1)
-    pressure, partial, _, _, _ = pl.pallas_call(
-        functools.partial(finish, n_dep),
-        in_specs=[SMEM] * 3 + [VMEM] * 12,
+    )(source_cell, start_step, bands_made, now, stiff, one, early_a, early_b, late_1)
+    changed = [kept(*padded)] * 2 + [kept(4, T, ROWS, 128)]
+    scalars, held = (source_cell, start_step, tf_weights), (bands_made, now, stiff, now_side, stiff_side)
+    three, looked, one, two, delta = pl.pallas_call(
+        functools.partial(finish_first, n_dep),
+        in_specs=[SMEM] * 3 + [VMEM] * 11,
         out_specs=[VMEM] * 5,
-        out_shape=[shape(Z, X, 512), shape(n_dep, X, 128)] + [kept(*padded)] * 2 + [kept(4, T, ROWS, 128)],
+        out_shape=[kept(4, X, 512), kept(BUMPS + 2, T, X, 128)] + changed,
         scratch_shapes=[pltpu.SMEM((4, BUMPS), f32)],
         input_output_aliases={8: 2, 9: 3, 10: 4},
         compiler_params=params,
-        name="finish",
-    )(
-        source_cell, start_step, tf_weights, bands_made, now, stiff, now_side, stiff_side, one, two, delta, halo_stiff,
-        halo_two, late_a, late_b,
-    )
+        cost_estimate=busy(4.0),
+        name="finish_first",
+    )(*scalars, *held, one, two, delta, halo_stiff, halo_two, late_a)
+    pressure, partial, _, _, _ = pl.pallas_call(
+        functools.partial(finish_second, n_dep),
+        in_specs=[SMEM] * 3 + [VMEM] * 13,
+        out_specs=[HBM] + [VMEM] * 4,
+        out_shape=[pltpu.HBM((Z, X, 512), f32), kept(n_dep, X, 128)] + changed,
+        scratch_shapes=[pltpu.SMEM((4, BUMPS), f32), pltpu.VMEM((4, X, 512), f32), pltpu.SemaphoreType.DMA((2,))],
+        input_output_aliases={8: 2, 9: 3, 10: 4},
+        compiler_params=params,
+        cost_estimate=busy(4.0),
+        name="finish_second",
+    )(*scalars, *held, one, two, delta, halo_stiff, halo_two, late_b, three, looked)
     parts = lax.all_to_all(partial, "dep", 0, 0, tiled=True)
     image = pl.pallas_call(
         composite,

time: 67.6 us -> 65.4 us (0.967); the launches traced: 66.5 us -> 65.1 us
  blocking collectives: 19.1 us -> 15.1 us
  Pallas kernels: 18.6 us -> 19.8 us
  starting transfers between devices: 17.1 us -> 18.3 us
    all_to_all x1, blocking collectives: 19.1 us -> 15.1 us  [on_device(): parts = lax.all_to_all(partial, 'dep', 0, 0, tiled=True)]
    ppermute x6, starting transfers between devices: 17.1 us -> 18.3 us  [swap(): return lax.ppermute(v, ('lat', 'dep'), swaps(n_lat, n_dep, kind))]
    pallas_call x2 -> x3, Pallas kernels: 10.1 us -> 11.3 us  [the longest x1 4.23 us: on_device(): pl.pallas_call(functools.partial(finish_second, n_dep), in_specs=[SMEM] *...]
  transfers between devices with their start and end apart: 6 -> 6, of which waited for: 3 -> 3; matrix products, arithmetic and copies ran while one was open for 0% -> 0% of each run, Pallas kernels for 12% -> 19%
where the time goes in v7:
time: 65.4 us; the launch traced here: 65.1 us
  Pallas kernels  19.8 us (30%)
  starting transfers between devices  18.3 us (28%)
  blocking collectives  15.1 us (23%)
  waiting for transfers between devices  10.6 us (16%)
  between operations  1.42 us (2%)
    ppermute x6, starting transfers between devices, swap(): return lax.ppermute(v, ('lat', 'dep'), swaps(n_lat, n_dep, kind))  18.3 us
    all_to_all x1, blocking collectives, on_device(): parts = lax.all_to_all(partial, 'dep', 0, 0, tiled=True)  15.1 us
    ppermute x6, waiting for transfers between devices, swap(): return lax.ppermute(v, ('lat', 'dep'), swaps(n_lat, n_dep, kind))  10.6 us
    pallas_call x1, Pallas kernels, on_device(): pl.pallas_call(functools.partial(finish_second, n_dep), in_specs=[SMEM] *...  4.23 us
    pallas_call x1, Pallas kernels, on_device(): pl.pallas_call(functools.partial(finish_first, n_dep), in_specs=[SMEM] *...  3.55 us
    pallas_call x1, Pallas kernels, on_device(): pl.pallas_call(couple, in_specs=[SMEM] * 2 + [VMEM] * 6 + [pl.BlockSpec(m...  3.48 us
    pallas_call x1, Pallas kernels, on_device(): pl.pallas_call(advance_outer, in_specs=[SMEM] * 2 + [VMEM] * 7, out_specs...  2.55 us
    pallas_call x1, Pallas kernels, on_device(): pl.pallas_call(advance_inner, in_specs=[SMEM] + [VMEM] * 3, out_specs=[VM...  2.36 us
  transfers between devices with their start and end apart: 6, of which 3 were waited for; matrix products, arithmetic and copies ran while one was open for 0% of the time, Pallas kernels for 19%

profile of v7, /device:TPU:1, one launch (start us, length us, event | category | flops | bytes accessed | tf_op | source)
XLA Modules:
  0.0 65.1 jit_solution(12863000055312133834)
XLA Ops:
  0.6 0.0 copy-start
  0.6 2.3 %pack.1 = (f32[4,4,64,128]{3,2,1,0:T(8,128)S(1)}, f32[4,4,64,128]{3,2,1,0:T(8,128)S(1)}, f32[8,4,16,128]{3,2,1,0:T(8,128)S(1)}, f32[8,4,16,128]{3,2,1,0:T(8,128)...) custom-call(f32[16]{0:T(128)} %courant.1, f32[8,64,512]{2,1,0:T(8,128)} %now_in.1, ...), custom_call_target="tpu_custom_call" | custom-call | tf_op jit(solution)/shard_map/pack/pallas_call | solution.py:577
  2.9 8.8 %collective-permute-start = (f32[8,4,16,128]{3,2,1,0:T(8,128)S(1)}, f32[8,4,16,128]{3,2,1,0:T(8,128)S(1)}, u32[]{:S(2)}, u32[]{:S(2)}) collective-permute-start(f32[8,4,16,128]{3,2,1,0:T(8,128)S(1)} %get-tuple-element.41), channel_id=1, source_target_pairs={{0,16},{1,17},{2,18},{3,19},{4,20},{5,21},{6,22},{7,23},{8,24},{9,... | collective-permute-start | bytes 786440 | tf_op jit(solution)/shard_map/ppermute | solution.py:558
  11.7 1.9 %collective-permute-start.1 = (f32[8,4,16,128]{3,2,1,0:T(8,128)S(1)}, f32[8,4,16,128]{3,2,1,0:T(8,128)S(1)}, u32[]{:S(2)}, u32[]{:S(2)}) collective-permute-start(f32[8,4,16,128]{3,2,1,0:T(8,128)S(1)} %get-tuple-element.42), channel_id=1, source_target_pairs={{16,32},{17,33},{18,34},{19,35},{20,36},{21,37},{22,38},{23,39},{2... | collective-permute-start | bytes 786440 | tf_op jit(solution)/shard_map/ppermute | solution.py:558
  13.6 1.9 %collective-permute-start.2 = (f32[4,4,64,128]{3,2,1,0:T(8,128)S(1)}, f32[4,4,64,128]{3,2,1,0:T(8,128)S(1)}, u32[]{:S(2)}, u32[]{:S(2)}) collective-permute-start(f32[4,4,64,128]{3,2,1,0:T(8,128)S(1)} %get-tuple-element.47), channel_id=1, source_target_pairs={{0,1},{1,0},{2,3},{3,2},{4,5},{5,4},{6,7},{7,6},{8,9},{9,8},{10,11... | collective-permute-start | bytes 1572872 | tf_op jit(solution)/shard_map/ppermute | solution.py:558
  15.6 0.7 %collective-permute-start.3 = (f32[4,4,64,128]{3,2,1,0:T(8,128)S(1)}, f32[4,4,64,128]{3,2,1,0:T(8,128)S(1)}, u32[]{:S(2)}, u32[]{:S(2)}) collective-permute-start(f32[4,4,64,128]{3,2,1,0:T(8,128)S(1)} %get-tuple-element.48), channel_id=1, source_target_pairs={{1,2},{2,1},{3,4},{4,3},{5,6},{6,5},{7,8},{8,7},{9,10},{10,9},{11,... | collective-permute-start | bytes 1572872 | tf_op jit(solution)/shard_map/ppermute | solution.py:558
  16.9 0.0 copy-done
  16.9 0.0 copy-start.2
  16.9 2.4 %advance_inner.1 = (f32[12,4,96,128]{3,2,1,0:T(8,128)S(1)}, f32[8,4,64,128]{3,2,1,0:T(8,128)S(1)}, f32[12,4,96,128]{3,2,1,0:T(8,128)S(1)}, f32[8,4,16,128]{3,2,1,0:T(8,128)S(1)}, bf16[512,256]{1,0:T(8,128)(2,1)S(1)}) custom-call(f32[16]{0:T(128)S(1)} %copy-done, f32[8,64,512]{2,1,0:T(8,128)S(1)} %get-tuple-element.33.now, ...), custom_call_target="tpu_custom_call" | custom-call | flops 3000000000 | bytes 9000000 | tf_op jit(solution)/shard_map/advance_inner/pallas_call | solution.py:594
  19.3 0.0 collective-permute-done.lat_a
  19.3 0.4 collective-permute-done.1.lat_b
  19.7 0.0 copy-done.2
  19.7 2.6 %advance_outer.1 = (f32[12,4,96,128]{3,2,1,0:T(8,128)S(1)}, f32[12,4,96,128]{3,2,1,0:T(8,128)S(1)}, f32[8,4,16,128]{3,2,1,0:T(8,128)S(1)}, f32[8,4,16,128]{3,2,1,0:T(8,128)S(1)}, f32[4,4,96,128]{3,2,1,0:T(8,128)S(1)}) custom-call(s32[3]{0:T(128)S(1)} %copy-done.2, s32[1]{0:T(128)S(6)} %copy.27.start, ...), custom_call_target="tpu_custom_call", output_to_operand_aliasing={{0}: (3, {}), {1}: (5, {})} | custom-call | flops 5000000000 | bytes 15000000 | tf_op jit(solution)/shard_map/advance_outer/pallas_call | solution.py:603
  22.3 0.1 pack_late.1
  22.4 4.2 %collective-permute-start.4 = (f32[4,4,72,128]{3,2,1,0:T(8,128)S(1)}, f32[4,4,72,128]{3,2,1,0:T(8,128)S(1)}, u32[]{:S(2)}, u32[]{:S(2)}) collective-permute-start(f32[4,4,72,128]{3,2,1,0:T(8,128)S(1)} %get-tuple-element.50.sent), channel_id=1, source_target_pairs={{0,1},{1,0},{2,3},{3,2},{4,5},{5,4},{6,7},{7,6},{8,9},{9,8},{10,11... | collective-permute-start | bytes 1769480 | tf_op jit(solution)/shard_map/ppermute | solution.py:558
  26.6 0.7 %collective-permute-start.5 = (f32[4,4,72,128]{3,2,1,0:T(8,128)S(1)}, f32[4,4,72,128]{3,2,1,0:T(8,128)S(1)}, u32[]{:S(2)}, u32[]{:S(2)}) collective-permute-start(f32[4,4,72,128]{3,2,1,0:T(8,128)S(1)} %get-tuple-element.59), channel_id=1, source_target_pairs={{1,2},{2,1},{3,4},{4,3},{5,6},{6,5},{7,8},{8,7},{9,10},{10,9},{11,... | collective-permute-start | bytes 1769480 | tf_op jit(solution)/shard_map/ppermute | solution.py:558
  27.3 2.1 %collective-permute-done.2.early_a = f32[4,4,64,128]{3,2,1,0:T(8,128)S(1)} collective-permute-done((f32[4,4,64,128]{3,2,1,0:T(8,128)S(1)}, f32[4,4,64,128]{3,2,1,0:T(8,128)S(1)}, u32[]{:S(2)}, u32[]{:S(2)}) %collective-permute-start.2) | collective-permute-done | bytes 524320 | tf_op jit(solution)/shard_map/ppermute | solution.py:558
  29.4 0.0 collective-permute-done.3.early_b
  29.5 0.0 copy-start.1
  29.5 3.5 %couple.1 = (f32[12,4,96,128]{3,2,1,0:T(8,128)S(1)}, f32[12,4,96,128]{3,2,1,0:T(8,128)S(1)}, f32[4,4,96,128]{3,2,1,0:T(8,128)S(1)}, f32[4,4,64,128]{3,2,1,0:T(8,128)S(1)}, f32[4,4,64,128]{3,2,1,0:T(8,128)S(1)}) custom-call(s32[3]{0:T(128)S(1)} %copy-done.2, s32[1]{0:T(128)S(6)} %copy.27.start, ...), custom_call_target="tpu_custom_call", output_to_operand_aliasing={{0}: (5, {})} | custom-call | flops 4000000000 | bytes 12000000 | tf_op jit(solution)/shard_map/couple/pallas_call | solution.py:624
  32.9 8.1 %collective-permute-done.4.late = f32[4,4,72,128]{3,2,1,0:T(8,128)S(1)} collective-permute-done((f32[4,4,72,128]{3,2,1,0:T(8,128)S(1)}, f32[4,4,72,128]{3,2,1,0:T(8,128)S(1)}, u32[]{:S(2)}, u32[]{:S(2)}) %collective-permute-start.4) | collective-permute-done | bytes 589856 | tf_op jit(solution)/shard_map/ppermute | solution.py:558
  41.1 0.0 copy-done.1
  41.1 3.6 %finish_first.1 = (f32[4,64,512]{2,1,0:T(8,128)S(1)}, f32[10,4,64,128]{3,2,1,0:T(8,128)S(1)}, f32[12,4,96,128]{3,2,1,0:T(8,128)S(1)}, f32[12,4,96,128]{3,2,1,0:T(8,128)S(1)}, f32[4,4,96,128]{3,2,1,0:T(8,128)S(1)}) custom-call(s32[3]{0:T(128)S(1)} %copy-done.2, s32[1]{0:T(128)S(6)} %copy.27.start, ...), custom_call_target="tpu_custom_call", output_to_operand_aliasing={{2}: (8, {}), {3}: (9, {}), {4}: (10, {})} | custom-call | flops 4000000000 | bytes 12000000 | tf_op jit(solution)/shard_map/finish_first/pallas_call | solution.py:636
  44.6 0.0 collective-permute-done.5.late
  44.6 4.2 %finish_second.1 = (f32[8,64,512]{2,1,0:T(8,128)}, f32[16,64,128]{2,1,0:T(8,128)S(1)}, f32[12,4,96,128]{3,2,1,0:T(8,128)S(1)}, f32[12,4,96,128]{3,2,1,0:T(8,128)S(1)}, f32[4,4,96,128]{3,2,1,0:T(8,128)S(1)}) custom-call(s32[3]{0:T(128)S(1)} %copy-done.2, s32[1]{0:T(128)S(6)} %copy.27.start, ...), custom_call_target="tpu_custom_call", output_to_operand_aliasing={{2}: (8, {}), {3}: (9, {}), {4}: (10, {})} | custom-call | flops 4000000000 | bytes 12000000 | tf_op jit(solution)/shard_map/finish_second/pallas_call | solution.py:647
  48.9 15.1 %all_to_all.5.parts = f32[16,64,128]{2,1,0:T(8,128)S(1)} all-to-all(f32[16,64,128]{2,1,0:T(8,128)S(1)} %get-tuple-element.63), channel_id=1, replica_groups=mesh['lat'=32,'dep'=16] {'dep'}, dimensions={0} | all-to-all | bytes 1048576 | tf_op jit(solution)/shard_map/all_to_all | solution.py:658
  63.9 1.2 %composite.1 = f32[128,64]{1,0:T(8,128)} custom-call(f32[16,64,128]{2,1,0:T(8,128)S(1)} %all_to_all.5.parts), custom_call_target="tpu_custom_call" | custom-call | tf_op jit(solution)/shard_map/composite/pallas_call | solution.py:659
Async XLA Ops:
  0.6 16.3 %copy-start = (f32[16]{0:T(128)S(1)}, f32[16]{0:T(128)}, u32[]{:S(2)}) copy-start(f32[16]{0:T(128)} %courant.1) | copy-start | bytes 196
  2.9 16.4 %collective-permute-start = (f32[8,4,16,128]{3,2,1,0:T(8,128)S(1)}, f32[8,4,16,128]{3,2,1,0:T(8,128)S(1)}, u32[]{:S(2)}, u32[]{:S(2)}) collective-permute-start(f32[8,4,16,128]{3,2,1,0:T(8,128)S(1)} %get-tuple-element.41), channel_id=1, source_target_pairs={{0,16},{1,17},{2,18},{3,19},{4,20},{5,21},{6,22},{7,23},{8,24},{9,... | collective-permute-start | bytes 786440 | tf_op jit(solution)/shard_map/ppermute | solution.py:558
  11.7 8.0 %collective-permute-start.1 = (f32[8,4,16,128]{3,2,1,0:T(8,128)S(1)}, f32[8,4,16,128]{3,2,1,0:T(8,128)S(1)}, u32[]{:S(2)}, u32[]{:S(2)}) collective-permute-start(f32[8,4,16,128]{3,2,1,0:T(8,128)S(1)} %get-tuple-element.42), channel_id=1, source_target_pairs={{16,32},{17,33},{18,34},{19,35},{20,36},{21,37},{22,38},{23,39},{2... | collective-permute-start | bytes 786440 | tf_op jit(solution)/shard_map/ppermute | solution.py:558
  13.6 15.8 %collective-permute-start.2 = (f32[4,4,64,128]{3,2,1,0:T(8,128)S(1)}, f32[4,4,64,128]{3,2,1,0:T(8,128)S(1)}, u32[]{:S(2)}, u32[]{:S(2)}) collective-permute-start(f32[4,4,64,128]{3,2,1,0:T(8,128)S(1)} %get-tuple-element.47), channel_id=1, source_target_pairs={{0,1},{1,0},{2,3},{3,2},{4,5},{5,4},{6,7},{7,6},{8,9},{9,8},{10,11... | collective-permute-start | bytes 1572872 | tf_op jit(solution)/shard_map/ppermute | solution.py:558
  15.6 13.9 %collective-permute-start.3 = (f32[4,4,64,128]{3,2,1,0:T(8,128)S(1)}, f32[4,4,64,128]{3,2,1,0:T(8,128)S(1)}, u32[]{:S(2)}, u32[]{:S(2)}) collective-permute-start(f32[4,4,64,128]{3,2,1,0:T(8,128)S(1)} %get-tuple-element.48), channel_id=1, source_target_pairs={{1,2},{2,1},{3,4},{4,3},{5,6},{6,5},{7,8},{8,7},{9,10},{10,9},{11,... | collective-permute-start | bytes 1572872 | tf_op jit(solution)/shard_map/ppermute | solution.py:558
  16.9 2.8 %copy-start.2 = (s32[3]{0:T(128)S(1)}, s32[3]{0:T(128)}, u32[]{:S(2)}) copy-start(s32[3]{0:T(128)} %cell.7) | copy-start | bytes 40
  22.4 18.7 %collective-permute-start.4 = (f32[4,4,72,128]{3,2,1,0:T(8,128)S(1)}, f32[4,4,72,128]{3,2,1,0:T(8,128)S(1)}, u32[]{:S(2)}, u32[]{:S(2)}) collective-permute-start(f32[4,4,72,128]{3,2,1,0:T(8,128)S(1)} %get-tuple-element.50.sent), channel_id=1, source_target_pairs={{0,1},{1,0},{2,3},{3,2},{4,5},{5,4},{6,7},{7,6},{8,9},{9,8},{10,11... | collective-permute-start | bytes 1769480 | tf_op jit(solution)/shard_map/ppermute | solution.py:558
  26.6 18.0 %collective-permute-start.5 = (f32[4,4,72,128]{3,2,1,0:T(8,128)S(1)}, f32[4,4,72,128]{3,2,1,0:T(8,128)S(1)}, u32[]{:S(2)}, u32[]{:S(2)}) collective-permute-start(f32[4,4,72,128]{3,2,1,0:T(8,128)S(1)} %get-tuple-element.59), channel_id=1, source_target_pairs={{1,2},{2,1},{3,4},{4,3},{5,6},{6,5},{7,8},{8,7},{9,10},{10,9},{11,... | collective-permute-start | bytes 1769480 | tf_op jit(solution)/shard_map/ppermute | solution.py:558
  29.5 11.6 %copy-start.1 = (f32[4,8]{1,0:T(4,128)S(1)}, f32[4,8]{1,0:T(4,128)}, u32[]{:S(2)}) copy-start(f32[4,8]{1,0:T(4,128)} %transfer.3) | copy-start | bytes 388

commit v8 on v7

--- a/solution.py
+++ b/solution.py
@@ -116,8 +116,8 @@
     return cell[0] - lax.axis_index("dep") * Z, cell[1] - lax.axis_index("lat") * X, cell[2]
 
 
-def wavelet(start, step):
-    level = jnp.full((1, 128), start[0] + step, jnp.int32).astype(jnp.float32)
+def wavelets(start):
+    level = (lax.broadcasted_iota(jnp.int32, (8, 128), 0) + start[0]).astype(jnp.float32)
     shifted = 0.3 * (level - 10.0)
     return 4.0 * (1.0 - 2.0 * shifted * shifted) * jnp.exp(-shifted * shifted)
 
@@ -134,17 +134,21 @@
     courant_in, now_in, prev_in, mat_in, early_1, early_2, side_1, side_2, now, prev, mat, courant, sems,
 ):
     up1, right1 = ways()
-    copies = [
-        pltpu.make_async_copy(src, dst, sems.at[n])
-        for n, (src, dst) in enumerate(((courant_in, courant), (mat_in, mat), (now_in, now), (prev_in, prev)))
-    ]
-    for copy in copies:
-        copy.start()
+    scalars = pltpu.make_async_copy(courant_in, courant, sems.at[0])
+    scalars.start()
+    copies = {}
+    for n, pair in enumerate((0, 3, 1, 2)):
+        for m, (src, dst) in enumerate(((mat_in, mat), (now_in, now), (prev_in, prev))):
+            layers = pl.ds(2 * pair, 2)
+            copies[n, m] = pltpu.make_async_copy(src.at[layers], dst.at[layers], sems.at[1 + 3 * n + m])
+    order = [(0, 0), (1, 0), (0, 1), (1, 1), (2, 0), (3, 0), (2, 1), (3, 1), (0, 2), (1, 2), (2, 2), (3, 2)]
+    for key in order:
+        copies[key].start()
     upper_half = (lax.broadcasted_iota(jnp.int32, (8, 128), 0) >= 4).astype(jnp.int32)
-    copies[0].wait()
+    scalars.wait()
     table = stiffness_table(courant)
-    copies[1].wait()
-    copies[2].wait()
+    for key in order[:4]:
+        copies[key].wait()
     for slot, out in enumerate((early_1, early_2)):
         first = 6 * up1 if slot == 0 else 6 - 6 * up1
         for k in range(2):
@@ -154,7 +158,8 @@
                 for t in range(X // 8):
                     rows = slice(8 * t, 8 * t + 8)
                     out[2 + k, i, rows, :] = stiffness(table, mat[first + k, rows, lanes])
-    copies[3].wait()
+    for key in order[4:]:
+        copies[key].wait()
     for slot, out in enumerate((side_1, side_2)):
         right = right1 if slot == 0 else 1 - right1
         rows = pl.ds(pl.multiple_of((X - 8) * right, 8), 8)
@@ -171,9 +176,10 @@
 OUTER = ((CORE - 8, 16), (CORE + X - 8, 16))
 
 
-def advance_inner(courant, now, prev, mat, now_out, stiff_out, one_out, prev_out, bands):
+def advance_inner(courant, start, now, prev, mat, now_out, stiff_out, one_out, prev_out, bands, amplitudes):
     table = stiffness_table(courant)
     bands[...] = band()
+    amplitudes[...] = wavelets(start)
     zeros = jnp.zeros((T, ROWS, 128), jnp.float32)
     for k in (0, 1, Z + 2, Z + 3):
         now_out[k] = zeros
@@ -204,7 +210,7 @@
 
 
 def advance_outer(
-    cell, start, bands, now_in, stiff_in, one_in, prev_in, lat_a, lat_b, now, one, now_side, stiff_side, two_out,
+    cell, amplitudes, bands, now_in, stiff_in, one_in, prev_in, lat_a, lat_b, now, one, now_side, stiff_side, two_out,
     prev_side,
 ):
     del now_in, one_in
@@ -239,7 +245,7 @@
 
     lax.fori_loop(0, Z, first, 0, unroll=2)
     place = source_place(cell)
-    strike(one, 2, place, wavelet(start, 0), (0, Z), [(CORE - 8, CORE + X + 8)])
+    strike(one, 2, place, amplitudes[0:1, :], (0, Z), [(CORE - 8, CORE + X + 8)])
 
     def second(n, carry):
         k = jnp.where(n < 2, n, n + 4)
@@ -253,7 +259,7 @@
     z = place[0]
     inner = (z >= 2) & (z < Z - 2)
     place = (jnp.where(inner, -1, jnp.where(z < 2, z, z - 4)),) + place[1:]
-    strike(two_out, 0, place, wavelet(start, 1), (0, 4), [(CORE, CORE + X)])
+    strike(two_out, 0, place, amplitudes[1:2, :], (0, 4), [(CORE, CORE + X)])
 
 
 def pack_late(now_side, stiff_side, one, two, out_a, out_b):
@@ -297,7 +303,21 @@
             yield place, i, 2.0 * c + halo_stiff[base + place, i, own, :] * lap
 
 
-def couple(cell, start, bands, now, stiff, one_in, early_a, early_b, sent, one, two, delta, halo_stiff, halo_two):
+def outer_second(k, bands, now, stiff, stiff_side, one, two):
+    for part in OUTER:
+        for row, i, c, lap in full_rows(one, k + 2, *part, bands[...]):
+            if CORE <= row < CORE + X:
+                st = stiff[k, i, row - CORE : row - CORE + 8, :]
+            else:
+                st = stiff_side[k, i, 0:8, :] if row < CORE else stiff_side[k, i, 8:16, :]
+            rows = slice(row, row + 8)
+            two[k + 2, i, rows, :] = 2.0 * c - now[k + 2, i, rows, :] + st * lap
+
+
+def couple(
+    cell, amplitudes, bands, now, stiff, now_side, stiff_side, one_in, early_a, early_b, sent, one, two, delta, halo_stiff,
+    halo_two,
+):
     del one_in, sent
     masks = lane_masks()
     up1 = ways()[0] == 1
@@ -328,7 +348,15 @@
         return carry
 
     lax.fori_loop(0, Z, second, 0, unroll=2)
-    strike(two, 2, source_place(cell), wavelet(start, 1), (0, Z), [(CORE + 8, CORE + X - 8)])
+
+    def middle(n, carry):
+        outer_second(n + 2, bands, now, stiff, stiff_side, one, two)
+        return carry
+
+    lax.fori_loop(0, 4, middle, 0, unroll=2)
+    place = source_place(cell)
+    strike(two, 2, place, amplitudes[1:2, :], (0, Z), [(CORE + 8, CORE + X - 8)])
+    strike(two, 2, place, amplitudes[1:2, :], (2, Z - 2), [(CORE - 8, CORE + 8), (CORE + X - 8, CORE + X + 8)])
     for high, base, near, far, n_in, n_next, zi in SIDES:
 
         def beyond(t, carry, base=base, near=near, far=far, n_in=n_in, n_next=n_next):
@@ -340,19 +368,26 @@
         lax.fori_loop(1, X // 8 - 1, beyond, 0)
 
 
-def complete(second_half, cell, start, bands, stiff, now, now_side, stiff_side, one, two, delta, halo_stiff, halo_two, late, three):
+def complete(
+    second_half, cell, amplitudes, bands, stiff, now, now_side, stiff_side, one, two, delta, halo_stiff, halo_two, late, three
+):
     masks = lane_masks()
     place = source_place(cell)
     high = 1 - ways()[0] if second_half else ways()[0]
     base, near, far, n_in, n_next, zi = 2 * high, 1 - high, high, (Z - 1) * high, 1 + (Z - 3) * high, (Z + 2) * high
 
     extra = slice(X, X + 8)
+    n_third, n_fourth = 2 + (Z - 5) * high, 3 + (Z - 7) * high
     for row in (CORE - 8, CORE + X):
         rows, half = slice(row, row + 8), slice(0, 8) if row < CORE else slice(8, 16)
         for i in range(T):
             zero_near, zero_far = late[near, i, extra, :], late[far, i, extra, :]
-            one[n_in + 2, i, rows, :] += stiff_side[n_in, i, half, :] * (16.0 * zero_near - zero_far)
-            one[n_next + 2, i, rows, :] -= stiff_side[n_next, i, half, :] * zero_near
+            more_in = stiff_side[n_in, i, half, :] * (16.0 * zero_near - zero_far)
+            less_next = stiff_side[n_next, i, half, :] * zero_near
+            one[n_in + 2, i, rows, :] += more_in
+            one[n_next + 2, i, rows, :] -= less_next
+            two[n_third + 2, i, rows, :] -= stiff_side[n_third, i, half, :] * (16.0 * less_next + more_in)
+            two[n_fourth + 2, i, rows, :] += stiff_side[n_fourth, i, half, :] * less_next
             first, second = now_side[n_in, i, half, :], now_side[n_next, i, half, :]
             for at, term in ((near, 16.0 * first - second), (far, -first)):
                 v = late[2 + at, i, extra, :]
@@ -378,24 +413,15 @@
         for k, i, v in halo_step(delta, one, halo_stiff, base, near, far, n_in, n_next, row, masks):
             two[zi + k, i, row : row + 8, :] = late[2 + k, i, row - CORE : row - CORE + 8, :] + v
 
-    count = 4 if second_half else 6
-    lowest = (Z - count) * high
+    lowest = (Z - 2) * high
 
     def second(n, carry):
-        k = lowest + n
-        for part in OUTER:
-            for row, i, c, lap in full_rows(one, k + 2, *part, bands[...]):
-                rows = slice(row, row + 8)
-                if CORE <= row < CORE + X:
-                    st = stiff[k, i, row - CORE : row - CORE + 8, :]
-                else:
-                    st = stiff_side[k, i, 0:8, :] if row < CORE else stiff_side[k, i, 8:16, :]
-                two[k + 2, i, rows, :] = 2.0 * c - now[k + 2, i, rows, :] + st * lap
-        return carry
-
-    lax.fori_loop(0, count, second, 0, unroll=2)
+        outer_second(lowest + n, bands, now, stiff, stiff_side, one, two)
+        return carry
+
+    lax.fori_loop(0, 2, second, 0, unroll=2)
     outer = [(CORE - 8, CORE + 8), (CORE + X - 8, CORE + X + 8)]
-    strike(two, 2, place, wavelet(start, 1), (lowest, lowest + count), outer)
+    strike(two, 2, place, amplitudes[1:2, :], (lowest, lowest + 2), outer)
 
     def third(n, carry):
         k = 4 * high + n
@@ -412,7 +438,7 @@
     @pl.when((n >= 0) & (n < 4) & (x >= 0) & (x < X))
     def _():
         ids = lax.broadcasted_iota(jnp.int32, (1, 512), 1)
-        amplitude = jnp.concatenate([wavelet(start, 2)] * T, axis=1)
+        amplitude = jnp.concatenate([amplitudes[2:3, :]] * T, axis=1)
         three[n, pl.ds(x, 1), :] = three[n, pl.ds(x, 1), :] + jnp.where(ids == y, amplitude, 0.0)
 
 
@@ -457,12 +483,12 @@
 
 
 def finish_first(
-    n_dep, cell, start, transfer, bands, now, stiff, now_side, stiff_side, one_in, two_in, delta_in, halo_stiff, halo_two,
+    n_dep, cell, amplitudes, transfer, bands, now, stiff, now_side, stiff_side, one_in, two_in, delta_in, halo_stiff, halo_two,
     late, three, looked, one, two, delta, weights,
 ):
     del one_in, two_in, delta_in
     weigh(n_dep, transfer, weights)
-    complete(False, cell, start, bands, stiff, now, now_side, stiff_side, one, two, delta, halo_stiff, halo_two, late, three)
+    complete(False, cell, amplitudes, bands, stiff, now, now_side, stiff_side, one, two, delta, halo_stiff, halo_two, late, three)
 
     def render(t, carry):
         own = pl.ds(pl.multiple_of(8 * t, 8), 8)
@@ -476,7 +502,7 @@
 
 
 def finish_second(
-    n_dep, cell, start, transfer, bands, now, stiff, now_side, stiff_side, one_in, two_in, delta_in, halo_stiff, halo_two,
+    n_dep, cell, amplitudes, transfer, bands, now, stiff, now_side, stiff_side, one_in, two_in, delta_in, halo_stiff, halo_two,
     late, other, looked, pressure, partial, one, two, delta, weights, three, sems,
 ):
     del one_in, two_in, delta_in
@@ -487,7 +513,7 @@
     ]
     copies[0].start()
     weigh(n_dep, transfer, weights)
-    complete(True, cell, start, bands, stiff, now, now_side, stiff_side, one, two, delta, halo_stiff, halo_two, late, three)
+    complete(True, cell, amplitudes, bands, stiff, now, now_side, stiff_side, one, two, delta, halo_stiff, halo_two, late, three)
     copies[1].start()
     group = lax.broadcasted_iota(jnp.int32, (8, 128), 1) // 32
     behind = high == 1
@@ -507,12 +533,11 @@
                     colour = colour + weights[n, j] * seen[j]
                 parts.append(colour)
             parts.append(depth * (-1.0 / LOG2E))
+            turned = [parts[0]] + [pltpu.roll(parts[n], 32 * n, 1) for n in range(1, 4)]
             for q in range(4):
-                packed = None
-                for n in range(4):
-                    shift = (32 * (n - q)) % 128
-                    moved = parts[n] if shift == 0 else pltpu.roll(parts[n], shift, 1)
-                    packed = moved if packed is None else jnp.where(group == n, moved, packed)
+                packed = turned[0]
+                for n in range(1, 4):
+                    packed = jnp.where(group == (n + q) % 4, turned[n], packed)
                 partial[4 * i + q, own, :] = packed
         return carry
 
@@ -522,17 +547,20 @@
 
 
 def composite(parts, image):
+    q = lax.axis_index("dep") % 4
     group = lax.broadcasted_iota(jnp.int32, (X, 128), 1) // 32
+    last = group == (q + 3) % 4
     before = jnp.zeros((X, 128), jnp.float32)
     total = jnp.zeros((X, 128), jnp.float32)
     for d in range(parts.shape[0]):
         v = parts[d]
         total = total + jnp.exp(-before) * v
-        depth = v
-        for n in range(3):
-            depth = jnp.where(group == n, pltpu.roll(v, 32 * (n + 1), 1), depth)
-        before = before + depth
-    image[...] = jnp.where(group == 3, 1.0 - jnp.exp(-before), total).T
+        depth = jnp.where(last, v, 0.0)
+        depth = depth + pltpu.roll(depth, 32, 1)
+        before = before + (depth + pltpu.roll(depth, 64, 1))
+    view = jnp.where(last, 1.0 - jnp.exp(-before), total).T
+    for g in range(4):
+        image[pl.ds(pl.multiple_of(32 * ((g + 4 - q) % 4), 32), 32), :] = view[32 * g : 32 * g + 32, :]
 
 
 def swaps(n_lat, n_dep, kind):
@@ -579,7 +607,7 @@
         in_specs=[HBM] * 4,
         out_specs=[VMEM] * 7,
         out_shape=[kept(4, T, X, 128)] * 2 + [kept(Z, T, 16, 128)] * 2 + blocks,
-        scratch_shapes=[pltpu.SMEM((16,), f32), pltpu.SemaphoreType.DMA((4,))],
+        scratch_shapes=[pltpu.SMEM((16,), f32), pltpu.SemaphoreType.DMA((13,))],
         compiler_params=params,
         name="pack",
     )(*(in_hbm(v) for v in (courant_table, pressure_now, pressure_prev, materials)))
@@ -591,18 +619,18 @@
     padded = (Z + 4, T, ROWS, 128)
     bands = pltpu.VMEM((512, 256), jnp.bfloat16)
     block, side = (Z, T, X, 128), (Z, T, 16, 128)
-    now, stiff, one, prev, bands_made = pl.pallas_call(
+    now, stiff, one, prev, bands_made, amplitudes = pl.pallas_call(
         advance_inner,
-        in_specs=[SMEM] + [VMEM] * 3,
-        out_specs=[VMEM] * 5,
-        out_shape=[kept(*padded), kept(*block), kept(*padded), kept(*side), bands],
+        in_specs=[SMEM] * 2 + [VMEM] * 3,
+        out_specs=[VMEM] * 6,
+        out_shape=[kept(*padded), kept(*block), kept(*padded), kept(*side), bands, kept(8, 128)],
         compiler_params=params,
         cost_estimate=busy(3.0),
         name="advance_inner",
-    )(courant_table, *inputs)
+    )(courant_table, start_step, *inputs)
     now, one, now_side, stiff_side, two = pl.pallas_call(
         advance_outer,
-        in_specs=[SMEM] * 2 + [VMEM] * 7,
+        in_specs=[SMEM] + [VMEM] * 8,
         out_specs=[VMEM] * 5,
         out_shape=[kept(*padded)] * 2 + [kept(*side)] * 2 + [kept(4, T, ROWS, 128)],
         scratch_shapes=[pltpu.VMEM(side, f32)],
@@ -610,7 +638,7 @@
         compiler_params=params,
         cost_estimate=busy(5.0),
         name="advance_outer",
-    )(source_cell, start_step, bands_made, now, stiff, one, prev, side_a, side_b)
+    )(source_cell, amplitudes, bands_made, now, stiff, one, prev, side_a, side_b)
     late_1, late_2 = pl.pallas_call(
         pack_late,
         in_specs=[VMEM] * 4,
@@ -623,19 +651,19 @@
     late_b = swap(late_2, "d2")
     one, two, delta, halo_stiff, halo_two = pl.pallas_call(
         couple,
-        in_specs=[SMEM] * 2 + [VMEM] * 6 + [pl.BlockSpec(memory_space=pl.ANY)],
+        in_specs=[SMEM] + [VMEM] * 9 + [pl.BlockSpec(memory_space=pl.ANY)],
         out_specs=[VMEM] * 5,
         out_shape=[kept(*padded)] * 2 + [kept(4, T, ROWS, 128)] + [kept(4, T, X, 128)] * 2,
-        input_output_aliases={5: 0},
+        input_output_aliases={7: 0},
         compiler_params=params,
         cost_estimate=busy(4.0),
         name="couple",
-    )(source_cell, start_step, bands_made, now, stiff, one, early_a, early_b, late_1)
+    )(source_cell, amplitudes, bands_made, now, stiff, now_side, stiff_side, one, early_a, early_b, late_1)
     changed = [kept(*padded)] * 2 + [kept(4, T, ROWS, 128)]
-    scalars, held = (source_cell, start_step, tf_weights), (bands_made, now, stiff, now_side, stiff_side)
+    scalars, held = (source_cell, amplitudes, tf_weights), (bands_made, now, stiff, now_side, stiff_side)
     three, looked, one, two, delta = pl.pallas_call(
         functools.partial(finish_first, n_dep),
-        in_specs=[SMEM] * 3 + [VMEM] * 11,
+        in_specs=[SMEM, VMEM, SMEM] + [VMEM] * 11,
         out_specs=[VMEM] * 5,
         out_shape=[kept(4, X, 512), kept(BUMPS + 2, T, X, 128)] + changed,
         scratch_shapes=[pltpu.SMEM((4, BUMPS), f32)],
@@ -646,7 +674,7 @@
     )(*scalars, *held, one, two, delta, halo_stiff, halo_two, late_a)
     pressure, partial, _, _, _ = pl.pallas_call(
         functools.partial(finish_second, n_dep),
-        in_specs=[SMEM] * 3 + [VMEM] * 13,
+        in_specs=[SMEM, VMEM, SMEM] + [VMEM] * 13,
         out_specs=[HBM] + [VMEM] * 4,
         out_shape=[pltpu.HBM((Z, X, 512), f32), kept(n_dep, X, 128)] + changed,
         scratch_shapes=[pltpu.SMEM((4, BUMPS), f32), pltpu.VMEM((4, X, 512), f32), pltpu.SemaphoreType.DMA((2,))],

time: 65.4 us -> 64.9 us (level)
  Pallas kernels: 19.8 us -> 19.1 us
    pallas_call x5, Pallas kernels: 16.2 us -> 15.4 us  [the longest x1 4.03 us: on_device(): pl.pallas_call(couple, in_specs=[SMEM] + [VMEM] * 9 + [pl.BlockSpec(memor...]
  transfers between devices with their start and end apart: 6 -> 6, of which waited for: 3 -> 3; matrix products, arithmetic and copies ran while one was open for 0% -> 0% of each run, Pallas kernels for 19% -> 18%
where the time goes in v8:
time: 64.9 us; the launch traced here: 64.6 us
  Pallas kernels  19.1 us (29%)
  starting transfers between devices  18.2 us (28%)
  blocking collectives  15.7 us (24%)
  waiting for transfers between devices  10.3 us (16%)
  between operations  1.42 us (2%)
    ppermute x6, starting transfers between devices, swap(): return lax.ppermute(v, ('lat', 'dep'), swaps(n_lat, n_dep, kind))  18.2 us
    all_to_all x1, blocking collectives, on_device(): parts = lax.all_to_all(partial, 'dep', 0, 0, tiled=True)  15.7 us
    ppermute x6, waiting for transfers between devices, swap(): return lax.ppermute(v, ('lat', 'dep'), swaps(n_lat, n_dep, kind))  10.3 us
    pallas_call x1, Pallas kernels, on_device(): pl.pallas_call(couple, in_specs=[SMEM] + [VMEM] * 9 + [pl.BlockSpec(memor...  4.03 us
    pallas_call x1, Pallas kernels, on_device(): pl.pallas_call(functools.partial(finish_second, n_dep), in_specs=[SMEM, V...  3.71 us
    pallas_call x1, Pallas kernels, on_device(): pl.pallas_call(functools.partial(finish_first, n_dep), in_specs=[SMEM, VM...  2.86 us
    pallas_call x1, Pallas kernels, on_device(): pl.pallas_call(advance_outer, in_specs=[SMEM] + [VMEM] * 8, out_specs=[VM...  2.52 us
    pallas_call x1, Pallas kernels, on_device(): pl.pallas_call(advance_inner, in_specs=[SMEM] * 2 + [VMEM] * 3, out_specs...  2.28 us
  transfers between devices with their start and end apart: 6, of which 3 were waited for; matrix products, arithmetic and copies ran while one was open for 0% of the time, Pallas kernels for 18%

profile of v8, /device:TPU:1, one launch (start us, length us, event | category | flops | bytes accessed | tf_op | source)
XLA Modules:
  0.0 64.6 jit_solution(15286963473268902788)
XLA Ops:
  0.6 0.0 copy-start
  0.6 2.2 %pack.1 = (f32[4,4,64,128]{3,2,1,0:T(8,128)S(1)}, f32[4,4,64,128]{3,2,1,0:T(8,128)S(1)}, f32[8,4,16,128]{3,2,1,0:T(8,128)S(1)}, f32[8,4,16,128]{3,2,1,0:T(8,128)...) custom-call(f32[16]{0:T(128)} %courant.1, f32[8,64,512]{2,1,0:T(8,128)} %now_in.1, ...), custom_call_target="tpu_custom_call" | custom-call | tf_op jit(solution)/shard_map/pack/pallas_call | solution.py:605
  2.8 8.8 %collective-permute-start = (f32[8,4,16,128]{3,2,1,0:T(8,128)S(1)}, f32[8,4,16,128]{3,2,1,0:T(8,128)S(1)}, u32[]{:S(2)}, u32[]{:S(2)}) collective-permute-start(f32[8,4,16,128]{3,2,1,0:T(8,128)S(1)} %get-tuple-element.43), channel_id=1, source_target_pairs={{0,16},{1,17},{2,18},{3,19},{4,20},{5,21},{6,22},{7,23},{8,24},{9,... | collective-permute-start | bytes 786440 | tf_op jit(solution)/shard_map/ppermute | solution.py:586
  11.6 1.9 %collective-permute-start.1 = (f32[8,4,16,128]{3,2,1,0:T(8,128)S(1)}, f32[8,4,16,128]{3,2,1,0:T(8,128)S(1)}, u32[]{:S(2)}, u32[]{:S(2)}) collective-permute-start(f32[8,4,16,128]{3,2,1,0:T(8,128)S(1)} %get-tuple-element.44), channel_id=1, source_target_pairs={{16,32},{17,33},{18,34},{19,35},{20,36},{21,37},{22,38},{23,39},{2... | collective-permute-start | bytes 786440 | tf_op jit(solution)/shard_map/ppermute | solution.py:586
  13.6 1.9 %collective-permute-start.2 = (f32[4,4,64,128]{3,2,1,0:T(8,128)S(1)}, f32[4,4,64,128]{3,2,1,0:T(8,128)S(1)}, u32[]{:S(2)}, u32[]{:S(2)}) collective-permute-start(f32[4,4,64,128]{3,2,1,0:T(8,128)S(1)} %get-tuple-element.49), channel_id=1, source_target_pairs={{0,1},{1,0},{2,3},{3,2},{4,5},{5,4},{6,7},{7,6},{8,9},{9,8},{10,11... | collective-permute-start | bytes 1572872 | tf_op jit(solution)/shard_map/ppermute | solution.py:586
  15.5 0.7 %collective-permute-start.3 = (f32[4,4,64,128]{3,2,1,0:T(8,128)S(1)}, f32[4,4,64,128]{3,2,1,0:T(8,128)S(1)}, u32[]{:S(2)}, u32[]{:S(2)}) collective-permute-start(f32[4,4,64,128]{3,2,1,0:T(8,128)S(1)} %get-tuple-element.50), channel_id=1, source_target_pairs={{1,2},{2,1},{3,4},{4,3},{5,6},{6,5},{7,8},{8,7},{9,10},{10,9},{11,... | collective-permute-start | bytes 1572872 | tf_op jit(solution)/shard_map/ppermute | solution.py:586
  16.8 0.0 copy-done
  16.9 0.0 copy-start.2
  16.9 2.3 %advance_inner.1 = (f32[12,4,96,128]{3,2,1,0:T(8,128)S(1)}, f32[8,4,64,128]{3,2,1,0:T(8,128)S(1)}, f32[12,4,96,128]{3,2,1,0:T(8,128)S(1)}, f32[8,4,16,128]{3,2,1...) custom-call(f32[16]{0:T(128)S(1)} %copy-done, s32[1]{0:T(128)S(6)} %copy.27.start, ...), custom_call_target="tpu_custom_call" | custom-call | flops 3000000000 | bytes 9000000 | tf_op jit(solution)/shard_map/advance_inner/pallas_call | solution.py:622
  19.2 0.0 collective-permute-done.lat_a
  19.2 0.5 collective-permute-done.1.lat_b
  19.6 0.0 copy-done.2
  19.6 2.5 %advance_outer.1 = (f32[12,4,96,128]{3,2,1,0:T(8,128)S(1)}, f32[12,4,96,128]{3,2,1,0:T(8,128)S(1)}, f32[8,4,16,128]{3,2,1,0:T(8,128)S(1)}, f32[8,4,16,128]{3,2,1,0:T(8,128)S(1)}, f32[4,4,96,128]{3,2,1,0:T(8,128)S(1)}) custom-call(s32[3]{0:T(128)S(1)} %copy-done.2, ...), custom_call_target="tpu_custom_call", output_to_operand_aliasing={{0}: (3, {}), {1}: (5, {})} | custom-call | flops 5000000000 | bytes 15000000 | tf_op jit(solution)/shard_map/advance_outer/pallas_call | solution.py:631
  22.2 0.1 pack_late.1
  22.3 4.2 %collective-permute-start.4 = (f32[4,4,72,128]{3,2,1,0:T(8,128)S(1)}, f32[4,4,72,128]{3,2,1,0:T(8,128)S(1)}, u32[]{:S(2)}, u32[]{:S(2)}) collective-permute-start(f32[4,4,72,128]{3,2,1,0:T(8,128)S(1)} %get-tuple-element.52.sent), channel_id=1, source_target_pairs={{0,1},{1,0},{2,3},{3,2},{4,5},{5,4},{6,7},{7,6},{8,9},{9,8},{10,11... | collective-permute-start | bytes 1769480 | tf_op jit(solution)/shard_map/ppermute | solution.py:586
  26.4 0.7 %collective-permute-start.5 = (f32[4,4,72,128]{3,2,1,0:T(8,128)S(1)}, f32[4,4,72,128]{3,2,1,0:T(8,128)S(1)}, u32[]{:S(2)}, u32[]{:S(2)}) collective-permute-start(f32[4,4,72,128]{3,2,1,0:T(8,128)S(1)} %get-tuple-element.61), channel_id=1, source_target_pairs={{1,2},{2,1},{3,4},{4,3},{5,6},{6,5},{7,8},{8,7},{9,10},{10,9},{11,... | collective-permute-start | bytes 1769480 | tf_op jit(solution)/shard_map/ppermute | solution.py:586
  27.1 2.2 %collective-permute-done.2.early_a = f32[4,4,64,128]{3,2,1,0:T(8,128)S(1)} collective-permute-done((f32[4,4,64,128]{3,2,1,0:T(8,128)S(1)}, f32[4,4,64,128]{3,2,1,0:T(8,128)S(1)}, u32[]{:S(2)}, u32[]{:S(2)}) %collective-permute-start.2) | collective-permute-done | bytes 524320 | tf_op jit(solution)/shard_map/ppermute | solution.py:586
  29.4 0.0 collective-permute-done.3.early_b
  29.4 0.0 copy-start.1
  29.4 4.0 %couple.1 = (f32[12,4,96,128]{3,2,1,0:T(8,128)S(1)}, f32[12,4,96,128]{3,2,1,0:T(8,128)S(1)}, f32[4,4,96,128]{3,2,1,0:T(8,128)S(1)}, f32[4,4,64,128]{3,2,1,0:T(8,128)S(1)}, f32[4,4,64,128]{3,2,1,0:T(8,128)S(1)}) custom-call(s32[3]{0:T(128)S(1)} %copy-done.2, f32[8,128]{1,0:T(8,128)S(1)} %get-tuple-element.37.amplitudes, ...), custom_call_target="tpu_custom_call", output_to_operand_aliasing={{0}: (7, {})} | custom-call | flops 4000000000 | bytes 12000000 | tf_op jit(solution)/shard_map/couple/pallas_call | solution.py:652
  33.4 7.6 %collective-permute-done.4.late = f32[4,4,72,128]{3,2,1,0:T(8,128)S(1)} collective-permute-done((f32[4,4,72,128]{3,2,1,0:T(8,128)S(1)}, f32[4,4,72,128]{3,2,1,0:T(8,128)S(1)}, u32[]{:S(2)}, u32[]{:S(2)}) %collective-permute-start.4) | collective-permute-done | bytes 589856 | tf_op jit(solution)/shard_map/ppermute | solution.py:586
  41.0 0.0 copy-done.1
  41.0 2.9 %finish_first.1 = (f32[4,64,512]{2,1,0:T(8,128)S(1)}, f32[10,4,64,128]{3,2,1,0:T(8,128)S(1)}, f32[12,4,96,128]{3,2,1,0:T(8,128)S(1)}, f32[12,4,96,128]{3,2,1,0:T(8,128)S(1)}, f32[4,4,96,128]{3,2,1,0:T(8,128)S(1)}) custom-call(s32[3]{0:T(128)S(1)} %copy-done.2, ...), custom_call_target="tpu_custom_call", output_to_operand_aliasing={{2}: (8, {}), {3}: (9, {}), {4}: (10, {})} | custom-call | flops 4000000000 | bytes 12000000 | tf_op jit(solution)/shard_map/finish_first/pallas_call | solution.py:664
  43.8 0.0 collective-permute-done.5.late
  43.9 3.7 %finish_second.1 = (f32[8,64,512]{2,1,0:T(8,128)}, f32[16,64,128]{2,1,0:T(8,128)S(1)}, f32[12,4,96,128]{3,2,1,0:T(8,128)S(1)}, f32[12,4,96,128]{3,2,1,0:T(8,128)S(1)}, f32[4,4,96,128]{3,2,1,0:T(8,128)S(1)}) custom-call(s32[3]{0:T(128)S(1)} %copy-done.2, ...), custom_call_target="tpu_custom_call", output_to_operand_aliasing={{2}: (8, {}), {3}: (9, {}), {4}: (10, {})} | custom-call | flops 4000000000 | bytes 12000000 | tf_op jit(solution)/shard_map/finish_second/pallas_call | solution.py:675
  47.6 15.7 %all_to_all.5.parts = f32[16,64,128]{2,1,0:T(8,128)S(1)} all-to-all(f32[16,64,128]{2,1,0:T(8,128)S(1)} %get-tuple-element.65), channel_id=1, replica_groups=mesh['lat'=32,'dep'=16] {'dep'}, dimensions={0} | all-to-all | bytes 1048576 | tf_op jit(solution)/shard_map/all_to_all | solution.py:686
  63.3 1.3 %composite.1 = f32[128,64]{1,0:T(8,128)} custom-call(f32[16,64,128]{2,1,0:T(8,128)S(1)} %all_to_all.5.parts), custom_call_target="tpu_custom_call" | custom-call | tf_op jit(solution)/shard_map/composite/pallas_call | solution.py:687
Async XLA Ops:
  0.6 16.2 %copy-start = (f32[16]{0:T(128)S(1)}, f32[16]{0:T(128)}, u32[]{:S(2)}) copy-start(f32[16]{0:T(128)} %courant.1) | copy-start | bytes 196
  2.8 16.3 %collective-permute-start = (f32[8,4,16,128]{3,2,1,0:T(8,128)S(1)}, f32[8,4,16,128]{3,2,1,0:T(8,128)S(1)}, u32[]{:S(2)}, u32[]{:S(2)}) collective-permute-start(f32[8,4,16,128]{3,2,1,0:T(8,128)S(1)} %get-tuple-element.43), channel_id=1, source_target_pairs={{0,16},{1,17},{2,18},{3,19},{4,20},{5,21},{6,22},{7,23},{8,24},{9,... | collective-permute-start | bytes 786440 | tf_op jit(solution)/shard_map/ppermute | solution.py:586
  11.6 8.0 %collective-permute-start.1 = (f32[8,4,16,128]{3,2,1,0:T(8,128)S(1)}, f32[8,4,16,128]{3,2,1,0:T(8,128)S(1)}, u32[]{:S(2)}, u32[]{:S(2)}) collective-permute-start(f32[8,4,16,128]{3,2,1,0:T(8,128)S(1)} %get-tuple-element.44), channel_id=1, source_target_pairs={{16,32},{17,33},{18,34},{19,35},{20,36},{21,37},{22,38},{23,39},{2... | collective-permute-start | bytes 786440 | tf_op jit(solution)/shard_map/ppermute | solution.py:586
  13.6 15.8 %collective-permute-start.2 = (f32[4,4,64,128]{3,2,1,0:T(8,128)S(1)}, f32[4,4,64,128]{3,2,1,0:T(8,128)S(1)}, u32[]{:S(2)}, u32[]{:S(2)}) collective-permute-start(f32[4,4,64,128]{3,2,1,0:T(8,128)S(1)} %get-tuple-element.49), channel_id=1, source_target_pairs={{0,1},{1,0},{2,3},{3,2},{4,5},{5,4},{6,7},{7,6},{8,9},{9,8},{10,11... | collective-permute-start | bytes 1572872 | tf_op jit(solution)/shard_map/ppermute | solution.py:586
  15.5 13.9 %collective-permute-start.3 = (f32[4,4,64,128]{3,2,1,0:T(8,128)S(1)}, f32[4,4,64,128]{3,2,1,0:T(8,128)S(1)}, u32[]{:S(2)}, u32[]{:S(2)}) collective-permute-start(f32[4,4,64,128]{3,2,1,0:T(8,128)S(1)} %get-tuple-element.50), channel_id=1, source_target_pairs={{1,2},{2,1},{3,4},{4,3},{5,6},{6,5},{7,8},{8,7},{9,10},{10,9},{11,... | collective-permute-start | bytes 1572872 | tf_op jit(solution)/shard_map/ppermute | solution.py:586
  16.9 2.8 %copy-start.2 = (s32[3]{0:T(128)S(1)}, s32[3]{0:T(128)}, u32[]{:S(2)}) copy-start(s32[3]{0:T(128)} %cell.7) | copy-start | bytes 40
  22.3 18.7 %collective-permute-start.4 = (f32[4,4,72,128]{3,2,1,0:T(8,128)S(1)}, f32[4,4,72,128]{3,2,1,0:T(8,128)S(1)}, u32[]{:S(2)}, u32[]{:S(2)}) collective-permute-start(f32[4,4,72,128]{3,2,1,0:T(8,128)S(1)} %get-tuple-element.52.sent), channel_id=1, source_target_pairs={{0,1},{1,0},{2,3},{3,2},{4,5},{5,4},{6,7},{7,6},{8,9},{9,8},{10,11... | collective-permute-start | bytes 1769480 | tf_op jit(solution)/shard_map/ppermute | solution.py:586
  26.4 17.4 %collective-permute-start.5 = (f32[4,4,72,128]{3,2,1,0:T(8,128)S(1)}, f32[4,4,72,128]{3,2,1,0:T(8,128)S(1)}, u32[]{:S(2)}, u32[]{:S(2)}) collective-permute-start(f32[4,4,72,128]{3,2,1,0:T(8,128)S(1)} %get-tuple-element.61), channel_id=1, source_target_pairs={{1,2},{2,1},{3,4},{4,3},{5,6},{6,5},{7,8},{8,7},{9,10},{10,9},{11,... | collective-permute-start | bytes 1769480 | tf_op jit(solution)/shard_map/ppermute | solution.py:586
  29.4 11.6 %copy-start.1 = (f32[4,8]{1,0:T(4,128)S(1)}, f32[4,8]{1,0:T(4,128)}, u32[]{:S(2)}) copy-start(f32[4,8]{1,0:T(4,128)} %transfer.3) | copy-start | bytes 388

commit v9 on v8

--- a/solution.py
+++ b/solution.py
@@ -3,6 +3,7 @@
 
 import jax
 import jax.numpy as jnp
+import numpy as np
 from jax import lax
 from jax.experimental import pallas as pl
 from jax.experimental.pallas import tpu as pltpu
@@ -55,9 +56,8 @@
 
 
 def band():
-    shape = (512, 256)
-    d = jnp.abs(lax.broadcasted_iota(jnp.int32, shape, 0) % 256 - lax.broadcasted_iota(jnp.int32, shape, 1))
-    return jnp.where(d == 0, -90.0, jnp.where(d == 1, 16.0, jnp.where(d == 2, -1.0, 0.0))).astype(jnp.bfloat16)
+    d = np.abs(np.arange(512)[:, None] % 256 - np.arange(256)[None])
+    return np.where(d == 0, -90.0, np.where(d == 1, 16.0, np.where(d == 2, -1.0, 0.0)))
 
 
 def full_rows(ref, k, first, count, bands):
@@ -109,7 +109,7 @@
 
 
 def ways():
-    return (lax.axis_index("dep") + 1) % 2, (lax.axis_index("lat") + 1) % 2
+    return lax.axis_index("dep") % 2, (lax.axis_index("lat") + 1) % 2
 
 
 def source_place(cell):
@@ -176,9 +176,12 @@
 OUTER = ((CORE - 8, 16), (CORE + X - 8, 16))
 
 
-def advance_inner(courant, start, now, prev, mat, now_out, stiff_out, one_out, prev_out, bands, amplitudes):
+def advance_inner(
+    courant, start, bands_in, now, prev, mat, now_out, stiff_out, one_out, prev_out, bands, amplitudes, sem,
+):
     table = stiffness_table(courant)
-    bands[...] = band()
+    copy = pltpu.make_async_copy(bands_in, bands, sem)
+    copy.start()
     amplitudes[...] = wavelets(start)
     zeros = jnp.zeros((T, ROWS, 128), jnp.float32)
     for k in (0, 1, Z + 2, Z + 3):
@@ -191,6 +194,7 @@
         return carry
 
     lax.fori_loop(0, Z, fill, 0)
+    copy.wait()
 
     def first(k, carry):
         for i in range(T):
@@ -550,14 +554,16 @@
     q = lax.axis_index("dep") % 4
     group = lax.broadcasted_iota(jnp.int32, (X, 128), 1) // 32
     last = group == (q + 3) % 4
+    others = [group == (q + n) % 4 for n in range(3)]
     before = jnp.zeros((X, 128), jnp.float32)
     total = jnp.zeros((X, 128), jnp.float32)
     for d in range(parts.shape[0]):
         v = parts[d]
         total = total + jnp.exp(-before) * v
-        depth = jnp.where(last, v, 0.0)
-        depth = depth + pltpu.roll(depth, 32, 1)
-        before = before + (depth + pltpu.roll(depth, 64, 1))
+        depth = v
+        for n in range(3):
+            depth = jnp.where(others[n], pltpu.roll(v, 32 * (n + 1), 1), depth)
+        before = before + depth
     view = jnp.where(last, 1.0 - jnp.exp(-before), total).T
     for g in range(4):
         image[pl.ds(pl.multiple_of(32 * ((g + 4 - q) % 4), 32), 32), :] = view[32 * g : 32 * g + 32, :]
@@ -569,7 +575,7 @@
         for dep in range(n_dep):
             other_lat, other_dep = lat, dep
             if kind in ("d1", "d2"):
-                up = (dep % 2 == 0) == (kind == "d1")
+                up = (dep % 2 == 1) == (kind == "d1")
                 other_dep = dep + 1 if up else dep - 1
             else:
                 right = (lat % 2 == 0) == (kind == "l1")
@@ -621,13 +627,14 @@
     block, side = (Z, T, X, 128), (Z, T, 16, 128)
     now, stiff, one, prev, bands_made, amplitudes = pl.pallas_call(
         advance_inner,
-        in_specs=[SMEM] * 2 + [VMEM] * 3,
+        in_specs=[SMEM] * 2 + [HBM] + [VMEM] * 3,
         out_specs=[VMEM] * 6,
         out_shape=[kept(*padded), kept(*block), kept(*padded), kept(*side), bands, kept(8, 128)],
+        scratch_shapes=[pltpu.SemaphoreType.DMA(())],
         compiler_params=params,
         cost_estimate=busy(3.0),
         name="advance_inner",
-    )(courant_table, start_step, *inputs)
+    )(courant_table, start_step, in_hbm(jnp.asarray(band(), jnp.bfloat16)), *inputs)
     now, one, now_side, stiff_side, two = pl.pallas_call(
         advance_outer,
         in_specs=[SMEM] + [VMEM] * 8,

time: 64.9 us -> 64.9 us (level)
  the two profiles are of different devices: /device:TPU:1 before, /device:TPU:97 now
where the time goes in v9:
time: 64.9 us; the launch traced here: 64.6 us
  Pallas kernels  19.6 us (30%)
  starting transfers between devices  19.4 us (30%)
  blocking collectives  19 us (29%)
  waiting for transfers between devices  5.11 us (8%)
  between operations  1.46 us (2%)
    ppermute x6, starting transfers between devices, swap(): return lax.ppermute(v, ('lat', 'dep'), swaps(n_lat, n_dep, kind))  19.4 us
    all_to_all x1, blocking collectives, on_device(): parts = lax.all_to_all(partial, 'dep', 0, 0, tiled=True)  19 us
    ppermute x6, waiting for transfers between devices, swap(): return lax.ppermute(v, ('lat', 'dep'), swaps(n_lat, n_dep, kind))  5.11 us
    pallas_call x1, Pallas kernels, on_device(): pl.pallas_call(couple, in_specs=[SMEM] + [VMEM] * 9 + [pl.BlockSpec(memor...  4.03 us
    pallas_call x1, Pallas kernels, on_device(): pl.pallas_call(functools.partial(finish_second, n_dep), in_specs=[SMEM, V...  3.7 us
    pallas_call x1, Pallas kernels, on_device(): pl.pallas_call(advance_inner, in_specs=[SMEM] * 2 + [HBM] + [VMEM] * 3, o...  2.94 us
    pallas_call x1, Pallas kernels, on_device(): pl.pallas_call(functools.partial(finish_first, n_dep), in_specs=[SMEM, VM...  2.88 us
    pallas_call x1, Pallas kernels, on_device(): pl.pallas_call(advance_outer, in_specs=[SMEM] + [VMEM] * 8, out_specs=[VM...  2.52 us
  transfers between devices with their start and end apart: 6, of which 1 were waited for; matrix products, arithmetic and copies ran while one was open for 0% of the time, Pallas kernels for 19%

profile of v9, /device:TPU:97, one launch (start us, length us, event | category | flops | bytes accessed | tf_op | source)
XLA Modules:
  0.0 64.6 jit_solution(412307004022262670)
XLA Ops:
  0.6 0.0 copy-start
  0.6 2.2 %pack.1 = (f32[4,4,64,128]{3,2,1,0:T(8,128)S(1)}, f32[4,4,64,128]{3,2,1,0:T(8,128)S(1)}, f32[8,4,16,128]{3,2,1,0:T(8,128)S(1)}, f32[8,4,16,128]{3,2,1,0:T(8,128)...) custom-call(f32[16]{0:T(128)} %courant.1, f32[8,64,512]{2,1,0:T(8,128)} %now_in.1, ...), custom_call_target="tpu_custom_call" | custom-call | tf_op jit(solution)/shard_map/pack/pallas_call | solution.py:611
  2.8 2.6 %collective-permute-start = (f32[8,4,16,128]{3,2,1,0:T(8,128)S(1)}, f32[8,4,16,128]{3,2,1,0:T(8,128)S(1)}, u32[]{:S(2)}, u32[]{:S(2)}) collective-permute-start(f32[8,4,16,128]{3,2,1,0:T(8,128)S(1)} %get-tuple-element.43), channel_id=1, source_target_pairs={{0,16},{1,17},{2,18},{3,19},{4,20},{5,21},{6,22},{7,23},{8,24},{9,... | collective-permute-start | bytes 786440 | tf_op jit(solution)/shard_map/ppermute | solution.py:592
  5.4 4.7 %collective-permute-start.1 = (f32[8,4,16,128]{3,2,1,0:T(8,128)S(1)}, f32[8,4,16,128]{3,2,1,0:T(8,128)S(1)}, u32[]{:S(2)}, u32[]{:S(2)}) collective-permute-start(f32[8,4,16,128]{3,2,1,0:T(8,128)S(1)} %get-tuple-element.44), channel_id=1, source_target_pairs={{16,32},{17,33},{18,34},{19,35},{20,36},{21,37},{22,38},{23,39},{2... | collective-permute-start | bytes 786440 | tf_op jit(solution)/shard_map/ppermute | solution.py:592
  10.1 0.7 %collective-permute-start.2 = (f32[4,4,64,128]{3,2,1,0:T(8,128)S(1)}, f32[4,4,64,128]{3,2,1,0:T(8,128)S(1)}, u32[]{:S(2)}, u32[]{:S(2)}) collective-permute-start(f32[4,4,64,128]{3,2,1,0:T(8,128)S(1)} %get-tuple-element.49), channel_id=1, source_target_pairs={{1,2},{2,1},{3,4},{4,3},{5,6},{6,5},{7,8},{8,7},{9,10},{10,9},{11,... | collective-permute-start | bytes 1572872 | tf_op jit(solution)/shard_map/ppermute | solution.py:592
  10.8 5.5 %collective-permute-start.3 = (f32[4,4,64,128]{3,2,1,0:T(8,128)S(1)}, f32[4,4,64,128]{3,2,1,0:T(8,128)S(1)}, u32[]{:S(2)}, u32[]{:S(2)}) collective-permute-start(f32[4,4,64,128]{3,2,1,0:T(8,128)S(1)} %get-tuple-element.50), channel_id=1, source_target_pairs={{0,1},{1,0},{2,3},{3,2},{4,5},{5,4},{6,7},{7,6},{8,9},{9,8},{10,11... | collective-permute-start | bytes 1572872 | tf_op jit(solution)/shard_map/ppermute | solution.py:592
  17.0 0.0 copy-done
  17.0 0.0 copy-start.2
  17.0 2.9 %advance_inner.1 = (f32[12,4,96,128]{3,2,1,0:T(8,128)S(1)}, f32[8,4,64,128]{3,2,1,0:T(8,128)S(1)}, f32[12,4,96,128]{3,2,1,0:T(8,128)S(1)}, f32[8,4,16,128]{3,2,1...) custom-call(f32[16]{0:T(128)S(1)} %copy-done, s32[1]{0:T(128)S(6)} %copy.28.start, ...), custom_call_target="tpu_custom_call" | custom-call | flops 3000000000 | bytes 9000000 | tf_op jit(solution)/shard_map/advance_inner/pallas_call | solution.py:628
  20.0 0.0 collective-permute-done.lat_a
  20.0 0.0 collective-permute-done.1.lat_b
  20.0 0.0 copy-done.2
  20.0 2.5 %advance_outer.1 = (f32[12,4,96,128]{3,2,1,0:T(8,128)S(1)}, f32[12,4,96,128]{3,2,1,0:T(8,128)S(1)}, f32[8,4,16,128]{3,2,1,0:T(8,128)S(1)}, f32[8,4,16,128]{3,2,1,0:T(8,128)S(1)}, f32[4,4,96,128]{3,2,1,0:T(8,128)S(1)}) custom-call(s32[3]{0:T(128)S(1)} %copy-done.2, ...), custom_call_target="tpu_custom_call", output_to_operand_aliasing={{0}: (3, {}), {1}: (5, {})} | custom-call | flops 5000000000 | bytes 15000000 | tf_op jit(solution)/shard_map/advance_outer/pallas_call | solution.py:638
  22.5 0.1 pack_late.1
  22.6 0.7 %collective-permute-start.4 = (f32[4,4,72,128]{3,2,1,0:T(8,128)S(1)}, f32[4,4,72,128]{3,2,1,0:T(8,128)S(1)}, u32[]{:S(2)}, u32[]{:S(2)}) collective-permute-start(f32[4,4,72,128]{3,2,1,0:T(8,128)S(1)} %get-tuple-element.52.sent), channel_id=1, source_target_pairs={{1,2},{2,1},{3,4},{4,3},{5,6},{6,5},{7,8},{8,7},{9,10},{10,9},{11,... | collective-permute-start | bytes 1769480 | tf_op jit(solution)/shard_map/ppermute | solution.py:592
  23.3 5.2 %collective-permute-start.5 = (f32[4,4,72,128]{3,2,1,0:T(8,128)S(1)}, f32[4,4,72,128]{3,2,1,0:T(8,128)S(1)}, u32[]{:S(2)}, u32[]{:S(2)}) collective-permute-start(f32[4,4,72,128]{3,2,1,0:T(8,128)S(1)} %get-tuple-element.61), channel_id=1, source_target_pairs={{0,1},{1,0},{2,3},{3,2},{4,5},{5,4},{6,7},{7,6},{8,9},{9,8},{10,11... | collective-permute-start | bytes 1769480 | tf_op jit(solution)/shard_map/ppermute | solution.py:592
  28.6 0.0 collective-permute-done.2.early_a
  28.6 0.0 collective-permute-done.3.early_b
  28.6 0.0 copy-start.1
  28.6 4.0 %couple.1 = (f32[12,4,96,128]{3,2,1,0:T(8,128)S(1)}, f32[12,4,96,128]{3,2,1,0:T(8,128)S(1)}, f32[4,4,96,128]{3,2,1,0:T(8,128)S(1)}, f32[4,4,64,128]{3,2,1,0:T(8,128)S(1)}, f32[4,4,64,128]{3,2,1,0:T(8,128)S(1)}) custom-call(s32[3]{0:T(128)S(1)} %copy-done.2, f32[8,128]{1,0:T(8,128)S(1)} %get-tuple-element.37.amplitudes, ...), custom_call_target="tpu_custom_call", output_to_operand_aliasing={{0}: (7, {})} | custom-call | flops 4000000000 | bytes 12000000 | tf_op jit(solution)/shard_map/couple/pallas_call | solution.py:659
  32.7 0.0 collective-permute-done.4.late
  32.7 0.0 copy-done.1
  32.7 2.9 %finish_first.1 = (f32[4,64,512]{2,1,0:T(8,128)S(1)}, f32[10,4,64,128]{3,2,1,0:T(8,128)S(1)}, f32[12,4,96,128]{3,2,1,0:T(8,128)S(1)}, f32[12,4,96,128]{3,2,1,0:T(8,128)S(1)}, f32[4,4,96,128]{3,2,1,0:T(8,128)S(1)}) custom-call(s32[3]{0:T(128)S(1)} %copy-done.2, ...), custom_call_target="tpu_custom_call", output_to_operand_aliasing={{2}: (8, {}), {3}: (9, {}), {4}: (10, {})} | custom-call | flops 4000000000 | bytes 12000000 | tf_op jit(solution)/shard_map/finish_first/pallas_call | solution.py:671
  35.6 5.1 %collective-permute-done.5.late = f32[4,4,72,128]{3,2,1,0:T(8,128)S(1)} collective-permute-done((f32[4,4,72,128]{3,2,1,0:T(8,128)S(1)}, f32[4,4,72,128]{3,2,1,0:T(8,128)S(1)}, u32[]{:S(2)}, u32[]{:S(2)}) %collective-permute-start.5) | collective-permute-done | bytes 589856 | tf_op jit(solution)/shard_map/ppermute | solution.py:592
  40.7 3.7 %finish_second.1 = (f32[8,64,512]{2,1,0:T(8,128)}, f32[16,64,128]{2,1,0:T(8,128)S(1)}, f32[12,4,96,128]{3,2,1,0:T(8,128)S(1)}, f32[12,4,96,128]{3,2,1,0:T(8,128)S(1)}, f32[4,4,96,128]{3,2,1,0:T(8,128)S(1)}) custom-call(s32[3]{0:T(128)S(1)} %copy-done.2, ...), custom_call_target="tpu_custom_call", output_to_operand_aliasing={{2}: (8, {}), {3}: (9, {}), {4}: (10, {})} | custom-call | flops 4000000000 | bytes 12000000 | tf_op jit(solution)/shard_map/finish_second/pallas_call | solution.py:682
  44.4 19.0 %all_to_all.5.parts = f32[16,64,128]{2,1,0:T(8,128)S(1)} all-to-all(f32[16,64,128]{2,1,0:T(8,128)S(1)} %get-tuple-element.65), channel_id=1, replica_groups=mesh['lat'=32,'dep'=16] {'dep'}, dimensions={0} | all-to-all | bytes 1048576 | tf_op jit(solution)/shard_map/all_to_all | solution.py:693
  63.4 1.2 %composite.1 = f32[128,64]{1,0:T(8,128)} custom-call(f32[16,64,128]{2,1,0:T(8,128)S(1)} %all_to_all.5.parts), custom_call_target="tpu_custom_call" | custom-call | tf_op jit(solution)/shard_map/composite/pallas_call | solution.py:694
Async XLA Ops:
  0.6 16.4 %copy-start = (f32[16]{0:T(128)S(1)}, f32[16]{0:T(128)}, u32[]{:S(2)}) copy-start(f32[16]{0:T(128)} %courant.1) | copy-start | bytes 196
  2.8 17.1 %collective-permute-start = (f32[8,4,16,128]{3,2,1,0:T(8,128)S(1)}, f32[8,4,16,128]{3,2,1,0:T(8,128)S(1)}, u32[]{:S(2)}, u32[]{:S(2)}) collective-permute-start(f32[8,4,16,128]{3,2,1,0:T(8,128)S(1)} %get-tuple-element.43), channel_id=1, source_target_pairs={{0,16},{1,17},{2,18},{3,19},{4,20},{5,21},{6,22},{7,23},{8,24},{9,... | collective-permute-start | bytes 786440 | tf_op jit(solution)/shard_map/ppermute | solution.py:592
  5.4 14.5 %collective-permute-start.1 = (f32[8,4,16,128]{3,2,1,0:T(8,128)S(1)}, f32[8,4,16,128]{3,2,1,0:T(8,128)S(1)}, u32[]{:S(2)}, u32[]{:S(2)}) collective-permute-start(f32[8,4,16,128]{3,2,1,0:T(8,128)S(1)} %get-tuple-element.44), channel_id=1, source_target_pairs={{16,32},{17,33},{18,34},{19,35},{20,36},{21,37},{22,38},{23,39},{2... | collective-permute-start | bytes 786440 | tf_op jit(solution)/shard_map/ppermute | solution.py:592
  10.1 18.5 %collective-permute-start.2 = (f32[4,4,64,128]{3,2,1,0:T(8,128)S(1)}, f32[4,4,64,128]{3,2,1,0:T(8,128)S(1)}, u32[]{:S(2)}, u32[]{:S(2)}) collective-permute-start(f32[4,4,64,128]{3,2,1,0:T(8,128)S(1)} %get-tuple-element.49), channel_id=1, source_target_pairs={{1,2},{2,1},{3,4},{4,3},{5,6},{6,5},{7,8},{8,7},{9,10},{10,9},{11,... | collective-permute-start | bytes 1572872 | tf_op jit(solution)/shard_map/ppermute | solution.py:592
  10.8 17.8 %collective-permute-start.3 = (f32[4,4,64,128]{3,2,1,0:T(8,128)S(1)}, f32[4,4,64,128]{3,2,1,0:T(8,128)S(1)}, u32[]{:S(2)}, u32[]{:S(2)}) collective-permute-start(f32[4,4,64,128]{3,2,1,0:T(8,128)S(1)} %get-tuple-element.50), channel_id=1, source_target_pairs={{0,1},{1,0},{2,3},{3,2},{4,5},{5,4},{6,7},{7,6},{8,9},{9,8},{10,11... | collective-permute-start | bytes 1572872 | tf_op jit(solution)/shard_map/ppermute | solution.py:592
  17.0 3.0 %copy-start.2 = (s32[3]{0:T(128)S(1)}, s32[3]{0:T(128)}, u32[]{:S(2)}) copy-start(s32[3]{0:T(128)} %cell.7) | copy-start | bytes 40
  22.6 10.0 %collective-permute-start.4 = (f32[4,4,72,128]{3,2,1,0:T(8,128)S(1)}, f32[4,4,72,128]{3,2,1,0:T(8,128)S(1)}, u32[]{:S(2)}, u32[]{:S(2)}) collective-permute-start(f32[4,4,72,128]{3,2,1,0:T(8,128)S(1)} %get-tuple-element.52.sent), channel_id=1, source_target_pairs={{1,2},{2,1},{3,4},{4,3},{5,6},{6,5},{7,8},{8,7},{9,10},{10,9},{11,... | collective-permute-start | bytes 1769480 | tf_op jit(solution)/shard_map/ppermute | solution.py:592
  23.3 17.3 %collective-permute-start.5 = (f32[4,4,72,128]{3,2,1,0:T(8,128)S(1)}, f32[4,4,72,128]{3,2,1,0:T(8,128)S(1)}, u32[]{:S(2)}, u32[]{:S(2)}) collective-permute-start(f32[4,4,72,128]{3,2,1,0:T(8,128)S(1)} %get-tuple-element.61), channel_id=1, source_target_pairs={{0,1},{1,0},{2,3},{3,2},{4,5},{5,4},{6,7},{7,6},{8,9},{9,8},{10,11... | collective-permute-start | bytes 1769480 | tf_op jit(solution)/shard_map/ppermute | solution.py:592
  28.6 4.1 %copy-start.1 = (f32[4,8]{1,0:T(4,128)S(1)}, f32[4,8]{1,0:T(4,128)}, u32[]{:S(2)}) copy-start(f32[4,8]{1,0:T(4,128)} %transfer.3) | copy-start | bytes 388

commit v10 on v8

--- a/solution.py
+++ b/solution.py
@@ -55,40 +55,48 @@
 
 
 def band():
-    shape = (512, 256)
-    d = jnp.abs(lax.broadcasted_iota(jnp.int32, shape, 0) % 256 - lax.broadcasted_iota(jnp.int32, shape, 1))
-    return jnp.where(d == 0, -90.0, jnp.where(d == 1, 16.0, jnp.where(d == 2, -1.0, 0.0))).astype(jnp.bfloat16)
-
-
-def full_rows(ref, k, first, count, bands):
-    rows = slice(first, first + count)
-    factors = []
-    for h in range(2):
-        v = jnp.concatenate([ref[k, 2 * h, rows, :], ref[k, 2 * h + 1, rows, :]], axis=1)
-        high = v.astype(jnp.bfloat16)
-        low = (v - high.astype(jnp.float32)).astype(jnp.bfloat16)
-        factors.append(jnp.concatenate([high, low], axis=1))
+    shape = (256, 256)
+    d = jnp.abs(lax.broadcasted_iota(jnp.int32, shape, 0) - lax.broadcasted_iota(jnp.int32, shape, 1))
+    half = jnp.where(d == 0, -90.0, jnp.where(d == 1, 16.0, jnp.where(d == 2, -1.0, 0.0))).astype(jnp.bfloat16)
+    return jnp.concatenate([half, half], axis=0)
+
+
+def full_rows(ref, layers, ranges, bands):
+    factors, places = [], []
+    for k in layers:
+        for first, count in ranges:
+            rows = slice(first, first + count)
+            places.append((k, first, count))
+            for h in range(2):
+                v = jnp.concatenate([ref[k, 2 * h, rows, :], ref[k, 2 * h + 1, rows, :]], axis=1)
+                high = v.astype(jnp.bfloat16)
+                low = (v - high.astype(jnp.float32)).astype(jnp.bfloat16)
+                factors.append(jnp.concatenate([high, low], axis=1))
     product = jnp.dot(jnp.concatenate(factors, axis=0), bands, preferred_element_type=jnp.float32)
     low1, low2, high1, high2 = lane_masks()
-    for r in range(0, count, 8):
-        row = first + r
-        here = slice(row, row + 8)
-        for i in range(T):
-            c = ref[k, i, here, :]
-            inside = product[count * (i // 2) + r : count * (i // 2) + r + 8, 128 * (i % 2) : 128 * (i % 2) + 128]
-            near = ref[k, i, row - 1 : row + 7, :] + ref[k, i, row + 1 : row + 9, :]
-            far = ref[k, i, row - 2 : row + 6, :] + ref[k, i, row + 2 : row + 10, :]
-            near = near + (ref[k - 1, i, here, :] + ref[k + 1, i, here, :])
-            far = far + (ref[k - 2, i, here, :] + ref[k + 2, i, here, :])
-            if i == 1:
-                v = ref[k, 2, here, :]
-                near = near + jnp.where(high1, pltpu.roll(v, 127, 1), 0.0)
-                far = far + jnp.where(high2, pltpu.roll(v, 126, 1), 0.0)
-            if i == 2:
-                v = ref[k, 1, here, :]
-                near = near + jnp.where(low1, pltpu.roll(v, 1, 1), 0.0)
-                far = far + jnp.where(low2, pltpu.roll(v, 2, 1), 0.0)
-            yield row, i, c, inside + (16.0 * near - far)
+    start = 0
+    for k, first, count in places:
+        for r in range(0, count, 8):
+            row = first + r
+            here = slice(row, row + 8)
+            for i in range(T):
+                c = ref[k, i, here, :]
+                at = start + count * (i // 2) + r
+                inside = product[at : at + 8, 128 * (i % 2) : 128 * (i % 2) + 128]
+                near = ref[k, i, row - 1 : row + 7, :] + ref[k, i, row + 1 : row + 9, :]
+                far = ref[k, i, row - 2 : row + 6, :] + ref[k, i, row + 2 : row + 10, :]
+                near = near + (ref[k - 1, i, here, :] + ref[k + 1, i, here, :])
+                far = far + (ref[k - 2, i, here, :] + ref[k + 2, i, here, :])
+                if i == 1:
+                    v = ref[k, 2, here, :]
+                    near = near + jnp.where(high1, pltpu.roll(v, 127, 1), 0.0)
+                    far = far + jnp.where(high2, pltpu.roll(v, 126, 1), 0.0)
+                if i == 2:
+                    v = ref[k, 1, here, :]
+                    near = near + jnp.where(low1, pltpu.roll(v, 1, 1), 0.0)
+                    far = far + jnp.where(low2, pltpu.roll(v, 2, 1), 0.0)
+                yield k, row, i, c, inside + (16.0 * near - far)
+        start += 2 * count
 
 
 def strike(ref, outer, place, amplitude, layers, rows):
@@ -109,7 +117,7 @@
 
 
 def ways():
-    return (lax.axis_index("dep") + 1) % 2, (lax.axis_index("lat") + 1) % 2
+    return lax.axis_index("dep") % 2, (lax.axis_index("lat") + 1) % 2
 
 
 def source_place(cell):
@@ -172,7 +180,8 @@
                 out[k, i, 8:16, :] = jnp.where(keep, prev[k, rows, lanes], moved)
 
 
-INNER = CORE + 8, X - 16
+INNER = ((CORE + 8, X - 16),)
+INSIDE = ((CORE, X),)
 OUTER = ((CORE - 8, 16), (CORE + X - 8, 16))
 
 
@@ -192,21 +201,22 @@
 
     lax.fori_loop(0, Z, fill, 0)
 
-    def first(k, carry):
-        for i in range(T):
-            lanes = slice(128 * i, 128 * i + 128)
-            prev_out[k, i, 0:8, :] = prev[k, 0:8, lanes]
-            prev_out[k, i, 8:16, :] = prev[k, X - 8 : X, lanes]
-            for t in range(X // 8):
-                rows = slice(8 * t, 8 * t + 8)
-                stiff_out[k, i, rows, :] = stiffness(table, mat[k, rows, lanes])
-        for row, i, c, lap in full_rows(now_out, k + 2, *INNER, bands[...]):
+    def first(n, carry):
+        for k in (2 * n, 2 * n + 1):
+            for i in range(T):
+                lanes = slice(128 * i, 128 * i + 128)
+                prev_out[k, i, 0:8, :] = prev[k, 0:8, lanes]
+                prev_out[k, i, 8:16, :] = prev[k, X - 8 : X, lanes]
+                for t in range(X // 8):
+                    rows = slice(8 * t, 8 * t + 8)
+                    stiff_out[k, i, rows, :] = stiffness(table, mat[k, rows, lanes])
+        for k, row, i, c, lap in full_rows(now_out, (2 * n + 2, 2 * n + 3), INNER, bands[...]):
             own = slice(row - CORE, row - CORE + 8)
-            before = prev[k, own, 128 * i : 128 * i + 128]
-            one_out[k + 2, i, row : row + 8, :] = 2.0 * c - before + stiff_out[k, i, own, :] * lap
-        return carry
-
-    lax.fori_loop(0, Z, first, 0, unroll=2)
+            before = prev[k - 2, own, 128 * i : 128 * i + 128]
+            one_out[k, i, row : row + 8, :] = 2.0 * c - before + stiff_out[k - 2, i, own, :] * lap
+        return carry
+
+    lax.fori_loop(0, Z // 2, first, 0)
 
 
 def advance_outer(
@@ -231,31 +241,30 @@
 
     lax.fori_loop(0, Z, fill, 0)
 
-    def first(k, carry):
-        for part in OUTER:
-            for row, i, c, lap in full_rows(now, k + 2, *part, bands[...]):
-                if row < CORE or row == CORE + X:
-                    half = slice(0, 8) if row < CORE else slice(8, 16)
-                    before, stiff = prev_side[k, i, half, :], stiff_side[k, i, half, :]
-                else:
-                    half = slice(0, 8) if row == CORE else slice(8, 16)
-                    before, stiff = prev_in[k, i, half, :], stiff_in[k, i, row - CORE : row - CORE + 8, :]
-                one[k + 2, i, row : row + 8, :] = 2.0 * c - before + stiff * lap
-        return carry
-
-    lax.fori_loop(0, Z, first, 0, unroll=2)
+    def first(n, carry):
+        for k, row, i, c, lap in full_rows(now, (2 * n + 2, 2 * n + 3), OUTER, bands[...]):
+            if row < CORE or row == CORE + X:
+                half = slice(0, 8) if row < CORE else slice(8, 16)
+                before, stiff = prev_side[k - 2, i, half, :], stiff_side[k - 2, i, half, :]
+            else:
+                half = slice(0, 8) if row == CORE else slice(8, 16)
+                before, stiff = prev_in[k - 2, i, half, :], stiff_in[k - 2, i, row - CORE : row - CORE + 8, :]
+            one[k, i, row : row + 8, :] = 2.0 * c - before + stiff * lap
+        return carry
+
+    lax.fori_loop(0, Z // 2, first, 0)
     place = source_place(cell)
     strike(one, 2, place, amplitudes[0:1, :], (0, Z), [(CORE - 8, CORE + X + 8)])
 
     def second(n, carry):
-        k = jnp.where(n < 2, n, n + 4)
-        for row, i, c, lap in full_rows(one, k + 2, CORE, X, bands[...]):
+        base = 6 * n
+        for k, row, i, c, lap in full_rows(one, (base + 2, base + 3), INSIDE, bands[...]):
             rows = slice(row, row + 8)
-            stiff = stiff_in[k, i, row - CORE : row - CORE + 8, :]
-            two_out[n, i, rows, :] = 2.0 * c - now[k + 2, i, rows, :] + stiff * lap
-        return carry
-
-    lax.fori_loop(0, 4, second, 0, unroll=2)
+            stiff = stiff_in[k - 2, i, row - CORE : row - CORE + 8, :]
+            two_out[k - 2 - 4 * n, i, rows, :] = 2.0 * c - now[k, i, rows, :] + stiff * lap
+        return carry
+
+    lax.fori_loop(0, 2, second, 0)
     z = place[0]
     inner = (z >= 2) & (z < Z - 2)
     place = (jnp.where(inner, -1, jnp.where(z < 2, z, z - 4)),) + place[1:]
@@ -303,15 +312,14 @@
             yield place, i, 2.0 * c + halo_stiff[base + place, i, own, :] * lap
 
 
-def outer_second(k, bands, now, stiff, stiff_side, one, two):
-    for part in OUTER:
-        for row, i, c, lap in full_rows(one, k + 2, *part, bands[...]):
-            if CORE <= row < CORE + X:
-                st = stiff[k, i, row - CORE : row - CORE + 8, :]
-            else:
-                st = stiff_side[k, i, 0:8, :] if row < CORE else stiff_side[k, i, 8:16, :]
-            rows = slice(row, row + 8)
-            two[k + 2, i, rows, :] = 2.0 * c - now[k + 2, i, rows, :] + st * lap
+def outer_second(first, bands, now, stiff, stiff_side, one, two):
+    for k, row, i, c, lap in full_rows(one, (first + 2, first + 3), OUTER, bands[...]):
+        if CORE <= row < CORE + X:
+            st = stiff[k - 2, i, row - CORE : row - CORE + 8, :]
+        else:
+            st = stiff_side[k - 2, i, 0:8, :] if row < CORE else stiff_side[k - 2, i, 8:16, :]
+        rows = slice(row, row + 8)
+        two[k, i, rows, :] = 2.0 * c - now[k, i, rows, :] + st * lap
 
 
 def couple(
@@ -341,19 +349,19 @@
 
         lax.fori_loop(0, X // 8, tile, 0)
 
-    def second(k, carry):
-        for row, i, c, lap in full_rows(one, k + 2, *INNER, bands[...]):
+    def second(n, carry):
+        for k, row, i, c, lap in full_rows(one, (2 * n + 2, 2 * n + 3), INNER, bands[...]):
             rows, own = slice(row, row + 8), slice(row - CORE, row - CORE + 8)
-            two[k + 2, i, rows, :] = 2.0 * c - now[k + 2, i, rows, :] + stiff[k, i, own, :] * lap
-        return carry
-
-    lax.fori_loop(0, Z, second, 0, unroll=2)
+            two[k, i, rows, :] = 2.0 * c - now[k, i, rows, :] + stiff[k - 2, i, own, :] * lap
+        return carry
+
+    lax.fori_loop(0, Z // 2, second, 0)
 
     def middle(n, carry):
-        outer_second(n + 2, bands, now, stiff, stiff_side, one, two)
-        return carry
-
-    lax.fori_loop(0, 4, middle, 0, unroll=2)
+        outer_second(2 * n + 2, bands, now, stiff, stiff_side, one, two)
+        return carry
+
+    lax.fori_loop(0, 2, middle, 0)
     place = source_place(cell)
     strike(two, 2, place, amplitudes[1:2, :], (0, Z), [(CORE + 8, CORE + X - 8)])
     strike(two, 2, place, amplitudes[1:2, :], (2, Z - 2), [(CORE - 8, CORE + 8), (CORE + X - 8, CORE + X + 8)])
@@ -415,23 +423,19 @@
 
     lowest = (Z - 2) * high
 
-    def second(n, carry):
-        outer_second(lowest + n, bands, now, stiff, stiff_side, one, two)
-        return carry
-
-    lax.fori_loop(0, 2, second, 0, unroll=2)
+    outer_second(lowest, bands, now, stiff, stiff_side, one, two)
     outer = [(CORE - 8, CORE + 8), (CORE + X - 8, CORE + X + 8)]
     strike(two, 2, place, amplitudes[1:2, :], (lowest, lowest + 2), outer)
 
     def third(n, carry):
-        k = 4 * high + n
-        for row, i, c, lap in full_rows(two, k + 2, CORE, X, bands[...]):
+        base = 4 * high + 2 * n
+        for k, row, i, c, lap in full_rows(two, (base + 2, base + 3), INSIDE, bands[...]):
             own = slice(row - CORE, row - CORE + 8)
-            before = one[k + 2, i, row : row + 8, :]
-            three[n, own, 128 * i : 128 * i + 128] = 2.0 * c - before + stiff[k, i, own, :] * lap
-        return carry
-
-    lax.fori_loop(0, 4, third, 0, unroll=2)
+            before = one[k, i, row : row + 8, :]
+            three[k - 2 - 4 * high, own, 128 * i : 128 * i + 128] = 2.0 * c - before + stiff[k - 2, i, own, :] * lap
+        return carry
+
+    lax.fori_loop(0, 2, third, 0)
     z, x, y = place
     n = z - 4 * high
 
@@ -550,14 +554,16 @@
     q = lax.axis_index("dep") % 4
     group = lax.broadcasted_iota(jnp.int32, (X, 128), 1) // 32
     last = group == (q + 3) % 4
+    others = [group == (q + n) % 4 for n in range(3)]
     before = jnp.zeros((X, 128), jnp.float32)
     total = jnp.zeros((X, 128), jnp.float32)
     for d in range(parts.shape[0]):
         v = parts[d]
         total = total + jnp.exp(-before) * v
-        depth = jnp.where(last, v, 0.0)
-        depth = depth + pltpu.roll(depth, 32, 1)
-        before = before + (depth + pltpu.roll(depth, 64, 1))
+        depth = v
+        for n in range(3):
+            depth = jnp.where(others[n], pltpu.roll(v, 32 * (n + 1), 1), depth)
+        before = before + depth
     view = jnp.where(last, 1.0 - jnp.exp(-before), total).T
     for g in range(4):
         image[pl.ds(pl.multiple_of(32 * ((g + 4 - q) % 4), 32), 32), :] = view[32 * g : 32 * g + 32, :]
@@ -569,7 +575,7 @@
         for dep in range(n_dep):
             other_lat, other_dep = lat, dep
             if kind in ("d1", "d2"):
-                up = (dep % 2 == 0) == (kind == "d1")
+                up = (dep % 2 == 1) == (kind == "d1")
                 other_dep = dep + 1 if up else dep - 1
             else:
                 right = (lat % 2 == 0) == (kind == "l1")

time: 64.9 us -> 64.6 us (level)
  the two profiles are of different devices: /device:TPU:1 before, /device:TPU:256 now
where the time goes in v10:
time: 64.6 us; the launch traced here: 64.3 us
  blocking collectives  20.4 us (32%)
  Pallas kernels  18 us (28%)
  starting transfers between devices  17.4 us (27%)
  waiting for transfers between devices  7.04 us (11%)
  between operations  1.45 us (2%)
    all_to_all x1, blocking collectives, on_device(): parts = lax.all_to_all(partial, 'dep', 0, 0, tiled=True)  20.4 us
    ppermute x6, starting transfers between devices, swap(): return lax.ppermute(v, ('lat', 'dep'), swaps(n_lat, n_dep, kind))  17.4 us
    ppermute x6, waiting for transfers between devices, swap(): return lax.ppermute(v, ('lat', 'dep'), swaps(n_lat, n_dep, kind))  7.04 us
    pallas_call x1, Pallas kernels, on_device(): pl.pallas_call(couple, in_specs=[SMEM] + [VMEM] * 9 + [pl.BlockSpec(memor...  3.84 us
    pallas_call x1, Pallas kernels, on_device(): pl.pallas_call(functools.partial(finish_second, n_dep), in_specs=[SMEM, V...  3.64 us
    pallas_call x1, Pallas kernels, on_device(): pl.pallas_call(functools.partial(finish_first, n_dep), in_specs=[SMEM, VM...  2.81 us
    pallas_call x1, Pallas kernels, on_device(): pl.pallas_call(pack, in_specs=[HBM] * 4, out_specs=[VMEM] * 7, out_shape=...  2.19 us
    pallas_call x1, Pallas kernels, on_device(): pl.pallas_call(advance_inner, in_specs=[SMEM] * 2 + [VMEM] * 3, out_specs...  2.14 us
  transfers between devices with their start and end apart: 6, of which 2 were waited for; matrix products, arithmetic and copies ran while one was open for 0% of the time, Pallas kernels for 17%

profile of v10, /device:TPU:256, one launch (start us, length us, event | category | flops | bytes accessed | tf_op | source)
XLA Modules:
  0.0 64.3 jit_solution(14889921754129378275)
XLA Ops:
  0.6 0.0 copy-start
  0.6 2.2 %pack.1 = (f32[4,4,64,128]{3,2,1,0:T(8,128)S(1)}, f32[4,4,64,128]{3,2,1,0:T(8,128)S(1)}, f32[8,4,16,128]{3,2,1,0:T(8,128)S(1)}, f32[8,4,16,128]{3,2,1,0:T(8,128)...) custom-call(f32[16]{0:T(128)} %courant.1, f32[8,64,512]{2,1,0:T(8,128)} %now_in.1, ...), custom_call_target="tpu_custom_call" | custom-call | tf_op jit(solution)/shard_map/pack/pallas_call | solution.py:611
  2.8 1.9 %collective-permute-start = (f32[8,4,16,128]{3,2,1,0:T(8,128)S(1)}, f32[8,4,16,128]{3,2,1,0:T(8,128)S(1)}, u32[]{:S(2)}, u32[]{:S(2)}) collective-permute-start(f32[8,4,16,128]{3,2,1,0:T(8,128)S(1)} %get-tuple-element.43), channel_id=1, source_target_pairs={{0,16},{1,17},{2,18},{3,19},{4,20},{5,21},{6,22},{7,23},{8,24},{9,... | collective-permute-start | bytes 786440 | tf_op jit(solution)/shard_map/ppermute | solution.py:592
  4.8 2.1 %collective-permute-start.1 = (f32[8,4,16,128]{3,2,1,0:T(8,128)S(1)}, f32[8,4,16,128]{3,2,1,0:T(8,128)S(1)}, u32[]{:S(2)}, u32[]{:S(2)}) collective-permute-start(f32[8,4,16,128]{3,2,1,0:T(8,128)S(1)} %get-tuple-element.44), channel_id=1, source_target_pairs={{16,32},{17,33},{18,34},{19,35},{20,36},{21,37},{22,38},{23,39},{2... | collective-permute-start | bytes 786440 | tf_op jit(solution)/shard_map/ppermute | solution.py:592
  6.9 0.7 %collective-permute-start.2 = (f32[4,4,64,128]{3,2,1,0:T(8,128)S(1)}, f32[4,4,64,128]{3,2,1,0:T(8,128)S(1)}, u32[]{:S(2)}, u32[]{:S(2)}) collective-permute-start(f32[4,4,64,128]{3,2,1,0:T(8,128)S(1)} %get-tuple-element.49), channel_id=1, source_target_pairs={{1,2},{2,1},{3,4},{4,3},{5,6},{6,5},{7,8},{8,7},{9,10},{10,9},{11,... | collective-permute-start | bytes 1572872 | tf_op jit(solution)/shard_map/ppermute | solution.py:592
  7.6 6.1 %collective-permute-start.3 = (f32[4,4,64,128]{3,2,1,0:T(8,128)S(1)}, f32[4,4,64,128]{3,2,1,0:T(8,128)S(1)}, u32[]{:S(2)}, u32[]{:S(2)}) collective-permute-start(f32[4,4,64,128]{3,2,1,0:T(8,128)S(1)} %get-tuple-element.50), channel_id=1, source_target_pairs={{0,1},{1,0},{2,3},{3,2},{4,5},{5,4},{6,7},{7,6},{8,9},{9,8},{10,11... | collective-permute-start | bytes 1572872 | tf_op jit(solution)/shard_map/ppermute | solution.py:592
  14.4 0.0 copy-done
  14.4 0.0 copy-start.2
  14.4 2.1 %advance_inner.1 = (f32[12,4,96,128]{3,2,1,0:T(8,128)S(1)}, f32[8,4,64,128]{3,2,1,0:T(8,128)S(1)}, f32[12,4,96,128]{3,2,1,0:T(8,128)S(1)}, f32[8,4,16,128]{3,2,1...) custom-call(f32[16]{0:T(128)S(1)} %copy-done, s32[1]{0:T(128)S(6)} %copy.27.start, ...), custom_call_target="tpu_custom_call" | custom-call | flops 3000000000 | bytes 9000000 | tf_op jit(solution)/shard_map/advance_inner/pallas_call | solution.py:628
  16.5 0.0 collective-permute-done.lat_a
  16.5 0.0 collective-permute-done.1.lat_b
  16.5 0.0 copy-done.2
  16.6 2.1 %advance_outer.1 = (f32[12,4,96,128]{3,2,1,0:T(8,128)S(1)}, f32[12,4,96,128]{3,2,1,0:T(8,128)S(1)}, f32[8,4,16,128]{3,2,1,0:T(8,128)S(1)}, f32[8,4,16,128]{3,2,1,0:T(8,128)S(1)}, f32[4,4,96,128]{3,2,1,0:T(8,128)S(1)}) custom-call(s32[3]{0:T(128)S(1)} %copy-done.2, ...), custom_call_target="tpu_custom_call", output_to_operand_aliasing={{0}: (3, {}), {1}: (5, {})} | custom-call | flops 5000000000 | bytes 15000000 | tf_op jit(solution)/shard_map/advance_outer/pallas_call | solution.py:637
  18.7 0.1 pack_late.1
  18.8 0.7 %collective-permute-start.4 = (f32[4,4,72,128]{3,2,1,0:T(8,128)S(1)}, f32[4,4,72,128]{3,2,1,0:T(8,128)S(1)}, u32[]{:S(2)}, u32[]{:S(2)}) collective-permute-start(f32[4,4,72,128]{3,2,1,0:T(8,128)S(1)} %get-tuple-element.52.sent), channel_id=1, source_target_pairs={{1,2},{2,1},{3,4},{4,3},{5,6},{6,5},{7,8},{8,7},{9,10},{10,9},{11,... | collective-permute-start | bytes 1769480 | tf_op jit(solution)/shard_map/ppermute | solution.py:592
  19.5 5.8 %collective-permute-start.5 = (f32[4,4,72,128]{3,2,1,0:T(8,128)S(1)}, f32[4,4,72,128]{3,2,1,0:T(8,128)S(1)}, u32[]{:S(2)}, u32[]{:S(2)}) collective-permute-start(f32[4,4,72,128]{3,2,1,0:T(8,128)S(1)} %get-tuple-element.61), channel_id=1, source_target_pairs={{0,1},{1,0},{2,3},{3,2},{4,5},{5,4},{6,7},{7,6},{8,9},{9,8},{10,11... | collective-permute-start | bytes 1769480 | tf_op jit(solution)/shard_map/ppermute | solution.py:592
  25.3 0.0 collective-permute-done.2.early_a
  25.3 1.1 %collective-permute-done.3.early_b = f32[4,4,64,128]{3,2,1,0:T(8,128)S(1)} collective-permute-done((f32[4,4,64,128]{3,2,1,0:T(8,128)S(1)}, f32[4,4,64,128]{3,2,1,0:T(8,128)S(1)}, u32[]{:S(2)}, u32[]{:S(2)}) %collective-permute-start.3) | collective-permute-done | bytes 524320 | tf_op jit(solution)/shard_map/ppermute | solution.py:592
  26.5 0.0 copy-start.1
  26.5 3.8 %couple.1 = (f32[12,4,96,128]{3,2,1,0:T(8,128)S(1)}, f32[12,4,96,128]{3,2,1,0:T(8,128)S(1)}, f32[4,4,96,128]{3,2,1,0:T(8,128)S(1)}, f32[4,4,64,128]{3,2,1,0:T(8,128)S(1)}, f32[4,4,64,128]{3,2,1,0:T(8,128)S(1)}) custom-call(s32[3]{0:T(128)S(1)} %copy-done.2, f32[8,128]{1,0:T(8,128)S(1)} %get-tuple-element.37.amplitudes, ...), custom_call_target="tpu_custom_call", output_to_operand_aliasing={{0}: (7, {})} | custom-call | flops 4000000000 | bytes 12000000 | tf_op jit(solution)/shard_map/couple/pallas_call | solution.py:658
  30.3 0.0 collective-permute-done.4.late
  30.3 0.0 copy-done.1
  30.3 2.8 %finish_first.1 = (f32[4,64,512]{2,1,0:T(8,128)S(1)}, f32[10,4,64,128]{3,2,1,0:T(8,128)S(1)}, f32[12,4,96,128]{3,2,1,0:T(8,128)S(1)}, f32[12,4,96,128]{3,2,1,0:T(8,128)S(1)}, f32[4,4,96,128]{3,2,1,0:T(8,128)S(1)}) custom-call(s32[3]{0:T(128)S(1)} %copy-done.2, ...), custom_call_target="tpu_custom_call", output_to_operand_aliasing={{2}: (8, {}), {3}: (9, {}), {4}: (10, {})} | custom-call | flops 4000000000 | bytes 12000000 | tf_op jit(solution)/shard_map/finish_first/pallas_call | solution.py:670
  33.2 5.9 %collective-permute-done.5.late = f32[4,4,72,128]{3,2,1,0:T(8,128)S(1)} collective-permute-done((f32[4,4,72,128]{3,2,1,0:T(8,128)S(1)}, f32[4,4,72,128]{3,2,1,0:T(8,128)S(1)}, u32[]{:S(2)}, u32[]{:S(2)}) %collective-permute-start.5) | collective-permute-done | bytes 589856 | tf_op jit(solution)/shard_map/ppermute | solution.py:592
  39.1 3.6 %finish_second.1 = (f32[8,64,512]{2,1,0:T(8,128)}, f32[16,64,128]{2,1,0:T(8,128)S(1)}, f32[12,4,96,128]{3,2,1,0:T(8,128)S(1)}, f32[12,4,96,128]{3,2,1,0:T(8,128)S(1)}, f32[4,4,96,128]{3,2,1,0:T(8,128)S(1)}) custom-call(s32[3]{0:T(128)S(1)} %copy-done.2, ...), custom_call_target="tpu_custom_call", output_to_operand_aliasing={{2}: (8, {}), {3}: (9, {}), {4}: (10, {})} | custom-call | flops 4000000000 | bytes 12000000 | tf_op jit(solution)/shard_map/finish_second/pallas_call | solution.py:681
  42.7 20.4 %all_to_all.5.parts = f32[16,64,128]{2,1,0:T(8,128)S(1)} all-to-all(f32[16,64,128]{2,1,0:T(8,128)S(1)} %get-tuple-element.65), channel_id=1, replica_groups=mesh['lat'=32,'dep'=16] {'dep'}, dimensions={0} | all-to-all | bytes 1048576 | tf_op jit(solution)/shard_map/all_to_all | solution.py:692
  63.1 1.2 %composite.1 = f32[128,64]{1,0:T(8,128)} custom-call(f32[16,64,128]{2,1,0:T(8,128)S(1)} %all_to_all.5.parts), custom_call_target="tpu_custom_call" | custom-call | tf_op jit(solution)/shard_map/composite/pallas_call | solution.py:693
Async XLA Ops:
  0.6 13.7 %copy-start = (f32[16]{0:T(128)S(1)}, f32[16]{0:T(128)}, u32[]{:S(2)}) copy-start(f32[16]{0:T(128)} %courant.1) | copy-start | bytes 196
  2.8 13.7 %collective-permute-start = (f32[8,4,16,128]{3,2,1,0:T(8,128)S(1)}, f32[8,4,16,128]{3,2,1,0:T(8,128)S(1)}, u32[]{:S(2)}, u32[]{:S(2)}) collective-permute-start(f32[8,4,16,128]{3,2,1,0:T(8,128)S(1)} %get-tuple-element.43), channel_id=1, source_target_pairs={{0,16},{1,17},{2,18},{3,19},{4,20},{5,21},{6,22},{7,23},{8,24},{9,... | collective-permute-start | bytes 786440 | tf_op jit(solution)/shard_map/ppermute | solution.py:592
  4.8 11.8 %collective-permute-start.1 = (f32[8,4,16,128]{3,2,1,0:T(8,128)S(1)}, f32[8,4,16,128]{3,2,1,0:T(8,128)S(1)}, u32[]{:S(2)}, u32[]{:S(2)}) collective-permute-start(f32[8,4,16,128]{3,2,1,0:T(8,128)S(1)} %get-tuple-element.44), channel_id=1, source_target_pairs={{16,32},{17,33},{18,34},{19,35},{20,36},{21,37},{22,38},{23,39},{2... | collective-permute-start | bytes 786440 | tf_op jit(solution)/shard_map/ppermute | solution.py:592
  6.9 18.4 %collective-permute-start.2 = (f32[4,4,64,128]{3,2,1,0:T(8,128)S(1)}, f32[4,4,64,128]{3,2,1,0:T(8,128)S(1)}, u32[]{:S(2)}, u32[]{:S(2)}) collective-permute-start(f32[4,4,64,128]{3,2,1,0:T(8,128)S(1)} %get-tuple-element.49), channel_id=1, source_target_pairs={{1,2},{2,1},{3,4},{4,3},{5,6},{6,5},{7,8},{8,7},{9,10},{10,9},{11,... | collective-permute-start | bytes 1572872 | tf_op jit(solution)/shard_map/ppermute | solution.py:592
  7.6 18.9 %collective-permute-start.3 = (f32[4,4,64,128]{3,2,1,0:T(8,128)S(1)}, f32[4,4,64,128]{3,2,1,0:T(8,128)S(1)}, u32[]{:S(2)}, u32[]{:S(2)}) collective-permute-start(f32[4,4,64,128]{3,2,1,0:T(8,128)S(1)} %get-tuple-element.50), channel_id=1, source_target_pairs={{0,1},{1,0},{2,3},{3,2},{4,5},{5,4},{6,7},{7,6},{8,9},{9,8},{10,11... | collective-permute-start | bytes 1572872 | tf_op jit(solution)/shard_map/ppermute | solution.py:592
  14.4 2.2 %copy-start.2 = (s32[3]{0:T(128)S(1)}, s32[3]{0:T(128)}, u32[]{:S(2)}) copy-start(s32[3]{0:T(128)} %cell.7) | copy-start | bytes 40
  18.8 11.5 %collective-permute-start.4 = (f32[4,4,72,128]{3,2,1,0:T(8,128)S(1)}, f32[4,4,72,128]{3,2,1,0:T(8,128)S(1)}, u32[]{:S(2)}, u32[]{:S(2)}) collective-permute-start(f32[4,4,72,128]{3,2,1,0:T(8,128)S(1)} %get-tuple-element.52.sent), channel_id=1, source_target_pairs={{1,2},{2,1},{3,4},{4,3},{5,6},{6,5},{7,8},{8,7},{9,10},{10,9},{11,... | collective-permute-start | bytes 1769480 | tf_op jit(solution)/shard_map/ppermute | solution.py:592
  19.5 19.6 %collective-permute-start.5 = (f32[4,4,72,128]{3,2,1,0:T(8,128)S(1)}, f32[4,4,72,128]{3,2,1,0:T(8,128)S(1)}, u32[]{:S(2)}, u32[]{:S(2)}) collective-permute-start(f32[4,4,72,128]{3,2,1,0:T(8,128)S(1)} %get-tuple-element.61), channel_id=1, source_target_pairs={{0,1},{1,0},{2,3},{3,2},{4,5},{5,4},{6,7},{7,6},{8,9},{9,8},{10,11... | collective-permute-start | bytes 1769480 | tf_op jit(solution)/shard_map/ppermute | solution.py:592
  26.5 3.9 %copy-start.1 = (f32[4,8]{1,0:T(4,128)S(1)}, f32[4,8]{1,0:T(4,128)}, u32[]{:S(2)}) copy-start(f32[4,8]{1,0:T(4,128)} %transfer.3) | copy-start | bytes 388

commit v11 on v10

--- a/solution.py
+++ b/solution.py
@@ -293,6 +293,17 @@
     return jnp.minimum(jnp.maximum(p, -7.4), 7.4)
 
 
+ORDERS = (
+    (4, 9, 7, 10, 1, 5, 15, 13, 12, 3, 2, 14, 11, 8, 0, 6),
+    (14, 8, 0, 9, 2, 1, 15, 3, 12, 13, 6, 4, 5, 11, 7, 10),
+)
+
+
+def rank(dep):
+    even, odd = (order.index(dep) for order in ORDERS)
+    return even + (odd - even) * (lax.axis_index("lat") % 2)
+
+
 SIDES = ((False, 0, 1, 0, 0, 1, 0), (True, 2, 0, 1, Z - 1, Z - 2, Z + 2))
 
 
@@ -542,7 +553,7 @@
                 packed = turned[0]
                 for n in range(1, 4):
                     packed = jnp.where(group == (n + q) % 4, turned[n], packed)
-                partial[4 * i + q, own, :] = packed
+                partial[rank(4 * i + q), own, :] = packed
         return carry
 
     lax.fori_loop(0, X // 8, render, 0)
@@ -558,7 +569,7 @@
     before = jnp.zeros((X, 128), jnp.float32)
     total = jnp.zeros((X, 128), jnp.float32)
     for d in range(parts.shape[0]):
-        v = parts[d]
+        v = parts[rank(d)]
         total = total + jnp.exp(-before) * v
         depth = v
         for n in range(3):
@@ -689,7 +700,8 @@
         cost_estimate=busy(4.0),
         name="finish_second",
     )(*scalars, *held, one, two, delta, halo_stiff, halo_two, late_b, three, looked)
-    parts = lax.all_to_all(partial, "dep", 0, 0, tiled=True)
+    groups = [[lat * n_dep + dep for dep in ORDERS[lat % 2]] for lat in range(n_lat)]
+    parts = lax.all_to_all(partial, ("lat", "dep"), 0, 0, axis_index_groups=groups, tiled=True)
     image = pl.pallas_call(
         composite,
         in_specs=[VMEM],

time: 64.6 us -> 62.5 us (0.967)
  blocking collectives: 20.4 us -> 18.2 us
    all_to_all x1, blocking collectives: 20.4 us -> 18.2 us  [on_device(): lax.all_to_all(partial, ('lat', 'dep'), 0, 0, axis_index_groups=groups, t...]
  transfers between devices with their start and end apart: 6 -> 6, of which waited for: 2 -> 2; matrix products, arithmetic and copies ran while one was open for 0% -> 0% of each run, Pallas kernels for 17% -> 18%
where the time goes in v11:
time: 62.5 us; the launch traced here: 62.2 us
  blocking collectives  18.2 us (29%)
  Pallas kernels  18.1 us (29%)
  starting transfers between devices  17.4 us (28%)
  waiting for transfers between devices  7.04 us (11%)
  between operations  1.45 us (2%)
    all_to_all x1, blocking collectives, on_device(): lax.all_to_all(partial, ('lat', 'dep'), 0, 0, axis_index_groups=groups, t...  18.2 us
    ppermute x6, starting transfers between devices, swap(): return lax.ppermute(v, ('lat', 'dep'), swaps(n_lat, n_dep, kind))  17.4 us
    ppermute x6, waiting for transfers between devices, swap(): return lax.ppermute(v, ('lat', 'dep'), swaps(n_lat, n_dep, kind))  7.04 us
    pallas_call x1, Pallas kernels, on_device(): pl.pallas_call(couple, in_specs=[SMEM] + [VMEM] * 9 + [pl.BlockSpec(memor...  3.84 us
    pallas_call x1, Pallas kernels, on_device(): pl.pallas_call(functools.partial(finish_second, n_dep), in_specs=[SMEM, V...  3.69 us
    pallas_call x1, Pallas kernels, on_device(): pl.pallas_call(functools.partial(finish_first, n_dep), in_specs=[SMEM, VM...  2.81 us
    pallas_call x1, Pallas kernels, on_device(): pl.pallas_call(pack, in_specs=[HBM] * 4, out_specs=[VMEM] * 7, out_shape=...  2.19 us
    pallas_call x1, Pallas kernels, on_device(): pl.pallas_call(advance_inner, in_specs=[SMEM] * 2 + [VMEM] * 3, out_specs...  2.14 us
  transfers between devices with their start and end apart: 6, of which 2 were waited for; matrix products, arithmetic and copies ran while one was open for 0% of the time, Pallas kernels for 18%

profile of v11, /device:TPU:256, one launch (start us, length us, event | category | flops | bytes accessed | tf_op | source)
XLA Modules:
  0.0 62.2 jit_solution(4326649709991342819)
XLA Ops:
  0.6 0.0 copy-start
  0.6 2.2 %pack.1 = (f32[4,4,64,128]{3,2,1,0:T(8,128)S(1)}, f32[4,4,64,128]{3,2,1,0:T(8,128)S(1)}, f32[8,4,16,128]{3,2,1,0:T(8,128)S(1)}, f32[8,4,16,128]{3,2,1,0:T(8,128)...) custom-call(f32[16]{0:T(128)} %courant.1, f32[8,64,512]{2,1,0:T(8,128)} %now_in.1, ...), custom_call_target="tpu_custom_call" | custom-call | tf_op jit(solution)/shard_map/pack/pallas_call | solution.py:622
  2.8 1.9 %collective-permute-start = (f32[8,4,16,128]{3,2,1,0:T(8,128)S(1)}, f32[8,4,16,128]{3,2,1,0:T(8,128)S(1)}, u32[]{:S(2)}, u32[]{:S(2)}) collective-permute-start(f32[8,4,16,128]{3,2,1,0:T(8,128)S(1)} %get-tuple-element.43), channel_id=1, source_target_pairs={{0,16},{1,17},{2,18},{3,19},{4,20},{5,21},{6,22},{7,23},{8,24},{9,... | collective-permute-start | bytes 786440 | tf_op jit(solution)/shard_map/ppermute | solution.py:603
  4.8 2.1 %collective-permute-start.1 = (f32[8,4,16,128]{3,2,1,0:T(8,128)S(1)}, f32[8,4,16,128]{3,2,1,0:T(8,128)S(1)}, u32[]{:S(2)}, u32[]{:S(2)}) collective-permute-start(f32[8,4,16,128]{3,2,1,0:T(8,128)S(1)} %get-tuple-element.44), channel_id=1, source_target_pairs={{16,32},{17,33},{18,34},{19,35},{20,36},{21,37},{22,38},{23,39},{2... | collective-permute-start | bytes 786440 | tf_op jit(solution)/shard_map/ppermute | solution.py:603
  6.9 0.7 %collective-permute-start.2 = (f32[4,4,64,128]{3,2,1,0:T(8,128)S(1)}, f32[4,4,64,128]{3,2,1,0:T(8,128)S(1)}, u32[]{:S(2)}, u32[]{:S(2)}) collective-permute-start(f32[4,4,64,128]{3,2,1,0:T(8,128)S(1)} %get-tuple-element.49), channel_id=1, source_target_pairs={{1,2},{2,1},{3,4},{4,3},{5,6},{6,5},{7,8},{8,7},{9,10},{10,9},{11,... | collective-permute-start | bytes 1572872 | tf_op jit(solution)/shard_map/ppermute | solution.py:603
  7.6 6.1 %collective-permute-start.3 = (f32[4,4,64,128]{3,2,1,0:T(8,128)S(1)}, f32[4,4,64,128]{3,2,1,0:T(8,128)S(1)}, u32[]{:S(2)}, u32[]{:S(2)}) collective-permute-start(f32[4,4,64,128]{3,2,1,0:T(8,128)S(1)} %get-tuple-element.50), channel_id=1, source_target_pairs={{0,1},{1,0},{2,3},{3,2},{4,5},{5,4},{6,7},{7,6},{8,9},{9,8},{10,11... | collective-permute-start | bytes 1572872 | tf_op jit(solution)/shard_map/ppermute | solution.py:603
  14.4 0.0 copy-done
  14.4 0.0 copy-start.2
  14.4 2.1 %advance_inner.1 = (f32[12,4,96,128]{3,2,1,0:T(8,128)S(1)}, f32[8,4,64,128]{3,2,1,0:T(8,128)S(1)}, f32[12,4,96,128]{3,2,1,0:T(8,128)S(1)}, f32[8,4,16,128]{3,2,1...) custom-call(f32[16]{0:T(128)S(1)} %copy-done, s32[1]{0:T(128)S(6)} %copy.27.start, ...), custom_call_target="tpu_custom_call" | custom-call | flops 3000000000 | bytes 9000000 | tf_op jit(solution)/shard_map/advance_inner/pallas_call | solution.py:639
  16.5 0.0 collective-permute-done.lat_a
  16.5 0.0 collective-permute-done.1.lat_b
  16.5 0.0 copy-done.2
  16.6 2.1 %advance_outer.1 = (f32[12,4,96,128]{3,2,1,0:T(8,128)S(1)}, f32[12,4,96,128]{3,2,1,0:T(8,128)S(1)}, f32[8,4,16,128]{3,2,1,0:T(8,128)S(1)}, f32[8,4,16,128]{3,2,1,0:T(8,128)S(1)}, f32[4,4,96,128]{3,2,1,0:T(8,128)S(1)}) custom-call(s32[3]{0:T(128)S(1)} %copy-done.2, ...), custom_call_target="tpu_custom_call", output_to_operand_aliasing={{0}: (3, {}), {1}: (5, {})} | custom-call | flops 5000000000 | bytes 15000000 | tf_op jit(solution)/shard_map/advance_outer/pallas_call | solution.py:648
  18.7 0.1 pack_late.1
  18.8 0.7 %collective-permute-start.4 = (f32[4,4,72,128]{3,2,1,0:T(8,128)S(1)}, f32[4,4,72,128]{3,2,1,0:T(8,128)S(1)}, u32[]{:S(2)}, u32[]{:S(2)}) collective-permute-start(f32[4,4,72,128]{3,2,1,0:T(8,128)S(1)} %get-tuple-element.52.sent), channel_id=1, source_target_pairs={{1,2},{2,1},{3,4},{4,3},{5,6},{6,5},{7,8},{8,7},{9,10},{10,9},{11,... | collective-permute-start | bytes 1769480 | tf_op jit(solution)/shard_map/ppermute | solution.py:603
  19.5 5.8 %collective-permute-start.5 = (f32[4,4,72,128]{3,2,1,0:T(8,128)S(1)}, f32[4,4,72,128]{3,2,1,0:T(8,128)S(1)}, u32[]{:S(2)}, u32[]{:S(2)}) collective-permute-start(f32[4,4,72,128]{3,2,1,0:T(8,128)S(1)} %get-tuple-element.61), channel_id=1, source_target_pairs={{0,1},{1,0},{2,3},{3,2},{4,5},{5,4},{6,7},{7,6},{8,9},{9,8},{10,11... | collective-permute-start | bytes 1769480 | tf_op jit(solution)/shard_map/ppermute | solution.py:603
  25.3 0.0 collective-permute-done.2.early_a
  25.3 1.1 %collective-permute-done.3.early_b = f32[4,4,64,128]{3,2,1,0:T(8,128)S(1)} collective-permute-done((f32[4,4,64,128]{3,2,1,0:T(8,128)S(1)}, f32[4,4,64,128]{3,2,1,0:T(8,128)S(1)}, u32[]{:S(2)}, u32[]{:S(2)}) %collective-permute-start.3) | collective-permute-done | bytes 524320 | tf_op jit(solution)/shard_map/ppermute | solution.py:603
  26.5 0.0 copy-start.1
  26.5 3.8 %couple.1 = (f32[12,4,96,128]{3,2,1,0:T(8,128)S(1)}, f32[12,4,96,128]{3,2,1,0:T(8,128)S(1)}, f32[4,4,96,128]{3,2,1,0:T(8,128)S(1)}, f32[4,4,64,128]{3,2,1,0:T(8,128)S(1)}, f32[4,4,64,128]{3,2,1,0:T(8,128)S(1)}) custom-call(s32[3]{0:T(128)S(1)} %copy-done.2, f32[8,128]{1,0:T(8,128)S(1)} %get-tuple-element.37.amplitudes, ...), custom_call_target="tpu_custom_call", output_to_operand_aliasing={{0}: (7, {})} | custom-call | flops 4000000000 | bytes 12000000 | tf_op jit(solution)/shard_map/couple/pallas_call | solution.py:669
  30.3 0.0 collective-permute-done.4.late
  30.3 0.0 copy-done.1
  30.3 2.8 %finish_first.1 = (f32[4,64,512]{2,1,0:T(8,128)S(1)}, f32[10,4,64,128]{3,2,1,0:T(8,128)S(1)}, f32[12,4,96,128]{3,2,1,0:T(8,128)S(1)}, f32[12,4,96,128]{3,2,1,0:T(8,128)S(1)}, f32[4,4,96,128]{3,2,1,0:T(8,128)S(1)}) custom-call(s32[3]{0:T(128)S(1)} %copy-done.2, ...), custom_call_target="tpu_custom_call", output_to_operand_aliasing={{2}: (8, {}), {3}: (9, {}), {4}: (10, {})} | custom-call | flops 4000000000 | bytes 12000000 | tf_op jit(solution)/shard_map/finish_first/pallas_call | solution.py:681
  33.2 5.9 %collective-permute-done.5.late = f32[4,4,72,128]{3,2,1,0:T(8,128)S(1)} collective-permute-done((f32[4,4,72,128]{3,2,1,0:T(8,128)S(1)}, f32[4,4,72,128]{3,2,1,0:T(8,128)S(1)}, u32[]{:S(2)}, u32[]{:S(2)}) %collective-permute-start.5) | collective-permute-done | bytes 589856 | tf_op jit(solution)/shard_map/ppermute | solution.py:603
  39.1 3.7 %finish_second.1 = (f32[8,64,512]{2,1,0:T(8,128)}, f32[16,64,128]{2,1,0:T(8,128)S(1)}, f32[12,4,96,128]{3,2,1,0:T(8,128)S(1)}, f32[12,4,96,128]{3,2,1,0:T(8,128)S(1)}, f32[4,4,96,128]{3,2,1,0:T(8,128)S(1)}) custom-call(s32[3]{0:T(128)S(1)} %copy-done.2, ...), custom_call_target="tpu_custom_call", output_to_operand_aliasing={{2}: (8, {}), {3}: (9, {}), {4}: (10, {})} | custom-call | flops 4000000000 | bytes 12000000 | tf_op jit(solution)/shard_map/finish_second/pallas_call | solution.py:692
  42.8 18.2 %all_to_all.5.parts = f32[16,64,128]{2,1,0:T(8,128)S(1)} all-to-all(f32[16,64,128]{2,1,0:T(8,128)S(1)} %get-tuple-element.65), channel_id=1, replica_groups={{4,9,7,10,1,5,15,13,12,3,2,14,11,8,0,6},{30,24,16,25,18,17,31,19,28,29,..., dimensions={0} | all-to-all | bytes 1048576 | tf_op jit(solution)/shard_map/all_to_all | solution.py:704
  61.0 1.2 %composite.1 = f32[128,64]{1,0:T(8,128)} custom-call(f32[16,64,128]{2,1,0:T(8,128)S(1)} %all_to_all.5.parts), custom_call_target="tpu_custom_call" | custom-call | tf_op jit(solution)/shard_map/composite/pallas_call | solution.py:705
Async XLA Ops:
  0.6 13.7 %copy-start = (f32[16]{0:T(128)S(1)}, f32[16]{0:T(128)}, u32[]{:S(2)}) copy-start(f32[16]{0:T(128)} %courant.1) | copy-start | bytes 196
  2.8 13.7 %collective-permute-start = (f32[8,4,16,128]{3,2,1,0:T(8,128)S(1)}, f32[8,4,16,128]{3,2,1,0:T(8,128)S(1)}, u32[]{:S(2)}, u32[]{:S(2)}) collective-permute-start(f32[8,4,16,128]{3,2,1,0:T(8,128)S(1)} %get-tuple-element.43), channel_id=1, source_target_pairs={{0,16},{1,17},{2,18},{3,19},{4,20},{5,21},{6,22},{7,23},{8,24},{9,... | collective-permute-start | bytes 786440 | tf_op jit(solution)/shard_map/ppermute | solution.py:603
  4.8 11.8 %collective-permute-start.1 = (f32[8,4,16,128]{3,2,1,0:T(8,128)S(1)}, f32[8,4,16,128]{3,2,1,0:T(8,128)S(1)}, u32[]{:S(2)}, u32[]{:S(2)}) collective-permute-start(f32[8,4,16,128]{3,2,1,0:T(8,128)S(1)} %get-tuple-element.44), channel_id=1, source_target_pairs={{16,32},{17,33},{18,34},{19,35},{20,36},{21,37},{22,38},{23,39},{2... | collective-permute-start | bytes 786440 | tf_op jit(solution)/shard_map/ppermute | solution.py:603
  6.9 18.4 %collective-permute-start.2 = (f32[4,4,64,128]{3,2,1,0:T(8,128)S(1)}, f32[4,4,64,128]{3,2,1,0:T(8,128)S(1)}, u32[]{:S(2)}, u32[]{:S(2)}) collective-permute-start(f32[4,4,64,128]{3,2,1,0:T(8,128)S(1)} %get-tuple-element.49), channel_id=1, source_target_pairs={{1,2},{2,1},{3,4},{4,3},{5,6},{6,5},{7,8},{8,7},{9,10},{10,9},{11,... | collective-permute-start | bytes 1572872 | tf_op jit(solution)/shard_map/ppermute | solution.py:603
  7.6 18.9 %collective-permute-start.3 = (f32[4,4,64,128]{3,2,1,0:T(8,128)S(1)}, f32[4,4,64,128]{3,2,1,0:T(8,128)S(1)}, u32[]{:S(2)}, u32[]{:S(2)}) collective-permute-start(f32[4,4,64,128]{3,2,1,0:T(8,128)S(1)} %get-tuple-element.50), channel_id=1, source_target_pairs={{0,1},{1,0},{2,3},{3,2},{4,5},{5,4},{6,7},{7,6},{8,9},{9,8},{10,11... | collective-permute-start | bytes 1572872 | tf_op jit(solution)/shard_map/ppermute | solution.py:603
  14.4 2.2 %copy-start.2 = (s32[3]{0:T(128)S(1)}, s32[3]{0:T(128)}, u32[]{:S(2)}) copy-start(s32[3]{0:T(128)} %cell.7) | copy-start | bytes 40
  18.8 11.5 %collective-permute-start.4 = (f32[4,4,72,128]{3,2,1,0:T(8,128)S(1)}, f32[4,4,72,128]{3,2,1,0:T(8,128)S(1)}, u32[]{:S(2)}, u32[]{:S(2)}) collective-permute-start(f32[4,4,72,128]{3,2,1,0:T(8,128)S(1)} %get-tuple-element.52.sent), channel_id=1, source_target_pairs={{1,2},{2,1},{3,4},{4,3},{5,6},{6,5},{7,8},{8,7},{9,10},{10,9},{11,... | collective-permute-start | bytes 1769480 | tf_op jit(solution)/shard_map/ppermute | solution.py:603
  19.5 19.6 %collective-permute-start.5 = (f32[4,4,72,128]{3,2,1,0:T(8,128)S(1)}, f32[4,4,72,128]{3,2,1,0:T(8,128)S(1)}, u32[]{:S(2)}, u32[]{:S(2)}) collective-permute-start(f32[4,4,72,128]{3,2,1,0:T(8,128)S(1)} %get-tuple-element.61), channel_id=1, source_target_pairs={{0,1},{1,0},{2,3},{3,2},{4,5},{5,4},{6,7},{7,6},{8,9},{9,8},{10,11... | collective-permute-start | bytes 1769480 | tf_op jit(solution)/shard_map/ppermute | solution.py:603
  26.5 3.9 %copy-start.1 = (f32[4,8]{1,0:T(4,128)S(1)}, f32[4,8]{1,0:T(4,128)}, u32[]{:S(2)}) copy-start(f32[4,8]{1,0:T(4,128)} %transfer.3) | copy-start | bytes 388

commit v12 on v11

--- a/solution.py
+++ b/solution.py
@@ -294,8 +294,8 @@
 
 
 ORDERS = (
-    (4, 9, 7, 10, 1, 5, 15, 13, 12, 3, 2, 14, 11, 8, 0, 6),
-    (14, 8, 0, 9, 2, 1, 15, 3, 12, 13, 6, 4, 5, 11, 7, 10),
+    (8, 2, 0, 15, 1, 13, 12, 9, 3, 7, 4, 10, 14, 11, 6, 5),
+    (10, 15, 7, 4, 12, 5, 8, 0, 13, 3, 2, 1, 6, 9, 14, 11),
 )
 
 

time: 62.5 us -> 61.5 us (0.984)
  the two profiles are of different devices: /device:TPU:256 before, /device:TPU:224 now
where the time goes in v12:
time: 61.5 us; the launch traced here: 61.2 us
  blocking collectives  18.4 us (30%)
  Pallas kernels  18.1 us (29%)
  starting transfers between devices  17.3 us (28%)
  waiting for transfers between devices  5.87 us (10%)
  between operations  1.46 us (2%)
    all_to_all x1, blocking collectives, on_device(): lax.all_to_all(partial, ('lat', 'dep'), 0, 0, axis_index_groups=groups, t...  18.4 us
    ppermute x6, starting transfers between devices, swap(): return lax.ppermute(v, ('lat', 'dep'), swaps(n_lat, n_dep, kind))  17.3 us
    ppermute x6, waiting for transfers between devices, swap(): return lax.ppermute(v, ('lat', 'dep'), swaps(n_lat, n_dep, kind))  5.87 us
    pallas_call x1, Pallas kernels, on_device(): pl.pallas_call(couple, in_specs=[SMEM] + [VMEM] * 9 + [pl.BlockSpec(memor...  3.85 us
    pallas_call x1, Pallas kernels, on_device(): pl.pallas_call(functools.partial(finish_second, n_dep), in_specs=[SMEM, V...  3.67 us
    pallas_call x1, Pallas kernels, on_device(): pl.pallas_call(functools.partial(finish_first, n_dep), in_specs=[SMEM, VM...  2.82 us
    pallas_call x1, Pallas kernels, on_device(): pl.pallas_call(pack, in_specs=[HBM] * 4, out_specs=[VMEM] * 7, out_shape=...  2.19 us
    pallas_call x1, Pallas kernels, on_device(): pl.pallas_call(advance_inner, in_specs=[SMEM] * 2 + [VMEM] * 3, out_specs...  2.14 us
  transfers between devices with their start and end apart: 6, of which 1 were waited for; matrix products, arithmetic and copies ran while one was open for 0% of the time, Pallas kernels for 18%

profile of v12, /device:TPU:224, one launch (start us, length us, event | category | flops | bytes accessed | tf_op | source)
XLA Modules:
  0.0 61.2 jit_solution(5077707374301605804)
XLA Ops:
  0.6 0.0 copy-start
  0.6 2.2 %pack.1 = (f32[4,4,64,128]{3,2,1,0:T(8,128)S(1)}, f32[4,4,64,128]{3,2,1,0:T(8,128)S(1)}, f32[8,4,16,128]{3,2,1,0:T(8,128)S(1)}, f32[8,4,16,128]{3,2,1,0:T(8,128)...) custom-call(f32[16]{0:T(128)} %courant.1, f32[8,64,512]{2,1,0:T(8,128)} %now_in.1, ...), custom_call_target="tpu_custom_call" | custom-call | tf_op jit(solution)/shard_map/pack/pallas_call | solution.py:622
  2.8 1.9 %collective-permute-start = (f32[8,4,16,128]{3,2,1,0:T(8,128)S(1)}, f32[8,4,16,128]{3,2,1,0:T(8,128)S(1)}, u32[]{:S(2)}, u32[]{:S(2)}) collective-permute-start(f32[8,4,16,128]{3,2,1,0:T(8,128)S(1)} %get-tuple-element.43), channel_id=1, source_target_pairs={{0,16},{1,17},{2,18},{3,19},{4,20},{5,21},{6,22},{7,23},{8,24},{9,... | collective-permute-start | bytes 786440 | tf_op jit(solution)/shard_map/ppermute | solution.py:603
  4.8 2.1 %collective-permute-start.1 = (f32[8,4,16,128]{3,2,1,0:T(8,128)S(1)}, f32[8,4,16,128]{3,2,1,0:T(8,128)S(1)}, u32[]{:S(2)}, u32[]{:S(2)}) collective-permute-start(f32[8,4,16,128]{3,2,1,0:T(8,128)S(1)} %get-tuple-element.44), channel_id=1, source_target_pairs={{16,32},{17,33},{18,34},{19,35},{20,36},{21,37},{22,38},{23,39},{2... | collective-permute-start | bytes 786440 | tf_op jit(solution)/shard_map/ppermute | solution.py:603
  6.9 0.7 %collective-permute-start.2 = (f32[4,4,64,128]{3,2,1,0:T(8,128)S(1)}, f32[4,4,64,128]{3,2,1,0:T(8,128)S(1)}, u32[]{:S(2)}, u32[]{:S(2)}) collective-permute-start(f32[4,4,64,128]{3,2,1,0:T(8,128)S(1)} %get-tuple-element.49), channel_id=1, source_target_pairs={{1,2},{2,1},{3,4},{4,3},{5,6},{6,5},{7,8},{8,7},{9,10},{10,9},{11,... | collective-permute-start | bytes 1572872 | tf_op jit(solution)/shard_map/ppermute | solution.py:603
  7.6 6.1 %collective-permute-start.3 = (f32[4,4,64,128]{3,2,1,0:T(8,128)S(1)}, f32[4,4,64,128]{3,2,1,0:T(8,128)S(1)}, u32[]{:S(2)}, u32[]{:S(2)}) collective-permute-start(f32[4,4,64,128]{3,2,1,0:T(8,128)S(1)} %get-tuple-element.50), channel_id=1, source_target_pairs={{0,1},{1,0},{2,3},{3,2},{4,5},{5,4},{6,7},{7,6},{8,9},{9,8},{10,11... | collective-permute-start | bytes 1572872 | tf_op jit(solution)/shard_map/ppermute | solution.py:603
  14.4 0.0 copy-done
  14.4 0.0 copy-start.2
  14.4 2.1 %advance_inner.1 = (f32[12,4,96,128]{3,2,1,0:T(8,128)S(1)}, f32[8,4,64,128]{3,2,1,0:T(8,128)S(1)}, f32[12,4,96,128]{3,2,1,0:T(8,128)S(1)}, f32[8,4,16,128]{3,2,1...) custom-call(f32[16]{0:T(128)S(1)} %copy-done, s32[1]{0:T(128)S(6)} %copy.27.start, ...), custom_call_target="tpu_custom_call" | custom-call | flops 3000000000 | bytes 9000000 | tf_op jit(solution)/shard_map/advance_inner/pallas_call | solution.py:639
  16.5 0.0 collective-permute-done.lat_a
  16.5 0.0 collective-permute-done.1.lat_b
  16.5 0.0 copy-done.2
  16.6 2.1 %advance_outer.1 = (f32[12,4,96,128]{3,2,1,0:T(8,128)S(1)}, f32[12,4,96,128]{3,2,1,0:T(8,128)S(1)}, f32[8,4,16,128]{3,2,1,0:T(8,128)S(1)}, f32[8,4,16,128]{3,2,1,0:T(8,128)S(1)}, f32[4,4,96,128]{3,2,1,0:T(8,128)S(1)}) custom-call(s32[3]{0:T(128)S(1)} %copy-done.2, ...), custom_call_target="tpu_custom_call", output_to_operand_aliasing={{0}: (3, {}), {1}: (5, {})} | custom-call | flops 5000000000 | bytes 15000000 | tf_op jit(solution)/shard_map/advance_outer/pallas_call | solution.py:648
  18.7 0.1 pack_late.1
  18.8 0.7 %collective-permute-start.4 = (f32[4,4,72,128]{3,2,1,0:T(8,128)S(1)}, f32[4,4,72,128]{3,2,1,0:T(8,128)S(1)}, u32[]{:S(2)}, u32[]{:S(2)}) collective-permute-start(f32[4,4,72,128]{3,2,1,0:T(8,128)S(1)} %get-tuple-element.52.sent), channel_id=1, source_target_pairs={{1,2},{2,1},{3,4},{4,3},{5,6},{6,5},{7,8},{8,7},{9,10},{10,9},{11,... | collective-permute-start | bytes 1769480 | tf_op jit(solution)/shard_map/ppermute | solution.py:603
  19.5 5.8 %collective-permute-start.5 = (f32[4,4,72,128]{3,2,1,0:T(8,128)S(1)}, f32[4,4,72,128]{3,2,1,0:T(8,128)S(1)}, u32[]{:S(2)}, u32[]{:S(2)}) collective-permute-start(f32[4,4,72,128]{3,2,1,0:T(8,128)S(1)} %get-tuple-element.61), channel_id=1, source_target_pairs={{0,1},{1,0},{2,3},{3,2},{4,5},{5,4},{6,7},{7,6},{8,9},{9,8},{10,11... | collective-permute-start | bytes 1769480 | tf_op jit(solution)/shard_map/ppermute | solution.py:603
  25.3 0.0 collective-permute-done.2.early_a
  25.3 0.0 collective-permute-done.3.early_b
  25.3 0.0 copy-start.1
  25.3 3.9 %couple.1 = (f32[12,4,96,128]{3,2,1,0:T(8,128)S(1)}, f32[12,4,96,128]{3,2,1,0:T(8,128)S(1)}, f32[4,4,96,128]{3,2,1,0:T(8,128)S(1)}, f32[4,4,64,128]{3,2,1,0:T(8,128)S(1)}, f32[4,4,64,128]{3,2,1,0:T(8,128)S(1)}) custom-call(s32[3]{0:T(128)S(1)} %copy-done.2, f32[8,128]{1,0:T(8,128)S(1)} %get-tuple-element.37.amplitudes, ...), custom_call_target="tpu_custom_call", output_to_operand_aliasing={{0}: (7, {})} | custom-call | flops 4000000000 | bytes 12000000 | tf_op jit(solution)/shard_map/couple/pallas_call | solution.py:669
  29.2 0.0 collective-permute-done.4.late
  29.2 0.0 copy-done.1
  29.2 2.8 %finish_first.1 = (f32[4,64,512]{2,1,0:T(8,128)S(1)}, f32[10,4,64,128]{3,2,1,0:T(8,128)S(1)}, f32[12,4,96,128]{3,2,1,0:T(8,128)S(1)}, f32[12,4,96,128]{3,2,1,0:T(8,128)S(1)}, f32[4,4,96,128]{3,2,1,0:T(8,128)S(1)}) custom-call(s32[3]{0:T(128)S(1)} %copy-done.2, ...), custom_call_target="tpu_custom_call", output_to_operand_aliasing={{2}: (8, {}), {3}: (9, {}), {4}: (10, {})} | custom-call | flops 4000000000 | bytes 12000000 | tf_op jit(solution)/shard_map/finish_first/pallas_call | solution.py:681
  32.0 5.9 %collective-permute-done.5.late = f32[4,4,72,128]{3,2,1,0:T(8,128)S(1)} collective-permute-done((f32[4,4,72,128]{3,2,1,0:T(8,128)S(1)}, f32[4,4,72,128]{3,2,1,0:T(8,128)S(1)}, u32[]{:S(2)}, u32[]{:S(2)}) %collective-permute-start.5) | collective-permute-done | bytes 589856 | tf_op jit(solution)/shard_map/ppermute | solution.py:603
  37.9 3.7 %finish_second.1 = (f32[8,64,512]{2,1,0:T(8,128)}, f32[16,64,128]{2,1,0:T(8,128)S(1)}, f32[12,4,96,128]{3,2,1,0:T(8,128)S(1)}, f32[12,4,96,128]{3,2,1,0:T(8,128)S(1)}, f32[4,4,96,128]{3,2,1,0:T(8,128)S(1)}) custom-call(s32[3]{0:T(128)S(1)} %copy-done.2, ...), custom_call_target="tpu_custom_call", output_to_operand_aliasing={{2}: (8, {}), {3}: (9, {}), {4}: (10, {})} | custom-call | flops 4000000000 | bytes 12000000 | tf_op jit(solution)/shard_map/finish_second/pallas_call | solution.py:692
  41.6 18.4 %all_to_all.5.parts = f32[16,64,128]{2,1,0:T(8,128)S(1)} all-to-all(f32[16,64,128]{2,1,0:T(8,128)S(1)} %get-tuple-element.65), channel_id=1, replica_groups={{8,2,0,15,1,13,12,9,3,7,4,10,14,11,6,5},{26,31,23,20,28,21,24,16,29,19,..., dimensions={0} | all-to-all | bytes 1048576 | tf_op jit(solution)/shard_map/all_to_all | solution.py:704
  60.0 1.2 %composite.1 = f32[128,64]{1,0:T(8,128)} custom-call(f32[16,64,128]{2,1,0:T(8,128)S(1)} %all_to_all.5.parts), custom_call_target="tpu_custom_call" | custom-call | tf_op jit(solution)/shard_map/composite/pallas_call | solution.py:705
Async XLA Ops:
  0.6 13.7 %copy-start = (f32[16]{0:T(128)S(1)}, f32[16]{0:T(128)}, u32[]{:S(2)}) copy-start(f32[16]{0:T(128)} %courant.1) | copy-start | bytes 196
  2.8 13.7 %collective-permute-start = (f32[8,4,16,128]{3,2,1,0:T(8,128)S(1)}, f32[8,4,16,128]{3,2,1,0:T(8,128)S(1)}, u32[]{:S(2)}, u32[]{:S(2)}) collective-permute-start(f32[8,4,16,128]{3,2,1,0:T(8,128)S(1)} %get-tuple-element.43), channel_id=1, source_target_pairs={{0,16},{1,17},{2,18},{3,19},{4,20},{5,21},{6,22},{7,23},{8,24},{9,... | collective-permute-start | bytes 786440 | tf_op jit(solution)/shard_map/ppermute | solution.py:603
  4.8 11.8 %collective-permute-start.1 = (f32[8,4,16,128]{3,2,1,0:T(8,128)S(1)}, f32[8,4,16,128]{3,2,1,0:T(8,128)S(1)}, u32[]{:S(2)}, u32[]{:S(2)}) collective-permute-start(f32[8,4,16,128]{3,2,1,0:T(8,128)S(1)} %get-tuple-element.44), channel_id=1, source_target_pairs={{16,32},{17,33},{18,34},{19,35},{20,36},{21,37},{22,38},{23,39},{2... | collective-permute-start | bytes 786440 | tf_op jit(solution)/shard_map/ppermute | solution.py:603
  6.9 18.4 %collective-permute-start.2 = (f32[4,4,64,128]{3,2,1,0:T(8,128)S(1)}, f32[4,4,64,128]{3,2,1,0:T(8,128)S(1)}, u32[]{:S(2)}, u32[]{:S(2)}) collective-permute-start(f32[4,4,64,128]{3,2,1,0:T(8,128)S(1)} %get-tuple-element.49), channel_id=1, source_target_pairs={{1,2},{2,1},{3,4},{4,3},{5,6},{6,5},{7,8},{8,7},{9,10},{10,9},{11,... | collective-permute-start | bytes 1572872 | tf_op jit(solution)/shard_map/ppermute | solution.py:603
  7.6 17.7 %collective-permute-start.3 = (f32[4,4,64,128]{3,2,1,0:T(8,128)S(1)}, f32[4,4,64,128]{3,2,1,0:T(8,128)S(1)}, u32[]{:S(2)}, u32[]{:S(2)}) collective-permute-start(f32[4,4,64,128]{3,2,1,0:T(8,128)S(1)} %get-tuple-element.50), channel_id=1, source_target_pairs={{0,1},{1,0},{2,3},{3,2},{4,5},{5,4},{6,7},{7,6},{8,9},{9,8},{10,11... | collective-permute-start | bytes 1572872 | tf_op jit(solution)/shard_map/ppermute | solution.py:603
  14.4 2.2 %copy-start.2 = (s32[3]{0:T(128)S(1)}, s32[3]{0:T(128)}, u32[]{:S(2)}) copy-start(s32[3]{0:T(128)} %cell.7) | copy-start | bytes 40
  18.8 10.4 %collective-permute-start.4 = (f32[4,4,72,128]{3,2,1,0:T(8,128)S(1)}, f32[4,4,72,128]{3,2,1,0:T(8,128)S(1)}, u32[]{:S(2)}, u32[]{:S(2)}) collective-permute-start(f32[4,4,72,128]{3,2,1,0:T(8,128)S(1)} %get-tuple-element.52.sent), channel_id=1, source_target_pairs={{1,2},{2,1},{3,4},{4,3},{5,6},{6,5},{7,8},{8,7},{9,10},{10,9},{11,... | collective-permute-start | bytes 1769480 | tf_op jit(solution)/shard_map/ppermute | solution.py:603
  19.5 18.4 %collective-permute-start.5 = (f32[4,4,72,128]{3,2,1,0:T(8,128)S(1)}, f32[4,4,72,128]{3,2,1,0:T(8,128)S(1)}, u32[]{:S(2)}, u32[]{:S(2)}) collective-permute-start(f32[4,4,72,128]{3,2,1,0:T(8,128)S(1)} %get-tuple-element.61), channel_id=1, source_target_pairs={{0,1},{1,0},{2,3},{3,2},{4,5},{5,4},{6,7},{7,6},{8,9},{9,8},{10,11... | collective-permute-start | bytes 1769480 | tf_op jit(solution)/shard_map/ppermute | solution.py:603
  25.3 3.9 %copy-start.1 = (f32[4,8]{1,0:T(4,128)S(1)}, f32[4,8]{1,0:T(4,128)}, u32[]{:S(2)}) copy-start(f32[4,8]{1,0:T(4,128)} %transfer.3) | copy-start | bytes 388

commit v13 on v12

--- a/solution.py
+++ b/solution.py
@@ -427,7 +427,7 @@
             two[n_next + 2, i, rows, :] -= stiff[n_next, i, own, :] * one_near
         return carry
 
-    lax.fori_loop(0, X // 8, inner, 0)
+    lax.fori_loop(0, X // 8, inner, 0, unroll=2)
     for row in (CORE, CORE + X - 8):
         for k, i, v in halo_step(delta, one, halo_stiff, base, near, far, n_in, n_next, row, masks):
             two[zi + k, i, row : row + 8, :] = late[2 + k, i, row - CORE : row - CORE + 8, :] + v
@@ -513,7 +513,7 @@
                 looked[j, i, own, :] = v
         return carry
 
-    lax.fori_loop(0, X // 8, render, 0)
+    lax.fori_loop(0, X // 8, render, 0, unroll=2)
 
 
 def finish_second(
@@ -556,7 +556,7 @@
                 partial[rank(4 * i + q), own, :] = packed
         return carry
 
-    lax.fori_loop(0, X // 8, render, 0)
+    lax.fori_loop(0, X // 8, render, 0, unroll=2)
     for copy in copies:
         copy.wait()
 

time: 61.5 us -> 60.9 us (level)
  no operation moved by 1% of the time
where the time goes in v13:
time: 60.9 us; the launch traced here: 60.6 us
  blocking collectives  18.2 us (30%)
  Pallas kernels  17.5 us (29%)
  starting transfers between devices  17.3 us (28%)
  waiting for transfers between devices  6.06 us (10%)
  between operations  1.46 us (2%)
    all_to_all x1, blocking collectives, on_device(): lax.all_to_all(partial, ('lat', 'dep'), 0, 0, axis_index_groups=groups, t...  18.2 us
    ppermute x6, starting transfers between devices, swap(): return lax.ppermute(v, ('lat', 'dep'), swaps(n_lat, n_dep, kind))  17.3 us
    ppermute x6, waiting for transfers between devices, swap(): return lax.ppermute(v, ('lat', 'dep'), swaps(n_lat, n_dep, kind))  6.06 us
    pallas_call x1, Pallas kernels, on_device(): pl.pallas_call(couple, in_specs=[SMEM] + [VMEM] * 9 + [pl.BlockSpec(memor...  3.85 us
    pallas_call x1, Pallas kernels, on_device(): pl.pallas_call(functools.partial(finish_second, n_dep), in_specs=[SMEM, V...  3.28 us
    pallas_call x1, Pallas kernels, on_device(): pl.pallas_call(functools.partial(finish_first, n_dep), in_specs=[SMEM, VM...  2.63 us
    pallas_call x1, Pallas kernels, on_device(): pl.pallas_call(pack, in_specs=[HBM] * 4, out_specs=[VMEM] * 7, out_shape=...  2.19 us
    pallas_call x1, Pallas kernels, on_device(): pl.pallas_call(advance_inner, in_specs=[SMEM] * 2 + [VMEM] * 3, out_specs...  2.14 us
  transfers between devices with their start and end apart: 6, of which 1 were waited for; matrix products, arithmetic and copies ran while one was open for 0% of the time, Pallas kernels for 18%

profile of v13, /device:TPU:224, one launch (start us, length us, event | category | flops | bytes accessed | tf_op | source)
XLA Modules:
  0.0 60.6 jit_solution(5202334865956187510)
XLA Ops:
  0.6 0.0 copy-start
  0.6 2.2 %pack.1 = (f32[4,4,64,128]{3,2,1,0:T(8,128)S(1)}, f32[4,4,64,128]{3,2,1,0:T(8,128)S(1)}, f32[8,4,16,128]{3,2,1,0:T(8,128)S(1)}, f32[8,4,16,128]{3,2,1,0:T(8,128)...) custom-call(f32[16]{0:T(128)} %courant.1, f32[8,64,512]{2,1,0:T(8,128)} %now_in.1, ...), custom_call_target="tpu_custom_call" | custom-call | tf_op jit(solution)/shard_map/pack/pallas_call | solution.py:622
  2.8 1.9 %collective-permute-start = (f32[8,4,16,128]{3,2,1,0:T(8,128)S(1)}, f32[8,4,16,128]{3,2,1,0:T(8,128)S(1)}, u32[]{:S(2)}, u32[]{:S(2)}) collective-permute-start(f32[8,4,16,128]{3,2,1,0:T(8,128)S(1)} %get-tuple-element.43), channel_id=1, source_target_pairs={{0,16},{1,17},{2,18},{3,19},{4,20},{5,21},{6,22},{7,23},{8,24},{9,... | collective-permute-start | bytes 786440 | tf_op jit(solution)/shard_map/ppermute | solution.py:603
  4.8 2.1 %collective-permute-start.1 = (f32[8,4,16,128]{3,2,1,0:T(8,128)S(1)}, f32[8,4,16,128]{3,2,1,0:T(8,128)S(1)}, u32[]{:S(2)}, u32[]{:S(2)}) collective-permute-start(f32[8,4,16,128]{3,2,1,0:T(8,128)S(1)} %get-tuple-element.44), channel_id=1, source_target_pairs={{16,32},{17,33},{18,34},{19,35},{20,36},{21,37},{22,38},{23,39},{2... | collective-permute-start | bytes 786440 | tf_op jit(solution)/shard_map/ppermute | solution.py:603
  6.9 0.7 %collective-permute-start.2 = (f32[4,4,64,128]{3,2,1,0:T(8,128)S(1)}, f32[4,4,64,128]{3,2,1,0:T(8,128)S(1)}, u32[]{:S(2)}, u32[]{:S(2)}) collective-permute-start(f32[4,4,64,128]{3,2,1,0:T(8,128)S(1)} %get-tuple-element.49), channel_id=1, source_target_pairs={{1,2},{2,1},{3,4},{4,3},{5,6},{6,5},{7,8},{8,7},{9,10},{10,9},{11,... | collective-permute-start | bytes 1572872 | tf_op jit(solution)/shard_map/ppermute | solution.py:603
  7.6 6.1 %collective-permute-start.3 = (f32[4,4,64,128]{3,2,1,0:T(8,128)S(1)}, f32[4,4,64,128]{3,2,1,0:T(8,128)S(1)}, u32[]{:S(2)}, u32[]{:S(2)}) collective-permute-start(f32[4,4,64,128]{3,2,1,0:T(8,128)S(1)} %get-tuple-element.50), channel_id=1, source_target_pairs={{0,1},{1,0},{2,3},{3,2},{4,5},{5,4},{6,7},{7,6},{8,9},{9,8},{10,11... | collective-permute-start | bytes 1572872 | tf_op jit(solution)/shard_map/ppermute | solution.py:603
  14.4 0.0 copy-done
  14.4 0.0 copy-start.2
  14.4 2.1 %advance_inner.1 = (f32[12,4,96,128]{3,2,1,0:T(8,128)S(1)}, f32[8,4,64,128]{3,2,1,0:T(8,128)S(1)}, f32[12,4,96,128]{3,2,1,0:T(8,128)S(1)}, f32[8,4,16,128]{3,2,1...) custom-call(f32[16]{0:T(128)S(1)} %copy-done, s32[1]{0:T(128)S(6)} %copy.27.start, ...), custom_call_target="tpu_custom_call" | custom-call | flops 3000000000 | bytes 9000000 | tf_op jit(solution)/shard_map/advance_inner/pallas_call | solution.py:639
  16.5 0.0 collective-permute-done.lat_a
  16.5 0.0 collective-permute-done.1.lat_b
  16.5 0.0 copy-done.2
  16.6 2.1 %advance_outer.1 = (f32[12,4,96,128]{3,2,1,0:T(8,128)S(1)}, f32[12,4,96,128]{3,2,1,0:T(8,128)S(1)}, f32[8,4,16,128]{3,2,1,0:T(8,128)S(1)}, f32[8,4,16,128]{3,2,1,0:T(8,128)S(1)}, f32[4,4,96,128]{3,2,1,0:T(8,128)S(1)}) custom-call(s32[3]{0:T(128)S(1)} %copy-done.2, ...), custom_call_target="tpu_custom_call", output_to_operand_aliasing={{0}: (3, {}), {1}: (5, {})} | custom-call | flops 5000000000 | bytes 15000000 | tf_op jit(solution)/shard_map/advance_outer/pallas_call | solution.py:648
  18.7 0.1 pack_late.1
  18.8 0.7 %collective-permute-start.4 = (f32[4,4,72,128]{3,2,1,0:T(8,128)S(1)}, f32[4,4,72,128]{3,2,1,0:T(8,128)S(1)}, u32[]{:S(2)}, u32[]{:S(2)}) collective-permute-start(f32[4,4,72,128]{3,2,1,0:T(8,128)S(1)} %get-tuple-element.52.sent), channel_id=1, source_target_pairs={{1,2},{2,1},{3,4},{4,3},{5,6},{6,5},{7,8},{8,7},{9,10},{10,9},{11,... | collective-permute-start | bytes 1769480 | tf_op jit(solution)/shard_map/ppermute | solution.py:603
  19.5 5.8 %collective-permute-start.5 = (f32[4,4,72,128]{3,2,1,0:T(8,128)S(1)}, f32[4,4,72,128]{3,2,1,0:T(8,128)S(1)}, u32[]{:S(2)}, u32[]{:S(2)}) collective-permute-start(f32[4,4,72,128]{3,2,1,0:T(8,128)S(1)} %get-tuple-element.61), channel_id=1, source_target_pairs={{0,1},{1,0},{2,3},{3,2},{4,5},{5,4},{6,7},{7,6},{8,9},{9,8},{10,11... | collective-permute-start | bytes 1769480 | tf_op jit(solution)/shard_map/ppermute | solution.py:603
  25.3 0.0 collective-permute-done.2.early_a
  25.3 0.0 collective-permute-done.3.early_b
  25.3 0.0 copy-start.1
  25.3 3.9 %couple.1 = (f32[12,4,96,128]{3,2,1,0:T(8,128)S(1)}, f32[12,4,96,128]{3,2,1,0:T(8,128)S(1)}, f32[4,4,96,128]{3,2,1,0:T(8,128)S(1)}, f32[4,4,64,128]{3,2,1,0:T(8,128)S(1)}, f32[4,4,64,128]{3,2,1,0:T(8,128)S(1)}) custom-call(s32[3]{0:T(128)S(1)} %copy-done.2, f32[8,128]{1,0:T(8,128)S(1)} %get-tuple-element.37.amplitudes, ...), custom_call_target="tpu_custom_call", output_to_operand_aliasing={{0}: (7, {})} | custom-call | flops 4000000000 | bytes 12000000 | tf_op jit(solution)/shard_map/couple/pallas_call | solution.py:669
  29.2 0.0 collective-permute-done.4.late
  29.2 0.0 copy-done.1
  29.2 2.6 %finish_first.1 = (f32[4,64,512]{2,1,0:T(8,128)S(1)}, f32[10,4,64,128]{3,2,1,0:T(8,128)S(1)}, f32[12,4,96,128]{3,2,1,0:T(8,128)S(1)}, f32[12,4,96,128]{3,2,1,0:T(8,128)S(1)}, f32[4,4,96,128]{3,2,1,0:T(8,128)S(1)}) custom-call(s32[3]{0:T(128)S(1)} %copy-done.2, ...), custom_call_target="tpu_custom_call", output_to_operand_aliasing={{2}: (8, {}), {3}: (9, {}), {4}: (10, {})} | custom-call | flops 4000000000 | bytes 12000000 | tf_op jit(solution)/shard_map/finish_first/pallas_call | solution.py:681
  31.9 6.0 %collective-permute-done.5.late = f32[4,4,72,128]{3,2,1,0:T(8,128)S(1)} collective-permute-done((f32[4,4,72,128]{3,2,1,0:T(8,128)S(1)}, f32[4,4,72,128]{3,2,1,0:T(8,128)S(1)}, u32[]{:S(2)}, u32[]{:S(2)}) %collective-permute-start.5) | collective-permute-done | bytes 589856 | tf_op jit(solution)/shard_map/ppermute | solution.py:603
  37.9 3.3 %finish_second.1 = (f32[8,64,512]{2,1,0:T(8,128)}, f32[16,64,128]{2,1,0:T(8,128)S(1)}, f32[12,4,96,128]{3,2,1,0:T(8,128)S(1)}, f32[12,4,96,128]{3,2,1,0:T(8,128)S(1)}, f32[4,4,96,128]{3,2,1,0:T(8,128)S(1)}) custom-call(s32[3]{0:T(128)S(1)} %copy-done.2, ...), custom_call_target="tpu_custom_call", output_to_operand_aliasing={{2}: (8, {}), {3}: (9, {}), {4}: (10, {})} | custom-call | flops 4000000000 | bytes 12000000 | tf_op jit(solution)/shard_map/finish_second/pallas_call | solution.py:692
  41.2 18.2 %all_to_all.5.parts = f32[16,64,128]{2,1,0:T(8,128)S(1)} all-to-all(f32[16,64,128]{2,1,0:T(8,128)S(1)} %get-tuple-element.65), channel_id=1, replica_groups={{8,2,0,15,1,13,12,9,3,7,4,10,14,11,6,5},{26,31,23,20,28,21,24,16,29,19,..., dimensions={0} | all-to-all | bytes 1048576 | tf_op jit(solution)/shard_map/all_to_all | solution.py:704
  59.4 1.2 %composite.1 = f32[128,64]{1,0:T(8,128)} custom-call(f32[16,64,128]{2,1,0:T(8,128)S(1)} %all_to_all.5.parts), custom_call_target="tpu_custom_call" | custom-call | tf_op jit(solution)/shard_map/composite/pallas_call | solution.py:705
Async XLA Ops:
  0.6 13.7 %copy-start = (f32[16]{0:T(128)S(1)}, f32[16]{0:T(128)}, u32[]{:S(2)}) copy-start(f32[16]{0:T(128)} %courant.1) | copy-start | bytes 196
  2.8 13.7 %collective-permute-start = (f32[8,4,16,128]{3,2,1,0:T(8,128)S(1)}, f32[8,4,16,128]{3,2,1,0:T(8,128)S(1)}, u32[]{:S(2)}, u32[]{:S(2)}) collective-permute-start(f32[8,4,16,128]{3,2,1,0:T(8,128)S(1)} %get-tuple-element.43), channel_id=1, source_target_pairs={{0,16},{1,17},{2,18},{3,19},{4,20},{5,21},{6,22},{7,23},{8,24},{9,... | collective-permute-start | bytes 786440 | tf_op jit(solution)/shard_map/ppermute | solution.py:603
  4.8 11.8 %collective-permute-start.1 = (f32[8,4,16,128]{3,2,1,0:T(8,128)S(1)}, f32[8,4,16,128]{3,2,1,0:T(8,128)S(1)}, u32[]{:S(2)}, u32[]{:S(2)}) collective-permute-start(f32[8,4,16,128]{3,2,1,0:T(8,128)S(1)} %get-tuple-element.44), channel_id=1, source_target_pairs={{16,32},{17,33},{18,34},{19,35},{20,36},{21,37},{22,38},{23,39},{2... | collective-permute-start | bytes 786440 | tf_op jit(solution)/shard_map/ppermute | solution.py:603
  6.9 18.4 %collective-permute-start.2 = (f32[4,4,64,128]{3,2,1,0:T(8,128)S(1)}, f32[4,4,64,128]{3,2,1,0:T(8,128)S(1)}, u32[]{:S(2)}, u32[]{:S(2)}) collective-permute-start(f32[4,4,64,128]{3,2,1,0:T(8,128)S(1)} %get-tuple-element.49), channel_id=1, source_target_pairs={{1,2},{2,1},{3,4},{4,3},{5,6},{6,5},{7,8},{8,7},{9,10},{10,9},{11,... | collective-permute-start | bytes 1572872 | tf_op jit(solution)/shard_map/ppermute | solution.py:603
  7.6 17.7 %collective-permute-start.3 = (f32[4,4,64,128]{3,2,1,0:T(8,128)S(1)}, f32[4,4,64,128]{3,2,1,0:T(8,128)S(1)}, u32[]{:S(2)}, u32[]{:S(2)}) collective-permute-start(f32[4,4,64,128]{3,2,1,0:T(8,128)S(1)} %get-tuple-element.50), channel_id=1, source_target_pairs={{0,1},{1,0},{2,3},{3,2},{4,5},{5,4},{6,7},{7,6},{8,9},{9,8},{10,11... | collective-permute-start | bytes 1572872 | tf_op jit(solution)/shard_map/ppermute | solution.py:603
  14.4 2.2 %copy-start.2 = (s32[3]{0:T(128)S(1)}, s32[3]{0:T(128)}, u32[]{:S(2)}) copy-start(s32[3]{0:T(128)} %cell.7) | copy-start | bytes 40
  18.8 10.4 %collective-permute-start.4 = (f32[4,4,72,128]{3,2,1,0:T(8,128)S(1)}, f32[4,4,72,128]{3,2,1,0:T(8,128)S(1)}, u32[]{:S(2)}, u32[]{:S(2)}) collective-permute-start(f32[4,4,72,128]{3,2,1,0:T(8,128)S(1)} %get-tuple-element.52.sent), channel_id=1, source_target_pairs={{1,2},{2,1},{3,4},{4,3},{5,6},{6,5},{7,8},{8,7},{9,10},{10,9},{11,... | collective-permute-start | bytes 1769480 | tf_op jit(solution)/shard_map/ppermute | solution.py:603
  19.5 18.4 %collective-permute-start.5 = (f32[4,4,72,128]{3,2,1,0:T(8,128)S(1)}, f32[4,4,72,128]{3,2,1,0:T(8,128)S(1)}, u32[]{:S(2)}, u32[]{:S(2)}) collective-permute-start(f32[4,4,72,128]{3,2,1,0:T(8,128)S(1)} %get-tuple-element.61), channel_id=1, source_target_pairs={{0,1},{1,0},{2,3},{3,2},{4,5},{5,4},{6,7},{7,6},{8,9},{9,8},{10,11... | collective-permute-start | bytes 1769480 | tf_op jit(solution)/shard_map/ppermute | solution.py:603
  25.3 3.9 %copy-start.1 = (f32[4,8]{1,0:T(4,128)S(1)}, f32[4,8]{1,0:T(4,128)}, u32[]{:S(2)}) copy-start(f32[4,8]{1,0:T(4,128)} %transfer.3) | copy-start | bytes 388
